TPU v7x, 128 devices: a whole 4x4x4 slice. The times are simulated.
128 devices in a mesh: cells: 16 (over z, x), spots: 8 (over y, core).
Axes of the slice: x: 4, y: 4, z: 4, core: 2. Of those that a mesh axis runs over, the one named last changes fastest.
Arguments:
- map_logits: float32 [20480, 8192], P('cells', 'spots'), may hold values from -10 to 10
- filter_logits: float32 [20480], P('cells'), may hold values from -6 to 6
- expr: float32 [2048, 20480], P(None, 'cells'), may hold values from 0 to 2
- spatial: float32 [2048, 8192], P(None, 'spots'), may hold values from 0 to 2
- cell_type: int32 [20480], P('cells'), may hold values from -1 to 31, as said below
- slide_id: int32 [8192], P('spots'), may hold values from 0 to 2, as said below
- spot_mask: int32 [8192], P('spots'), may hold values 0 or 1
Outputs:
- loss_terms: float32 [5], replicated
- type_fraction: float32 [32, 8192], P(None, 'spots')
- grad_map: float32 [20480, 8192], P('cells', 'spots')
- grad_filter: float32 [20480], P('cells')
- grad_expr: float32 [2048, 20480], P('spots', 'cells')
Inputs may be any that keep to these rules, and one draw needn't show every extreme that they name: `cell_type`: rows come in one contiguous group per type label, every label of 0 to 31 present; each group is whole blocks of 128 rows, padded at its end with fewer than 128 rows of -1. `slide_id`: never falling; each slide covers 8192 // 4 spots or more.
All inputs are finite; a program needn't handle non-finite values. No bound on the sum of `spot_mask` on one device may be relied on, other than what follows from the above.
Results may differ from a plain program's by a relative error of at most 0.0003.
Values sent between devices are 32-bit elements; how exact they have to be, the bound alone decides.
No kernel may reach another device: no remote copies, remote signals or barrier semaphores. Data moves between devices by JAX's collectives and lax.ppermute only.
A program may use at most 128 MiB of HBM per device.

v0:
```python
import functools

import jax
import jax.numpy as jnp
from jax import lax
from jax.experimental import pallas as pl
from jax.experimental.pallas import tpu as pltpu
from jax.sharding import PartitionSpec as P

TYPES = 32
SLIDES = 3
RING = 4
F32 = jnp.float32
BF16 = jnp.bfloat16


def vmem(mib):
    return pltpu.CompilerParams(vmem_limit_bytes=mib << 20)


def fixed(shape):
    return pl.BlockSpec(shape, lambda *_: (0,) * len(shape), pipeline_mode=pl.Buffered(1))


def streamed(array):
    return pltpu.with_memory_space_constraint(array, pltpu.HBM)


RESIDENT = pl.BlockSpec(memory_space=pltpu.VMEM)


def cost(flops, moved):
    return pl.CostEstimate(flops=int(flops) // 8, bytes_accessed=int(moved) // 8, transcendentals=0)


NO_COST = pl.CostEstimate(flops=0, bytes_accessed=0, transcendentals=0)


def route(target):
    def flat(z, x, y, core):
        return ((z % RING * RING + x % RING) * RING + y % RING) * 2 + core

    return [
        (flat(z, x, y, core), flat(*target(z, x, y, core)))
        for z in range(RING)
        for x in range(RING)
        for y in range(RING)
        for core in range(2)
    ]


def send(array, target):
    return lax.ppermute(array, ("cells", "spots"), route(target))


def along(array, step):
    return send(array, lambda z, x, y, c: (z, x + step, y, c) if c == 0 else (z + step, x, y, c))


def across(array, step):
    return send(array, lambda z, x, y, c: (z + step, x, y, c) if c == 0 else (z, x + step, y, c))


def up(array, step):
    return send(array, lambda z, x, y, c: (z, x, y + step, c))


def swap(array, mz, mx, my, mc):
    return send(array, lambda z, x, y, c: (z ^ mz, x ^ mx, y ^ my, c ^ mc))


def swap_along(array, mask):
    return send(array, lambda z, x, y, c: (z, x ^ mask, y, c) if c == 0 else (z ^ mask, x, y, c))


def swap_across(array, mask):
    return send(array, lambda z, x, y, c: (z ^ mask, x, y, c) if c == 0 else (z, x ^ mask, y, c))


def after(value, *others):
    return lax.optimization_barrier((value, *others))[0]


def split(value):
    high = value.astype(BF16)
    return high, (value - high.astype(F32)).astype(BF16)


def product(left, right, dims):
    def one(a, b):
        return lax.dot_general(a, b, (dims, ((), ())), preferred_element_type=F32)

    return one(left[0], right[0]) + one(left[0], right[1]) + one(left[1], right[0])


def gene_group(ids, step, half, sub):
    return ((ids[0] + step) & 3) * RING + ((ids[1] + 2 * half + sub) & 3)


PIECES = [
    (step, half, sub)
    for step, half in ((0, 0), (0, 1), (-1, 0), (-1, 1), (1, 0), (1, 1), (2, 0), (2, 1))
    for sub in range(2)
]


def pick(index, values):
    out = values[0]
    for k, value in enumerate(values[1:]):
        out = jnp.where(index == k + 1, value, out)
    return out


def stacked(rows):
    row = lax.broadcasted_iota(jnp.int32, (8, rows[0].shape[0]), 0)
    out = jnp.zeros(row.shape, F32)
    for k, value in enumerate(rows):
        out = jnp.where(row == k, value[None, :], out)
    return out


def as_column(row):
    return jnp.broadcast_to(row, (128, 128)).T[:, :1]


def expo_kernel(ids, logits, kind, filt, *refs):
    expr, (masses, types, totals, out0, out1) = refs[:4], refs[4:]
    step = pl.program_id(0)
    count = logits.shape[0] // 128

    @pl.when(step == 0)
    def _():
        for out in (types, totals, out0, out1):
            out[...] = jnp.zeros_like(out)

    keeps = []
    lane = lax.broadcasted_iota(jnp.int32, (1, totals.shape[1]), 1)
    cell_sums = jnp.zeros(lane.shape, F32)
    for part in range(count):
        rows = slice(part * 128, part * 128 + 128)
        label = kind[pl.ds(step * count + part, 1), :]
        valid = (label >= 0).astype(F32)
        keep = valid * jax.nn.sigmoid(filt[pl.ds(step * count + part, 1), :])
        keeps.append(keep)
        for k, one in enumerate((valid, keep, keep - keep * keep)):
            cell_sums += jnp.where(lane == k, jnp.sum(one, axis=1, keepdims=True), 0.0)
        expo = jnp.exp(logits[rows]) * as_column(valid)
        masses[0, rows], masses[1, rows] = split(expo)
        whole = jnp.sum(expo, axis=0, keepdims=True)
        kept = jnp.sum(expo * as_column(keep), axis=0, keepdims=True)
        row = lax.broadcasted_iota(jnp.int32, types.shape, 0)
        types[...] += jnp.where(row == jnp.max(label, axis=1, keepdims=True), whole, 0.0)
        row = lax.broadcasted_iota(jnp.int32, totals.shape, 0)
        totals[...] += jnp.where(row == 0, whole, jnp.where(row == 1, kept, 0.0))
    totals[2:3, :] += cell_sums
    weighted = jnp.concatenate([part[...].reshape(-1, logits.shape[0]) for part in expr])
    weighted = weighted * jnp.concatenate(keeps, axis=1)
    part = product(split(weighted), masses, ((1,), (0,)))
    half = part.shape[0] // 2
    for index, out in enumerate((out0, out1)):
        new = part[index * half : index * half + half].reshape(-1, 8, part.shape[1])
        out[: half // 8] += new
        out[half // 8] = totals[...]


def expo_call(ids, parts, logits, kind, filt, expr):
    cells, spots = logits.shape
    blocks, groups, rows, _ = expr.shape
    block = 256

    def genes(part, sub):
        return pl.BlockSpec(
            (blocks, 1, rows, block), lambda i, ids: (0, gene_group(ids, *part, sub), 0, i)
        )

    return pl.pallas_call(
        expo_kernel,
        grid_spec=pltpu.PrefetchScalarGridSpec(
            num_scalar_prefetch=1,
            grid=(cells // block,),
            in_specs=[
                pl.BlockSpec((block, spots), lambda i, w: (i, 0)),
                fixed(kind.shape),
                fixed(filt.shape),
            ]
            + [genes(part, sub) for part in parts for sub in range(2)],
            out_specs=[
                pl.BlockSpec((2, block, spots), lambda i, w: (0, i, 0)),
                fixed((TYPES, spots)),
                fixed((8, spots)),
                fixed((blocks * rows // 4 + 1, 8, spots)),
                fixed((blocks * rows // 4 + 1, 8, spots)),
            ],
        ),
        out_shape=[
            jax.ShapeDtypeStruct((2, cells, spots), BF16),
            jax.ShapeDtypeStruct((TYPES, spots), F32),
            jax.ShapeDtypeStruct((8, spots), F32),
            jax.ShapeDtypeStruct((blocks * rows // 4 + 1, 8, spots), F32),
            jax.ShapeDtypeStruct((blocks * rows // 4 + 1, 8, spots), F32),
        ],
        compiler_params=vmem(16),
        cost_estimate=cost(0, cells * spots * 8),
        name="expo",
    )(ids, streamed(logits), kind, filt, *[streamed(expr)] * 4)


def pred_kernel(ids, expr_a, expr_b, keep, masses, totals, *refs):
    more, outs = refs[:-2], refs[-2:]
    rows = 2 * expr_a.shape[0] * expr_a.shape[2]
    weighted = jnp.concatenate(
        [part[...].reshape(rows // 2, keep.shape[1]) for part in (expr_a, expr_b)]
    )
    part = product(split(weighted * keep[...]), masses, ((1,), (0,)))
    part = part.reshape(rows // 8, 8, part.shape[1])
    for step, out in enumerate(outs):

        @pl.when(pl.program_id(0) == step)
        def _(step=step, out=out):
            if more:
                out[: rows // 8] = part + more[step][: rows // 8]
                out[rows // 8] = totals[...] + more[step][rows // 8]
            else:
                out[: rows // 8] = part
                out[rows // 8] = totals[...]


def pred_call(ids, parts, expr, keep, masses, totals, more=()):
    blocks, groups, rows, cells = expr.shape
    spots = masses.shape[2]
    tiles = blocks * rows // 4 + 1

    def genes(sub):
        def place(i, ids):
            step, half = (pick(i, [part[k] for part in parts]) for k in range(2))
            return (0, gene_group(ids, step, half, sub), 0, 0)

        return pl.BlockSpec((blocks, 1, rows, cells), place)

    return pl.pallas_call(
        pred_kernel,
        grid_spec=pltpu.PrefetchScalarGridSpec(
            num_scalar_prefetch=1,
            grid=(2,),
            in_specs=[
                genes(0),
                genes(1),
                fixed((1, cells)),
                RESIDENT,
                fixed((8, spots)),
            ]
            + [RESIDENT] * len(more),
            out_specs=[RESIDENT] * 2,
        ),
        out_shape=[jax.ShapeDtypeStruct((tiles, 8, spots), F32)] * 2,
        compiler_params=vmem(16),
        cost_estimate=cost(24 * blocks * rows * cells * spots, 4 * cells * spots + 16 * blocks * rows * (cells + spots)),
        name="pred",
    )(ids, *[streamed(expr)] * 2, keep, masses, totals, *more)


def merge_kernel(own0, own1, got0, got1, *outs):
    tiles = outs[0].shape[0] - 1
    for half, (own, got) in enumerate(((own0, got0), (own1, got1))):
        for sub in range(2):
            out = outs[2 * half + sub]
            out[:tiles] = own[sub * tiles : sub * tiles + tiles] + got[sub * tiles : sub * tiles + tiles]
            out[tiles] = own[2 * tiles] + got[2 * tiles]


def merge_call(own, got):
    tiles, _, spots = own[0].shape
    block = 256
    whole = pl.BlockSpec((tiles, 8, block), lambda i: (0, 0, i))
    piece = (tiles // 2 + 1, 8, spots)
    return pl.pallas_call(
        merge_kernel,
        grid=(spots // block,),
        in_specs=[whole] * 4,
        out_specs=[pl.BlockSpec((tiles // 2 + 1, 8, block), lambda i: (0, 0, i))] * 4,
        out_shape=[jax.ShapeDtypeStruct(piece, F32)] * 4,
        compiler_params=vmem(12),
        cost_estimate=NO_COST,
        name="merge",
    )(*own, *got)


def stats_kernel(ids, piece, spatial, spot, totals, gene, slide_sums):
    rows = piece.shape[0] * piece.shape[1]
    valid, slide = spot[0:1, :], spot[1:2, :]
    share = 1.0 / totals[0:1, :]
    mass = totals[1:2, :] * share
    value = piece[...].reshape(rows, piece.shape[2]) * share
    data = spatial[...].reshape(value.shape)
    cross, square = value * data, value * value
    lane = lax.broadcasted_iota(jnp.int32, (rows, 128), 1)
    sums = jnp.zeros((rows, 128), F32)
    for index, one in enumerate((cross, square, data * data)):
        sums = jnp.where(lane == index, jnp.sum(one * valid, axis=1, keepdims=True), sums)
    sums = sums.T
    gene[...] = jnp.zeros_like(gene)
    slide_sums[...] = jnp.zeros_like(slide_sums)
    for index in range(3):
        gene[pl.ds(16 * index + gene_group(ids, 0, 0, 0), 1), :] = sums[index : index + 1, :]
    lane = lax.broadcasted_iota(jnp.int32, (1, 128), 1)
    slides = jnp.zeros((1, 128), F32)
    logs = jnp.log(jnp.where(valid > 0, mass, 1.0))
    for k in range(SLIDES):
        inside = jnp.where(slide == k, valid, 0.0)
        for index, one in enumerate((inside, inside * mass, inside * logs)):
            total = jnp.sum(one, axis=1, keepdims=True)
            slides = jnp.where(lane == 3 * index + k, total, slides)
    slide_sums[0:1, :] = slides
    for index, one in enumerate((cross, square)):
        total = jnp.sum(one, axis=0, keepdims=True)
        for k in range(total.shape[1] // 128):
            at = 48 + 8 * index + k
            gene[at : at + 1, :] = total[:, 128 * k : 128 * k + 128]


def stats_call(ids, piece, spatial, spot, totals):
    blocks, rows, spots = piece.shape
    return pl.pallas_call(
        stats_kernel,
        grid_spec=pltpu.PrefetchScalarGridSpec(
            num_scalar_prefetch=1,
            grid=(1,),
            in_specs=[
                fixed((blocks, rows, spots)),
                pl.BlockSpec((blocks, 1, rows, spots), lambda i, ids: (0, gene_group(ids, 0, 0, 0), 0, 0)),
                fixed((8, spots)),
                fixed((8, spots)),
            ],
            out_specs=[fixed((64, 128)), fixed((8, 128))],
        ),
        out_shape=[jax.ShapeDtypeStruct((64, 128), F32), jax.ShapeDtypeStruct((8, 128), F32)],
        compiler_params=vmem(8),
        cost_estimate=NO_COST,
        name="stats",
    )(ids, piece, streamed(spatial), spot, totals)


def coef_kernel(ids, genes_slides, sums, spot, totals, gene, rows, scalars, pairs):
    valid, slide, squares = (spot[k : k + 1, :] for k in range(3))
    share = 1.0 / totals[0:1, :]
    mass = totals[1:2, :] * share
    genes = float(16 * sums.shape[1])

    def wide(index):
        return jnp.concatenate([sums[index + k : index + k + 1, :] for k in range(8)], axis=1)

    dots, own = wide(48), wide(56)
    dot, aa, bb = genes_slides[0:16, :], genes_slides[16:32, :], genes_slides[32:48, :]
    scale = lax.rsqrt(aa * bb + 1e-06)
    pairs[0:16, :] = dot * scale**3 * bb / genes
    pairs[16:32, :] = scale / genes
    pair = [pairs[pl.ds(k + gene_group(ids, *one), 1), :] for k in (0, 16) for one in PIECES]
    gene[...] = jnp.concatenate([*pair, jnp.zeros((96, 128), F32)]).T
    total = jnp.sum(jnp.sum(dot * scale, axis=1, keepdims=True), axis=0, keepdims=True)
    nvs = jnp.zeros((1, 1), F32)
    density = jnp.zeros((1, 1), F32)
    nk, tk = jnp.ones_like(valid), jnp.ones_like(valid)
    for k in range(SLIDES):
        count, held, logs = (genes_slides[48:49, 3 * j + k : 3 * j + k + 1] for j in range(3))
        some = count > 0
        safe = jnp.where(some, count, 1.0)
        nvs += count
        density += jnp.where(some, jnp.log(jnp.where(some, held, 1.0) / safe) - logs / safe, 0.0)
        here = (slide == k) & (valid > 0)
        nk = jnp.where(here, count, nk)
        tk = jnp.where(here, held, tk)
    scale = lax.rsqrt(own * squares + 1e-06)
    grad_mass = valid / SLIDES * (1.0 / tk - 1.0 / (nk * jnp.where(valid > 0, mass, 1.0)))
    mask = valid * share
    by_pred, by_data = dots * scale**3 * squares / nvs, scale / nvs
    for index, one in enumerate((by_pred * share * mask, by_data * mask, mask, share * mask)):
        rows[8 * index : 8 * index + 8, :] = jnp.broadcast_to(one, (8, one.shape[1]))
    rows[32:40, :] = jnp.concatenate([grad_mass * share, jnp.zeros((7, valid.shape[1]), F32)])
    cosines = jnp.sum(valid * dots * scale, axis=1, keepdims=True)
    lane = lax.broadcasted_iota(jnp.int32, (1, 128), 1)
    out = jnp.zeros((1, 128), F32)
    for index, one in enumerate((total / genes, cosines / nvs, density / SLIDES)):
        out = jnp.where(lane == index, one, out)
    scalars[...] = out


def coef_call(ids, genes_slides, sums, spot, totals):
    spots = spot.shape[1]
    return pl.pallas_call(
        coef_kernel,
        grid_spec=pltpu.PrefetchScalarGridSpec(
            num_scalar_prefetch=1,
            grid=(1,),
            in_specs=[fixed(genes_slides.shape), fixed(sums.shape), fixed((8, spots)), fixed((8, spots))],
            out_specs=[fixed((128, 128)), fixed((40, spots)), fixed((1, 128))],
            scratch_shapes=[pltpu.VMEM((32, 128), F32)],
        ),
        out_shape=[
            jax.ShapeDtypeStruct((128, 128), F32),
            jax.ShapeDtypeStruct((40, spots), F32),
            jax.ShapeDtypeStruct((1, 128), F32),
        ],
        compiler_params=vmem(6),
        cost_estimate=NO_COST,
        name="coef",
    )(ids, genes_slides, sums, spot, totals)


def grad_rows(pred, data, gene, spot, lane):
    by_pred = gene[:, lane : lane + 1].reshape(2, 8, 1)
    by_data = gene[:, 16 + lane : 17 + lane].reshape(2, 8, 1)
    pred, data = pred.reshape(2, 8, pred.shape[1]), data.reshape(2, 8, data.shape[1])
    grad = pred * (by_pred * spot[24:32, :] + spot[0:8, :])
    grad = grad - data * (by_data * spot[16:24, :] + spot[8:16, :])
    return grad.reshape(16, grad.shape[2]), jnp.sum(grad * pred, axis=0)


def grad_kernel(ids, *refs, count, lane, chips):
    pred, data, refs = refs[: 2 * count], refs[2 * count : 3 * count], refs[3 * count :]
    gene, spot, grad, column = refs[0], refs[1], refs[-2], refs[-1]
    step = pl.program_id(0)
    chip = (ids[2] + pick(step, chips)) & 3

    @pl.when(step == 0)
    def _():
        column[...] = jnp.zeros_like(column)

    total = jnp.zeros(column.shape, F32)
    for index, part in enumerate(pred):
        for sub in range(2):
            at = gene_group(ids, *PIECES[lane + 2 * index + sub])
            row = pl.multiple_of((at & 3) * 16, 16)
            to = pl.ds(pl.multiple_of(at * 16, 16), 16)
            for half in range(2):
                block = chip * 2 + half
                rows, inner = grad_rows(
                    part[sub, block],
                    data[index // 2][half, 0, pl.ds(row, 16), :],
                    gene[16 * half : 16 * half + 16, :],
                    spot,
                    lane + 2 * index + sub,
                )
                grad[0, block, to, :], grad[1, block, to, :] = split(rows)
                total += inner
    column[...] += total


def grad_call(ids, pred, spatial, gene, spot, lane, chips, done=()):
    blocks, groups, rows, spots = spatial.shape
    count = len(pred) // 2

    def chip(i, ids):
        return (ids[2] + pick(i, chips)) & 3

    def group(k):
        step = PIECES[lane + 4 * k][0]
        return pl.BlockSpec(
            (2, 1, rows, spots), lambda i, ids: (chip(i, ids), (ids[0] + step) & 3, 0, 0)
        )

    return pl.pallas_call(
        functools.partial(grad_kernel, count=count, lane=lane, chips=chips),
        grid_spec=pltpu.PrefetchScalarGridSpec(
            num_scalar_prefetch=1,
            grid=(len(chips),),
            in_specs=[RESIDENT] * (2 * count)
            + [group(k) for k in range(count)]
            + [pl.BlockSpec((32, 128), lambda i, ids: (chip(i, ids), 0)), fixed(spot.shape)]
            + [RESIDENT] * len(done),
            out_specs=[RESIDENT, fixed((8, spots))],
        ),
        out_shape=[
            jax.ShapeDtypeStruct((2, blocks, groups * rows, spots), BF16),
            jax.ShapeDtypeStruct((8, spots), F32),
        ],
        input_output_aliases={3 * count + 3: 0} if done else {},
        compiler_params=vmem(12),
        cost_estimate=NO_COST,
        name="grad",
    )(ids, *pred, *[streamed(spatial)] * count, gene, spot, *done)


def back_kernel(ids, grad, masses, expr, *refs, parts, first, last):
    more, (sums, *outs), (held, ready) = refs[: first + 4 * last], refs[first + 4 * last : -2], refs[-2:]
    step = pl.program_id(0)
    rows = grad.shape[2]

    def block(part):
        return ((ids[2] + part[0]) & 3) * 2 + (ids[3] ^ part[1])

    def fetch(k):
        start = pl.multiple_of(block(parts[k]) * rows, rows)
        return pltpu.make_async_copy(expr.at[pl.ds(start, rows), :], held.at[k], ready.at[k])

    @pl.when(step == 0)
    def _():
        for k in range(len(parts)):
            fetch(k).start()

    here = block([pick(step, [part[k] for part in parts]) for k in range(2)])
    left = grad[0, here], grad[1, here]
    if first:
        pair = split(jnp.concatenate([more[0][...], jnp.zeros_like(more[0])]))
        left = [jnp.concatenate(both) for both in zip(left, pair)]
    part = product(left, masses, ((1,), (1,)))

    @pl.when(step == 0)
    def _():
        if first:
            sums[...] = part[rows : rows + 8]
        elif last:
            sums[...] = more[0][...] + more[1][...] + more[2][...]
        else:
            sums[...] = jnp.zeros_like(sums)

    part = part[:rows]
    for k, out in enumerate(outs):

        @pl.when(step == k)
        def _(k=k, out=out):
            out[:rows, :] = part
            fetch(k).wait()

    sums[...] += jnp.sum((part * held[step]).reshape(-1, 8, part.shape[1]), axis=0)
    if last:

        @pl.when(step == len(parts) - 1)
        def _():
            total = jnp.sum(sums[...], axis=0, keepdims=True)
            sums[...] = jnp.zeros_like(sums)
            sums[0:1, :] = total
            sums[1:2, 0:128] = more[3][...]
            outs[0][rows:, :] = sums[...]


def back_call(ids, parts, grad, masses, expr, first=(), last=()):
    _, blocks, rows, spots = grad.shape
    cells = masses.shape[1]
    shapes = [(rows, cells)] * len(parts)
    if last:
        shapes[0] = (rows + 8, cells)
    return pl.pallas_call(
        functools.partial(back_kernel, parts=parts, first=len(first), last=len(last) // 4),
        grid_spec=pltpu.PrefetchScalarGridSpec(
            num_scalar_prefetch=1,
            grid=(len(parts),),
            in_specs=[RESIDENT, RESIDENT, pl.BlockSpec(memory_space=pl.ANY)]
            + [pl.BlockSpec((8, spots), lambda i, ids: (4, 0))] * len(first)
            + [fixed(one.shape) for one in last],
            out_specs=[fixed((8, cells))] + [RESIDENT] * len(parts),
            scratch_shapes=[
                pltpu.VMEM((len(parts), rows, cells), F32),
                pltpu.SemaphoreType.DMA((len(parts),)),
            ],
        ),
        out_shape=[jax.ShapeDtypeStruct((8, cells), F32)]
        + [jax.ShapeDtypeStruct(shape, F32) for shape in shapes],
        compiler_params=vmem(16),
        cost_estimate=NO_COST,
        name="back",
    )(ids, grad, masses, streamed(expr), *first, *last)


def lift_kernel(above, below, far_up, far_down, out_above, out_below):
    rows = far_up.shape[0]
    out_above[:rows, :] = above[:rows, :] + far_up[...]
    out_above[rows:, :] = above[rows:, :]
    out_below[:rows, :] = below[:rows, :]
    out_below[rows:, :] = below[rows:, :] + far_down[...]


def lift_call(above, below, far_up, far_down):
    rows, cells = far_up.shape
    block = 256
    far = pl.BlockSpec((rows, block), lambda i: (0, i))
    whole = pl.BlockSpec((2 * rows, block), lambda i: (0, i))
    return pl.pallas_call(
        lift_kernel,
        grid=(cells // block,),
        in_specs=[whole, whole, far, far],
        out_specs=[whole, whole],
        out_shape=[jax.ShapeDtypeStruct(above.shape, F32)] * 2,
        compiler_params=vmem(8),
        cost_estimate=pl.CostEstimate(flops=10**10, bytes_accessed=0, transcendentals=0),
        name="lift",
    )(above, below, far_up, far_down)


def map_kernel(expr, grad, masses, keep, spot, out, held, ready, *, scale):
    index = pl.program_id(0)
    quarter, block = held.shape[2:]
    count = held.shape[1]

    def fetch(at, k):
        columns = pl.ds(pl.multiple_of(at * block, block), block)
        return pltpu.make_async_copy(
            expr.at[pl.ds(k * quarter, quarter), columns], held.at[at & 1, k], ready.at[at & 1, k]
        )

    @pl.when(index == 0)
    def _():
        for k in range(count):
            fetch(index, k).start()

    @pl.when(index + 1 < pl.num_programs(0))
    def _():
        for k in range(count):
            fetch(index + 1, k).start()

    inner = spot[0:1, :]
    for k in range(count):
        fetch(index, k).wait()
        rows = slice(k * quarter, k * quarter + quarter)
        pair = grad[0, rows, :], grad[1, rows, :]
        inner = inner + product(split(held[index & 1, k]), pair, ((0,), (0,)))
    at = pl.multiple_of(index * block, block)
    expo = masses[0, pl.ds(at, block), :].astype(F32) + masses[1, pl.ds(at, block), :].astype(F32)
    for part in range(block // 128):
        rows = slice(part * 128, part * 128 + 128)
        weight = as_column(keep[pl.ds(index * (block // 128) + part, 1), :])
        out[rows, :] = (scale * expo[rows]) * (weight * inner[rows] - spot[1:2, :])


def map_call(expr, grad, masses, keep, spot, scale):
    genes, cells = expr.shape
    spots = masses.shape[2]
    block, count = 256, 4
    return pl.pallas_call(
        functools.partial(map_kernel, scale=scale),
        grid=(cells // block,),
        in_specs=[
            pl.BlockSpec(memory_space=pl.ANY),
            RESIDENT,
            RESIDENT,
            fixed(keep.shape),
            fixed((8, spots)),
        ],
        out_specs=pl.BlockSpec((block, spots), lambda i: (i, 0)),
        out_shape=jax.ShapeDtypeStruct((cells, spots), F32),
        scratch_shapes=[
            pltpu.VMEM((2, count, genes // count, block), F32),
            pltpu.SemaphoreType.DMA((2, count)),
        ],
        compiler_params=vmem(24),
        cost_estimate=NO_COST,
        name="grad_map",
    )(streamed(expr), grad, masses, keep, spot)


def finish_kernel(last, got1, got2, got3, totals, scalars, kind, filt, grad_filter, terms, *, all_cells):
    total = (last[...] + got2[...]) + (got1[...] + got3[...])
    nvalid, retained, reg_sum = (totals[2:3, k : k + 1] for k in range(3))
    valid = (kind[...] >= 0).astype(F32)
    sigma = jax.nn.sigmoid(filt[...])
    keep = sigma * valid
    shifted = (retained - 0.35 * nvalid) / (0.1 * all_cells)
    count_term = jnp.sqrt(shifted * shifted + 1.0)
    grad_keep = total[0:1, :] + shifted / count_term / (0.1 * all_cells) + (1.0 - 2.0 * keep) / nvalid
    grad_filter[...] = valid * sigma * (1.0 - sigma) * grad_keep * all_cells
    lane = lax.broadcasted_iota(jnp.int32, (1, 128), 1)
    out = jnp.zeros((1, 128), F32)
    parts = (scalars[:, 0:1], total[1:2, 1:2], scalars[:, 2:3], count_term, reg_sum / nvalid)
    for index, one in enumerate(parts):
        out = jnp.where(lane == index, one, out)
    terms[...] = out


def finish_call(last, got, totals, scalars, kind, filt, all_cells):
    return pl.pallas_call(
        functools.partial(finish_kernel, all_cells=float(all_cells)),
        grid=(1,),
        in_specs=[fixed(one.shape) for one in (last, *got, totals, scalars, kind, filt)],
        out_specs=[fixed(kind.shape), fixed((1, 128))],
        out_shape=[jax.ShapeDtypeStruct(kind.shape, F32), jax.ShapeDtypeStruct((1, 128), F32)],
        compiler_params=vmem(4),
        cost_estimate=NO_COST,
        name="finish",
    )(last, *got, totals, scalars, kind, filt)


def on_device(map_logits, filter_logits, expr, spatial, cell_type, slide_id, spot_mask):
    genes, cells = expr.shape
    spots = map_logits.shape[1]
    all_cells = cells * lax.axis_size("cells")
    all_spots = spots * lax.axis_size("spots")
    cell_place = lax.axis_index("cells")
    z, x = cell_place >> 2, cell_place & 3
    spot_place = lax.axis_index("spots")
    y, core = spot_place >> 1, spot_place & 1
    first = jnp.where(core == 0, x, z)
    second = jnp.where(core == 0, z, x)
    blocks = cells // 128

    valid = (cell_type >= 0).astype(F32)
    sigma = jax.nn.sigmoid(filter_logits)
    keep = sigma * valid
    spot_valid = spot_mask.astype(F32)
    kind2 = cell_type.reshape(blocks, 128)
    filt2 = filter_logits.reshape(blocks, 128)
    keep2 = keep.reshape(blocks, 128)

    expr4 = expr.reshape(8, 16, 16, cells)
    keep_row = keep.reshape(1, cells)

    ids = jnp.stack([first, second, y, core]).astype(jnp.int32)

    def pred_part(one, two, more, *others):
        return pred_call(after(ids, *others), (one, two), expr4, keep_row, masses, totals, more)

    masses, types, totals, *far = expo_call(
        ids, ((2, 0), (2, 1)), map_logits, kind2, filt2, expr4
    )
    far_right, far_left = along(far[0], 1), along(far[1], -1)
    near = pred_part((1, 1), (-1, 0), (), *far)
    near_right, near_left = along(near[0], 1), along(near[1], -1)
    late = pred_part((1, 0), (-1, 1), (far_right, far_left), *near)
    late_right, late_left = along(late[0], 1), along(late[1], -1)
    own = pred_part((0, 0), (0, 1), (near_left, near_right), *late)
    types = types + swap_across(after(types, *own), 1)
    mine, *pieces = merge_call(own, (late_right, late_left))
    pieces = [across(piece, step + 1) for step, piece in enumerate(pieces)]
    spatial_squares = jnp.sum(after(spatial, mine) ** 2, axis=0)
    types = types + swap_along(after(types, spatial_squares), 1)
    types = types + swap_along(types, 3)
    spot_rows = stacked([spot_valid, slide_id.astype(F32), spatial_squares])
    mine = after(mine, spot_rows, types)
    piece = mine + pieces[0] + pieces[1] + pieces[2]
    totals = piece[-1]
    piece = piece[:-1].reshape(8, 16, spots)
    share = 1.0 / totals[0]
    mass = totals[1] * share

    got = [across(piece, step) for step in (1, 2, 3)]
    sums, slides = stats_call(
        ids,
        piece,
        spatial.reshape(8, 16, 16, spots),
        spot_rows,
        totals,
    )
    sums = sums + swap_along(sums, 1)
    sums = sums + swap_along(sums, 3)
    mine = after((jnp.stack([piece, got[2]]), jnp.stack([got[1], got[0]])), sums)
    right0, left1 = along(mine[0], 1), along(mine[1], -1)
    right1, left0 = along(mine[1], 1), along(mine[0], -1)
    sums = sums + swap_across(after(sums, *mine), 1)
    sums = sums + swap_across(sums, 3)
    right0, left1, sums = lax.optimization_barrier((right0, left1, sums))
    far0, far1 = along(right0, 1), along(left1, -1)
    genes_slides = jnp.concatenate([sums[:48], slides])
    genes_slides = genes_slides + swap(genes_slides, 0, 0, 0, 1)
    genes_slides = genes_slides + swap(genes_slides, 0, 0, 1, 0)
    genes_slides = after(genes_slides, right1, left0)
    genes_slides = genes_slides + swap(genes_slides, 0, 0, 3, 0)
    pred = [*mine, right0, right1, left0, left1, far0, far1]
    gene_coef, spot_coef, scalars = coef_call(ids, genes_slides, sums, spot_rows, totals)
    spatial4 = spatial.reshape(8, RING, genes // 32, spots)
    grad, column_a = grad_call(ids, pred[:6], spatial4, gene_coef, spot_coef, 0, (0, 1, 2, 3))

    def last_grad(chips, grad, *others):
        return grad_call(
            after(ids, *others), pred[6:], spatial4, gene_coef, spot_coef, 12, chips, (grad,)
        )

    def back_part(steps, grad, *others, **rows):
        return back_call(after(ids, *others), steps, grad, masses, expr, **rows)

    rows = genes // 16
    grad, column_b = last_grad((2,), grad)
    sums_a, far_a = back_part([(2, 1)], grad, first=[spot_coef])
    far_got = swap(far_a, 0, 0, 0, 1)
    sums_b, far_b = back_part([(2, 0)], grad, far_a)
    far = far_b + far_got
    far_up, far_down = up(far[:rows], 1), up(far[rows:], -1)
    grad, column_c = last_grad((1, -1, 0), grad, far)
    sums_c, up_a, down_a, up_b, down_b = back_part([(1, 1), (-1, 1), (1, 0), (-1, 0)], grad)
    up_got, down_got = swap(up_a, 0, 0, 0, 1), swap(down_a, 0, 0, 0, 1)
    last, own_a, own_b = back_part(
        [(0, 1), (0, 0)], grad, up_b, last=[sums_a, sums_b, sums_c, scalars]
    )
    above, below = lift_call(up_b, down_b, *after((far_up, far_down), own_b))
    above, below = above + up_got, below + down_got
    near_up, near_down = up(above, 1), up(below, -1)
    own_got = swap(after(own_a, far_up, far_down), 0, 0, 0, 1)
    last = last + own_got[2 * rows :]
    own = own_b + own_got[: 2 * rows]

    column = jnp.sum(column_a + column_b + column_c, axis=0) * share + spot_coef[32] * mass
    map_rows = stacked([spot_coef[32], column])
    map_rows = after(map_rows, above, below, last)
    map_args = (expr, grad.reshape(2, genes, spots), masses, keep2, map_rows, all_cells * genes)
    got = [up(last, step) for step in (1, 2, 3)]
    grad_map = map_call(*map_args)
    got = after(tuple(got), grad_map)
    types = types + swap_across(after(types, grad_map), 3)
    grad_weighted = after(own, grad_map) + near_up + near_down
    grad_expr = grad_weighted * (keep * (genes * all_spots))[None, :]

    type_fraction = types * share

    grad_filter, loss_terms = finish_call(
        last, got, totals, scalars, cell_type.reshape(1, cells), filter_logits.reshape(1, cells), all_cells
    )
    return (loss_terms[0, :5], type_fraction, grad_map, grad_filter.reshape(cells), grad_expr)


def solution(mesh):
    in_specs = (
        P("cells", "spots"),
        P("cells"),
        P(None, "cells"),
        P(None, "spots"),
        P("cells"),
        P("spots"),
        P("spots"),
    )
    out_specs = (P(), P(None, "spots"), P("cells", "spots"), P("cells"), P("spots", "cells"))
    return jax.shard_map(
        on_device, mesh=mesh, in_specs=in_specs, out_specs=out_specs, check_vma=False
    )
```

profile of v0, /device:TPU:1, one launch (start us, length us, event | category | flops | bytes accessed | tf_op | source)
XLA Modules:
  0.0 214.7 jit_solution(6651627987541391423)
XLA Ops:
  2.1 9.5 %expo.1 = (bf16[2,1280,1024]{2,1,0:T(8,128)(2,1)S(1)}, f32[32,1024]{1,0:T(8,128)S(1)}, f32[8,1024]{1,0:T(8,128)S(1)}, f32[33,8,1024]{2,1,0:T(8,128)S(1)}, f32[33,8,1024]{2,1,0:T(8,128)S(1)}) custom-call(s32[4]{0:T(128)S(1)} %pad_add_fusion.ids, f32[1280,1024]{1,0:T(8,128)} %logits.1, s32[10,128]{1,0:T(8,128)S(1)} %bitcast.43, f32[10,128]{1,0:T(8,128)S(1)} %bitcast.44, ...), custom_call_target="tpu_custom_call" | custom-call | bytes 1310720 | tf_op jit(solution)/shard_map/expo/pallas_call | solution.py:176
  11.6 2.5 %collective-permute-start = (f32[33,8,1024]{2,1,0:T(8,128)S(1)}, f32[33,8,1024]{2,1,0:T(8,128)S(1)}, u32[]{:S(2)}, u32[]{:S(2)}) collective-permute-start(f32[33,8,1024]{2,1,0:T(8,128)S(1)} %get-tuple-element.73), channel_id=1, source_target_pairs={{0,8},{1,33},{2,10},{3,35},{4,12},{5,37},{6,14},{7,39},{8,16},{9,4... | collective-permute-start | bytes 3244040 | tf_op jit(solution)/shard_map/ppermute | solution.py:53
  14.2 2.2 %collective-permute-start.1 = (f32[33,8,1024]{2,1,0:T(8,128)S(1)}, f32[33,8,1024]{2,1,0:T(8,128)S(1)}, u32[]{:S(2)}, u32[]{:S(2)}) collective-permute-start(f32[33,8,1024]{2,1,0:T(8,128)S(1)} %get-tuple-element.74), channel_id=1, source_target_pairs={{0,24},{1,97},{2,26},{3,99},{4,28},{5,101},{6,30},{7,103},{8,0},{9... | collective-permute-start | bytes 3244040 | tf_op jit(solution)/shard_map/ppermute | solution.py:53
  16.4 6.5 %pred_.3 = (f32[33,8,1024]{2,1,0:T(8,128)S(1)}, f32[33,8,1024]{2,1,0:T(8,128)S(1)}) custom-call(s32[4]{0:T(128)S(1)} %pad_add_fusion.ids, f32[8,16,16,1280]{3,2,1,0:T(8,128)} %bitcast.50, f32[8,16,16,1280]{3,2,1,0:T(8,128)} %bitcast.51, f32[1,1280]{1,0:T(1,128)S(1)} %reshape.94.keep, bf16[2,1280,1024]{2,1,0:T(8,128)(2,1)S(1)} %get-tuple-element.76.masses, ...), custom_call_target="tpu_custom_call" | custom-call | flops 503316480 | bytes 1245184 | tf_op jit(solution)/shard_map/pred/pallas_call | solution.py:240
  22.9 1.5 collective-permute-start.2
  24.4 4.7 %collective-permute-done.refs_0_ = f32[33,8,1024]{2,1,0:T(8,128)S(1)} collective-permute-done((f32[33,8,1024]{2,1,0:T(8,128)S(1)}, f32[33,8,1024]{2,1,0:T(8,128)S(1)}, u32[]{:S(2)}, u32[]{:S(2)}) %collective-permute-start) | collective-permute-done | bytes 1081376 | tf_op jit(solution)/shard_map/ppermute | solution.py:53
  29.1 6.9 %pred_.4 = (f32[33,8,1024]{2,1,0:T(8,128)S(1)}, f32[33,8,1024]{2,1,0:T(8,128)S(1)}) custom-call(s32[4]{0:T(128)S(1)} %pad_add_fusion.ids, f32[8,16,16,1280]{3,2,1,0:T(8,128)} %bitcast.52, f32[8,16,16,1280]{3,2,1,0:T(8,128)} %bitcast.53, f32[1,1280]{1,0:T(1,128)S(1)} %reshape.94.keep, bf16[2,1280,1024]{2,1,0:T(8,128)(2,1)S(1)} %get-tuple-element.76.masses, ...), custom_call_target="tpu_custom_call" | custom-call | flops 503316480 | bytes 1245184 | tf_op jit(solution)/shard_map/pred/pallas_call | solution.py:240
  37.1 1.9 collective-permute-start.5
  40.7 6.6 %pred_.5 = (f32[33,8,1024]{2,1,0:T(8,128)S(1)}, f32[33,8,1024]{2,1,0:T(8,128)S(1)}) custom-call(s32[4]{0:T(128)S(1)} %pad_add_fusion.ids, f32[8,16,16,1280]{3,2,1,0:T(8,128)} %bitcast.54, f32[8,16,16,1280]{3,2,1,0:T(8,128)} %bitcast.55, f32[1,1280]{1,0:T(1,128)S(1)} %reshape.94.keep, bf16[2,1280,1024]{2,1,0:T(8,128)(2,1)S(1)} %get-tuple-element.76.masses, ...), custom_call_target="tpu_custom_call" | custom-call | flops 503316480 | bytes 1245184 | tf_op jit(solution)/shard_map/pred/pallas_call | solution.py:240
  48.3 4.6 %collective-permute-done.6 = f32[32,1024]{1,0:T(8,128)S(1)} collective-permute-done((f32[32,1024]{1,0:T(8,128)S(1)}, f32[32,1024]{1,0:T(8,128)S(1)}, u32[]{:S(2)}, u32[]{:S(2)}) %collective-permute-start.6) | collective-permute-done | bytes 131104 | tf_op jit(solution)/shard_map/ppermute | solution.py:53
  53.8 2.6 %collective-permute-start.10 = (f32[17,8,1024]{2,1,0:T(8,128)S(1)}, f32[17,8,1024]{2,1,0:T(8,128)S(1)}, u32[]{:S(2)}, u32[]{:S(2)}) collective-permute-start(f32[17,8,1024]{2,1,0:T(8,128)S(1)} %get-tuple-element.93), channel_id=1, source_target_pairs={{0,64},{1,17},{2,66},{3,19},{4,68},{5,21},{6,70},{7,23},{8,72},{9,... | collective-permute-start | bytes 1671176 | tf_op jit(solution)/shard_map/ppermute | solution.py:53
  58.5 1.4 collective-permute-start.7
  59.9 3.8 %collective-permute-done.7 = f32[32,1024]{1,0:T(8,128)S(1)} collective-permute-done((f32[32,1024]{1,0:T(8,128)S(1)}, f32[32,1024]{1,0:T(8,128)S(1)}, u32[]{:S(2)}, u32[]{:S(2)}) %collective-permute-start.7) | collective-permute-done | bytes 131104 | tf_op jit(solution)/shard_map/ppermute | solution.py:53
  63.7 3.5 %collective-permute-start.8 = (f32[32,1024]{1,0:T(8,128)S(1)}, f32[32,1024]{1,0:T(8,128)S(1)}, u32[]{:S(2)}, u32[]{:S(2)}) collective-permute-start(f32[32,1024]{1,0:T(8,128)S(1)} %add.78), channel_id=1, source_target_pairs={{0,24},{1,97},{2,26},{3,99},{4,28},{5,101},{6,30},{7,103},{8,16},{... | collective-permute-start | bytes 393224 | tf_op jit(solution)/shard_map/ppermute | solution.py:53
  67.3 4.0 %collective-permute-done.8 = f32[32,1024]{1,0:T(8,128)S(1)} collective-permute-done((f32[32,1024]{1,0:T(8,128)S(1)}, f32[32,1024]{1,0:T(8,128)S(1)}, u32[]{:S(2)}, u32[]{:S(2)}) %collective-permute-start.8) | collective-permute-done | bytes 131104 | tf_op jit(solution)/shard_map/ppermute | solution.py:53
  71.8 2.2 %collective-permute-start.13 = (f32[8,16,1024]{2,1,0:T(8,128)S(1)}, f32[8,16,1024]{2,1,0:T(8,128)S(1)}, u32[]{:S(2)}, u32[]{:S(2)}) collective-permute-start(f32[8,16,1024]{2,1,0:T(8,128)S(1)} %bitcast.38), channel_id=1, source_target_pairs={{0,64},{1,17},{2,66},{3,19},{4,68},{5,21},{6,70},{7,23},{8,72},{9,... | collective-permute-start | bytes 1572872 | tf_op jit(solution)/shard_map/ppermute | solution.py:53
  74.3 2.4 %collective-permute-start.12 = (f32[8,16,1024]{2,1,0:T(8,128)S(1)}, f32[8,16,1024]{2,1,0:T(8,128)S(1)}, u32[]{:S(2)}, u32[]{:S(2)}) collective-permute-start(f32[8,16,1024]{2,1,0:T(8,128)S(1)} %bitcast.40), channel_id=1, source_target_pairs={{0,96},{1,25},{2,98},{3,27},{4,100},{5,29},{6,102},{7,31},{8,104},... | collective-permute-start | bytes 1572872 | tf_op jit(solution)/shard_map/ppermute | solution.py:53
  76.7 1.9 stats.1
  79.7 2.5 %collective-permute-done.15 = f32[64,128]{1,0:T(8,128)S(1)} collective-permute-done((f32[64,128]{1,0:T(8,128)S(1)}, f32[64,128]{1,0:T(8,128)S(1)}, u32[]{:S(2)}, u32[]{:S(2)}) %collective-permute-start.15) | collective-permute-done | bytes 32800 | tf_op jit(solution)/shard_map/ppermute | solution.py:53
  82.1 2.1 collective-permute-start.16
  84.3 2.8 %collective-permute-done.16 = f32[64,128]{1,0:T(8,128)S(1)} collective-permute-done((f32[64,128]{1,0:T(8,128)S(1)}, f32[64,128]{1,0:T(8,128)S(1)}, u32[]{:S(2)}, u32[]{:S(2)}) %collective-permute-start.16) | collective-permute-done | bytes 32800 | tf_op jit(solution)/shard_map/ppermute | solution.py:53
  88.4 2.1 collective-permute-start.18
  91.4 1.9 collective-permute-done.19
  93.2 1.6 collective-permute-start.20
  94.9 2.7 %collective-permute-start.26 = (f32[2,8,16,1024]{3,2,1,0:T(8,128)S(1)}, f32[2,8,16,1024]{3,2,1,0:T(8,128)S(1)}, u32[]{:S(2)}, u32[]{:S(2)}) collective-permute-start(f32[2,8,16,1024]{3,2,1,0:T(8,128)S(1)} %pad_maximum_fusion.refs_0_), channel_id=1, source_target_pairs={{0,24},{1,97},{2,26},{3,99},{4,28},{5,101},{6,30},{7,103},{8,0},{9... | collective-permute-start | bytes 3145736 | tf_op jit(solution)/shard_map/ppermute | solution.py:53
  97.6 5.7 %collective-permute-done.17.refs_2_ = f32[2,8,16,1024]{3,2,1,0:T(8,128)S(1)} collective-permute-done((f32[2,8,16,1024]{3,2,1,0:T(8,128)S(1)}, f32[2,8,16,1024]{3,2,1,0:T(8,128)S(1)}, u32[]{:S(2)}, u32[]{:S(2)}) %collective-permute-start.17) | collective-permute-done | bytes 1048608 | tf_op jit(solution)/shard_map/ppermute | solution.py:53
  103.8 1.4 collective-permute-start.21
  105.2 1.3 collective-permute-start.22
  106.5 7.2 %collective-permute-start.23 = (f32[56,128]{1,0:T(8,128)S(1)}, f32[56,128]{1,0:T(8,128)S(1)}, u32[]{:S(2)}, u32[]{:S(2)}) collective-permute-start(f32[56,128]{1,0:T(8,128)S(1)} %pad_maximum_fusion.2), channel_id=1, source_target_pairs={{0,1},{1,0},{2,3},{3,2},{4,5},{5,4},{6,7},{7,6},{8,9},{9,8},{10,11... | collective-permute-start | bytes 86024 | tf_op jit(solution)/shard_map/ppermute | solution.py:53
  115.9 1.7 collective-permute-done.24
  117.7 2.8 %collective-permute-start.27 = (f32[56,128]{1,0:T(8,128)S(1)}, f32[56,128]{1,0:T(8,128)S(1)}, u32[]{:S(2)}, u32[]{:S(2)}) collective-permute-start(f32[56,128]{1,0:T(8,128)S(1)} %add.88), channel_id=1, source_target_pairs={{0,6},{1,7},{2,4},{3,5},{4,2},{5,3},{6,0},{7,1},{8,14},{9,15},{10,... | collective-permute-start | bytes 86024 | tf_op jit(solution)/shard_map/ppermute | solution.py:53
  120.5 1.6 collective-permute-done.27
  122.9 6.1 %grad.3 = (bf16[2,8,256,1024]{3,2,1,0:T(8,128)(2,1)S(1)}, f32[8,1024]{1,0:T(8,128)S(1)}) custom-call(s32[4]{0:T(128)S(1)} %pad_add_fusion.ids, f32[2,8,16,1024]{3,2,1,0:T(8,128)S(1)} %pad_maximum_fusion.refs_0_, f32[2,8,16,1024]{3,2,1,0:T(8,128)S(1)} %pad_maximum_fusion.1.refs_1_, f32[2,8,16,1024]{3,2,1,0:T(8,128)S(1)} %collective-permute-done.17.refs_2_, ...), custom_call_target="tpu_custom_call" | custom-call | tf_op jit(solution)/shard_map/grad/pallas_call | solution.py:461
  129.0 1.9 grad.4
  130.9 3.1 %back.4 = (f32[8,1280]{1,0:T(8,128)S(1)}, f32[256,1280]{1,0:T(8,128)S(1)}) custom-call(s32[4]{0:T(128)S(1)} %pad_add_fusion.ids, bf16[2,8,256,1024]{3,2,1,0:T(8,128)(2,1)S(1)} %get-tuple-element.107.grad.refs_5_, bf16[2,1280,1024]{2,1,0:T(8,128)(2,1)S(1)} %get-tuple-element.76.masses, f32[2048,1280]{1,0:T(8,128)} %expr.9, ...), custom_call_target="tpu_custom_call" | custom-call | tf_op jit(solution)/shard_map/back/pallas_call | solution.py:542
  134.0 4.9 %collective-permute-start.28 = (f32[256,1280]{1,0:T(8,128)S(1)}, f32[256,1280]{1,0:T(8,128)S(1)}, u32[]{:S(2)}, u32[]{:S(2)}) collective-permute-start(f32[256,1280]{1,0:T(8,128)S(1)} %get-tuple-element.108), channel_id=1, source_target_pairs={{0,1},{1,0},{2,3},{3,2},{4,5},{5,4},{6,7},{7,6},{8,9},{9,8},{10,11... | collective-permute-start | bytes 3932168 | tf_op jit(solution)/shard_map/ppermute | solution.py:53
  138.8 3.6 %back.5 = (f32[8,1280]{1,0:T(8,128)S(1)}, f32[256,1280]{1,0:T(8,128)S(1)}) custom-call(s32[4]{0:T(128)S(1)} %pad_add_fusion.ids, bf16[2,8,256,1024]{3,2,1,0:T(8,128)(2,1)S(1)} %get-tuple-element.107.grad.refs_5_, bf16[2,1280,1024]{2,1,0:T(8,128)(2,1)S(1)} %get-tuple-element.76.masses, f32[2048,1280]{1,0:T(8,128)} %expr.9), custom_call_target="tpu_custom_call" | custom-call | tf_op jit(solution)/shard_map/back/pallas_call | solution.py:542
  143.5 2.4 %collective-permute-start.30 = (f32[128,1280]{1,0:T(8,128)S(1)}, f32[128,1280]{1,0:T(8,128)S(1)}, u32[]{:S(2)}, u32[]{:S(2)}) collective-permute-start(f32[128,1280]{1,0:T(8,128)S(1)} %get-tuple-element.145), channel_id=1, source_target_pairs={{0,6},{1,7},{2,0},{3,1},{4,2},{5,3},{6,4},{7,5},{8,14},{9,15},{10,... | collective-permute-start | bytes 1966088 | tf_op jit(solution)/shard_map/ppermute | solution.py:53
  145.9 3.3 %grad.5 = (bf16[2,8,256,1024]{3,2,1,0:T(8,128)(2,1)S(1)}, f32[8,1024]{1,0:T(8,128)S(1)}) custom-call(s32[4]{0:T(128)S(1)} %pad_add_fusion.ids, f32[2,8,16,1024]{3,2,1,0:T(8,128)S(1)} %collective-permute-done.21.refs_0_, f32[2,8,16,1024]{3,2,1,0:T(8,128)S(1)} %collective-permute-done.22.refs_1_, ...), custom_call_target="tpu_custom_call", output_to_operand_aliasing={{0}: (6, {})} | custom-call | tf_op jit(solution)/shard_map/grad/pallas_call | solution.py:461
  149.2 11.0 %back.6 = (f32[8,1280]{1,0:T(8,128)S(1)}, f32[256,1280]{1,0:T(8,128)S(1)}, f32[256,1280]{1,0:T(8,128)S(1)}, f32[256,1280]{1,0:T(8,128)S(1)}, f32[256,1280]{1,0:T(8,128)S(1)}) custom-call(s32[4]{0:T(128)S(1)} %pad_add_fusion.ids, bf16[2,8,256,1024]{3,2,1,0:T(8,128)(2,1)S(1)} %get-tuple-element.112.grad, bf16[2,1280,1024]{2,1,0:T(8,128)(2,1)S(1)} %get-tuple-element.76.masses, ...), custom_call_target="tpu_custom_call" | custom-call | tf_op jit(solution)/shard_map/back/pallas_call | solution.py:542
  160.8 6.1 %back.7 = (f32[8,1280]{1,0:T(8,128)S(1)}, f32[264,1280]{1,0:T(8,128)S(1)}, f32[256,1280]{1,0:T(8,128)S(1)}) custom-call(s32[4]{0:T(128)S(1)} %pad_add_fusion.ids, bf16[2,8,256,1024]{3,2,1,0:T(8,128)(2,1)S(1)} %get-tuple-element.112.grad, bf16[2,1280,1024]{2,1,0:T(8,128)(2,1)S(1)} %get-tuple-element.76.masses, f32[2048,1280]{1,0:T(8,128)} %expr.9, ...), custom_call_target="tpu_custom_call" | custom-call | tf_op jit(solution)/shard_map/back/pallas_call | solution.py:542
  169.6 1.6 collective-permute-start.39
  172.6 3.8 %collective-permute-start.33 = (f32[8,1280]{1,0:T(8,128)S(1)}, f32[8,1280]{1,0:T(8,128)S(1)}, u32[]{:S(2)}, u32[]{:S(2)}) collective-permute-start(f32[8,1280]{1,0:T(8,128)S(1)} %slice_add_fusion.1.last), channel_id=1, source_target_pairs={{0,4},{1,5},{2,6},{3,7},{4,0},{5,1},{6,2},{7,3},{8,12},{9,13},{10,... | collective-permute-start | bytes 122888 | tf_op jit(solution)/shard_map/ppermute | solution.py:53
  176.6 21.1 %grad_map.1 = f32[1280,1024]{1,0:T(8,128)} custom-call(f32[2048,1280]{1,0:T(8,128)} %expr.9, bf16[2,2048,1024]{2,1,0:T(8,128)(2,1)S(1)} %bitcast.37, bf16[2,1280,1024]{2,1,0:T(8,128)(2,1)S(1)} %get-tuple-element.76.masses, f32[10,128]{1,0:T(8,128)S(1)} %bitcast.45, f32[8,1024]{1,0:T(8,128)S(1)} %select_select_fusion.spot), custom_call_target="tpu_custom_call" | custom-call | tf_op jit(solution)/shard_map/grad_map/pallas_call | solution.py:628
  197.7 8.1 %collective-permute-done.32.got1 = f32[8,1280]{1,0:T(8,128)S(1)} collective-permute-done((f32[8,1280]{1,0:T(8,128)S(1)}, f32[8,1280]{1,0:T(8,128)S(1)}, u32[]{:S(2)}, u32[]{:S(2)}) %collective-permute-start.32) | collective-permute-done | bytes 40992 | tf_op jit(solution)/shard_map/ppermute | solution.py:53
  205.8 2.9 %collective-permute-start.37 = (f32[32,1024]{1,0:T(8,128)S(1)}, f32[32,1024]{1,0:T(8,128)S(1)}, u32[]{:S(2)}, u32[]{:S(2)}) collective-permute-start(f32[32,1024]{1,0:T(8,128)S(1)} %add.79), channel_id=1, source_target_pairs={{0,96},{1,25},{2,98},{3,27},{4,100},{5,29},{6,102},{7,31},{8,104},... | collective-permute-start | bytes 393224 | tf_op jit(solution)/shard_map/ppermute | solution.py:53
  210.1 1.3 collective-permute-done.37
  212.1 2.6 %add_multiply_fusion = f32[256,1280]{1,0:T(8,128)} fusion(f32[256,1280]{1,0:T(8,128)S(1)} %collective-permute-done.39, f32[256,1280]{1,0:T(8,128)S(1)} %slice_add_fusion, f32[256,1280]{1,0:T(8,128)} %collective-permute-done.38, f32[1280]{0:T(1024)S(1)} %get-tuple-element.141), kind=kLoop, calls=%fused_computation.2 | loop fusion | flops 983040 | bytes 5248000 | tf_op jit(solution)/shard_map/mul | solution.py:797
  (107 shorter events, 23.7 us)
Async XLA Ops:
  0.7 0.7 copy-start
  1.4 0.7 copy-start.2
  11.6 17.5 %collective-permute-start = (f32[33,8,1024]{2,1,0:T(8,128)S(1)}, f32[33,8,1024]{2,1,0:T(8,128)S(1)}, u32[]{:S(2)}, u32[]{:S(2)}) collective-permute-start(f32[33,8,1024]{2,1,0:T(8,128)S(1)} %get-tuple-element.73), channel_id=1, source_target_pairs={{0,8},{1,33},{2,10},{3,35},{4,12},{5,37},{6,14},{7,39},{8,16},{9,4... | collective-permute-start | bytes 3244040 | tf_op jit(solution)/shard_map/ppermute | solution.py:53
  14.2 15.0 %collective-permute-start.1 = (f32[33,8,1024]{2,1,0:T(8,128)S(1)}, f32[33,8,1024]{2,1,0:T(8,128)S(1)}, u32[]{:S(2)}, u32[]{:S(2)}) collective-permute-start(f32[33,8,1024]{2,1,0:T(8,128)S(1)} %get-tuple-element.74), channel_id=1, source_target_pairs={{0,24},{1,97},{2,26},{3,99},{4,28},{5,101},{6,30},{7,103},{8,0},{9... | collective-permute-start | bytes 3244040 | tf_op jit(solution)/shard_map/ppermute | solution.py:53
  22.9 17.3 %collective-permute-start.2 = (f32[33,8,1024]{2,1,0:T(8,128)S(1)}, f32[33,8,1024]{2,1,0:T(8,128)S(1)}, u32[]{:S(2)}, u32[]{:S(2)}) collective-permute-start(f32[33,8,1024]{2,1,0:T(8,128)S(1)} %get-tuple-element.79), channel_id=1, source_target_pairs={{0,24},{1,97},{2,26},{3,99},{4,28},{5,101},{6,30},{7,103},{8,0},{9... | collective-permute-start | bytes 3244040 | tf_op jit(solution)/shard_map/ppermute | solution.py:53
  24.4 16.3 %collective-permute-start.3 = (f32[33,8,1024]{2,1,0:T(8,128)S(1)}, f32[33,8,1024]{2,1,0:T(8,128)S(1)}, u32[]{:S(2)}, u32[]{:S(2)}) collective-permute-start(f32[33,8,1024]{2,1,0:T(8,128)S(1)} %get-tuple-element.78), channel_id=1, source_target_pairs={{0,8},{1,33},{2,10},{3,35},{4,12},{5,37},{6,14},{7,39},{8,16},{9,4... | collective-permute-start | bytes 3244040 | tf_op jit(solution)/shard_map/ppermute | solution.py:53
  29.1 28.7 %slice-start = ((s8[8388608]{0:T(1024)(128)(4,1)}), s8[4194304]{0:T(1024)(128)(4,1)S(1)}, s32[]{:S(2)}) async-start(s8[8388608]{0:T(1024)(128)(4,1)} %bitcast.62), calls=%async_computation | async-start | bytes 8388608
  36.1 16.9 %collective-permute-start.4 = (f32[33,8,1024]{2,1,0:T(8,128)S(1)}, f32[33,8,1024]{2,1,0:T(8,128)S(1)}, u32[]{:S(2)}, u32[]{:S(2)}) collective-permute-start(f32[33,8,1024]{2,1,0:T(8,128)S(1)} %get-tuple-element.81), channel_id=1, source_target_pairs={{0,8},{1,33},{2,10},{3,35},{4,12},{5,37},{6,14},{7,39},{8,16},{9,4... | collective-permute-start | bytes 3244040 | tf_op jit(solution)/shard_map/ppermute | solution.py:53
  37.1 20.8 %slice-start.1 = ((s8[8388608]{0:T(1024)(128)(4,1)}), s8[4194304]{0:T(1024)(128)(4,1)S(1)}, s32[]{:S(2)}) async-start(s8[8388608]{0:T(1024)(128)(4,1)} %bitcast.62), calls=%async_computation.1 | async-start | bytes 8388608
  37.1 15.9 %collective-permute-start.5 = (f32[33,8,1024]{2,1,0:T(8,128)S(1)}, f32[33,8,1024]{2,1,0:T(8,128)S(1)}, u32[]{:S(2)}, u32[]{:S(2)}) collective-permute-start(f32[33,8,1024]{2,1,0:T(8,128)S(1)} %get-tuple-element.82), channel_id=1, source_target_pairs={{0,24},{1,97},{2,26},{3,99},{4,28},{5,101},{6,30},{7,103},{8,0},{9... | collective-permute-start | bytes 3244040 | tf_op jit(solution)/shard_map/ppermute | solution.py:53
  47.3 5.7 %collective-permute-start.6 = (f32[32,1024]{1,0:T(8,128)S(1)}, f32[32,1024]{1,0:T(8,128)S(1)}, u32[]{:S(2)}, u32[]{:S(2)}) collective-permute-start(f32[32,1024]{1,0:T(8,128)S(1)} %get-tuple-element.89), channel_id=1, source_target_pairs={{0,32},{1,9},{2,34},{3,11},{4,36},{5,13},{6,38},{7,15},{8,40},{9,1... | collective-permute-start | bytes 393224 | tf_op jit(solution)/shard_map/ppermute | solution.py:53
  53.8 17.5 %collective-permute-start.10 = (f32[17,8,1024]{2,1,0:T(8,128)S(1)}, f32[17,8,1024]{2,1,0:T(8,128)S(1)}, u32[]{:S(2)}, u32[]{:S(2)}) collective-permute-start(f32[17,8,1024]{2,1,0:T(8,128)S(1)} %get-tuple-element.93), channel_id=1, source_target_pairs={{0,64},{1,17},{2,66},{3,19},{4,68},{5,21},{6,70},{7,23},{8,72},{9,... | collective-permute-start | bytes 1671176 | tf_op jit(solution)/shard_map/ppermute | solution.py:53
  56.4 15.2 %collective-permute-start.11 = (f32[17,8,1024]{2,1,0:T(8,128)S(1)}, f32[17,8,1024]{2,1,0:T(8,128)S(1)}, u32[]{:S(2)}, u32[]{:S(2)}) collective-permute-start(f32[17,8,1024]{2,1,0:T(8,128)S(1)} %get-tuple-element.94), channel_id=1, source_target_pairs={{0,96},{1,25},{2,98},{3,27},{4,100},{5,29},{6,102},{7,31},{8,104},... | collective-permute-start | bytes 1671176 | tf_op jit(solution)/shard_map/ppermute | solution.py:53
  57.2 2.6 %copy-start.4 = (s32[1024]{0:T(1024)S(1)}, s32[1024]{0:T(1024)}, u32[]{:S(2)}) copy-start(s32[1024]{0:T(1024)} %param.12) | copy-start | bytes 12292
  57.2 2.6 %copy-start.5 = (s32[1024]{0:T(1024)S(1)}, s32[1024]{0:T(1024)}, u32[]{:S(2)}) copy-start(s32[1024]{0:T(1024)} %param.13) | copy-start | bytes 12292
  57.3 14.4 %collective-permute-start.9 = (f32[17,8,1024]{2,1,0:T(8,128)S(1)}, f32[17,8,1024]{2,1,0:T(8,128)S(1)}, u32[]{:S(2)}, u32[]{:S(2)}) collective-permute-start(f32[17,8,1024]{2,1,0:T(8,128)S(1)} %get-tuple-element.92), channel_id=1, source_target_pairs={{0,32},{1,9},{2,34},{3,11},{4,36},{5,13},{6,38},{7,15},{8,40},{9,1... | collective-permute-start | bytes 1671176 | tf_op jit(solution)/shard_map/ppermute | solution.py:53
  58.5 5.2 %collective-permute-start.7 = (f32[32,1024]{1,0:T(8,128)S(1)}, f32[32,1024]{1,0:T(8,128)S(1)}, u32[]{:S(2)}, u32[]{:S(2)}) collective-permute-start(f32[32,1024]{1,0:T(8,128)S(1)} %add.77), channel_id=1, source_target_pairs={{0,8},{1,33},{2,10},{3,35},{4,12},{5,37},{6,14},{7,39},{8,0},{9,41... | collective-permute-start | bytes 393224 | tf_op jit(solution)/shard_map/ppermute | solution.py:53
  63.7 7.6 %collective-permute-start.8 = (f32[32,1024]{1,0:T(8,128)S(1)}, f32[32,1024]{1,0:T(8,128)S(1)}, u32[]{:S(2)}, u32[]{:S(2)}) collective-permute-start(f32[32,1024]{1,0:T(8,128)S(1)} %add.78), channel_id=1, source_target_pairs={{0,24},{1,97},{2,26},{3,99},{4,28},{5,101},{6,30},{7,103},{8,16},{... | collective-permute-start | bytes 393224 | tf_op jit(solution)/shard_map/ppermute | solution.py:53
  71.8 15.3 %collective-permute-start.13 = (f32[8,16,1024]{2,1,0:T(8,128)S(1)}, f32[8,16,1024]{2,1,0:T(8,128)S(1)}, u32[]{:S(2)}, u32[]{:S(2)}) collective-permute-start(f32[8,16,1024]{2,1,0:T(8,128)S(1)} %bitcast.38), channel_id=1, source_target_pairs={{0,64},{1,17},{2,66},{3,19},{4,68},{5,21},{6,70},{7,23},{8,72},{9,... | collective-permute-start | bytes 1572872 | tf_op jit(solution)/shard_map/ppermute | solution.py:53
  74.1 13.3 %collective-permute-start.14 = (f32[8,16,1024]{2,1,0:T(8,128)S(1)}, f32[8,16,1024]{2,1,0:T(8,128)S(1)}, u32[]{:S(2)}, u32[]{:S(2)}) collective-permute-start(f32[8,16,1024]{2,1,0:T(8,128)S(1)} %bitcast.39), channel_id=1, source_target_pairs={{0,32},{1,9},{2,34},{3,11},{4,36},{5,13},{6,38},{7,15},{8,40},{9,1... | collective-permute-start | bytes 1572872 | tf_op jit(solution)/shard_map/ppermute | solution.py:53
  74.3 13.1 %collective-permute-start.12 = (f32[8,16,1024]{2,1,0:T(8,128)S(1)}, f32[8,16,1024]{2,1,0:T(8,128)S(1)}, u32[]{:S(2)}, u32[]{:S(2)}) collective-permute-start(f32[8,16,1024]{2,1,0:T(8,128)S(1)} %bitcast.40), channel_id=1, source_target_pairs={{0,96},{1,25},{2,98},{3,27},{4,100},{5,29},{6,102},{7,31},{8,104},... | collective-permute-start | bytes 1572872 | tf_op jit(solution)/shard_map/ppermute | solution.py:53
  78.7 3.5 %collective-permute-start.15 = (f32[64,128]{1,0:T(8,128)S(1)}, f32[64,128]{1,0:T(8,128)S(1)}, u32[]{:S(2)}, u32[]{:S(2)}) collective-permute-start(f32[64,128]{1,0:T(8,128)S(1)} %get-tuple-element.95), channel_id=1, source_target_pairs={{0,8},{1,33},{2,10},{3,35},{4,12},{5,37},{6,14},{7,39},{8,0},{9,41... | collective-permute-start | bytes 98312 | tf_op jit(solution)/shard_map/ppermute | solution.py:53
  82.1 5.0 %collective-permute-start.16 = (f32[64,128]{1,0:T(8,128)S(1)}, f32[64,128]{1,0:T(8,128)S(1)}, u32[]{:S(2)}, u32[]{:S(2)}) collective-permute-start(f32[64,128]{1,0:T(8,128)S(1)} %add.83), channel_id=1, source_target_pairs={{0,24},{1,97},{2,26},{3,99},{4,28},{5,101},{6,30},{7,103},{8,16},{... | collective-permute-start | bytes 98312 | tf_op jit(solution)/shard_map/ppermute | solution.py:53
  87.6 15.7 %collective-permute-start.17 = (f32[2,8,16,1024]{3,2,1,0:T(8,128)S(1)}, f32[2,8,16,1024]{3,2,1,0:T(8,128)S(1)}, u32[]{:S(2)}, u32[]{:S(2)}) collective-permute-start(f32[2,8,16,1024]{3,2,1,0:T(8,128)S(1)} %pad_maximum_fusion.refs_0_), channel_id=1, source_target_pairs={{0,8},{1,33},{2,10},{3,35},{4,12},{5,37},{6,14},{7,39},{8,16},{9,4... | collective-permute-start | bytes 3145736 | tf_op jit(solution)/shard_map/ppermute | solution.py:53
  88.4 15.5 %collective-permute-start.18 = (f32[2,8,16,1024]{3,2,1,0:T(8,128)S(1)}, f32[2,8,16,1024]{3,2,1,0:T(8,128)S(1)}, u32[]{:S(2)}, u32[]{:S(2)}) collective-permute-start(f32[2,8,16,1024]{3,2,1,0:T(8,128)S(1)} %pad_maximum_fusion.1.refs_1_), channel_id=1, source_target_pairs={{0,24},{1,97},{2,26},{3,99},{4,28},{5,101},{6,30},{7,103},{8,0},{9... | collective-permute-start | bytes 3145736 | tf_op jit(solution)/shard_map/ppermute | solution.py:53
  90.5 2.8 %collective-permute-start.19 = (f32[64,128]{1,0:T(8,128)S(1)}, f32[64,128]{1,0:T(8,128)S(1)}, u32[]{:S(2)}, u32[]{:S(2)}) collective-permute-start(f32[64,128]{1,0:T(8,128)S(1)} %add.84), channel_id=1, source_target_pairs={{0,32},{1,9},{2,34},{3,11},{4,36},{5,13},{6,38},{7,15},{8,40},{9,1... | collective-permute-start | bytes 98312 | tf_op jit(solution)/shard_map/ppermute | solution.py:53
  93.2 4.3 %collective-permute-start.20 = (f32[64,128]{1,0:T(8,128)S(1)}, f32[64,128]{1,0:T(8,128)S(1)}, u32[]{:S(2)}, u32[]{:S(2)}) collective-permute-start(f32[64,128]{1,0:T(8,128)S(1)} %add.85), channel_id=1, source_target_pairs={{0,96},{1,25},{2,98},{3,27},{4,100},{5,29},{6,102},{7,31},{8,104},... | collective-permute-start | bytes 98312 | tf_op jit(solution)/shard_map/ppermute | solution.py:53
  94.9 22.8 %collective-permute-start.25 = (f32[2,8,16,1024]{3,2,1,0:T(8,128)S(1)}, f32[2,8,16,1024]{3,2,1,0:T(8,128)S(1)}, u32[]{:S(2)}, u32[]{:S(2)}) collective-permute-start(f32[2,8,16,1024]{3,2,1,0:T(8,128)S(1)} %pad_maximum_fusion.1.refs_1_), channel_id=1, source_target_pairs={{0,8},{1,33},{2,10},{3,35},{4,12},{5,37},{6,14},{7,39},{8,16},{9,4... | collective-permute-start | bytes 3145736 | tf_op jit(solution)/shard_map/ppermute | solution.py:53
  94.9 22.8 %collective-permute-start.26 = (f32[2,8,16,1024]{3,2,1,0:T(8,128)S(1)}, f32[2,8,16,1024]{3,2,1,0:T(8,128)S(1)}, u32[]{:S(2)}, u32[]{:S(2)}) collective-permute-start(f32[2,8,16,1024]{3,2,1,0:T(8,128)S(1)} %pad_maximum_fusion.refs_0_), channel_id=1, source_target_pairs={{0,24},{1,97},{2,26},{3,99},{4,28},{5,101},{6,30},{7,103},{8,0},{9... | collective-permute-start | bytes 3145736 | tf_op jit(solution)/shard_map/ppermute | solution.py:53
  103.8 25.2 %collective-permute-start.21 = (f32[2,8,16,1024]{3,2,1,0:T(8,128)S(1)}, f32[2,8,16,1024]{3,2,1,0:T(8,128)S(1)}, u32[]{:S(2)}, u32[]{:S(2)}) collective-permute-start(f32[2,8,16,1024]{3,2,1,0:T(8,128)S(1)} %collective-permute-done.17.refs_2_), channel_id=1, source_target_pairs={{0,8},{1,33},{2,10},{3,35},{4,12},{5,37},{6,14},{7,39},{8,16},{9,4... | collective-permute-start | bytes 3145736 | tf_op jit(solution)/shard_map/ppermute | solution.py:53
  105.2 23.8 %collective-permute-start.22 = (f32[2,8,16,1024]{3,2,1,0:T(8,128)S(1)}, f32[2,8,16,1024]{3,2,1,0:T(8,128)S(1)}, u32[]{:S(2)}, u32[]{:S(2)}) collective-permute-start(f32[2,8,16,1024]{3,2,1,0:T(8,128)S(1)} %collective-permute-done.18.refs_5_), channel_id=1, source_target_pairs={{0,24},{1,97},{2,26},{3,99},{4,28},{5,101},{6,30},{7,103},{8,0},{9... | collective-permute-start | bytes 3145736 | tf_op jit(solution)/shard_map/ppermute | solution.py:53
  106.5 8.1 %collective-permute-start.23 = (f32[56,128]{1,0:T(8,128)S(1)}, f32[56,128]{1,0:T(8,128)S(1)}, u32[]{:S(2)}, u32[]{:S(2)}) collective-permute-start(f32[56,128]{1,0:T(8,128)S(1)} %pad_maximum_fusion.2), channel_id=1, source_target_pairs={{0,1},{1,0},{2,3},{3,2},{4,5},{5,4},{6,7},{7,6},{8,9},{9,8},{10,11... | collective-permute-start | bytes 86024 | tf_op jit(solution)/shard_map/ppermute | solution.py:53
  114.6 3.0 %collective-permute-start.24 = (f32[56,128]{1,0:T(8,128)S(1)}, f32[56,128]{1,0:T(8,128)S(1)}, u32[]{:S(2)}, u32[]{:S(2)}) collective-permute-start(f32[56,128]{1,0:T(8,128)S(1)} %fusion.3), channel_id=1, source_target_pairs={{0,2},{1,3},{2,0},{3,1},{4,6},{5,7},{6,4},{7,5},{8,10},{9,11},{10,... | collective-permute-start | bytes 86024 | tf_op jit(solution)/shard_map/ppermute | solution.py:53
  117.7 4.4 %collective-permute-start.27 = (f32[56,128]{1,0:T(8,128)S(1)}, f32[56,128]{1,0:T(8,128)S(1)}, u32[]{:S(2)}, u32[]{:S(2)}) collective-permute-start(f32[56,128]{1,0:T(8,128)S(1)} %add.88), channel_id=1, source_target_pairs={{0,6},{1,7},{2,4},{3,5},{4,2},{5,3},{6,0},{7,1},{8,14},{9,15},{10,... | collective-permute-start | bytes 86024 | tf_op jit(solution)/shard_map/ppermute | solution.py:53
  134.0 8.4 %collective-permute-start.28 = (f32[256,1280]{1,0:T(8,128)S(1)}, f32[256,1280]{1,0:T(8,128)S(1)}, u32[]{:S(2)}, u32[]{:S(2)}) collective-permute-start(f32[256,1280]{1,0:T(8,128)S(1)} %get-tuple-element.108), channel_id=1, source_target_pairs={{0,1},{1,0},{2,3},{3,2},{4,5},{5,4},{6,7},{7,6},{8,9},{9,8},{10,11... | collective-permute-start | bytes 3932168 | tf_op jit(solution)/shard_map/ppermute | solution.py:53
  142.6 3.3 %copy-start.1 = (s32[1280]{0:T(1024)S(1)}, s32[1280]{0:T(1024)}, u32[]{:S(2)}) copy-start(s32[1280]{0:T(1024)} %param.11) | copy-start | bytes 15364
  142.6 3.3 %copy-start.3 = (f32[1280]{0:T(1024)S(1)}, f32[1280]{0:T(1024)}, u32[]{:S(2)}) copy-start(f32[1280]{0:T(1024)} %param.8) | copy-start | bytes 15364
  142.7 24.3 %collective-permute-start.29 = (f32[128,1280]{1,0:T(8,128)S(1)}, f32[128,1280]{1,0:T(8,128)S(1)}, u32[]{:S(2)}, u32[]{:S(2)}) collective-permute-start(f32[128,1280]{1,0:T(8,128)S(1)} %get-tuple-element.146), channel_id=1, source_target_pairs={{0,2},{1,3},{2,4},{3,5},{4,6},{5,7},{6,0},{7,1},{8,10},{9,11},{10,... | collective-permute-start | bytes 1966088 | tf_op jit(solution)/shard_map/ppermute | solution.py:53
  143.5 23.5 %collective-permute-start.30 = (f32[128,1280]{1,0:T(8,128)S(1)}, f32[128,1280]{1,0:T(8,128)S(1)}, u32[]{:S(2)}, u32[]{:S(2)}) collective-permute-start(f32[128,1280]{1,0:T(8,128)S(1)} %get-tuple-element.145), channel_id=1, source_target_pairs={{0,6},{1,7},{2,0},{3,1},{4,2},{5,3},{6,4},{7,5},{8,14},{9,15},{10,... | collective-permute-start | bytes 1966088 | tf_op jit(solution)/shard_map/ppermute | solution.py:53
  160.2 8.1 %collective-permute-start.36 = (f32[256,1280]{1,0:T(8,128)S(1)}, f32[256,1280]{1,0:T(8,128)S(1)}, u32[]{:S(2)}, u32[]{:S(2)}) collective-permute-start(f32[256,1280]{1,0:T(8,128)S(1)} %get-tuple-element.132), channel_id=1, source_target_pairs={{0,1},{1,0},{2,3},{3,2},{4,5},{5,4},{6,7},{7,6},{8,9},{9,8},{10,11... | collective-permute-start | bytes 3932168 | tf_op jit(solution)/shard_map/ppermute | solution.py:53
  160.7 10.5 %collective-permute-start.35 = (f32[256,1280]{1,0:T(8,128)S(1)}, f32[256,1280]{1,0:T(8,128)S(1)}, u32[]{:S(2)}, u32[]{:S(2)}) collective-permute-start(f32[256,1280]{1,0:T(8,128)S(1)} %get-tuple-element.130), channel_id=1, source_target_pairs={{0,1},{1,0},{2,3},{3,2},{4,5},{5,4},{6,7},{7,6},{8,9},{9,8},{10,11... | collective-permute-start | bytes 3932168 | tf_op jit(solution)/shard_map/ppermute | solution.py:53
  167.0 5.6 %collective-permute-start.31 = (f32[264,1280]{1,0:T(8,128)S(1)}, f32[264,1280]{1,0:T(8,128)S(1)}, u32[]{:S(2)}, u32[]{:S(2)}) collective-permute-start(f32[264,1280]{1,0:T(8,128)S(1)} %get-tuple-element.121), channel_id=1, source_target_pairs={{0,1},{1,0},{2,3},{3,2},{4,5},{5,4},{6,7},{7,6},{8,9},{9,8},{10,11... | collective-permute-start | bytes 4055048 | tf_op jit(solution)/shard_map/ppermute | solution.py:53
  169.6 42.5 %collective-permute-start.39 = (f32[256,1280]{1,0:T(8,128)}, f32[256,1280]{1,0:T(8,128)S(1)}, u32[]{:S(2)}, u32[]{:S(2)}) collective-permute-start(f32[256,1280]{1,0:T(8,128)} %add.96), channel_id=1, source_target_pairs={{0,6},{1,7},{2,0},{3,1},{4,2},{5,3},{6,4},{7,5},{8,14},{9,15},{10,... | collective-permute-start | bytes 3932168 | tf_op jit(solution)/shard_map/ppermute | solution.py:53
  172.5 39.6 %collective-permute-start.38 = (f32[256,1280]{1,0:T(8,128)}, f32[256,1280]{1,0:T(8,128)}, u32[]{:S(2)}, u32[]{:S(2)}) collective-permute-start(f32[256,1280]{1,0:T(8,128)} %add.95), channel_id=1, source_target_pairs={{0,2},{1,3},{2,4},{3,5},{4,6},{5,7},{6,0},{7,1},{8,10},{9,11},{10,... | collective-permute-start | bytes 3932168 | tf_op jit(solution)/shard_map/ppermute | solution.py:53
  172.5 33.3 %collective-permute-start.32 = (f32[8,1280]{1,0:T(8,128)S(1)}, f32[8,1280]{1,0:T(8,128)S(1)}, u32[]{:S(2)}, u32[]{:S(2)}) collective-permute-start(f32[8,1280]{1,0:T(8,128)S(1)} %slice_add_fusion.1.last), channel_id=1, source_target_pairs={{0,2},{1,3},{2,4},{3,5},{4,6},{5,7},{6,0},{7,1},{8,10},{9,11},{10,... | collective-permute-start | bytes 122888 | tf_op jit(solution)/shard_map/ppermute | solution.py:53
  172.6 36.1 %collective-permute-start.33 = (f32[8,1280]{1,0:T(8,128)S(1)}, f32[8,1280]{1,0:T(8,128)S(1)}, u32[]{:S(2)}, u32[]{:S(2)}) collective-permute-start(f32[8,1280]{1,0:T(8,128)S(1)} %slice_add_fusion.1.last), channel_id=1, source_target_pairs={{0,4},{1,5},{2,6},{3,7},{4,0},{5,1},{6,2},{7,3},{8,12},{9,13},{10,... | collective-permute-start | bytes 122888 | tf_op jit(solution)/shard_map/ppermute | solution.py:53
  176.5 32.3 %collective-permute-start.34 = (f32[8,1280]{1,0:T(8,128)S(1)}, f32[8,1280]{1,0:T(8,128)S(1)}, u32[]{:S(2)}, u32[]{:S(2)}) collective-permute-start(f32[8,1280]{1,0:T(8,128)S(1)} %slice_add_fusion.1.last), channel_id=1, source_target_pairs={{0,6},{1,7},{2,0},{3,1},{4,2},{5,3},{6,4},{7,5},{8,14},{9,15},{10,... | collective-permute-start | bytes 122888 | tf_op jit(solution)/shard_map/ppermute | solution.py:53
  205.8 5.6 %collective-permute-start.37 = (f32[32,1024]{1,0:T(8,128)S(1)}, f32[32,1024]{1,0:T(8,128)S(1)}, u32[]{:S(2)}, u32[]{:S(2)}) collective-permute-start(f32[32,1024]{1,0:T(8,128)S(1)} %add.79), channel_id=1, source_target_pairs={{0,96},{1,25},{2,98},{3,27},{4,100},{5,29},{6,102},{7,31},{8,104},... | collective-permute-start | bytes 393224 | tf_op jit(solution)/shard_map/ppermute | solution.py:53
where the time goes:
time: 216 us; the launch traced here: 215 us
  Pallas kernels  90.2 us (42%)
  starting transfers between devices  66.8 us (31%)
  waiting for transfers between devices  46.3 us (21%)
  other arithmetic  8.23 us (4%)
    ppermute x40, starting transfers between devices, send(): return lax.ppermute(array, ('cells', 'spots'), route(target))  66.8 us
    ppermute x40, waiting for transfers between devices, send(): return lax.ppermute(array, ('cells', 'spots'), route(target))  46.3 us
    pallas_call x4, Pallas kernels, back_call(): pl.pallas_call(functools.partial(back_kernel, parts=parts, first=len(firs...  23.7 us
    pallas_call x1, Pallas kernels, map_call(): pl.pallas_call(functools.partial(map_kernel, scale=scale), grid=(cells //...  21.1 us
    pallas_call x3, Pallas kernels, pred_call(): pl.pallas_call(pred_kernel, grid_spec=pltpu.PrefetchScalarGridSpec(num_sc...  20.1 us
    pallas_call x3, Pallas kernels, grad_call(): pl.pallas_call(functools.partial(grad_kernel, count=count, lane=lane, chi...  11.3 us
    pallas_call x1, Pallas kernels, expo_call(): pl.pallas_call(expo_kernel, grid_spec=pltpu.PrefetchScalarGridSpec(num_sc...  9.5 us
  transfers between devices with their start and end apart: 40, of which 18 were waited for; matrix products, arithmetic and copies ran while one was open for 3% of the time, Pallas kernels for 35%

commit v1 on v0

--- a/solution.py
+++ b/solution.py
@@ -425,24 +425,28 @@
     def _():
         column[...] = jnp.zeros_like(column)
 
-    total = jnp.zeros(column.shape, F32)
-    for index, part in enumerate(pred):
-        for sub in range(2):
-            at = gene_group(ids, *PIECES[lane + 2 * index + sub])
-            row = pl.multiple_of((at & 3) * 16, 16)
-            to = pl.ds(pl.multiple_of(at * 16, 16), 16)
-            for half in range(2):
-                block = chip * 2 + half
+    def half_of(half, _):
+        block = chip * 2 + half
+        factors = gene[pl.ds(pl.multiple_of(16 * half, 16), 16), :]
+        total = jnp.zeros(column.shape, F32)
+        for index, part in enumerate(pred):
+            for sub in range(2):
+                at = gene_group(ids, *PIECES[lane + 2 * index + sub])
+                row = pl.multiple_of((at & 3) * 16, 16)
+                to = pl.ds(pl.multiple_of(at * 16, 16), 16)
                 rows, inner = grad_rows(
                     part[sub, block],
                     data[index // 2][half, 0, pl.ds(row, 16), :],
-                    gene[16 * half : 16 * half + 16, :],
+                    factors,
                     spot,
                     lane + 2 * index + sub,
                 )
                 grad[0, block, to, :], grad[1, block, to, :] = split(rows)
                 total += inner
-    column[...] += total
+        column[...] += total
+        return 0
+
+    lax.fori_loop(0, 2, half_of, 0)
 
 
 def grad_call(ids, pred, spatial, gene, spot, lane, chips, done=()):
@@ -518,7 +522,7 @@
 
         @pl.when(step == k)
         def _(k=k, out=out):
-            out[:rows, :] = part
+            out[...] = part
             fetch(k).wait()
 
     sums[...] += jnp.sum((part * held[step]).reshape(-1, 8, part.shape[1]), axis=0)
@@ -530,15 +534,11 @@
             sums[...] = jnp.zeros_like(sums)
             sums[0:1, :] = total
             sums[1:2, 0:128] = more[3][...]
-            outs[0][rows:, :] = sums[...]
 
 
 def back_call(ids, parts, grad, masses, expr, first=(), last=()):
     _, blocks, rows, spots = grad.shape
     cells = masses.shape[1]
-    shapes = [(rows, cells)] * len(parts)
-    if last:
-        shapes[0] = (rows + 8, cells)
     return pl.pallas_call(
         functools.partial(back_kernel, parts=parts, first=len(first), last=len(last) // 4),
         grid_spec=pltpu.PrefetchScalarGridSpec(
@@ -554,8 +554,8 @@
             ],
         ),
         out_shape=[jax.ShapeDtypeStruct((8, cells), F32)]
-        + [jax.ShapeDtypeStruct(shape, F32) for shape in shapes],
-        compiler_params=vmem(16),
+        + [jax.ShapeDtypeStruct((rows, cells), F32)] * len(parts),
+        compiler_params=vmem(22),
         cost_estimate=NO_COST,
         name="back",
     )(ids, grad, masses, streamed(expr), *first, *last)
@@ -584,6 +584,26 @@
         cost_estimate=pl.CostEstimate(flops=10**10, bytes_accessed=0, transcendentals=0),
         name="lift",
     )(above, below, far_up, far_down)
+
+
+def join_kernel(above, below, got_above, got_below, out_above, out_below):
+    out_above[...] = above[...] + got_above[...]
+    out_below[...] = below[...] + got_below[...]
+
+
+def join_call(above, below, got_above, got_below):
+    rows, cells = above.shape
+    whole = pl.BlockSpec((rows, 256), lambda i: (0, i))
+    return pl.pallas_call(
+        join_kernel,
+        grid=(cells // 256,),
+        in_specs=[whole] * 4,
+        out_specs=[whole] * 2,
+        out_shape=[jax.ShapeDtypeStruct(above.shape, F32)] * 2,
+        compiler_params=vmem(8),
+        cost_estimate=NO_COST,
+        name="join",
+    )(above, below, got_above, got_below)
 
 
 def map_kernel(expr, grad, masses, keep, spot, out, held, ready, *, scale):
@@ -656,7 +676,9 @@
     shifted = (retained - 0.35 * nvalid) / (0.1 * all_cells)
     count_term = jnp.sqrt(shifted * shifted + 1.0)
     grad_keep = total[0:1, :] + shifted / count_term / (0.1 * all_cells) + (1.0 - 2.0 * keep) / nvalid
-    grad_filter[...] = valid * sigma * (1.0 - sigma) * grad_keep * all_cells
+    row = valid * sigma * (1.0 - sigma) * grad_keep * all_cells
+    for k in range(grad_filter.shape[0]):
+        grad_filter[k : k + 1, :] = row[:, 128 * k : 128 * k + 128]
     lane = lax.broadcasted_iota(jnp.int32, (1, 128), 1)
     out = jnp.zeros((1, 128), F32)
     parts = (scalars[:, 0:1], total[1:2, 1:2], scalars[:, 2:3], count_term, reg_sum / nvalid)
@@ -670,8 +692,11 @@
         functools.partial(finish_kernel, all_cells=float(all_cells)),
         grid=(1,),
         in_specs=[fixed(one.shape) for one in (last, *got, totals, scalars, kind, filt)],
-        out_specs=[fixed(kind.shape), fixed((1, 128))],
-        out_shape=[jax.ShapeDtypeStruct(kind.shape, F32), jax.ShapeDtypeStruct((1, 128), F32)],
+        out_specs=[fixed((kind.shape[1] // 128, 128)), fixed((1, 128))],
+        out_shape=[
+            jax.ShapeDtypeStruct((kind.shape[1] // 128, 128), F32),
+            jax.ShapeDtypeStruct((1, 128), F32),
+        ],
         compiler_params=vmem(4),
         cost_estimate=NO_COST,
         name="finish",
@@ -716,7 +741,6 @@
     late = pred_part((1, 0), (-1, 1), (far_right, far_left), *near)
     late_right, late_left = along(late[0], 1), along(late[1], -1)
     own = pred_part((0, 0), (0, 1), (near_left, near_right), *late)
-    types = types + swap_across(after(types, *own), 1)
     mine, *pieces = merge_call(own, (late_right, late_left))
     pieces = [across(piece, step + 1) for step, piece in enumerate(pieces)]
     spatial_squares = jnp.sum(after(spatial, mine) ** 2, axis=0)
@@ -773,26 +797,29 @@
     far = far_b + far_got
     far_up, far_down = up(far[:rows], 1), up(far[rows:], -1)
     grad, column_c = last_grad((1, -1, 0), grad, far)
-    sums_c, up_a, down_a, up_b, down_b = back_part([(1, 1), (-1, 1), (1, 0), (-1, 0)], grad)
-    up_got, down_got = swap(up_a, 0, 0, 0, 1), swap(down_a, 0, 0, 0, 1)
-    last, own_a, own_b = back_part(
-        [(0, 1), (0, 0)], grad, up_b, last=[sums_a, sums_b, sums_c, scalars]
+    sums_c, up_a, down_a, own_a, up_b, down_b = back_part(
+        [(1, 1), (-1, 1), (0, 1), (1, 0), (-1, 0)], grad
     )
-    above, below = lift_call(up_b, down_b, *after((far_up, far_down), own_b))
-    above, below = above + up_got, below + down_got
+    up_got, down_got, own_got = (swap(one, 0, 0, 0, 1) for one in (up_a, down_a, own_a))
+    above, below = lift_call(up_b, down_b, far_up, far_down)
+    above, below = join_call(above, below, up_got, down_got)
     near_up, near_down = up(above, 1), up(below, -1)
-    own_got = swap(after(own_a, far_up, far_down), 0, 0, 0, 1)
-    last = last + own_got[2 * rows :]
-    own = own_b + own_got[: 2 * rows]
+    types_got = swap_across(after(types, above), 1)
+    last, own_b = back_part(
+        [(0, 0)], grad, above, below, own_got, last=[sums_a, sums_b, sums_c, scalars]
+    )
+    types = types + after(types_got, own_b)
+    own = own_b + own_got
 
     column = jnp.sum(column_a + column_b + column_c, axis=0) * share + spot_coef[32] * mass
     map_rows = stacked([spot_coef[32], column])
-    map_rows = after(map_rows, above, below, last)
     map_args = (expr, grad.reshape(2, genes, spots), masses, keep2, map_rows, all_cells * genes)
+    types_got = swap_across(types, 3)
+    last = last + swap(last, 0, 0, 0, 1)
     got = [up(last, step) for step in (1, 2, 3)]
-    grad_map = map_call(*map_args)
+    types = types + types_got
+    grad_map = map_call(*after(map_args[:-1], last, types), map_args[-1])
     got = after(tuple(got), grad_map)
-    types = types + swap_across(after(types, grad_map), 3)
     grad_weighted = after(own, grad_map) + near_up + near_down
     grad_expr = grad_weighted * (keep * (genes * all_spots))[None, :]
 

time: 216 us -> 208 us (0.963)
  starting transfers between devices: 66.8 us -> 54.5 us
  waiting for transfers between devices: 46.3 us -> 52.9 us
  other arithmetic: 8.23 us -> 3.77 us
    ppermute x40 -> x41, starting transfers between devices: 66.8 us -> 54.5 us  [send(): return lax.ppermute(array, ('cells', 'spots'), route(target))]
    ppermute x40 -> x41, waiting for transfers between devices: 46.3 us -> 52.9 us  [send(): return lax.ppermute(array, ('cells', 'spots'), route(target))]
    add x5 -> x3, other arithmetic: 2.79 us -> 0.16 us  [the longest x1 0.14 us: on_device(): own = own_b + own_got]
  transfers between devices with their start and end apart: 40 -> 41, of which waited for: 18 -> 19; matrix products, arithmetic and copies ran while one was open for 3% -> 1% of each run, Pallas kernels for 35% -> 37%
where the time goes in v1:
time: 208 us; the launch traced here: 207 us
  Pallas kernels  92.2 us (44%)
  starting transfers between devices  54.5 us (26%)
  waiting for transfers between devices  52.9 us (25%)
  other arithmetic  3.77 us (2%)
    ppermute x41, starting transfers between devices, send(): return lax.ppermute(array, ('cells', 'spots'), route(target))  54.5 us
    ppermute x41, waiting for transfers between devices, send(): return lax.ppermute(array, ('cells', 'spots'), route(target))  52.9 us
    pallas_call x4, Pallas kernels, back_call(): pl.pallas_call(functools.partial(back_kernel, parts=parts, first=len(firs...  23.7 us
    pallas_call x1, Pallas kernels, map_call(): pl.pallas_call(functools.partial(map_kernel, scale=scale), grid=(cells //...  21.3 us
    pallas_call x3, Pallas kernels, pred_call(): pl.pallas_call(pred_kernel, grid_spec=pltpu.PrefetchScalarGridSpec(num_sc...  20 us
    pallas_call x3, Pallas kernels, grad_call(): pl.pallas_call(functools.partial(grad_kernel, count=count, lane=lane, chi...  11.6 us
    pallas_call x1, Pallas kernels, expo_call(): pl.pallas_call(expo_kernel, grid_spec=pltpu.PrefetchScalarGridSpec(num_sc...  9.51 us
  transfers between devices with their start and end apart: 41, of which 19 were waited for; matrix products, arithmetic and copies ran while one was open for 1% of the time, Pallas kernels for 37%

profile of v1, /device:TPU:1, one launch (start us, length us, event | category | flops | bytes accessed | tf_op | source)
XLA Modules:
  0.0 206.5 jit_solution(16126220130532827336)
XLA Ops:
  2.1 9.5 %expo.1 = (bf16[2,1280,1024]{2,1,0:T(8,128)(2,1)S(1)}, f32[32,1024]{1,0:T(8,128)S(1)}, f32[8,1024]{1,0:T(8,128)S(1)}, f32[33,8,1024]{2,1,0:T(8,128)S(1)}, f32[33,8,1024]{2,1,0:T(8,128)S(1)}) custom-call(s32[4]{0:T(128)S(1)} %pad_add_fusion.ids, f32[1280,1024]{1,0:T(8,128)} %logits.1, s32[10,128]{1,0:T(8,128)S(1)} %bitcast.44, f32[10,128]{1,0:T(8,128)S(1)} %bitcast.45, ...), custom_call_target="tpu_custom_call" | custom-call | bytes 1310720 | tf_op jit(solution)/shard_map/expo/pallas_call | solution.py:176
  11.6 2.5 %collective-permute-start = (f32[33,8,1024]{2,1,0:T(8,128)S(1)}, f32[33,8,1024]{2,1,0:T(8,128)S(1)}, u32[]{:S(2)}, u32[]{:S(2)}) collective-permute-start(f32[33,8,1024]{2,1,0:T(8,128)S(1)} %get-tuple-element.76), channel_id=1, source_target_pairs={{0,8},{1,33},{2,10},{3,35},{4,12},{5,37},{6,14},{7,39},{8,16},{9,4... | collective-permute-start | bytes 3244040 | tf_op jit(solution)/shard_map/ppermute | solution.py:53
  14.2 2.2 %collective-permute-start.1 = (f32[33,8,1024]{2,1,0:T(8,128)S(1)}, f32[33,8,1024]{2,1,0:T(8,128)S(1)}, u32[]{:S(2)}, u32[]{:S(2)}) collective-permute-start(f32[33,8,1024]{2,1,0:T(8,128)S(1)} %get-tuple-element.77), channel_id=1, source_target_pairs={{0,24},{1,97},{2,26},{3,99},{4,28},{5,101},{6,30},{7,103},{8,0},{9... | collective-permute-start | bytes 3244040 | tf_op jit(solution)/shard_map/ppermute | solution.py:53
  16.4 6.5 %pred_.3 = (f32[33,8,1024]{2,1,0:T(8,128)S(1)}, f32[33,8,1024]{2,1,0:T(8,128)S(1)}) custom-call(s32[4]{0:T(128)S(1)} %pad_add_fusion.ids, f32[8,16,16,1280]{3,2,1,0:T(8,128)} %bitcast.51, f32[8,16,16,1280]{3,2,1,0:T(8,128)} %bitcast.52, f32[1,1280]{1,0:T(1,128)S(1)} %reshape.94.keep, bf16[2,1280,1024]{2,1,0:T(8,128)(2,1)S(1)} %get-tuple-element.138.masses, ...), custom_call_target="tpu_custom_call" | custom-call | flops 503316480 | bytes 1245184 | tf_op jit(solution)/shard_map/pred/pallas_call | solution.py:240
  22.9 1.5 collective-permute-start.2
  24.4 4.7 %collective-permute-done.refs_0_ = f32[33,8,1024]{2,1,0:T(8,128)S(1)} collective-permute-done((f32[33,8,1024]{2,1,0:T(8,128)S(1)}, f32[33,8,1024]{2,1,0:T(8,128)S(1)}, u32[]{:S(2)}, u32[]{:S(2)}) %collective-permute-start) | collective-permute-done | bytes 1081376 | tf_op jit(solution)/shard_map/ppermute | solution.py:53
  29.1 6.9 %pred_.4 = (f32[33,8,1024]{2,1,0:T(8,128)S(1)}, f32[33,8,1024]{2,1,0:T(8,128)S(1)}) custom-call(s32[4]{0:T(128)S(1)} %pad_add_fusion.ids, f32[8,16,16,1280]{3,2,1,0:T(8,128)} %bitcast.53, f32[8,16,16,1280]{3,2,1,0:T(8,128)} %bitcast.54, f32[1,1280]{1,0:T(1,128)S(1)} %reshape.94.keep, bf16[2,1280,1024]{2,1,0:T(8,128)(2,1)S(1)} %get-tuple-element.138.masses, ...), custom_call_target="tpu_custom_call" | custom-call | flops 503316480 | bytes 1245184 | tf_op jit(solution)/shard_map/pred/pallas_call | solution.py:240
  37.1 1.9 collective-permute-start.5
  40.7 6.6 %pred_.5 = (f32[33,8,1024]{2,1,0:T(8,128)S(1)}, f32[33,8,1024]{2,1,0:T(8,128)S(1)}) custom-call(s32[4]{0:T(128)S(1)} %pad_add_fusion.ids, f32[8,16,16,1280]{3,2,1,0:T(8,128)} %bitcast.55, f32[8,16,16,1280]{3,2,1,0:T(8,128)} %bitcast.56, f32[1,1280]{1,0:T(1,128)S(1)} %reshape.94.keep, bf16[2,1280,1024]{2,1,0:T(8,128)(2,1)S(1)} %get-tuple-element.138.masses, ...), custom_call_target="tpu_custom_call" | custom-call | flops 503316480 | bytes 1245184 | tf_op jit(solution)/shard_map/pred/pallas_call | solution.py:240
  47.3 5.0 %collective-permute-done.4.got0 = f32[33,8,1024]{2,1,0:T(8,128)S(1)} collective-permute-done((f32[33,8,1024]{2,1,0:T(8,128)S(1)}, f32[33,8,1024]{2,1,0:T(8,128)S(1)}, u32[]{:S(2)}, u32[]{:S(2)}) %collective-permute-start.4) | collective-permute-done | bytes 1081376 | tf_op jit(solution)/shard_map/ppermute | solution.py:53
  53.1 2.5 %collective-permute-start.10 = (f32[17,8,1024]{2,1,0:T(8,128)S(1)}, f32[17,8,1024]{2,1,0:T(8,128)S(1)}, u32[]{:S(2)}, u32[]{:S(2)}) collective-permute-start(f32[17,8,1024]{2,1,0:T(8,128)S(1)} %get-tuple-element.96), channel_id=1, source_target_pairs={{0,96},{1,25},{2,98},{3,27},{4,100},{5,29},{6,102},{7,31},{8,104},... | collective-permute-start | bytes 1671176 | tf_op jit(solution)/shard_map/ppermute | solution.py:53
  55.6 1.5 collective-permute-start.9
  59.2 4.3 %collective-permute-done.6 = f32[32,1024]{1,0:T(8,128)S(1)} collective-permute-done((f32[32,1024]{1,0:T(8,128)S(1)}, f32[32,1024]{1,0:T(8,128)S(1)}, u32[]{:S(2)}, u32[]{:S(2)}) %collective-permute-start.6) | collective-permute-done | bytes 131104 | tf_op jit(solution)/shard_map/ppermute | solution.py:53
  63.5 3.0 %collective-permute-start.7 = (f32[32,1024]{1,0:T(8,128)S(1)}, f32[32,1024]{1,0:T(8,128)S(1)}, u32[]{:S(2)}, u32[]{:S(2)}) collective-permute-start(f32[32,1024]{1,0:T(8,128)S(1)} %add.71), channel_id=1, source_target_pairs={{0,24},{1,97},{2,26},{3,99},{4,28},{5,101},{6,30},{7,103},{8,16},{... | collective-permute-start | bytes 393224 | tf_op jit(solution)/shard_map/ppermute | solution.py:53
  66.5 9.3 %collective-permute-done.7 = f32[32,1024]{1,0:T(8,128)S(1)} collective-permute-done((f32[32,1024]{1,0:T(8,128)S(1)}, f32[32,1024]{1,0:T(8,128)S(1)}, u32[]{:S(2)}, u32[]{:S(2)}) %collective-permute-start.7) | collective-permute-done | bytes 131104 | tf_op jit(solution)/shard_map/ppermute | solution.py:53
  76.1 2.3 %collective-permute-start.12 = (f32[8,16,1024]{2,1,0:T(8,128)S(1)}, f32[8,16,1024]{2,1,0:T(8,128)S(1)}, u32[]{:S(2)}, u32[]{:S(2)}) collective-permute-start(f32[8,16,1024]{2,1,0:T(8,128)S(1)} %bitcast.39), channel_id=1, source_target_pairs={{0,64},{1,17},{2,66},{3,19},{4,68},{5,21},{6,70},{7,23},{8,72},{9,... | collective-permute-start | bytes 1572872 | tf_op jit(solution)/shard_map/ppermute | solution.py:53
  78.7 2.4 %collective-permute-start.11 = (f32[8,16,1024]{2,1,0:T(8,128)S(1)}, f32[8,16,1024]{2,1,0:T(8,128)S(1)}, u32[]{:S(2)}, u32[]{:S(2)}) collective-permute-start(f32[8,16,1024]{2,1,0:T(8,128)S(1)} %bitcast.41), channel_id=1, source_target_pairs={{0,96},{1,25},{2,98},{3,27},{4,100},{5,29},{6,102},{7,31},{8,104},... | collective-permute-start | bytes 1572872 | tf_op jit(solution)/shard_map/ppermute | solution.py:53
  81.0 1.9 stats.1
  83.0 3.5 %collective-permute-done.14 = f32[64,128]{1,0:T(8,128)S(1)} collective-permute-done((f32[64,128]{1,0:T(8,128)S(1)}, f32[64,128]{1,0:T(8,128)S(1)}, u32[]{:S(2)}, u32[]{:S(2)}) %collective-permute-start.14) | collective-permute-done | bytes 32800 | tf_op jit(solution)/shard_map/ppermute | solution.py:53
  86.7 4.5 %collective-permute-done.15 = f32[64,128]{1,0:T(8,128)S(1)} collective-permute-done((f32[64,128]{1,0:T(8,128)S(1)}, f32[64,128]{1,0:T(8,128)S(1)}, u32[]{:S(2)}, u32[]{:S(2)}) %collective-permute-start.15) | collective-permute-done | bytes 32800 | tf_op jit(solution)/shard_map/ppermute | solution.py:53
  92.3 2.7 %collective-permute-start.17 = (f32[2,8,16,1024]{3,2,1,0:T(8,128)S(1)}, f32[2,8,16,1024]{3,2,1,0:T(8,128)S(1)}, u32[]{:S(2)}, u32[]{:S(2)}) collective-permute-start(f32[2,8,16,1024]{3,2,1,0:T(8,128)S(1)} %pad_maximum_fusion.1.refs_1_), channel_id=1, source_target_pairs={{0,24},{1,97},{2,26},{3,99},{4,28},{5,101},{6,30},{7,103},{8,0},{9... | collective-permute-start | bytes 3145736 | tf_op jit(solution)/shard_map/ppermute | solution.py:53
  95.7 2.7 %collective-permute-done.18 = f32[64,128]{1,0:T(8,128)S(1)} collective-permute-done((f32[64,128]{1,0:T(8,128)S(1)}, f32[64,128]{1,0:T(8,128)S(1)}, u32[]{:S(2)}, u32[]{:S(2)}) %collective-permute-start.18) | collective-permute-done | bytes 32800 | tf_op jit(solution)/shard_map/ppermute | solution.py:53
  99.5 2.7 %collective-permute-start.25 = (f32[2,8,16,1024]{3,2,1,0:T(8,128)S(1)}, f32[2,8,16,1024]{3,2,1,0:T(8,128)S(1)}, u32[]{:S(2)}, u32[]{:S(2)}) collective-permute-start(f32[2,8,16,1024]{3,2,1,0:T(8,128)S(1)} %pad_maximum_fusion.refs_0_), channel_id=1, source_target_pairs={{0,24},{1,97},{2,26},{3,99},{4,28},{5,101},{6,30},{7,103},{8,0},{9... | collective-permute-start | bytes 3145736 | tf_op jit(solution)/shard_map/ppermute | solution.py:53
  103.0 4.7 %collective-permute-done.16.refs_2_ = f32[2,8,16,1024]{3,2,1,0:T(8,128)S(1)} collective-permute-done((f32[2,8,16,1024]{3,2,1,0:T(8,128)S(1)}, f32[2,8,16,1024]{3,2,1,0:T(8,128)S(1)}, u32[]{:S(2)}, u32[]{:S(2)}) %collective-permute-start.16) | collective-permute-done | bytes 1048608 | tf_op jit(solution)/shard_map/ppermute | solution.py:53
  107.8 2.7 %collective-permute-start.21 = (f32[2,8,16,1024]{3,2,1,0:T(8,128)S(1)}, f32[2,8,16,1024]{3,2,1,0:T(8,128)S(1)}, u32[]{:S(2)}, u32[]{:S(2)}) collective-permute-start(f32[2,8,16,1024]{3,2,1,0:T(8,128)S(1)} %collective-permute-done.17.refs_5_), channel_id=1, source_target_pairs={{0,24},{1,97},{2,26},{3,99},{4,28},{5,101},{6,30},{7,103},{8,0},{9... | collective-permute-start | bytes 3145736 | tf_op jit(solution)/shard_map/ppermute | solution.py:53
  110.5 2.5 %collective-permute-start.22 = (f32[56,128]{1,0:T(8,128)S(1)}, f32[56,128]{1,0:T(8,128)S(1)}, u32[]{:S(2)}, u32[]{:S(2)}) collective-permute-start(f32[56,128]{1,0:T(8,128)S(1)} %pad_maximum_fusion.2), channel_id=1, source_target_pairs={{0,1},{1,0},{2,3},{3,2},{4,5},{5,4},{6,7},{7,6},{8,9},{9,8},{10,11... | collective-permute-start | bytes 86024 | tf_op jit(solution)/shard_map/ppermute | solution.py:53
  115.1 1.7 collective-permute-done.23
  116.9 2.1 %collective-permute-done.24.refs_3_ = f32[2,8,16,1024]{3,2,1,0:T(8,128)S(1)} collective-permute-done((f32[2,8,16,1024]{3,2,1,0:T(8,128)S(1)}, f32[2,8,16,1024]{3,2,1,0:T(8,128)S(1)}, u32[]{:S(2)}, u32[]{:S(2)}) %collective-permute-start.24) | collective-permute-done | bytes 1048608 | tf_op jit(solution)/shard_map/ppermute | solution.py:53
  119.0 2.7 %collective-permute-start.26 = (f32[56,128]{1,0:T(8,128)S(1)}, f32[56,128]{1,0:T(8,128)S(1)}, u32[]{:S(2)}, u32[]{:S(2)}) collective-permute-start(f32[56,128]{1,0:T(8,128)S(1)} %add.81), channel_id=1, source_target_pairs={{0,6},{1,7},{2,4},{3,5},{4,2},{5,3},{6,0},{7,1},{8,14},{9,15},{10,... | collective-permute-start | bytes 86024 | tf_op jit(solution)/shard_map/ppermute | solution.py:53
  121.8 1.6 collective-permute-done.26
  124.2 6.2 %grad.3 = (bf16[2,8,256,1024]{3,2,1,0:T(8,128)(2,1)S(1)}, f32[8,1024]{1,0:T(8,128)S(1)}) custom-call(s32[4]{0:T(128)S(1)} %pad_add_fusion.ids, f32[2,8,16,1024]{3,2,1,0:T(8,128)S(1)} %pad_maximum_fusion.refs_0_, f32[2,8,16,1024]{3,2,1,0:T(8,128)S(1)} %pad_maximum_fusion.1.refs_1_, f32[2,8,16,1024]{3,2,1,0:T(8,128)S(1)} %collective-permute-done.16.refs_2_, ...), custom_call_target="tpu_custom_call" | custom-call | tf_op jit(solution)/shard_map/grad/pallas_call | solution.py:465
  130.4 2.0 grad.4
  132.3 3.1 %back.4 = (f32[8,1280]{1,0:T(8,128)S(1)}, f32[256,1280]{1,0:T(8,128)S(1)}) custom-call(s32[4]{0:T(128)S(1)} %pad_add_fusion.ids, bf16[2,8,256,1024]{3,2,1,0:T(8,128)(2,1)S(1)} %get-tuple-element.109.grad.refs_5_, bf16[2,1280,1024]{2,1,0:T(8,128)(2,1)S(1)} %get-tuple-element.138.masses, f32[2048,1280]{1,0:T(8,128)} %expr.8, ...), custom_call_target="tpu_custom_call" | custom-call | tf_op jit(solution)/shard_map/back/pallas_call | solution.py:542
  135.4 2.7 %collective-permute-start.27 = (f32[256,1280]{1,0:T(8,128)S(1)}, f32[256,1280]{1,0:T(8,128)S(1)}, u32[]{:S(2)}, u32[]{:S(2)}) collective-permute-start(f32[256,1280]{1,0:T(8,128)S(1)} %get-tuple-element.110), channel_id=1, source_target_pairs={{0,1},{1,0},{2,3},{3,2},{4,5},{5,4},{6,7},{7,6},{8,9},{9,8},{10,11... | collective-permute-start | bytes 3932168 | tf_op jit(solution)/shard_map/ppermute | solution.py:53
  138.2 3.6 %back.5 = (f32[8,1280]{1,0:T(8,128)S(1)}, f32[256,1280]{1,0:T(8,128)S(1)}) custom-call(s32[4]{0:T(128)S(1)} %pad_add_fusion.ids, bf16[2,8,256,1024]{3,2,1,0:T(8,128)(2,1)S(1)} %get-tuple-element.109.grad.refs_5_, bf16[2,1280,1024]{2,1,0:T(8,128)(2,1)S(1)} %get-tuple-element.138.masses, f32[2048,1280]{1,0:T(8,128)} %expr.8), custom_call_target="tpu_custom_call" | custom-call | tf_op jit(solution)/shard_map/back/pallas_call | solution.py:542
  142.5 2.7 %collective-permute-start.29 = (f32[128,1280]{1,0:T(8,128)S(1)}, f32[128,1280]{1,0:T(8,128)S(1)}, u32[]{:S(2)}, u32[]{:S(2)}) collective-permute-start(f32[128,1280]{1,0:T(8,128)S(1)} %get-tuple-element.153), channel_id=1, source_target_pairs={{0,6},{1,7},{2,0},{3,1},{4,2},{5,3},{6,4},{7,5},{8,14},{9,15},{10,... | collective-permute-start | bytes 1966088 | tf_op jit(solution)/shard_map/ppermute | solution.py:53
  145.1 3.5 %grad.5 = (bf16[2,8,256,1024]{3,2,1,0:T(8,128)(2,1)S(1)}, f32[8,1024]{1,0:T(8,128)S(1)}) custom-call(s32[4]{0:T(128)S(1)} %pad_add_fusion.ids, f32[2,8,16,1024]{3,2,1,0:T(8,128)S(1)} %collective-permute-done.20.refs_0_, f32[2,8,16,1024]{3,2,1,0:T(8,128)S(1)} %collective-permute-done.21.refs_1_, ...), custom_call_target="tpu_custom_call", output_to_operand_aliasing={{0}: (6, {})} | custom-call | tf_op jit(solution)/shard_map/grad/pallas_call | solution.py:465
  148.6 13.5 %back.6 = (f32[8,1280]{1,0:T(8,128)S(1)}, f32[256,1280]{1,0:T(8,128)S(1)}, f32[256,1280]{1,0:T(8,128)S(1)}, f32[256,1280]{1,0:T(8,128)S(1)}, f32[256,1280]{1,0:T(8,128)S(1)}, /*index=5*/f32[256,1280]{1,0:T(8,128)S(1)}) custom-call(s32[4]{0:T(128)S(1)} %pad_add_fusion.ids, bf16[2,8,256,1024]{3,2,1,0:T(8,128)(2,1)S(1)} %get-tuple-element.114.grad, ...), custom_call_target="tpu_custom_call" | custom-call | tf_op jit(solution)/shard_map/back/pallas_call | solution.py:542
  163.8 1.4 collective-permute-done.30.got_above
  165.2 1.9 collective-permute-done.31.got_below
  168.1 2.7 %collective-permute-start.40 = (f32[256,1280]{1,0:T(8,128)S(1)}, f32[256,1280]{1,0:T(8,128)S(1)}, u32[]{:S(2)}, u32[]{:S(2)}) collective-permute-start(f32[256,1280]{1,0:T(8,128)S(1)} %get-tuple-element.122), channel_id=1, source_target_pairs={{0,6},{1,7},{2,0},{3,1},{4,2},{5,3},{6,4},{7,5},{8,14},{9,15},{10,... | collective-permute-start | bytes 3932168 | tf_op jit(solution)/shard_map/ppermute | solution.py:53
  170.8 1.7 collective-permute-start.37
  172.5 3.6 %back.7 = (f32[8,1280]{1,0:T(8,128)S(1)}, f32[256,1280]{1,0:T(8,128)S(1)}) custom-call(s32[4]{0:T(128)S(1)} %pad_add_fusion.ids, bf16[2,8,256,1024]{3,2,1,0:T(8,128)(2,1)S(1)} %get-tuple-element.114.grad, bf16[2,1280,1024]{2,1,0:T(8,128)(2,1)S(1)} %get-tuple-element.138.masses, f32[2048,1280]{1,0:T(8,128)} %expr.8, ...), custom_call_target="tpu_custom_call" | custom-call | tf_op jit(solution)/shard_map/back/pallas_call | solution.py:542
  176.3 2.3 %collective-permute-start.38 = (f32[32,1024]{1,0:T(8,128)S(1)}, f32[32,1024]{1,0:T(8,128)S(1)}, u32[]{:S(2)}, u32[]{:S(2)}) collective-permute-start(f32[32,1024]{1,0:T(8,128)S(1)} %add.88), channel_id=1, source_target_pairs={{0,96},{1,25},{2,98},{3,27},{4,100},{5,29},{6,102},{7,31},{8,104},... | collective-permute-start | bytes 393224 | tf_op jit(solution)/shard_map/ppermute | solution.py:53
  178.9 1.4 collective-permute-start.35
  180.3 1.4 collective-permute-done.38
  182.5 21.3 %grad_map.1 = f32[1280,1024]{1,0:T(8,128)} custom-call(f32[2048,1280]{1,0:T(8,128)} %expr.8, bf16[2,2048,1024]{2,1,0:T(8,128)(2,1)S(1)} %bitcast.38, bf16[2,1280,1024]{2,1,0:T(8,128)(2,1)S(1)} %get-tuple-element.138.masses, f32[10,128]{1,0:T(8,128)S(1)} %bitcast.46, f32[8,1024]{1,0:T(8,128)S(1)} %select_select_fusion.spot), custom_call_target="tpu_custom_call" | custom-call | tf_op jit(solution)/shard_map/grad_map/pallas_call | solution.py:648
  205.1 1.4 add_multiply_fusion
  (107 shorter events, 20.9 us)
Async XLA Ops:
  0.7 0.7 copy-start
  11.6 17.5 %collective-permute-start = (f32[33,8,1024]{2,1,0:T(8,128)S(1)}, f32[33,8,1024]{2,1,0:T(8,128)S(1)}, u32[]{:S(2)}, u32[]{:S(2)}) collective-permute-start(f32[33,8,1024]{2,1,0:T(8,128)S(1)} %get-tuple-element.76), channel_id=1, source_target_pairs={{0,8},{1,33},{2,10},{3,35},{4,12},{5,37},{6,14},{7,39},{8,16},{9,4... | collective-permute-start | bytes 3244040 | tf_op jit(solution)/shard_map/ppermute | solution.py:53
  14.2 14.9 %collective-permute-start.1 = (f32[33,8,1024]{2,1,0:T(8,128)S(1)}, f32[33,8,1024]{2,1,0:T(8,128)S(1)}, u32[]{:S(2)}, u32[]{:S(2)}) collective-permute-start(f32[33,8,1024]{2,1,0:T(8,128)S(1)} %get-tuple-element.77), channel_id=1, source_target_pairs={{0,24},{1,97},{2,26},{3,99},{4,28},{5,101},{6,30},{7,103},{8,0},{9... | collective-permute-start | bytes 3244040 | tf_op jit(solution)/shard_map/ppermute | solution.py:53
  22.9 17.4 %collective-permute-start.2 = (f32[33,8,1024]{2,1,0:T(8,128)S(1)}, f32[33,8,1024]{2,1,0:T(8,128)S(1)}, u32[]{:S(2)}, u32[]{:S(2)}) collective-permute-start(f32[33,8,1024]{2,1,0:T(8,128)S(1)} %get-tuple-element.82), channel_id=1, source_target_pairs={{0,24},{1,97},{2,26},{3,99},{4,28},{5,101},{6,30},{7,103},{8,0},{9... | collective-permute-start | bytes 3244040 | tf_op jit(solution)/shard_map/ppermute | solution.py:53
  24.3 16.4 %collective-permute-start.3 = (f32[33,8,1024]{2,1,0:T(8,128)S(1)}, f32[33,8,1024]{2,1,0:T(8,128)S(1)}, u32[]{:S(2)}, u32[]{:S(2)}) collective-permute-start(f32[33,8,1024]{2,1,0:T(8,128)S(1)} %get-tuple-element.81), channel_id=1, source_target_pairs={{0,8},{1,33},{2,10},{3,35},{4,12},{5,37},{6,14},{7,39},{8,16},{9,4... | collective-permute-start | bytes 3244040 | tf_op jit(solution)/shard_map/ppermute | solution.py:53
  29.1 28.0 %slice-start = ((s8[8388608]{0:T(1024)(128)(4,1)}), s8[4194304]{0:T(1024)(128)(4,1)S(1)}, s32[]{:S(2)}) async-start(s8[8388608]{0:T(1024)(128)(4,1)} %bitcast.63), calls=%async_computation | async-start | bytes 8388608
  36.0 16.3 %collective-permute-start.4 = (f32[33,8,1024]{2,1,0:T(8,128)S(1)}, f32[33,8,1024]{2,1,0:T(8,128)S(1)}, u32[]{:S(2)}, u32[]{:S(2)}) collective-permute-start(f32[33,8,1024]{2,1,0:T(8,128)S(1)} %get-tuple-element.84), channel_id=1, source_target_pairs={{0,8},{1,33},{2,10},{3,35},{4,12},{5,37},{6,14},{7,39},{8,16},{9,4... | collective-permute-start | bytes 3244040 | tf_op jit(solution)/shard_map/ppermute | solution.py:53
  37.1 20.0 %slice-start.1 = ((s8[8388608]{0:T(1024)(128)(4,1)}), s8[4194304]{0:T(1024)(128)(4,1)S(1)}, s32[]{:S(2)}) async-start(s8[8388608]{0:T(1024)(128)(4,1)} %bitcast.63), calls=%async_computation.1 | async-start | bytes 8388608
  37.1 15.2 %collective-permute-start.5 = (f32[33,8,1024]{2,1,0:T(8,128)S(1)}, f32[33,8,1024]{2,1,0:T(8,128)S(1)}, u32[]{:S(2)}, u32[]{:S(2)}) collective-permute-start(f32[33,8,1024]{2,1,0:T(8,128)S(1)} %get-tuple-element.85), channel_id=1, source_target_pairs={{0,24},{1,97},{2,26},{3,99},{4,28},{5,101},{6,30},{7,103},{8,0},{9... | collective-permute-start | bytes 3244040 | tf_op jit(solution)/shard_map/ppermute | solution.py:53
  53.1 22.7 %collective-permute-start.10 = (f32[17,8,1024]{2,1,0:T(8,128)S(1)}, f32[17,8,1024]{2,1,0:T(8,128)S(1)}, u32[]{:S(2)}, u32[]{:S(2)}) collective-permute-start(f32[17,8,1024]{2,1,0:T(8,128)S(1)} %get-tuple-element.96), channel_id=1, source_target_pairs={{0,96},{1,25},{2,98},{3,27},{4,100},{5,29},{6,102},{7,31},{8,104},... | collective-permute-start | bytes 1671176 | tf_op jit(solution)/shard_map/ppermute | solution.py:53
  55.6 20.2 %collective-permute-start.8 = (f32[17,8,1024]{2,1,0:T(8,128)S(1)}, f32[17,8,1024]{2,1,0:T(8,128)S(1)}, u32[]{:S(2)}, u32[]{:S(2)}) collective-permute-start(f32[17,8,1024]{2,1,0:T(8,128)S(1)} %get-tuple-element.94), channel_id=1, source_target_pairs={{0,32},{1,9},{2,34},{3,11},{4,36},{5,13},{6,38},{7,15},{8,40},{9,1... | collective-permute-start | bytes 1671176 | tf_op jit(solution)/shard_map/ppermute | solution.py:53
  55.6 3.5 %copy-start.4 = (s32[1024]{0:T(1024)S(1)}, s32[1024]{0:T(1024)}, u32[]{:S(2)}) copy-start(s32[1024]{0:T(1024)} %param.12) | copy-start | bytes 12292
  55.6 3.5 %copy-start.5 = (s32[1024]{0:T(1024)S(1)}, s32[1024]{0:T(1024)}, u32[]{:S(2)}) copy-start(s32[1024]{0:T(1024)} %param.13) | copy-start | bytes 12292
  55.6 20.2 %collective-permute-start.9 = (f32[17,8,1024]{2,1,0:T(8,128)S(1)}, f32[17,8,1024]{2,1,0:T(8,128)S(1)}, u32[]{:S(2)}, u32[]{:S(2)}) collective-permute-start(f32[17,8,1024]{2,1,0:T(8,128)S(1)} %get-tuple-element.95), channel_id=1, source_target_pairs={{0,64},{1,17},{2,66},{3,19},{4,68},{5,21},{6,70},{7,23},{8,72},{9,... | collective-permute-start | bytes 1671176 | tf_op jit(solution)/shard_map/ppermute | solution.py:53
  57.8 5.7 %collective-permute-start.6 = (f32[32,1024]{1,0:T(8,128)S(1)}, f32[32,1024]{1,0:T(8,128)S(1)}, u32[]{:S(2)}, u32[]{:S(2)}) collective-permute-start(f32[32,1024]{1,0:T(8,128)S(1)} %get-tuple-element.92), channel_id=1, source_target_pairs={{0,8},{1,33},{2,10},{3,35},{4,12},{5,37},{6,14},{7,39},{8,0},{9,41... | collective-permute-start | bytes 393224 | tf_op jit(solution)/shard_map/ppermute | solution.py:53
  63.5 12.3 %collective-permute-start.7 = (f32[32,1024]{1,0:T(8,128)S(1)}, f32[32,1024]{1,0:T(8,128)S(1)}, u32[]{:S(2)}, u32[]{:S(2)}) collective-permute-start(f32[32,1024]{1,0:T(8,128)S(1)} %add.71), channel_id=1, source_target_pairs={{0,24},{1,97},{2,26},{3,99},{4,28},{5,101},{6,30},{7,103},{8,16},{... | collective-permute-start | bytes 393224 | tf_op jit(solution)/shard_map/ppermute | solution.py:53
  76.1 15.1 %collective-permute-start.12 = (f32[8,16,1024]{2,1,0:T(8,128)S(1)}, f32[8,16,1024]{2,1,0:T(8,128)S(1)}, u32[]{:S(2)}, u32[]{:S(2)}) collective-permute-start(f32[8,16,1024]{2,1,0:T(8,128)S(1)} %bitcast.39), channel_id=1, source_target_pairs={{0,64},{1,17},{2,66},{3,19},{4,68},{5,21},{6,70},{7,23},{8,72},{9,... | collective-permute-start | bytes 1572872 | tf_op jit(solution)/shard_map/ppermute | solution.py:53
  78.3 13.6 %collective-permute-start.13 = (f32[8,16,1024]{2,1,0:T(8,128)S(1)}, f32[8,16,1024]{2,1,0:T(8,128)S(1)}, u32[]{:S(2)}, u32[]{:S(2)}) collective-permute-start(f32[8,16,1024]{2,1,0:T(8,128)S(1)} %bitcast.40), channel_id=1, source_target_pairs={{0,32},{1,9},{2,34},{3,11},{4,36},{5,13},{6,38},{7,15},{8,40},{9,1... | collective-permute-start | bytes 1572872 | tf_op jit(solution)/shard_map/ppermute | solution.py:53
  78.7 13.4 %collective-permute-start.11 = (f32[8,16,1024]{2,1,0:T(8,128)S(1)}, f32[8,16,1024]{2,1,0:T(8,128)S(1)}, u32[]{:S(2)}, u32[]{:S(2)}) collective-permute-start(f32[8,16,1024]{2,1,0:T(8,128)S(1)} %bitcast.41), channel_id=1, source_target_pairs={{0,96},{1,25},{2,98},{3,27},{4,100},{5,29},{6,102},{7,31},{8,104},... | collective-permute-start | bytes 1572872 | tf_op jit(solution)/shard_map/ppermute | solution.py:53
  82.9 3.6 %collective-permute-start.14 = (f32[64,128]{1,0:T(8,128)S(1)}, f32[64,128]{1,0:T(8,128)S(1)}, u32[]{:S(2)}, u32[]{:S(2)}) collective-permute-start(f32[64,128]{1,0:T(8,128)S(1)} %get-tuple-element.97), channel_id=1, source_target_pairs={{0,8},{1,33},{2,10},{3,35},{4,12},{5,37},{6,14},{7,39},{8,0},{9,41... | collective-permute-start | bytes 98312 | tf_op jit(solution)/shard_map/ppermute | solution.py:53
  86.5 4.7 %collective-permute-start.15 = (f32[64,128]{1,0:T(8,128)S(1)}, f32[64,128]{1,0:T(8,128)S(1)}, u32[]{:S(2)}, u32[]{:S(2)}) collective-permute-start(f32[64,128]{1,0:T(8,128)S(1)} %add.76), channel_id=1, source_target_pairs={{0,24},{1,97},{2,26},{3,99},{4,28},{5,101},{6,30},{7,103},{8,16},{... | collective-permute-start | bytes 98312 | tf_op jit(solution)/shard_map/ppermute | solution.py:53
  92.2 15.6 %collective-permute-start.16 = (f32[2,8,16,1024]{3,2,1,0:T(8,128)S(1)}, f32[2,8,16,1024]{3,2,1,0:T(8,128)S(1)}, u32[]{:S(2)}, u32[]{:S(2)}) collective-permute-start(f32[2,8,16,1024]{3,2,1,0:T(8,128)S(1)} %pad_maximum_fusion.refs_0_), channel_id=1, source_target_pairs={{0,8},{1,33},{2,10},{3,35},{4,12},{5,37},{6,14},{7,39},{8,16},{9,4... | collective-permute-start | bytes 3145736 | tf_op jit(solution)/shard_map/ppermute | solution.py:53
  92.3 15.5 %collective-permute-start.17 = (f32[2,8,16,1024]{3,2,1,0:T(8,128)S(1)}, f32[2,8,16,1024]{3,2,1,0:T(8,128)S(1)}, u32[]{:S(2)}, u32[]{:S(2)}) collective-permute-start(f32[2,8,16,1024]{3,2,1,0:T(8,128)S(1)} %pad_maximum_fusion.1.refs_1_), channel_id=1, source_target_pairs={{0,24},{1,97},{2,26},{3,99},{4,28},{5,101},{6,30},{7,103},{8,0},{9... | collective-permute-start | bytes 3145736 | tf_op jit(solution)/shard_map/ppermute | solution.py:53
  94.9 3.4 %collective-permute-start.18 = (f32[64,128]{1,0:T(8,128)S(1)}, f32[64,128]{1,0:T(8,128)S(1)}, u32[]{:S(2)}, u32[]{:S(2)}) collective-permute-start(f32[64,128]{1,0:T(8,128)S(1)} %add.77), channel_id=1, source_target_pairs={{0,32},{1,9},{2,34},{3,11},{4,36},{5,13},{6,38},{7,15},{8,40},{9,1... | collective-permute-start | bytes 98312 | tf_op jit(solution)/shard_map/ppermute | solution.py:53
  98.4 4.7 %collective-permute-start.19 = (f32[64,128]{1,0:T(8,128)S(1)}, f32[64,128]{1,0:T(8,128)S(1)}, u32[]{:S(2)}, u32[]{:S(2)}) collective-permute-start(f32[64,128]{1,0:T(8,128)S(1)} %add.78), channel_id=1, source_target_pairs={{0,96},{1,25},{2,98},{3,27},{4,100},{5,29},{6,102},{7,31},{8,104},... | collective-permute-start | bytes 98312 | tf_op jit(solution)/shard_map/ppermute | solution.py:53
  99.5 19.5 %collective-permute-start.24 = (f32[2,8,16,1024]{3,2,1,0:T(8,128)S(1)}, f32[2,8,16,1024]{3,2,1,0:T(8,128)S(1)}, u32[]{:S(2)}, u32[]{:S(2)}) collective-permute-start(f32[2,8,16,1024]{3,2,1,0:T(8,128)S(1)} %pad_maximum_fusion.1.refs_1_), channel_id=1, source_target_pairs={{0,8},{1,33},{2,10},{3,35},{4,12},{5,37},{6,14},{7,39},{8,16},{9,4... | collective-permute-start | bytes 3145736 | tf_op jit(solution)/shard_map/ppermute | solution.py:53
  99.5 19.5 %collective-permute-start.25 = (f32[2,8,16,1024]{3,2,1,0:T(8,128)S(1)}, f32[2,8,16,1024]{3,2,1,0:T(8,128)S(1)}, u32[]{:S(2)}, u32[]{:S(2)}) collective-permute-start(f32[2,8,16,1024]{3,2,1,0:T(8,128)S(1)} %pad_maximum_fusion.refs_0_), channel_id=1, source_target_pairs={{0,24},{1,97},{2,26},{3,99},{4,28},{5,101},{6,30},{7,103},{8,0},{9... | collective-permute-start | bytes 3145736 | tf_op jit(solution)/shard_map/ppermute | solution.py:53
  107.8 22.6 %collective-permute-start.20 = (f32[2,8,16,1024]{3,2,1,0:T(8,128)S(1)}, f32[2,8,16,1024]{3,2,1,0:T(8,128)S(1)}, u32[]{:S(2)}, u32[]{:S(2)}) collective-permute-start(f32[2,8,16,1024]{3,2,1,0:T(8,128)S(1)} %collective-permute-done.16.refs_2_), channel_id=1, source_target_pairs={{0,8},{1,33},{2,10},{3,35},{4,12},{5,37},{6,14},{7,39},{8,16},{9,4... | collective-permute-start | bytes 3145736 | tf_op jit(solution)/shard_map/ppermute | solution.py:53
  107.8 22.6 %collective-permute-start.21 = (f32[2,8,16,1024]{3,2,1,0:T(8,128)S(1)}, f32[2,8,16,1024]{3,2,1,0:T(8,128)S(1)}, u32[]{:S(2)}, u32[]{:S(2)}) collective-permute-start(f32[2,8,16,1024]{3,2,1,0:T(8,128)S(1)} %collective-permute-done.17.refs_5_), channel_id=1, source_target_pairs={{0,24},{1,97},{2,26},{3,99},{4,28},{5,101},{6,30},{7,103},{8,0},{9... | collective-permute-start | bytes 3145736 | tf_op jit(solution)/shard_map/ppermute | solution.py:53
  110.5 3.4 %collective-permute-start.22 = (f32[56,128]{1,0:T(8,128)S(1)}, f32[56,128]{1,0:T(8,128)S(1)}, u32[]{:S(2)}, u32[]{:S(2)}) collective-permute-start(f32[56,128]{1,0:T(8,128)S(1)} %pad_maximum_fusion.2), channel_id=1, source_target_pairs={{0,1},{1,0},{2,3},{3,2},{4,5},{5,4},{6,7},{7,6},{8,9},{9,8},{10,11... | collective-permute-start | bytes 86024 | tf_op jit(solution)/shard_map/ppermute | solution.py:53
  113.8 3.0 %collective-permute-start.23 = (f32[56,128]{1,0:T(8,128)S(1)}, f32[56,128]{1,0:T(8,128)S(1)}, u32[]{:S(2)}, u32[]{:S(2)}) collective-permute-start(f32[56,128]{1,0:T(8,128)S(1)} %fusion.3), channel_id=1, source_target_pairs={{0,2},{1,3},{2,0},{3,1},{4,6},{5,7},{6,4},{7,5},{8,10},{9,11},{10,... | collective-permute-start | bytes 86024 | tf_op jit(solution)/shard_map/ppermute | solution.py:53
  119.0 4.3 %collective-permute-start.26 = (f32[56,128]{1,0:T(8,128)S(1)}, f32[56,128]{1,0:T(8,128)S(1)}, u32[]{:S(2)}, u32[]{:S(2)}) collective-permute-start(f32[56,128]{1,0:T(8,128)S(1)} %add.81), channel_id=1, source_target_pairs={{0,6},{1,7},{2,4},{3,5},{4,2},{5,3},{6,0},{7,1},{8,14},{9,15},{10,... | collective-permute-start | bytes 86024 | tf_op jit(solution)/shard_map/ppermute | solution.py:53
  135.4 6.3 %collective-permute-start.27 = (f32[256,1280]{1,0:T(8,128)S(1)}, f32[256,1280]{1,0:T(8,128)S(1)}, u32[]{:S(2)}, u32[]{:S(2)}) collective-permute-start(f32[256,1280]{1,0:T(8,128)S(1)} %get-tuple-element.110), channel_id=1, source_target_pairs={{0,1},{1,0},{2,3},{3,2},{4,5},{5,4},{6,7},{7,6},{8,9},{9,8},{10,11... | collective-permute-start | bytes 3932168 | tf_op jit(solution)/shard_map/ppermute | solution.py:53
  142.0 21.0 %collective-permute-start.28 = (f32[128,1280]{1,0:T(8,128)S(1)}, f32[128,1280]{1,0:T(8,128)S(1)}, u32[]{:S(2)}, u32[]{:S(2)}) collective-permute-start(f32[128,1280]{1,0:T(8,128)S(1)} %get-tuple-element.154), channel_id=1, source_target_pairs={{0,2},{1,3},{2,4},{3,5},{4,6},{5,7},{6,0},{7,1},{8,10},{9,11},{10,... | collective-permute-start | bytes 1966088 | tf_op jit(solution)/shard_map/ppermute | solution.py:53
  142.5 20.5 %collective-permute-start.29 = (f32[128,1280]{1,0:T(8,128)S(1)}, f32[128,1280]{1,0:T(8,128)S(1)}, u32[]{:S(2)}, u32[]{:S(2)}) collective-permute-start(f32[128,1280]{1,0:T(8,128)S(1)} %get-tuple-element.153), channel_id=1, source_target_pairs={{0,6},{1,7},{2,0},{3,1},{4,2},{5,3},{6,4},{7,5},{8,14},{9,15},{10,... | collective-permute-start | bytes 1966088 | tf_op jit(solution)/shard_map/ppermute | solution.py:53
  162.1 3.1 %collective-permute-start.30 = (f32[256,1280]{1,0:T(8,128)S(1)}, f32[256,1280]{1,0:T(8,128)S(1)}, u32[]{:S(2)}, u32[]{:S(2)}) collective-permute-start(f32[256,1280]{1,0:T(8,128)S(1)} %get-tuple-element.119), channel_id=1, source_target_pairs={{0,1},{1,0},{2,3},{3,2},{4,5},{5,4},{6,7},{7,6},{8,9},{9,8},{10,11... | collective-permute-start | bytes 3932168 | tf_op jit(solution)/shard_map/ppermute | solution.py:53
  162.5 4.6 %collective-permute-start.31 = (f32[256,1280]{1,0:T(8,128)S(1)}, f32[256,1280]{1,0:T(8,128)S(1)}, u32[]{:S(2)}, u32[]{:S(2)}) collective-permute-start(f32[256,1280]{1,0:T(8,128)S(1)} %get-tuple-element.120), channel_id=1, source_target_pairs={{0,1},{1,0},{2,3},{3,2},{4,5},{5,4},{6,7},{7,6},{8,9},{9,8},{10,11... | collective-permute-start | bytes 3932168 | tf_op jit(solution)/shard_map/ppermute | solution.py:53
  162.7 9.8 %collective-permute-start.32 = (f32[256,1280]{1,0:T(8,128)S(1)}, f32[256,1280]{1,0:T(8,128)S(1)}, u32[]{:S(2)}, u32[]{:S(2)}) collective-permute-start(f32[256,1280]{1,0:T(8,128)S(1)} %get-tuple-element.123), channel_id=1, source_target_pairs={{0,1},{1,0},{2,3},{3,2},{4,5},{5,4},{6,7},{7,6},{8,9},{9,8},{10,11... | collective-permute-start | bytes 3932168 | tf_op jit(solution)/shard_map/ppermute | solution.py:53
  167.1 3.7 %copy-start.1 = (s32[1280]{0:T(1024)S(1)}, s32[1280]{0:T(1024)}, u32[]{:S(2)}) copy-start(s32[1280]{0:T(1024)} %param.11) | copy-start | bytes 15364
  167.1 3.7 %copy-start.3 = (f32[1280]{0:T(1024)S(1)}, f32[1280]{0:T(1024)}, u32[]{:S(2)}) copy-start(f32[1280]{0:T(1024)} %param.8) | copy-start | bytes 15364
  168.0 37.1 %collective-permute-start.39 = (f32[256,1280]{1,0:T(8,128)S(1)}, f32[256,1280]{1,0:T(8,128)S(1)}, u32[]{:S(2)}, u32[]{:S(2)}) collective-permute-start(f32[256,1280]{1,0:T(8,128)S(1)} %get-tuple-element.121), channel_id=1, source_target_pairs={{0,2},{1,3},{2,4},{3,5},{4,6},{5,7},{6,0},{7,1},{8,10},{9,11},{10,... | collective-permute-start | bytes 3932168 | tf_op jit(solution)/shard_map/ppermute | solution.py:53
  168.1 37.1 %collective-permute-start.40 = (f32[256,1280]{1,0:T(8,128)S(1)}, f32[256,1280]{1,0:T(8,128)S(1)}, u32[]{:S(2)}, u32[]{:S(2)}) collective-permute-start(f32[256,1280]{1,0:T(8,128)S(1)} %get-tuple-element.122), channel_id=1, source_target_pairs={{0,6},{1,7},{2,0},{3,1},{4,2},{5,3},{6,4},{7,5},{8,14},{9,15},{10,... | collective-permute-start | bytes 3932168 | tf_op jit(solution)/shard_map/ppermute | solution.py:53
  170.8 5.4 %collective-permute-start.37 = (f32[32,1024]{1,0:T(8,128)S(1)}, f32[32,1024]{1,0:T(8,128)S(1)}, u32[]{:S(2)}, u32[]{:S(2)}) collective-permute-start(f32[32,1024]{1,0:T(8,128)S(1)} %add.72), channel_id=1, source_target_pairs={{0,32},{1,9},{2,34},{3,11},{4,36},{5,13},{6,38},{7,15},{8,40},{9,1... | collective-permute-start | bytes 393224 | tf_op jit(solution)/shard_map/ppermute | solution.py:53
  176.1 2.7 %collective-permute-start.33 = (f32[8,1280]{1,0:T(8,128)S(1)}, f32[8,1280]{1,0:T(8,128)S(1)}, u32[]{:S(2)}, u32[]{:S(2)}) collective-permute-start(f32[8,1280]{1,0:T(8,128)S(1)} %get-tuple-element.129), channel_id=1, source_target_pairs={{0,1},{1,0},{2,3},{3,2},{4,5},{5,4},{6,7},{7,6},{8,9},{9,8},{10,11... | collective-permute-start | bytes 122888 | tf_op jit(solution)/shard_map/ppermute | solution.py:53
  176.3 5.4 %collective-permute-start.38 = (f32[32,1024]{1,0:T(8,128)S(1)}, f32[32,1024]{1,0:T(8,128)S(1)}, u32[]{:S(2)}, u32[]{:S(2)}) collective-permute-start(f32[32,1024]{1,0:T(8,128)S(1)} %add.88), channel_id=1, source_target_pairs={{0,96},{1,25},{2,98},{3,27},{4,100},{5,29},{6,102},{7,31},{8,104},... | collective-permute-start | bytes 393224 | tf_op jit(solution)/shard_map/ppermute | solution.py:53
  178.8 25.0 %collective-permute-start.34 = (f32[8,1280]{1,0:T(8,128)S(1)}, f32[8,1280]{1,0:T(8,128)S(1)}, u32[]{:S(2)}, u32[]{:S(2)}) collective-permute-start(f32[8,1280]{1,0:T(8,128)S(1)} %add.84.last), channel_id=1, source_target_pairs={{0,2},{1,3},{2,4},{3,5},{4,6},{5,7},{6,0},{7,1},{8,10},{9,11},{10,... | collective-permute-start | bytes 122888 | tf_op jit(solution)/shard_map/ppermute | solution.py:53
  178.9 24.9 %collective-permute-start.35 = (f32[8,1280]{1,0:T(8,128)S(1)}, f32[8,1280]{1,0:T(8,128)S(1)}, u32[]{:S(2)}, u32[]{:S(2)}) collective-permute-start(f32[8,1280]{1,0:T(8,128)S(1)} %add.84.last), channel_id=1, source_target_pairs={{0,4},{1,5},{2,6},{3,7},{4,0},{5,1},{6,2},{7,3},{8,12},{9,13},{10,... | collective-permute-start | bytes 122888 | tf_op jit(solution)/shard_map/ppermute | solution.py:53
  181.7 22.2 %collective-permute-start.36 = (f32[8,1280]{1,0:T(8,128)S(1)}, f32[8,1280]{1,0:T(8,128)S(1)}, u32[]{:S(2)}, u32[]{:S(2)}) collective-permute-start(f32[8,1280]{1,0:T(8,128)S(1)} %add.84.last), channel_id=1, source_target_pairs={{0,6},{1,7},{2,0},{3,1},{4,2},{5,3},{6,4},{7,5},{8,14},{9,15},{10,... | collective-permute-start | bytes 122888 | tf_op jit(solution)/shard_map/ppermute | solution.py:53
  (1 other events, 0.7 us)

commit v2 on v1

--- a/solution.py
+++ b/solution.py
@@ -202,30 +202,39 @@
         compiler_params=vmem(16),
         cost_estimate=cost(0, cells * spots * 8),
         name="expo",
-    )(ids, streamed(logits), kind, filt, *[streamed(expr)] * 4)
-
-
-def pred_kernel(ids, expr_a, expr_b, keep, masses, totals, *refs):
+    )(ids, streamed(logits), streamed(kind), streamed(filt), *[streamed(expr)] * 4)
+
+
+def pred_kernel(ids, expr_a, expr_b, keep, masses, totals, *refs, cuts):
     more, outs = refs[:-2], refs[-2:]
     rows = 2 * expr_a.shape[0] * expr_a.shape[2]
     weighted = jnp.concatenate(
         [part[...].reshape(rows // 2, keep.shape[1]) for part in (expr_a, expr_b)]
     )
-    part = product(split(weighted * keep[...]), masses, ((1,), (0,)))
-    part = part.reshape(rows // 8, 8, part.shape[1])
-    for step, out in enumerate(outs):
-
-        @pl.when(pl.program_id(0) == step)
-        def _(step=step, out=out):
-            if more:
-                out[: rows // 8] = part + more[step][: rows // 8]
-                out[rows // 8] = totals[...] + more[step][rows // 8]
-            else:
-                out[: rows // 8] = part
-                out[rows // 8] = totals[...]
-
-
-def pred_call(ids, parts, expr, keep, masses, totals, more=()):
+    weighted = split(weighted * keep[...])
+    width = masses.shape[2] // cuts
+
+    def half(index, _):
+        columns = pl.ds(pl.multiple_of(index * width, width), width)
+        part = product(weighted, (masses[0, :, columns], masses[1, :, columns]), ((1,), (0,)))
+        part = part.reshape(rows // 8, 8, width)
+        for step, out in enumerate(outs):
+
+            @pl.when(pl.program_id(0) == step)
+            def _(step=step, out=out):
+                if more:
+                    out[: rows // 8, :, columns] = part + more[step][: rows // 8, :, columns]
+                    out[rows // 8, :, columns] = totals[:, columns] + more[step][rows // 8, :, columns]
+                else:
+                    out[: rows // 8, :, columns] = part
+                    out[rows // 8, :, columns] = totals[:, columns]
+
+        return 0
+
+    lax.fori_loop(0, cuts, half, 0)
+
+
+def pred_call(ids, parts, expr, keep, masses, totals, more, cuts):
     blocks, groups, rows, cells = expr.shape
     spots = masses.shape[2]
     tiles = blocks * rows // 4 + 1
@@ -238,7 +247,7 @@
         return pl.BlockSpec((blocks, 1, rows, cells), place)
 
     return pl.pallas_call(
-        pred_kernel,
+        functools.partial(pred_kernel, cuts=cuts),
         grid_spec=pltpu.PrefetchScalarGridSpec(
             num_scalar_prefetch=1,
             grid=(2,),
@@ -485,7 +494,7 @@
 
 
 def back_kernel(ids, grad, masses, expr, *refs, parts, first, last):
-    more, (sums, *outs), (held, ready) = refs[: first + 4 * last], refs[first + 4 * last : -2], refs[-2:]
+    more, (sums, *outs), (held, ready) = refs[: first + 5 * last], refs[first + 5 * last : -2], refs[-2:]
     step = pl.program_id(0)
     rows = grad.shape[2]
 
@@ -500,6 +509,13 @@
     def _():
         for k in range(len(parts)):
             fetch(k).start()
+
+    @pl.when(step == 0)
+    def _():
+        if last:
+            sums[...] = more[0][...] + more[1][...] + more[2][...] + more[3][...]
+        else:
+            sums[...] = jnp.zeros_like(sums)
 
     here = block([pick(step, [part[k] for part in parts]) for k in range(2)])
     left = grad[0, here], grad[1, here]
@@ -507,17 +523,9 @@
         pair = split(jnp.concatenate([more[0][...], jnp.zeros_like(more[0])]))
         left = [jnp.concatenate(both) for both in zip(left, pair)]
     part = product(left, masses, ((1,), (1,)))
-
-    @pl.when(step == 0)
-    def _():
-        if first:
-            sums[...] = part[rows : rows + 8]
-        elif last:
-            sums[...] = more[0][...] + more[1][...] + more[2][...]
-        else:
-            sums[...] = jnp.zeros_like(sums)
-
-    part = part[:rows]
+    if first:
+        sums[...] = part[rows : rows + 8]
+        part = part[:rows]
     for k, out in enumerate(outs):
 
         @pl.when(step == k)
@@ -533,14 +541,14 @@
             total = jnp.sum(sums[...], axis=0, keepdims=True)
             sums[...] = jnp.zeros_like(sums)
             sums[0:1, :] = total
-            sums[1:2, 0:128] = more[3][...]
+            sums[1:2, 0:128] = more[4][...]
 
 
 def back_call(ids, parts, grad, masses, expr, first=(), last=()):
     _, blocks, rows, spots = grad.shape
     cells = masses.shape[1]
     return pl.pallas_call(
-        functools.partial(back_kernel, parts=parts, first=len(first), last=len(last) // 4),
+        functools.partial(back_kernel, parts=parts, first=len(first), last=len(last) // 5),
         grid_spec=pltpu.PrefetchScalarGridSpec(
             num_scalar_prefetch=1,
             grid=(len(parts),),
@@ -729,18 +737,18 @@
 
     ids = jnp.stack([first, second, y, core]).astype(jnp.int32)
 
-    def pred_part(one, two, more, *others):
-        return pred_call(after(ids, *others), (one, two), expr4, keep_row, masses, totals, more)
+    def pred_part(one, two, more, cuts, *others):
+        return pred_call(after(ids, *others), (one, two), expr4, keep_row, masses, totals, more, cuts)
 
     masses, types, totals, *far = expo_call(
         ids, ((2, 0), (2, 1)), map_logits, kind2, filt2, expr4
     )
     far_right, far_left = along(far[0], 1), along(far[1], -1)
-    near = pred_part((1, 1), (-1, 0), (), *far)
+    near = pred_part((1, 1), (-1, 0), (), 2, *far)
     near_right, near_left = along(near[0], 1), along(near[1], -1)
-    late = pred_part((1, 0), (-1, 1), (far_right, far_left), *near)
+    late = pred_part((1, 0), (-1, 1), (far_right, far_left), 1, *near)
     late_right, late_left = along(late[0], 1), along(late[1], -1)
-    own = pred_part((0, 0), (0, 1), (near_left, near_right), *late)
+    own = pred_part((0, 0), (0, 1), (near_left, near_right), 2, *late)
     mine, *pieces = merge_call(own, (late_right, late_left))
     pieces = [across(piece, step + 1) for step, piece in enumerate(pieces)]
     spatial_squares = jnp.sum(after(spatial, mine) ** 2, axis=0)
@@ -797,16 +805,16 @@
     far = far_b + far_got
     far_up, far_down = up(far[:rows], 1), up(far[rows:], -1)
     grad, column_c = last_grad((1, -1, 0), grad, far)
-    sums_c, up_a, down_a, own_a, up_b, down_b = back_part(
-        [(1, 1), (-1, 1), (0, 1), (1, 0), (-1, 0)], grad
-    )
+    sums_c, up_a, down_a, own_a = back_part([(1, 1), (-1, 1), (0, 1)], grad)
     up_got, down_got, own_got = (swap(one, 0, 0, 0, 1) for one in (up_a, down_a, own_a))
+    sums_d, up_b, down_b = back_part([(1, 0), (-1, 0)], grad, up_a)
     above, below = lift_call(up_b, down_b, far_up, far_down)
+    types = types + swap_across(after(types, above), 1)
     above, below = join_call(above, below, up_got, down_got)
     near_up, near_down = up(above, 1), up(below, -1)
-    types_got = swap_across(after(types, above), 1)
+    types_got = swap_across(types, 3)
     last, own_b = back_part(
-        [(0, 0)], grad, above, below, own_got, last=[sums_a, sums_b, sums_c, scalars]
+        [(0, 0)], grad, above, below, own_got, types, last=[sums_a, sums_b, sums_c, sums_d, scalars]
     )
     types = types + after(types_got, own_b)
     own = own_b + own_got
@@ -814,10 +822,8 @@
     column = jnp.sum(column_a + column_b + column_c, axis=0) * share + spot_coef[32] * mass
     map_rows = stacked([spot_coef[32], column])
     map_args = (expr, grad.reshape(2, genes, spots), masses, keep2, map_rows, all_cells * genes)
-    types_got = swap_across(types, 3)
     last = last + swap(last, 0, 0, 0, 1)
     got = [up(last, step) for step in (1, 2, 3)]
-    types = types + types_got
     grad_map = map_call(*after(map_args[:-1], last, types), map_args[-1])
     got = after(tuple(got), grad_map)
     grad_weighted = after(own, grad_map) + near_up + near_down

time: 208 us -> 207 us (level)
    pallas_call x4 -> x5, Pallas kernels: 23.7 us -> 23.1 us  [back_call(): pl.pallas_call(functools.partial(back_kernel, parts=parts, first=len(firs...]
  transfers between devices with their start and end apart: 41 -> 41, of which waited for: 19 -> 18; matrix products, arithmetic and copies ran while one was open for 1% -> 1% of each run, Pallas kernels for 37% -> 38%
where the time goes in v2:
time: 207 us; the launch traced here: 206 us
  Pallas kernels  93.9 us (45%)
  starting transfers between devices  55.4 us (27%)
  waiting for transfers between devices  51.1 us (25%)
  other arithmetic  3.86 us (2%)
    ppermute x41, starting transfers between devices, send(): return lax.ppermute(array, ('cells', 'spots'), route(target))  55.4 us
    ppermute x41, waiting for transfers between devices, send(): return lax.ppermute(array, ('cells', 'spots'), route(target))  51.1 us
    pallas_call x5, Pallas kernels, back_call(): pl.pallas_call(functools.partial(back_kernel, parts=parts, first=len(firs...  23.1 us
    pallas_call x3, Pallas kernels, pred_call(): pl.pallas_call(functools.partial(pred_kernel, cuts=cuts), grid_spec=pltpu...  21.9 us
    pallas_call x1, Pallas kernels, map_call(): pl.pallas_call(functools.partial(map_kernel, scale=scale), grid=(cells //...  21.3 us
    pallas_call x3, Pallas kernels, grad_call(): pl.pallas_call(functools.partial(grad_kernel, count=count, lane=lane, chi...  11.7 us
    pallas_call x1, Pallas kernels, expo_call(): pl.pallas_call(expo_kernel, grid_spec=pltpu.PrefetchScalarGridSpec(num_sc...  9.85 us
  transfers between devices with their start and end apart: 41, of which 18 were waited for; matrix products, arithmetic and copies ran while one was open for 1% of the time, Pallas kernels for 38%

profile of v2, /device:TPU:1, one launch (start us, length us, event | category | flops | bytes accessed | tf_op | source)
XLA Modules:
  0.0 206.0 jit_solution(11369150315646759316)
XLA Ops:
  0.7 9.9 %expo.1 = (bf16[2,1280,1024]{2,1,0:T(8,128)(2,1)S(1)}, f32[32,1024]{1,0:T(8,128)S(1)}, f32[8,1024]{1,0:T(8,128)S(1)}, f32[33,8,1024]{2,1,0:T(8,128)S(1)}, f32[33,8,1024]{2,1,0:T(8,128)S(1)}) custom-call(s32[4]{0:T(128)S(1)} %pad_add_fusion.ids, f32[1280,1024]{1,0:T(8,128)} %logits.1, s32[10,128]{1,0:T(8,128)} %bitcast.66, f32[10,128]{1,0:T(8,128)} %bitcast.67, ...), custom_call_target="tpu_custom_call" | custom-call | bytes 1310720 | tf_op jit(solution)/shard_map/expo/pallas_call | solution.py:176
  10.6 2.5 %collective-permute-start = (f32[33,8,1024]{2,1,0:T(8,128)S(1)}, f32[33,8,1024]{2,1,0:T(8,128)S(1)}, u32[]{:S(2)}, u32[]{:S(2)}) collective-permute-start(f32[33,8,1024]{2,1,0:T(8,128)S(1)} %get-tuple-element.78), channel_id=1, source_target_pairs={{0,8},{1,33},{2,10},{3,35},{4,12},{5,37},{6,14},{7,39},{8,16},{9,4... | collective-permute-start | bytes 3244040 | tf_op jit(solution)/shard_map/ppermute | solution.py:53
  13.1 2.3 %collective-permute-start.1 = (f32[33,8,1024]{2,1,0:T(8,128)S(1)}, f32[33,8,1024]{2,1,0:T(8,128)S(1)}, u32[]{:S(2)}, u32[]{:S(2)}) collective-permute-start(f32[33,8,1024]{2,1,0:T(8,128)S(1)} %get-tuple-element.79), channel_id=1, source_target_pairs={{0,24},{1,97},{2,26},{3,99},{4,28},{5,101},{6,30},{7,103},{8,0},{9... | collective-permute-start | bytes 3244040 | tf_op jit(solution)/shard_map/ppermute | solution.py:53
  15.4 7.5 %pred_.3 = (f32[33,8,1024]{2,1,0:T(8,128)S(1)}, f32[33,8,1024]{2,1,0:T(8,128)S(1)}) custom-call(s32[4]{0:T(128)S(1)} %pad_add_fusion.ids, f32[8,16,16,1280]{3,2,1,0:T(8,128)} %bitcast.49, f32[8,16,16,1280]{3,2,1,0:T(8,128)} %bitcast.50, f32[1,1280]{1,0:T(1,128)S(1)} %reshape.94.keep, bf16[2,1280,1024]{2,1,0:T(8,128)(2,1)S(1)} %get-tuple-element.142.masses, ...), custom_call_target="tpu_custom_call" | custom-call | flops 503316480 | bytes 1245184 | tf_op jit(solution)/shard_map/pred/pallas_call | solution.py:249
  22.9 1.4 collective-permute-start.2
  24.5 3.6 %collective-permute-done.refs_0_ = f32[33,8,1024]{2,1,0:T(8,128)S(1)} collective-permute-done((f32[33,8,1024]{2,1,0:T(8,128)S(1)}, f32[33,8,1024]{2,1,0:T(8,128)S(1)}, u32[]{:S(2)}, u32[]{:S(2)}) %collective-permute-start) | collective-permute-done | bytes 1081376 | tf_op jit(solution)/shard_map/ppermute | solution.py:53
  28.0 6.9 %pred_.4 = (f32[33,8,1024]{2,1,0:T(8,128)S(1)}, f32[33,8,1024]{2,1,0:T(8,128)S(1)}) custom-call(s32[4]{0:T(128)S(1)} %pad_add_fusion.ids, f32[8,16,16,1280]{3,2,1,0:T(8,128)} %bitcast.51, f32[8,16,16,1280]{3,2,1,0:T(8,128)} %bitcast.52, f32[1,1280]{1,0:T(1,128)S(1)} %reshape.94.keep, bf16[2,1280,1024]{2,1,0:T(8,128)(2,1)S(1)} %get-tuple-element.142.masses, ...), custom_call_target="tpu_custom_call" | custom-call | flops 503316480 | bytes 1245184 | tf_op jit(solution)/shard_map/pred/pallas_call | solution.py:249
  36.0 2.0 collective-permute-start.5
  39.9 7.6 %pred_.5 = (f32[33,8,1024]{2,1,0:T(8,128)S(1)}, f32[33,8,1024]{2,1,0:T(8,128)S(1)}) custom-call(s32[4]{0:T(128)S(1)} %pad_add_fusion.ids, f32[8,16,16,1280]{3,2,1,0:T(8,128)} %bitcast.53, f32[8,16,16,1280]{3,2,1,0:T(8,128)} %bitcast.54, f32[1,1280]{1,0:T(1,128)S(1)} %reshape.94.keep, bf16[2,1280,1024]{2,1,0:T(8,128)(2,1)S(1)} %get-tuple-element.142.masses, ...), custom_call_target="tpu_custom_call" | custom-call | flops 503316480 | bytes 1245184 | tf_op jit(solution)/shard_map/pred/pallas_call | solution.py:249
  47.5 4.0 %collective-permute-done.4.got0 = f32[33,8,1024]{2,1,0:T(8,128)S(1)} collective-permute-done((f32[33,8,1024]{2,1,0:T(8,128)S(1)}, f32[33,8,1024]{2,1,0:T(8,128)S(1)}, u32[]{:S(2)}, u32[]{:S(2)}) %collective-permute-start.4) | collective-permute-done | bytes 1081376 | tf_op jit(solution)/shard_map/ppermute | solution.py:53
  52.3 2.5 %collective-permute-start.10 = (f32[17,8,1024]{2,1,0:T(8,128)S(1)}, f32[17,8,1024]{2,1,0:T(8,128)S(1)}, u32[]{:S(2)}, u32[]{:S(2)}) collective-permute-start(f32[17,8,1024]{2,1,0:T(8,128)S(1)} %get-tuple-element.98), channel_id=1, source_target_pairs={{0,96},{1,25},{2,98},{3,27},{4,100},{5,29},{6,102},{7,31},{8,104},... | collective-permute-start | bytes 1671176 | tf_op jit(solution)/shard_map/ppermute | solution.py:53
  54.8 1.4 collective-permute-start.9
  58.1 4.5 %collective-permute-done.6 = f32[32,1024]{1,0:T(8,128)S(1)} collective-permute-done((f32[32,1024]{1,0:T(8,128)S(1)}, f32[32,1024]{1,0:T(8,128)S(1)}, u32[]{:S(2)}, u32[]{:S(2)}) %collective-permute-start.6) | collective-permute-done | bytes 131104 | tf_op jit(solution)/shard_map/ppermute | solution.py:53
  62.6 2.7 %collective-permute-start.7 = (f32[32,1024]{1,0:T(8,128)S(1)}, f32[32,1024]{1,0:T(8,128)S(1)}, u32[]{:S(2)}, u32[]{:S(2)}) collective-permute-start(f32[32,1024]{1,0:T(8,128)S(1)} %add.71), channel_id=1, source_target_pairs={{0,24},{1,97},{2,26},{3,99},{4,28},{5,101},{6,30},{7,103},{8,16},{... | collective-permute-start | bytes 393224 | tf_op jit(solution)/shard_map/ppermute | solution.py:53
  65.4 9.6 %collective-permute-done.7 = f32[32,1024]{1,0:T(8,128)S(1)} collective-permute-done((f32[32,1024]{1,0:T(8,128)S(1)}, f32[32,1024]{1,0:T(8,128)S(1)}, u32[]{:S(2)}, u32[]{:S(2)}) %collective-permute-start.7) | collective-permute-done | bytes 131104 | tf_op jit(solution)/shard_map/ppermute | solution.py:53
  75.2 2.1 %collective-permute-start.12 = (f32[8,16,1024]{2,1,0:T(8,128)S(1)}, f32[8,16,1024]{2,1,0:T(8,128)S(1)}, u32[]{:S(2)}, u32[]{:S(2)}) collective-permute-start(f32[8,16,1024]{2,1,0:T(8,128)S(1)} %bitcast.39), channel_id=1, source_target_pairs={{0,64},{1,17},{2,66},{3,19},{4,68},{5,21},{6,70},{7,23},{8,72},{9,... | collective-permute-start | bytes 1572872 | tf_op jit(solution)/shard_map/ppermute | solution.py:53
  77.7 2.4 %collective-permute-start.11 = (f32[8,16,1024]{2,1,0:T(8,128)S(1)}, f32[8,16,1024]{2,1,0:T(8,128)S(1)}, u32[]{:S(2)}, u32[]{:S(2)}) collective-permute-start(f32[8,16,1024]{2,1,0:T(8,128)S(1)} %bitcast.41), channel_id=1, source_target_pairs={{0,96},{1,25},{2,98},{3,27},{4,100},{5,29},{6,102},{7,31},{8,104},... | collective-permute-start | bytes 1572872 | tf_op jit(solution)/shard_map/ppermute | solution.py:53
  80.0 1.9 stats.1
  82.1 3.5 %collective-permute-done.14 = f32[64,128]{1,0:T(8,128)S(1)} collective-permute-done((f32[64,128]{1,0:T(8,128)S(1)}, f32[64,128]{1,0:T(8,128)S(1)}, u32[]{:S(2)}, u32[]{:S(2)}) %collective-permute-start.14) | collective-permute-done | bytes 32800 | tf_op jit(solution)/shard_map/ppermute | solution.py:53
  85.6 4.6 %collective-permute-done.15 = f32[64,128]{1,0:T(8,128)S(1)} collective-permute-done((f32[64,128]{1,0:T(8,128)S(1)}, f32[64,128]{1,0:T(8,128)S(1)}, u32[]{:S(2)}, u32[]{:S(2)}) %collective-permute-start.15) | collective-permute-done | bytes 32800 | tf_op jit(solution)/shard_map/ppermute | solution.py:53
  91.4 2.7 %collective-permute-start.17 = (f32[2,8,16,1024]{3,2,1,0:T(8,128)S(1)}, f32[2,8,16,1024]{3,2,1,0:T(8,128)S(1)}, u32[]{:S(2)}, u32[]{:S(2)}) collective-permute-start(f32[2,8,16,1024]{3,2,1,0:T(8,128)S(1)} %pad_maximum_fusion.1.refs_1_), channel_id=1, source_target_pairs={{0,24},{1,97},{2,26},{3,99},{4,28},{5,101},{6,30},{7,103},{8,0},{9... | collective-permute-start | bytes 3145736 | tf_op jit(solution)/shard_map/ppermute | solution.py:53
  94.7 2.8 %collective-permute-done.18 = f32[64,128]{1,0:T(8,128)S(1)} collective-permute-done((f32[64,128]{1,0:T(8,128)S(1)}, f32[64,128]{1,0:T(8,128)S(1)}, u32[]{:S(2)}, u32[]{:S(2)}) %collective-permute-start.18) | collective-permute-done | bytes 32800 | tf_op jit(solution)/shard_map/ppermute | solution.py:53
  98.6 2.7 %collective-permute-start.25 = (f32[2,8,16,1024]{3,2,1,0:T(8,128)S(1)}, f32[2,8,16,1024]{3,2,1,0:T(8,128)S(1)}, u32[]{:S(2)}, u32[]{:S(2)}) collective-permute-start(f32[2,8,16,1024]{3,2,1,0:T(8,128)S(1)} %pad_maximum_fusion.refs_0_), channel_id=1, source_target_pairs={{0,24},{1,97},{2,26},{3,99},{4,28},{5,101},{6,30},{7,103},{8,0},{9... | collective-permute-start | bytes 3145736 | tf_op jit(solution)/shard_map/ppermute | solution.py:53
  102.2 4.7 %collective-permute-done.16.refs_2_ = f32[2,8,16,1024]{3,2,1,0:T(8,128)S(1)} collective-permute-done((f32[2,8,16,1024]{3,2,1,0:T(8,128)S(1)}, f32[2,8,16,1024]{3,2,1,0:T(8,128)S(1)}, u32[]{:S(2)}, u32[]{:S(2)}) %collective-permute-start.16) | collective-permute-done | bytes 1048608 | tf_op jit(solution)/shard_map/ppermute | solution.py:53
  106.9 2.7 %collective-permute-start.21 = (f32[2,8,16,1024]{3,2,1,0:T(8,128)S(1)}, f32[2,8,16,1024]{3,2,1,0:T(8,128)S(1)}, u32[]{:S(2)}, u32[]{:S(2)}) collective-permute-start(f32[2,8,16,1024]{3,2,1,0:T(8,128)S(1)} %collective-permute-done.17.refs_5_), channel_id=1, source_target_pairs={{0,24},{1,97},{2,26},{3,99},{4,28},{5,101},{6,30},{7,103},{8,0},{9... | collective-permute-start | bytes 3145736 | tf_op jit(solution)/shard_map/ppermute | solution.py:53
  109.6 2.6 %collective-permute-start.22 = (f32[56,128]{1,0:T(8,128)S(1)}, f32[56,128]{1,0:T(8,128)S(1)}, u32[]{:S(2)}, u32[]{:S(2)}) collective-permute-start(f32[56,128]{1,0:T(8,128)S(1)} %pad_maximum_fusion.2), channel_id=1, source_target_pairs={{0,1},{1,0},{2,3},{3,2},{4,5},{5,4},{6,7},{7,6},{8,9},{9,8},{10,11... | collective-permute-start | bytes 86024 | tf_op jit(solution)/shard_map/ppermute | solution.py:53
  113.1 1.3 collective-permute-start.23
  114.4 1.7 collective-permute-done.23
  116.1 2.0 collective-permute-done.24.refs_3_
  118.2 2.7 %collective-permute-start.26 = (f32[56,128]{1,0:T(8,128)S(1)}, f32[56,128]{1,0:T(8,128)S(1)}, u32[]{:S(2)}, u32[]{:S(2)}) collective-permute-start(f32[56,128]{1,0:T(8,128)S(1)} %add.81), channel_id=1, source_target_pairs={{0,6},{1,7},{2,4},{3,5},{4,2},{5,3},{6,0},{7,1},{8,14},{9,15},{10,... | collective-permute-start | bytes 86024 | tf_op jit(solution)/shard_map/ppermute | solution.py:53
  120.9 1.6 collective-permute-done.26
  123.3 6.2 %grad.3 = (bf16[2,8,256,1024]{3,2,1,0:T(8,128)(2,1)S(1)}, f32[8,1024]{1,0:T(8,128)S(1)}) custom-call(s32[4]{0:T(128)S(1)} %pad_add_fusion.ids, f32[2,8,16,1024]{3,2,1,0:T(8,128)S(1)} %pad_maximum_fusion.refs_0_, f32[2,8,16,1024]{3,2,1,0:T(8,128)S(1)} %pad_maximum_fusion.1.refs_1_, f32[2,8,16,1024]{3,2,1,0:T(8,128)S(1)} %collective-permute-done.16.refs_2_, ...), custom_call_target="tpu_custom_call" | custom-call | tf_op jit(solution)/shard_map/grad/pallas_call | solution.py:474
  129.5 2.0 grad.4
  131.5 3.1 %back.5 = (f32[8,1280]{1,0:T(8,128)S(1)}, f32[256,1280]{1,0:T(8,128)S(1)}) custom-call(s32[4]{0:T(128)S(1)} %pad_add_fusion.ids, bf16[2,8,256,1024]{3,2,1,0:T(8,128)(2,1)S(1)} %get-tuple-element.111.grad.refs_5_, bf16[2,1280,1024]{2,1,0:T(8,128)(2,1)S(1)} %get-tuple-element.142.masses, f32[2048,1280]{1,0:T(8,128)} %expr.10, ...), custom_call_target="tpu_custom_call" | custom-call | tf_op jit(solution)/shard_map/back/pallas_call | solution.py:550
  134.6 2.9 %collective-permute-start.27 = (f32[256,1280]{1,0:T(8,128)S(1)}, f32[256,1280]{1,0:T(8,128)S(1)}, u32[]{:S(2)}, u32[]{:S(2)}) collective-permute-start(f32[256,1280]{1,0:T(8,128)S(1)} %get-tuple-element.112), channel_id=1, source_target_pairs={{0,1},{1,0},{2,3},{3,2},{4,5},{5,4},{6,7},{7,6},{8,9},{9,8},{10,11... | collective-permute-start | bytes 3932168 | tf_op jit(solution)/shard_map/ppermute | solution.py:53
  137.5 3.6 %back.6 = (f32[8,1280]{1,0:T(8,128)S(1)}, f32[256,1280]{1,0:T(8,128)S(1)}) custom-call(s32[4]{0:T(128)S(1)} %pad_add_fusion.ids, bf16[2,8,256,1024]{3,2,1,0:T(8,128)(2,1)S(1)} %get-tuple-element.111.grad.refs_5_, bf16[2,1280,1024]{2,1,0:T(8,128)(2,1)S(1)} %get-tuple-element.142.masses, f32[2048,1280]{1,0:T(8,128)} %expr.10), custom_call_target="tpu_custom_call" | custom-call | tf_op jit(solution)/shard_map/back/pallas_call | solution.py:550
  141.9 2.6 %collective-permute-start.29 = (f32[128,1280]{1,0:T(8,128)S(1)}, f32[128,1280]{1,0:T(8,128)S(1)}, u32[]{:S(2)}, u32[]{:S(2)}) collective-permute-start(f32[128,1280]{1,0:T(8,128)S(1)} %get-tuple-element.157), channel_id=1, source_target_pairs={{0,6},{1,7},{2,0},{3,1},{4,2},{5,3},{6,4},{7,5},{8,14},{9,15},{10,... | collective-permute-start | bytes 1966088 | tf_op jit(solution)/shard_map/ppermute | solution.py:53
  144.5 3.5 %grad.5 = (bf16[2,8,256,1024]{3,2,1,0:T(8,128)(2,1)S(1)}, f32[8,1024]{1,0:T(8,128)S(1)}) custom-call(s32[4]{0:T(128)S(1)} %pad_add_fusion.ids, f32[2,8,16,1024]{3,2,1,0:T(8,128)S(1)} %collective-permute-done.20.refs_0_, f32[2,8,16,1024]{3,2,1,0:T(8,128)S(1)} %collective-permute-done.21.refs_1_, ...), custom_call_target="tpu_custom_call", output_to_operand_aliasing={{0}: (6, {})} | custom-call | tf_op jit(solution)/shard_map/grad/pallas_call | solution.py:474
  148.0 8.0 %back.7 = (f32[8,1280]{1,0:T(8,128)S(1)}, f32[256,1280]{1,0:T(8,128)S(1)}, f32[256,1280]{1,0:T(8,128)S(1)}, f32[256,1280]{1,0:T(8,128)S(1)}) custom-call(s32[4]{0:T(128)S(1)} %pad_add_fusion.ids, bf16[2,8,256,1024]{3,2,1,0:T(8,128)(2,1)S(1)} %get-tuple-element.116.grad, bf16[2,1280,1024]{2,1,0:T(8,128)(2,1)S(1)} %get-tuple-element.142.masses, f32[2048,1280]{1,0:T(8,128)} %expr.10), custom_call_target="tpu_custom_call" | custom-call | tf_op jit(solution)/shard_map/back/pallas_call | solution.py:550
  156.6 5.5 %back.8 = (f32[8,1280]{1,0:T(8,128)S(1)}, f32[256,1280]{1,0:T(8,128)S(1)}, f32[256,1280]{1,0:T(8,128)S(1)}) custom-call(s32[4]{0:T(128)S(1)} %pad_add_fusion.ids, bf16[2,8,256,1024]{3,2,1,0:T(8,128)(2,1)S(1)} %get-tuple-element.116.grad, bf16[2,1280,1024]{2,1,0:T(8,128)(2,1)S(1)} %get-tuple-element.142.masses, f32[2048,1280]{1,0:T(8,128)} %expr.10), custom_call_target="tpu_custom_call" | custom-call | tf_op jit(solution)/shard_map/back/pallas_call | solution.py:550
  164.2 2.7 %collective-permute-start.40 = (f32[256,1280]{1,0:T(8,128)S(1)}, f32[256,1280]{1,0:T(8,128)S(1)}, u32[]{:S(2)}, u32[]{:S(2)}) collective-permute-start(f32[256,1280]{1,0:T(8,128)S(1)} %get-tuple-element.125), channel_id=1, source_target_pairs={{0,6},{1,7},{2,0},{3,1},{4,2},{5,3},{6,4},{7,5},{8,14},{9,15},{10,... | collective-permute-start | bytes 3932168 | tf_op jit(solution)/shard_map/ppermute | solution.py:53
  166.9 1.4 collective-permute-start.33
  168.3 2.8 %collective-permute-done.33 = f32[32,1024]{1,0:T(8,128)S(1)} collective-permute-done((f32[32,1024]{1,0:T(8,128)S(1)}, f32[32,1024]{1,0:T(8,128)S(1)}, u32[]{:S(2)}, u32[]{:S(2)}) %collective-permute-start.33) | collective-permute-done | bytes 131104 | tf_op jit(solution)/shard_map/ppermute | solution.py:53
  171.2 3.0 %collective-permute-start.38 = (f32[32,1024]{1,0:T(8,128)S(1)}, f32[32,1024]{1,0:T(8,128)S(1)}, u32[]{:S(2)}, u32[]{:S(2)}) collective-permute-start(f32[32,1024]{1,0:T(8,128)S(1)} %add.84), channel_id=1, source_target_pairs={{0,96},{1,25},{2,98},{3,27},{4,100},{5,29},{6,102},{7,31},{8,104},... | collective-permute-start | bytes 393224 | tf_op jit(solution)/shard_map/ppermute | solution.py:53
  174.2 3.0 %back.9 = (f32[8,1280]{1,0:T(8,128)S(1)}, f32[256,1280]{1,0:T(8,128)S(1)}) custom-call(s32[4]{0:T(128)S(1)} %pad_add_fusion.ids, bf16[2,8,256,1024]{3,2,1,0:T(8,128)(2,1)S(1)} %get-tuple-element.116.grad, bf16[2,1280,1024]{2,1,0:T(8,128)(2,1)S(1)} %get-tuple-element.142.masses, f32[2048,1280]{1,0:T(8,128)} %expr.10, ...), custom_call_target="tpu_custom_call" | custom-call | tf_op jit(solution)/shard_map/back/pallas_call | solution.py:550
  178.5 1.4 collective-permute-start.36
  182.0 21.3 %grad_map.1 = f32[1280,1024]{1,0:T(8,128)} custom-call(f32[2048,1280]{1,0:T(8,128)} %expr.10, bf16[2,2048,1024]{2,1,0:T(8,128)(2,1)S(1)} %bitcast.38, bf16[2,1280,1024]{2,1,0:T(8,128)(2,1)S(1)} %get-tuple-element.142.masses, f32[10,128]{1,0:T(8,128)S(1)} %bitcast.44, f32[8,1024]{1,0:T(8,128)S(1)} %select_select_fusion.spot), custom_call_target="tpu_custom_call" | custom-call | tf_op jit(solution)/shard_map/grad_map/pallas_call | solution.py:656
  204.7 1.3 add_multiply_fusion
  (104 shorter events, 20.4 us)
Async XLA Ops:
  0.7 14.7 %copy-start = (s32[1280]{0:T(1024)S(1)}, s32[1280]{0:T(1024)}, u32[]{:S(2)}) copy-start(s32[1280]{0:T(1024)} %param.11) | copy-start | bytes 15364
  0.7 14.7 %copy-start.1 = (f32[1280]{0:T(1024)S(1)}, f32[1280]{0:T(1024)}, u32[]{:S(2)}) copy-start(f32[1280]{0:T(1024)} %param.8) | copy-start | bytes 15364
  10.6 17.5 %collective-permute-start = (f32[33,8,1024]{2,1,0:T(8,128)S(1)}, f32[33,8,1024]{2,1,0:T(8,128)S(1)}, u32[]{:S(2)}, u32[]{:S(2)}) collective-permute-start(f32[33,8,1024]{2,1,0:T(8,128)S(1)} %get-tuple-element.78), channel_id=1, source_target_pairs={{0,8},{1,33},{2,10},{3,35},{4,12},{5,37},{6,14},{7,39},{8,16},{9,4... | collective-permute-start | bytes 3244040 | tf_op jit(solution)/shard_map/ppermute | solution.py:53
  13.1 14.9 %collective-permute-start.1 = (f32[33,8,1024]{2,1,0:T(8,128)S(1)}, f32[33,8,1024]{2,1,0:T(8,128)S(1)}, u32[]{:S(2)}, u32[]{:S(2)}) collective-permute-start(f32[33,8,1024]{2,1,0:T(8,128)S(1)} %get-tuple-element.79), channel_id=1, source_target_pairs={{0,24},{1,97},{2,26},{3,99},{4,28},{5,101},{6,30},{7,103},{8,0},{9... | collective-permute-start | bytes 3244040 | tf_op jit(solution)/shard_map/ppermute | solution.py:53
  22.9 16.2 %collective-permute-start.2 = (f32[33,8,1024]{2,1,0:T(8,128)S(1)}, f32[33,8,1024]{2,1,0:T(8,128)S(1)}, u32[]{:S(2)}, u32[]{:S(2)}) collective-permute-start(f32[33,8,1024]{2,1,0:T(8,128)S(1)} %get-tuple-element.84), channel_id=1, source_target_pairs={{0,24},{1,97},{2,26},{3,99},{4,28},{5,101},{6,30},{7,103},{8,0},{9... | collective-permute-start | bytes 3244040 | tf_op jit(solution)/shard_map/ppermute | solution.py:53
  24.4 15.5 %collective-permute-start.3 = (f32[33,8,1024]{2,1,0:T(8,128)S(1)}, f32[33,8,1024]{2,1,0:T(8,128)S(1)}, u32[]{:S(2)}, u32[]{:S(2)}) collective-permute-start(f32[33,8,1024]{2,1,0:T(8,128)S(1)} %get-tuple-element.83), channel_id=1, source_target_pairs={{0,8},{1,33},{2,10},{3,35},{4,12},{5,37},{6,14},{7,39},{8,16},{9,4... | collective-permute-start | bytes 3244040 | tf_op jit(solution)/shard_map/ppermute | solution.py:53
  28.0 28.2 %slice-start = ((s8[8388608]{0:T(1024)(128)(4,1)}), s8[4194304]{0:T(1024)(128)(4,1)S(1)}, s32[]{:S(2)}) async-start(s8[8388608]{0:T(1024)(128)(4,1)} %bitcast.61), calls=%async_computation | async-start | bytes 8388608
  35.0 16.5 %collective-permute-start.4 = (f32[33,8,1024]{2,1,0:T(8,128)S(1)}, f32[33,8,1024]{2,1,0:T(8,128)S(1)}, u32[]{:S(2)}, u32[]{:S(2)}) collective-permute-start(f32[33,8,1024]{2,1,0:T(8,128)S(1)} %get-tuple-element.86), channel_id=1, source_target_pairs={{0,8},{1,33},{2,10},{3,35},{4,12},{5,37},{6,14},{7,39},{8,16},{9,4... | collective-permute-start | bytes 3244040 | tf_op jit(solution)/shard_map/ppermute | solution.py:53
  36.0 20.2 %slice-start.1 = ((s8[8388608]{0:T(1024)(128)(4,1)}), s8[4194304]{0:T(1024)(128)(4,1)S(1)}, s32[]{:S(2)}) async-start(s8[8388608]{0:T(1024)(128)(4,1)} %bitcast.61), calls=%async_computation.1 | async-start | bytes 8388608
  36.0 15.4 %collective-permute-start.5 = (f32[33,8,1024]{2,1,0:T(8,128)S(1)}, f32[33,8,1024]{2,1,0:T(8,128)S(1)}, u32[]{:S(2)}, u32[]{:S(2)}) collective-permute-start(f32[33,8,1024]{2,1,0:T(8,128)S(1)} %get-tuple-element.87), channel_id=1, source_target_pairs={{0,24},{1,97},{2,26},{3,99},{4,28},{5,101},{6,30},{7,103},{8,0},{9... | collective-permute-start | bytes 3244040 | tf_op jit(solution)/shard_map/ppermute | solution.py:53
  52.3 22.7 %collective-permute-start.10 = (f32[17,8,1024]{2,1,0:T(8,128)S(1)}, f32[17,8,1024]{2,1,0:T(8,128)S(1)}, u32[]{:S(2)}, u32[]{:S(2)}) collective-permute-start(f32[17,8,1024]{2,1,0:T(8,128)S(1)} %get-tuple-element.98), channel_id=1, source_target_pairs={{0,96},{1,25},{2,98},{3,27},{4,100},{5,29},{6,102},{7,31},{8,104},... | collective-permute-start | bytes 1671176 | tf_op jit(solution)/shard_map/ppermute | solution.py:53
  54.8 20.2 %collective-permute-start.8 = (f32[17,8,1024]{2,1,0:T(8,128)S(1)}, f32[17,8,1024]{2,1,0:T(8,128)S(1)}, u32[]{:S(2)}, u32[]{:S(2)}) collective-permute-start(f32[17,8,1024]{2,1,0:T(8,128)S(1)} %get-tuple-element.96), channel_id=1, source_target_pairs={{0,32},{1,9},{2,34},{3,11},{4,36},{5,13},{6,38},{7,15},{8,40},{9,1... | collective-permute-start | bytes 1671176 | tf_op jit(solution)/shard_map/ppermute | solution.py:53
  54.8 3.2 %copy-start.2 = (s32[1024]{0:T(1024)S(1)}, s32[1024]{0:T(1024)}, u32[]{:S(2)}) copy-start(s32[1024]{0:T(1024)} %param.12) | copy-start | bytes 12292
  54.8 3.2 %copy-start.3 = (s32[1024]{0:T(1024)S(1)}, s32[1024]{0:T(1024)}, u32[]{:S(2)}) copy-start(s32[1024]{0:T(1024)} %param.13) | copy-start | bytes 12292
  54.8 20.2 %collective-permute-start.9 = (f32[17,8,1024]{2,1,0:T(8,128)S(1)}, f32[17,8,1024]{2,1,0:T(8,128)S(1)}, u32[]{:S(2)}, u32[]{:S(2)}) collective-permute-start(f32[17,8,1024]{2,1,0:T(8,128)S(1)} %get-tuple-element.97), channel_id=1, source_target_pairs={{0,64},{1,17},{2,66},{3,19},{4,68},{5,21},{6,70},{7,23},{8,72},{9,... | collective-permute-start | bytes 1671176 | tf_op jit(solution)/shard_map/ppermute | solution.py:53
  56.9 5.7 %collective-permute-start.6 = (f32[32,1024]{1,0:T(8,128)S(1)}, f32[32,1024]{1,0:T(8,128)S(1)}, u32[]{:S(2)}, u32[]{:S(2)}) collective-permute-start(f32[32,1024]{1,0:T(8,128)S(1)} %get-tuple-element.94), channel_id=1, source_target_pairs={{0,8},{1,33},{2,10},{3,35},{4,12},{5,37},{6,14},{7,39},{8,0},{9,41... | collective-permute-start | bytes 393224 | tf_op jit(solution)/shard_map/ppermute | solution.py:53
  62.6 12.3 %collective-permute-start.7 = (f32[32,1024]{1,0:T(8,128)S(1)}, f32[32,1024]{1,0:T(8,128)S(1)}, u32[]{:S(2)}, u32[]{:S(2)}) collective-permute-start(f32[32,1024]{1,0:T(8,128)S(1)} %add.71), channel_id=1, source_target_pairs={{0,24},{1,97},{2,26},{3,99},{4,28},{5,101},{6,30},{7,103},{8,16},{... | collective-permute-start | bytes 393224 | tf_op jit(solution)/shard_map/ppermute | solution.py:53
  75.2 15.0 %collective-permute-start.12 = (f32[8,16,1024]{2,1,0:T(8,128)S(1)}, f32[8,16,1024]{2,1,0:T(8,128)S(1)}, u32[]{:S(2)}, u32[]{:S(2)}) collective-permute-start(f32[8,16,1024]{2,1,0:T(8,128)S(1)} %bitcast.39), channel_id=1, source_target_pairs={{0,64},{1,17},{2,66},{3,19},{4,68},{5,21},{6,70},{7,23},{8,72},{9,... | collective-permute-start | bytes 1572872 | tf_op jit(solution)/shard_map/ppermute | solution.py:53
  77.4 13.8 %collective-permute-start.13 = (f32[8,16,1024]{2,1,0:T(8,128)S(1)}, f32[8,16,1024]{2,1,0:T(8,128)S(1)}, u32[]{:S(2)}, u32[]{:S(2)}) collective-permute-start(f32[8,16,1024]{2,1,0:T(8,128)S(1)} %bitcast.40), channel_id=1, source_target_pairs={{0,32},{1,9},{2,34},{3,11},{4,36},{5,13},{6,38},{7,15},{8,40},{9,1... | collective-permute-start | bytes 1572872 | tf_op jit(solution)/shard_map/ppermute | solution.py:53
  77.7 13.6 %collective-permute-start.11 = (f32[8,16,1024]{2,1,0:T(8,128)S(1)}, f32[8,16,1024]{2,1,0:T(8,128)S(1)}, u32[]{:S(2)}, u32[]{:S(2)}) collective-permute-start(f32[8,16,1024]{2,1,0:T(8,128)S(1)} %bitcast.41), channel_id=1, source_target_pairs={{0,96},{1,25},{2,98},{3,27},{4,100},{5,29},{6,102},{7,31},{8,104},... | collective-permute-start | bytes 1572872 | tf_op jit(solution)/shard_map/ppermute | solution.py:53
  82.0 3.6 %collective-permute-start.14 = (f32[64,128]{1,0:T(8,128)S(1)}, f32[64,128]{1,0:T(8,128)S(1)}, u32[]{:S(2)}, u32[]{:S(2)}) collective-permute-start(f32[64,128]{1,0:T(8,128)S(1)} %get-tuple-element.99), channel_id=1, source_target_pairs={{0,8},{1,33},{2,10},{3,35},{4,12},{5,37},{6,14},{7,39},{8,0},{9,41... | collective-permute-start | bytes 98312 | tf_op jit(solution)/shard_map/ppermute | solution.py:53
  85.5 4.7 %collective-permute-start.15 = (f32[64,128]{1,0:T(8,128)S(1)}, f32[64,128]{1,0:T(8,128)S(1)}, u32[]{:S(2)}, u32[]{:S(2)}) collective-permute-start(f32[64,128]{1,0:T(8,128)S(1)} %add.76), channel_id=1, source_target_pairs={{0,24},{1,97},{2,26},{3,99},{4,28},{5,101},{6,30},{7,103},{8,16},{... | collective-permute-start | bytes 98312 | tf_op jit(solution)/shard_map/ppermute | solution.py:53
  91.4 15.6 %collective-permute-start.16 = (f32[2,8,16,1024]{3,2,1,0:T(8,128)S(1)}, f32[2,8,16,1024]{3,2,1,0:T(8,128)S(1)}, u32[]{:S(2)}, u32[]{:S(2)}) collective-permute-start(f32[2,8,16,1024]{3,2,1,0:T(8,128)S(1)} %pad_maximum_fusion.refs_0_), channel_id=1, source_target_pairs={{0,8},{1,33},{2,10},{3,35},{4,12},{5,37},{6,14},{7,39},{8,16},{9,4... | collective-permute-start | bytes 3145736 | tf_op jit(solution)/shard_map/ppermute | solution.py:53
  91.4 15.5 %collective-permute-start.17 = (f32[2,8,16,1024]{3,2,1,0:T(8,128)S(1)}, f32[2,8,16,1024]{3,2,1,0:T(8,128)S(1)}, u32[]{:S(2)}, u32[]{:S(2)}) collective-permute-start(f32[2,8,16,1024]{3,2,1,0:T(8,128)S(1)} %pad_maximum_fusion.1.refs_1_), channel_id=1, source_target_pairs={{0,24},{1,97},{2,26},{3,99},{4,28},{5,101},{6,30},{7,103},{8,0},{9... | collective-permute-start | bytes 3145736 | tf_op jit(solution)/shard_map/ppermute | solution.py:53
  94.1 3.4 %collective-permute-start.18 = (f32[64,128]{1,0:T(8,128)S(1)}, f32[64,128]{1,0:T(8,128)S(1)}, u32[]{:S(2)}, u32[]{:S(2)}) collective-permute-start(f32[64,128]{1,0:T(8,128)S(1)} %add.77), channel_id=1, source_target_pairs={{0,32},{1,9},{2,34},{3,11},{4,36},{5,13},{6,38},{7,15},{8,40},{9,1... | collective-permute-start | bytes 98312 | tf_op jit(solution)/shard_map/ppermute | solution.py:53
  97.5 4.7 %collective-permute-start.19 = (f32[64,128]{1,0:T(8,128)S(1)}, f32[64,128]{1,0:T(8,128)S(1)}, u32[]{:S(2)}, u32[]{:S(2)}) collective-permute-start(f32[64,128]{1,0:T(8,128)S(1)} %add.78), channel_id=1, source_target_pairs={{0,96},{1,25},{2,98},{3,27},{4,100},{5,29},{6,102},{7,31},{8,104},... | collective-permute-start | bytes 98312 | tf_op jit(solution)/shard_map/ppermute | solution.py:53
  98.6 19.6 %collective-permute-start.24 = (f32[2,8,16,1024]{3,2,1,0:T(8,128)S(1)}, f32[2,8,16,1024]{3,2,1,0:T(8,128)S(1)}, u32[]{:S(2)}, u32[]{:S(2)}) collective-permute-start(f32[2,8,16,1024]{3,2,1,0:T(8,128)S(1)} %pad_maximum_fusion.1.refs_1_), channel_id=1, source_target_pairs={{0,8},{1,33},{2,10},{3,35},{4,12},{5,37},{6,14},{7,39},{8,16},{9,4... | collective-permute-start | bytes 3145736 | tf_op jit(solution)/shard_map/ppermute | solution.py:53
  98.6 19.6 %collective-permute-start.25 = (f32[2,8,16,1024]{3,2,1,0:T(8,128)S(1)}, f32[2,8,16,1024]{3,2,1,0:T(8,128)S(1)}, u32[]{:S(2)}, u32[]{:S(2)}) collective-permute-start(f32[2,8,16,1024]{3,2,1,0:T(8,128)S(1)} %pad_maximum_fusion.refs_0_), channel_id=1, source_target_pairs={{0,24},{1,97},{2,26},{3,99},{4,28},{5,101},{6,30},{7,103},{8,0},{9... | collective-permute-start | bytes 3145736 | tf_op jit(solution)/shard_map/ppermute | solution.py:53
  106.9 22.5 %collective-permute-start.20 = (f32[2,8,16,1024]{3,2,1,0:T(8,128)S(1)}, f32[2,8,16,1024]{3,2,1,0:T(8,128)S(1)}, u32[]{:S(2)}, u32[]{:S(2)}) collective-permute-start(f32[2,8,16,1024]{3,2,1,0:T(8,128)S(1)} %collective-permute-done.16.refs_2_), channel_id=1, source_target_pairs={{0,8},{1,33},{2,10},{3,35},{4,12},{5,37},{6,14},{7,39},{8,16},{9,4... | collective-permute-start | bytes 3145736 | tf_op jit(solution)/shard_map/ppermute | solution.py:53
  106.9 22.6 %collective-permute-start.21 = (f32[2,8,16,1024]{3,2,1,0:T(8,128)S(1)}, f32[2,8,16,1024]{3,2,1,0:T(8,128)S(1)}, u32[]{:S(2)}, u32[]{:S(2)}) collective-permute-start(f32[2,8,16,1024]{3,2,1,0:T(8,128)S(1)} %collective-permute-done.17.refs_5_), channel_id=1, source_target_pairs={{0,24},{1,97},{2,26},{3,99},{4,28},{5,101},{6,30},{7,103},{8,0},{9... | collective-permute-start | bytes 3145736 | tf_op jit(solution)/shard_map/ppermute | solution.py:53
  109.6 3.5 %collective-permute-start.22 = (f32[56,128]{1,0:T(8,128)S(1)}, f32[56,128]{1,0:T(8,128)S(1)}, u32[]{:S(2)}, u32[]{:S(2)}) collective-permute-start(f32[56,128]{1,0:T(8,128)S(1)} %pad_maximum_fusion.2), channel_id=1, source_target_pairs={{0,1},{1,0},{2,3},{3,2},{4,5},{5,4},{6,7},{7,6},{8,9},{9,8},{10,11... | collective-permute-start | bytes 86024 | tf_op jit(solution)/shard_map/ppermute | solution.py:53
  113.1 3.0 %collective-permute-start.23 = (f32[56,128]{1,0:T(8,128)S(1)}, f32[56,128]{1,0:T(8,128)S(1)}, u32[]{:S(2)}, u32[]{:S(2)}) collective-permute-start(f32[56,128]{1,0:T(8,128)S(1)} %fusion.3), channel_id=1, source_target_pairs={{0,2},{1,3},{2,0},{3,1},{4,6},{5,7},{6,4},{7,5},{8,10},{9,11},{10,... | collective-permute-start | bytes 86024 | tf_op jit(solution)/shard_map/ppermute | solution.py:53
  118.2 4.3 %collective-permute-start.26 = (f32[56,128]{1,0:T(8,128)S(1)}, f32[56,128]{1,0:T(8,128)S(1)}, u32[]{:S(2)}, u32[]{:S(2)}) collective-permute-start(f32[56,128]{1,0:T(8,128)S(1)} %add.81), channel_id=1, source_target_pairs={{0,6},{1,7},{2,4},{3,5},{4,2},{5,3},{6,0},{7,1},{8,14},{9,15},{10,... | collective-permute-start | bytes 86024 | tf_op jit(solution)/shard_map/ppermute | solution.py:53
  134.6 6.5 %collective-permute-start.27 = (f32[256,1280]{1,0:T(8,128)S(1)}, f32[256,1280]{1,0:T(8,128)S(1)}, u32[]{:S(2)}, u32[]{:S(2)}) collective-permute-start(f32[256,1280]{1,0:T(8,128)S(1)} %get-tuple-element.112), channel_id=1, source_target_pairs={{0,1},{1,0},{2,3},{3,2},{4,5},{5,4},{6,7},{7,6},{8,9},{9,8},{10,11... | collective-permute-start | bytes 3932168 | tf_op jit(solution)/shard_map/ppermute | solution.py:53
  141.4 21.0 %collective-permute-start.28 = (f32[128,1280]{1,0:T(8,128)S(1)}, f32[128,1280]{1,0:T(8,128)S(1)}, u32[]{:S(2)}, u32[]{:S(2)}) collective-permute-start(f32[128,1280]{1,0:T(8,128)S(1)} %get-tuple-element.158), channel_id=1, source_target_pairs={{0,2},{1,3},{2,4},{3,5},{4,6},{5,7},{6,0},{7,1},{8,10},{9,11},{10,... | collective-permute-start | bytes 1966088 | tf_op jit(solution)/shard_map/ppermute | solution.py:53
  141.9 20.5 %collective-permute-start.29 = (f32[128,1280]{1,0:T(8,128)S(1)}, f32[128,1280]{1,0:T(8,128)S(1)}, u32[]{:S(2)}, u32[]{:S(2)}) collective-permute-start(f32[128,1280]{1,0:T(8,128)S(1)} %get-tuple-element.157), channel_id=1, source_target_pairs={{0,6},{1,7},{2,0},{3,1},{4,2},{5,3},{6,4},{7,5},{8,14},{9,15},{10,... | collective-permute-start | bytes 1966088 | tf_op jit(solution)/shard_map/ppermute | solution.py:53
  156.0 7.2 %collective-permute-start.30 = (f32[256,1280]{1,0:T(8,128)S(1)}, f32[256,1280]{1,0:T(8,128)S(1)}, u32[]{:S(2)}, u32[]{:S(2)}) collective-permute-start(f32[256,1280]{1,0:T(8,128)S(1)} %get-tuple-element.117), channel_id=1, source_target_pairs={{0,1},{1,0},{2,3},{3,2},{4,5},{5,4},{6,7},{7,6},{8,9},{9,8},{10,11... | collective-permute-start | bytes 3932168 | tf_op jit(solution)/shard_map/ppermute | solution.py:53
  156.3 6.9 %collective-permute-start.31 = (f32[256,1280]{1,0:T(8,128)S(1)}, f32[256,1280]{1,0:T(8,128)S(1)}, u32[]{:S(2)}, u32[]{:S(2)}) collective-permute-start(f32[256,1280]{1,0:T(8,128)S(1)} %get-tuple-element.123), channel_id=1, source_target_pairs={{0,1},{1,0},{2,3},{3,2},{4,5},{5,4},{6,7},{7,6},{8,9},{9,8},{10,11... | collective-permute-start | bytes 3932168 | tf_op jit(solution)/shard_map/ppermute | solution.py:53
  162.1 12.1 %collective-permute-start.32 = (f32[256,1280]{1,0:T(8,128)S(1)}, f32[256,1280]{1,0:T(8,128)S(1)}, u32[]{:S(2)}, u32[]{:S(2)}) collective-permute-start(f32[256,1280]{1,0:T(8,128)S(1)} %get-tuple-element.126), channel_id=1, source_target_pairs={{0,1},{1,0},{2,3},{3,2},{4,5},{5,4},{6,7},{7,6},{8,9},{9,8},{10,11... | collective-permute-start | bytes 3932168 | tf_op jit(solution)/shard_map/ppermute | solution.py:53
  164.2 40.5 %collective-permute-start.39 = (f32[256,1280]{1,0:T(8,128)S(1)}, f32[256,1280]{1,0:T(8,128)S(1)}, u32[]{:S(2)}, u32[]{:S(2)}) collective-permute-start(f32[256,1280]{1,0:T(8,128)S(1)} %get-tuple-element.124), channel_id=1, source_target_pairs={{0,2},{1,3},{2,4},{3,5},{4,6},{5,7},{6,0},{7,1},{8,10},{9,11},{10,... | collective-permute-start | bytes 3932168 | tf_op jit(solution)/shard_map/ppermute | solution.py:53
  164.2 40.5 %collective-permute-start.40 = (f32[256,1280]{1,0:T(8,128)S(1)}, f32[256,1280]{1,0:T(8,128)S(1)}, u32[]{:S(2)}, u32[]{:S(2)}) collective-permute-start(f32[256,1280]{1,0:T(8,128)S(1)} %get-tuple-element.125), channel_id=1, source_target_pairs={{0,6},{1,7},{2,0},{3,1},{4,2},{5,3},{6,4},{7,5},{8,14},{9,15},{10,... | collective-permute-start | bytes 3932168 | tf_op jit(solution)/shard_map/ppermute | solution.py:53
  166.9 4.2 %collective-permute-start.33 = (f32[32,1024]{1,0:T(8,128)S(1)}, f32[32,1024]{1,0:T(8,128)S(1)}, u32[]{:S(2)}, u32[]{:S(2)}) collective-permute-start(f32[32,1024]{1,0:T(8,128)S(1)} %add.72), channel_id=1, source_target_pairs={{0,32},{1,9},{2,34},{3,11},{4,36},{5,13},{6,38},{7,15},{8,40},{9,1... | collective-permute-start | bytes 393224 | tf_op jit(solution)/shard_map/ppermute | solution.py:53
  171.2 6.2 %collective-permute-start.38 = (f32[32,1024]{1,0:T(8,128)S(1)}, f32[32,1024]{1,0:T(8,128)S(1)}, u32[]{:S(2)}, u32[]{:S(2)}) collective-permute-start(f32[32,1024]{1,0:T(8,128)S(1)} %add.84), channel_id=1, source_target_pairs={{0,96},{1,25},{2,98},{3,27},{4,100},{5,29},{6,102},{7,31},{8,104},... | collective-permute-start | bytes 393224 | tf_op jit(solution)/shard_map/ppermute | solution.py:53
  177.2 1.3 collective-permute-start.34
  178.5 24.9 %collective-permute-start.35 = (f32[8,1280]{1,0:T(8,128)S(1)}, f32[8,1280]{1,0:T(8,128)S(1)}, u32[]{:S(2)}, u32[]{:S(2)}) collective-permute-start(f32[8,1280]{1,0:T(8,128)S(1)} %add.85.last), channel_id=1, source_target_pairs={{0,2},{1,3},{2,4},{3,5},{4,6},{5,7},{6,0},{7,1},{8,10},{9,11},{10,... | collective-permute-start | bytes 122888 | tf_op jit(solution)/shard_map/ppermute | solution.py:53
  178.5 24.9 %collective-permute-start.36 = (f32[8,1280]{1,0:T(8,128)S(1)}, f32[8,1280]{1,0:T(8,128)S(1)}, u32[]{:S(2)}, u32[]{:S(2)}) collective-permute-start(f32[8,1280]{1,0:T(8,128)S(1)} %add.85.last), channel_id=1, source_target_pairs={{0,4},{1,5},{2,6},{3,7},{4,0},{5,1},{6,2},{7,3},{8,12},{9,13},{10,... | collective-permute-start | bytes 122888 | tf_op jit(solution)/shard_map/ppermute | solution.py:53
  179.9 23.5 %collective-permute-start.37 = (f32[8,1280]{1,0:T(8,128)S(1)}, f32[8,1280]{1,0:T(8,128)S(1)}, u32[]{:S(2)}, u32[]{:S(2)}) collective-permute-start(f32[8,1280]{1,0:T(8,128)S(1)} %add.85.last), channel_id=1, source_target_pairs={{0,6},{1,7},{2,0},{3,1},{4,2},{5,3},{6,4},{7,5},{8,14},{9,15},{10,... | collective-permute-start | bytes 122888 | tf_op jit(solution)/shard_map/ppermute | solution.py:53

commit v3 on v2

--- a/solution.py
+++ b/solution.py
@@ -346,7 +346,7 @@
         compiler_params=vmem(8),
         cost_estimate=NO_COST,
         name="stats",
-    )(ids, piece, streamed(spatial), spot, totals)
+    )(ids, piece, spatial, spot, totals)
 
 
 def coef_kernel(ids, genes_slides, sums, spot, totals, gene, rows, scalars, pairs):
@@ -490,11 +490,11 @@
         compiler_params=vmem(12),
         cost_estimate=NO_COST,
         name="grad",
-    )(ids, *pred, *[streamed(spatial)] * count, gene, spot, *done)
+    )(ids, *pred, *[spatial] * count, gene, spot, *done)
 
 
 def back_kernel(ids, grad, masses, expr, *refs, parts, first, last):
-    more, (sums, *outs), (held, ready) = refs[: first + 5 * last], refs[first + 5 * last : -2], refs[-2:]
+    more, (sums, *outs), (held, ready) = refs[: first + 4 * last], refs[first + 4 * last : -2], refs[-2:]
     step = pl.program_id(0)
     rows = grad.shape[2]
 
@@ -513,7 +513,7 @@
     @pl.when(step == 0)
     def _():
         if last:
-            sums[...] = more[0][...] + more[1][...] + more[2][...] + more[3][...]
+            sums[...] = more[0][...] + more[1][...] + more[2][...]
         else:
             sums[...] = jnp.zeros_like(sums)
 
@@ -541,14 +541,14 @@
             total = jnp.sum(sums[...], axis=0, keepdims=True)
             sums[...] = jnp.zeros_like(sums)
             sums[0:1, :] = total
-            sums[1:2, 0:128] = more[4][...]
+            sums[1:2, 0:128] = more[3][...]
 
 
 def back_call(ids, parts, grad, masses, expr, first=(), last=()):
     _, blocks, rows, spots = grad.shape
     cells = masses.shape[1]
     return pl.pallas_call(
-        functools.partial(back_kernel, parts=parts, first=len(first), last=len(last) // 5),
+        functools.partial(back_kernel, parts=parts, first=len(first), last=len(last) // 4),
         grid_spec=pltpu.PrefetchScalarGridSpec(
             num_scalar_prefetch=1,
             grid=(len(parts),),
@@ -807,22 +807,20 @@
     grad, column_c = last_grad((1, -1, 0), grad, far)
     sums_c, up_a, down_a, own_a = back_part([(1, 1), (-1, 1), (0, 1)], grad)
     up_got, down_got, own_got = (swap(one, 0, 0, 0, 1) for one in (up_a, down_a, own_a))
-    sums_d, up_b, down_b = back_part([(1, 0), (-1, 0)], grad, up_a)
+    last, up_b, down_b, own_b = back_part(
+        [(1, 0), (-1, 0), (0, 0)], grad, up_a, last=[sums_a, sums_b, sums_c, scalars]
+    )
+    last = last + swap(last, 0, 0, 0, 1)
     above, below = lift_call(up_b, down_b, far_up, far_down)
-    types = types + swap_across(after(types, above), 1)
     above, below = join_call(above, below, up_got, down_got)
     near_up, near_down = up(above, 1), up(below, -1)
-    types_got = swap_across(types, 3)
-    last, own_b = back_part(
-        [(0, 0)], grad, above, below, own_got, types, last=[sums_a, sums_b, sums_c, sums_d, scalars]
-    )
-    types = types + after(types_got, own_b)
+    types = types + swap_across(after(types, up_b), 1)
+    types = types + swap_across(after(types, above), 3)
     own = own_b + own_got
 
     column = jnp.sum(column_a + column_b + column_c, axis=0) * share + spot_coef[32] * mass
     map_rows = stacked([spot_coef[32], column])
     map_args = (expr, grad.reshape(2, genes, spots), masses, keep2, map_rows, all_cells * genes)
-    last = last + swap(last, 0, 0, 0, 1)
     got = [up(last, step) for step in (1, 2, 3)]
     grad_map = map_call(*after(map_args[:-1], last, types), map_args[-1])
     got = after(tuple(got), grad_map)

time: 207 us -> 202 us (0.976)
  Pallas kernels: 93.9 us -> 88.3 us
    pallas_call x3, Pallas kernels: 11.7 us -> 7.63 us  [grad_call(): pl.pallas_call(functools.partial(grad_kernel, count=count, lane=lane, chi...]
    pallas_call x5 -> x4, Pallas kernels: 23.1 us -> 22.5 us  [back_call(): pl.pallas_call(functools.partial(back_kernel, parts=parts, first=len(firs...]
  transfers between devices with their start and end apart: 41 -> 41, of which waited for: 18 -> 19; matrix products, arithmetic and copies ran while one was open for 1% -> 1% of each run, Pallas kernels for 38% -> 37%
where the time goes in v3:
time: 202 us; the launch traced here: 201 us
  Pallas kernels  88.3 us (44%)
  starting transfers between devices  54.3 us (27%)
  waiting for transfers between devices  52.7 us (26%)
  other arithmetic  3.74 us (2%)
    ppermute x41, starting transfers between devices, send(): return lax.ppermute(array, ('cells', 'spots'), route(target))  54.3 us
    ppermute x41, waiting for transfers between devices, send(): return lax.ppermute(array, ('cells', 'spots'), route(target))  52.7 us
    pallas_call x4, Pallas kernels, back_call(): pl.pallas_call(functools.partial(back_kernel, parts=parts, first=len(firs...  22.5 us
    pallas_call x3, Pallas kernels, pred_call(): pl.pallas_call(functools.partial(pred_kernel, cuts=cuts), grid_spec=pltpu...  21.9 us
    pallas_call x1, Pallas kernels, map_call(): pl.pallas_call(functools.partial(map_kernel, scale=scale), grid=(cells //...  21.3 us
    pallas_call x1, Pallas kernels, expo_call(): pl.pallas_call(expo_kernel, grid_spec=pltpu.PrefetchScalarGridSpec(num_sc...  9.85 us
    pallas_call x3, Pallas kernels, grad_call(): pl.pallas_call(functools.partial(grad_kernel, count=count, lane=lane, chi...  7.63 us
  transfers between devices with their start and end apart: 41, of which 19 were waited for; matrix products, arithmetic and copies ran while one was open for 1% of the time, Pallas kernels for 37%

profile of v3, /device:TPU:1, one launch (start us, length us, event | category | flops | bytes accessed | tf_op | source)
XLA Modules:
  0.0 200.7 jit_solution(1822700148144847742)
XLA Ops:
  0.7 9.9 %expo.1 = (bf16[2,1280,1024]{2,1,0:T(8,128)(2,1)S(1)}, f32[32,1024]{1,0:T(8,128)S(1)}, f32[8,1024]{1,0:T(8,128)S(1)}, f32[33,8,1024]{2,1,0:T(8,128)S(1)}, f32[33,8,1024]{2,1,0:T(8,128)S(1)}) custom-call(s32[4]{0:T(128)S(1)} %pad_add_fusion.ids, f32[1280,1024]{1,0:T(8,128)} %logits.1, s32[10,128]{1,0:T(8,128)} %bitcast.66, f32[10,128]{1,0:T(8,128)} %bitcast.67, ...), custom_call_target="tpu_custom_call" | custom-call | bytes 1310720 | tf_op jit(solution)/shard_map/expo/pallas_call | solution.py:176
  10.6 2.5 %collective-permute-start = (f32[33,8,1024]{2,1,0:T(8,128)S(1)}, f32[33,8,1024]{2,1,0:T(8,128)S(1)}, u32[]{:S(2)}, u32[]{:S(2)}) collective-permute-start(f32[33,8,1024]{2,1,0:T(8,128)S(1)} %get-tuple-element.76), channel_id=1, source_target_pairs={{0,8},{1,33},{2,10},{3,35},{4,12},{5,37},{6,14},{7,39},{8,16},{9,4... | collective-permute-start | bytes 3244040 | tf_op jit(solution)/shard_map/ppermute | solution.py:53
  13.1 2.3 %collective-permute-start.1 = (f32[33,8,1024]{2,1,0:T(8,128)S(1)}, f32[33,8,1024]{2,1,0:T(8,128)S(1)}, u32[]{:S(2)}, u32[]{:S(2)}) collective-permute-start(f32[33,8,1024]{2,1,0:T(8,128)S(1)} %get-tuple-element.77), channel_id=1, source_target_pairs={{0,24},{1,97},{2,26},{3,99},{4,28},{5,101},{6,30},{7,103},{8,0},{9... | collective-permute-start | bytes 3244040 | tf_op jit(solution)/shard_map/ppermute | solution.py:53
  15.4 7.5 %pred_.3 = (f32[33,8,1024]{2,1,0:T(8,128)S(1)}, f32[33,8,1024]{2,1,0:T(8,128)S(1)}) custom-call(s32[4]{0:T(128)S(1)} %pad_add_fusion.ids, f32[8,16,16,1280]{3,2,1,0:T(8,128)} %bitcast.57, f32[8,16,16,1280]{3,2,1,0:T(8,128)} %bitcast.58, f32[1,1280]{1,0:T(1,128)S(1)} %reshape.94.keep, bf16[2,1280,1024]{2,1,0:T(8,128)(2,1)S(1)} %get-tuple-element.135.masses, ...), custom_call_target="tpu_custom_call" | custom-call | flops 503316480 | bytes 1245184 | tf_op jit(solution)/shard_map/pred/pallas_call | solution.py:249
  22.9 1.4 collective-permute-start.2
  24.5 3.6 %collective-permute-done.refs_0_ = f32[33,8,1024]{2,1,0:T(8,128)S(1)} collective-permute-done((f32[33,8,1024]{2,1,0:T(8,128)S(1)}, f32[33,8,1024]{2,1,0:T(8,128)S(1)}, u32[]{:S(2)}, u32[]{:S(2)}) %collective-permute-start) | collective-permute-done | bytes 1081376 | tf_op jit(solution)/shard_map/ppermute | solution.py:53
  28.0 6.9 %pred_.4 = (f32[33,8,1024]{2,1,0:T(8,128)S(1)}, f32[33,8,1024]{2,1,0:T(8,128)S(1)}) custom-call(s32[4]{0:T(128)S(1)} %pad_add_fusion.ids, f32[8,16,16,1280]{3,2,1,0:T(8,128)} %bitcast.59, f32[8,16,16,1280]{3,2,1,0:T(8,128)} %bitcast.60, f32[1,1280]{1,0:T(1,128)S(1)} %reshape.94.keep, bf16[2,1280,1024]{2,1,0:T(8,128)(2,1)S(1)} %get-tuple-element.135.masses, ...), custom_call_target="tpu_custom_call" | custom-call | flops 503316480 | bytes 1245184 | tf_op jit(solution)/shard_map/pred/pallas_call | solution.py:249
  36.0 2.0 collective-permute-start.5
  39.9 7.6 %pred_.5 = (f32[33,8,1024]{2,1,0:T(8,128)S(1)}, f32[33,8,1024]{2,1,0:T(8,128)S(1)}) custom-call(s32[4]{0:T(128)S(1)} %pad_add_fusion.ids, f32[8,16,16,1280]{3,2,1,0:T(8,128)} %bitcast.61, f32[8,16,16,1280]{3,2,1,0:T(8,128)} %bitcast.62, f32[1,1280]{1,0:T(1,128)S(1)} %reshape.94.keep, bf16[2,1280,1024]{2,1,0:T(8,128)(2,1)S(1)} %get-tuple-element.135.masses, ...), custom_call_target="tpu_custom_call" | custom-call | flops 503316480 | bytes 1245184 | tf_op jit(solution)/shard_map/pred/pallas_call | solution.py:249
  47.5 4.0 %collective-permute-done.4.got0 = f32[33,8,1024]{2,1,0:T(8,128)S(1)} collective-permute-done((f32[33,8,1024]{2,1,0:T(8,128)S(1)}, f32[33,8,1024]{2,1,0:T(8,128)S(1)}, u32[]{:S(2)}, u32[]{:S(2)}) %collective-permute-start.4) | collective-permute-done | bytes 1081376 | tf_op jit(solution)/shard_map/ppermute | solution.py:53
  52.3 2.5 %collective-permute-start.10 = (f32[17,8,1024]{2,1,0:T(8,128)S(1)}, f32[17,8,1024]{2,1,0:T(8,128)S(1)}, u32[]{:S(2)}, u32[]{:S(2)}) collective-permute-start(f32[17,8,1024]{2,1,0:T(8,128)S(1)} %get-tuple-element.96), channel_id=1, source_target_pairs={{0,96},{1,25},{2,98},{3,27},{4,100},{5,29},{6,102},{7,31},{8,104},... | collective-permute-start | bytes 1671176 | tf_op jit(solution)/shard_map/ppermute | solution.py:53
  54.8 1.4 collective-permute-start.9
  58.1 4.5 %collective-permute-done.6 = f32[32,1024]{1,0:T(8,128)S(1)} collective-permute-done((f32[32,1024]{1,0:T(8,128)S(1)}, f32[32,1024]{1,0:T(8,128)S(1)}, u32[]{:S(2)}, u32[]{:S(2)}) %collective-permute-start.6) | collective-permute-done | bytes 131104 | tf_op jit(solution)/shard_map/ppermute | solution.py:53
  62.6 2.7 %collective-permute-start.7 = (f32[32,1024]{1,0:T(8,128)S(1)}, f32[32,1024]{1,0:T(8,128)S(1)}, u32[]{:S(2)}, u32[]{:S(2)}) collective-permute-start(f32[32,1024]{1,0:T(8,128)S(1)} %add.71), channel_id=1, source_target_pairs={{0,24},{1,97},{2,26},{3,99},{4,28},{5,101},{6,30},{7,103},{8,16},{... | collective-permute-start | bytes 393224 | tf_op jit(solution)/shard_map/ppermute | solution.py:53
  65.4 9.6 %collective-permute-done.7 = f32[32,1024]{1,0:T(8,128)S(1)} collective-permute-done((f32[32,1024]{1,0:T(8,128)S(1)}, f32[32,1024]{1,0:T(8,128)S(1)}, u32[]{:S(2)}, u32[]{:S(2)}) %collective-permute-start.7) | collective-permute-done | bytes 131104 | tf_op jit(solution)/shard_map/ppermute | solution.py:53
  75.2 2.1 %collective-permute-start.12 = (f32[8,16,1024]{2,1,0:T(8,128)S(1)}, f32[8,16,1024]{2,1,0:T(8,128)S(1)}, u32[]{:S(2)}, u32[]{:S(2)}) collective-permute-start(f32[8,16,1024]{2,1,0:T(8,128)S(1)} %bitcast.47), channel_id=1, source_target_pairs={{0,64},{1,17},{2,66},{3,19},{4,68},{5,21},{6,70},{7,23},{8,72},{9,... | collective-permute-start | bytes 1572872 | tf_op jit(solution)/shard_map/ppermute | solution.py:53
  77.7 2.4 %collective-permute-start.11 = (f32[8,16,1024]{2,1,0:T(8,128)S(1)}, f32[8,16,1024]{2,1,0:T(8,128)S(1)}, u32[]{:S(2)}, u32[]{:S(2)}) collective-permute-start(f32[8,16,1024]{2,1,0:T(8,128)S(1)} %bitcast.49), channel_id=1, source_target_pairs={{0,96},{1,25},{2,98},{3,27},{4,100},{5,29},{6,102},{7,31},{8,104},... | collective-permute-start | bytes 1572872 | tf_op jit(solution)/shard_map/ppermute | solution.py:53
  81.0 3.5 %collective-permute-done.14 = f32[64,128]{1,0:T(8,128)S(1)} collective-permute-done((f32[64,128]{1,0:T(8,128)S(1)}, f32[64,128]{1,0:T(8,128)S(1)}, u32[]{:S(2)}, u32[]{:S(2)}) %collective-permute-start.14) | collective-permute-done | bytes 32800 | tf_op jit(solution)/shard_map/ppermute | solution.py:53
  84.6 4.6 %collective-permute-done.15 = f32[64,128]{1,0:T(8,128)S(1)} collective-permute-done((f32[64,128]{1,0:T(8,128)S(1)}, f32[64,128]{1,0:T(8,128)S(1)}, u32[]{:S(2)}, u32[]{:S(2)}) %collective-permute-start.15) | collective-permute-done | bytes 32800 | tf_op jit(solution)/shard_map/ppermute | solution.py:53
  89.2 1.9 collective-permute-done.13
  91.4 2.7 %collective-permute-start.17 = (f32[2,8,16,1024]{3,2,1,0:T(8,128)S(1)}, f32[2,8,16,1024]{3,2,1,0:T(8,128)S(1)}, u32[]{:S(2)}, u32[]{:S(2)}) collective-permute-start(f32[2,8,16,1024]{3,2,1,0:T(8,128)S(1)} %pad_maximum_fusion.1.refs_1_), channel_id=1, source_target_pairs={{0,24},{1,97},{2,26},{3,99},{4,28},{5,101},{6,30},{7,103},{8,0},{9... | collective-permute-start | bytes 3145736 | tf_op jit(solution)/shard_map/ppermute | solution.py:53
  94.7 2.8 %collective-permute-done.18 = f32[64,128]{1,0:T(8,128)S(1)} collective-permute-done((f32[64,128]{1,0:T(8,128)S(1)}, f32[64,128]{1,0:T(8,128)S(1)}, u32[]{:S(2)}, u32[]{:S(2)}) %collective-permute-start.18) | collective-permute-done | bytes 32800 | tf_op jit(solution)/shard_map/ppermute | solution.py:53
  97.5 1.7 collective-permute-start.19
  99.2 2.7 %collective-permute-start.25 = (f32[2,8,16,1024]{3,2,1,0:T(8,128)S(1)}, f32[2,8,16,1024]{3,2,1,0:T(8,128)S(1)}, u32[]{:S(2)}, u32[]{:S(2)}) collective-permute-start(f32[2,8,16,1024]{3,2,1,0:T(8,128)S(1)} %pad_maximum_fusion.refs_0_), channel_id=1, source_target_pairs={{0,24},{1,97},{2,26},{3,99},{4,28},{5,101},{6,30},{7,103},{8,0},{9... | collective-permute-start | bytes 3145736 | tf_op jit(solution)/shard_map/ppermute | solution.py:53
  102.2 4.7 %collective-permute-done.16.refs_2_ = f32[2,8,16,1024]{3,2,1,0:T(8,128)S(1)} collective-permute-done((f32[2,8,16,1024]{3,2,1,0:T(8,128)S(1)}, f32[2,8,16,1024]{3,2,1,0:T(8,128)S(1)}, u32[]{:S(2)}, u32[]{:S(2)}) %collective-permute-start.16) | collective-permute-done | bytes 1048608 | tf_op jit(solution)/shard_map/ppermute | solution.py:53
  106.9 2.7 %collective-permute-start.21 = (f32[2,8,16,1024]{3,2,1,0:T(8,128)S(1)}, f32[2,8,16,1024]{3,2,1,0:T(8,128)S(1)}, u32[]{:S(2)}, u32[]{:S(2)}) collective-permute-start(f32[2,8,16,1024]{3,2,1,0:T(8,128)S(1)} %collective-permute-done.17.refs_5_), channel_id=1, source_target_pairs={{0,24},{1,97},{2,26},{3,99},{4,28},{5,101},{6,30},{7,103},{8,0},{9... | collective-permute-start | bytes 3145736 | tf_op jit(solution)/shard_map/ppermute | solution.py:53
  109.6 2.6 %collective-permute-start.22 = (f32[56,128]{1,0:T(8,128)S(1)}, f32[56,128]{1,0:T(8,128)S(1)}, u32[]{:S(2)}, u32[]{:S(2)}) collective-permute-start(f32[56,128]{1,0:T(8,128)S(1)} %pad_maximum_fusion.2), channel_id=1, source_target_pairs={{0,1},{1,0},{2,3},{3,2},{4,5},{5,4},{6,7},{7,6},{8,9},{9,8},{10,11... | collective-permute-start | bytes 86024 | tf_op jit(solution)/shard_map/ppermute | solution.py:53
  113.1 1.3 collective-permute-start.23
  114.4 1.7 collective-permute-done.23
  116.1 2.0 %collective-permute-done.24.refs_3_ = f32[2,8,16,1024]{3,2,1,0:T(8,128)S(1)} collective-permute-done((f32[2,8,16,1024]{3,2,1,0:T(8,128)S(1)}, f32[2,8,16,1024]{3,2,1,0:T(8,128)S(1)}, u32[]{:S(2)}, u32[]{:S(2)}) %collective-permute-start.24) | collective-permute-done | bytes 1048608 | tf_op jit(solution)/shard_map/ppermute | solution.py:53
  118.1 2.7 %collective-permute-start.26 = (f32[56,128]{1,0:T(8,128)S(1)}, f32[56,128]{1,0:T(8,128)S(1)}, u32[]{:S(2)}, u32[]{:S(2)}) collective-permute-start(f32[56,128]{1,0:T(8,128)S(1)} %add.81), channel_id=1, source_target_pairs={{0,6},{1,7},{2,4},{3,5},{4,2},{5,3},{6,0},{7,1},{8,14},{9,15},{10,... | collective-permute-start | bytes 86024 | tf_op jit(solution)/shard_map/ppermute | solution.py:53
  120.9 1.6 collective-permute-done.26
  123.3 4.7 %grad.3 = (bf16[2,8,256,1024]{3,2,1,0:T(8,128)(2,1)S(1)}, f32[8,1024]{1,0:T(8,128)S(1)}) custom-call(s32[4]{0:T(128)S(1)} %pad_add_fusion.ids, f32[2,8,16,1024]{3,2,1,0:T(8,128)S(1)} %pad_maximum_fusion.refs_0_, f32[2,8,16,1024]{3,2,1,0:T(8,128)S(1)} %pad_maximum_fusion.1.refs_1_, f32[2,8,16,1024]{3,2,1,0:T(8,128)S(1)} %collective-permute-done.16.refs_2_, ...), custom_call_target="tpu_custom_call" | custom-call | tf_op jit(solution)/shard_map/grad/pallas_call | solution.py:474
  128.0 1.4 collective-permute-done.20.refs_0_
  130.3 3.1 %back.4 = (f32[8,1280]{1,0:T(8,128)S(1)}, f32[256,1280]{1,0:T(8,128)S(1)}) custom-call(s32[4]{0:T(128)S(1)} %pad_add_fusion.ids, bf16[2,8,256,1024]{3,2,1,0:T(8,128)(2,1)S(1)} %get-tuple-element.109.grad.refs_5_, bf16[2,1280,1024]{2,1,0:T(8,128)(2,1)S(1)} %get-tuple-element.135.masses, f32[2048,1280]{1,0:T(8,128)} %expr.8, ...), custom_call_target="tpu_custom_call" | custom-call | tf_op jit(solution)/shard_map/back/pallas_call | solution.py:550
  133.4 2.1 %collective-permute-start.27 = (f32[256,1280]{1,0:T(8,128)S(1)}, f32[256,1280]{1,0:T(8,128)S(1)}, u32[]{:S(2)}, u32[]{:S(2)}) collective-permute-start(f32[256,1280]{1,0:T(8,128)S(1)} %get-tuple-element.110), channel_id=1, source_target_pairs={{0,1},{1,0},{2,3},{3,2},{4,5},{5,4},{6,7},{7,6},{8,9},{9,8},{10,11... | collective-permute-start | bytes 3932168 | tf_op jit(solution)/shard_map/ppermute | solution.py:53
  135.6 3.5 %back.5 = (f32[8,1280]{1,0:T(8,128)S(1)}, f32[256,1280]{1,0:T(8,128)S(1)}) custom-call(s32[4]{0:T(128)S(1)} %pad_add_fusion.ids, bf16[2,8,256,1024]{3,2,1,0:T(8,128)(2,1)S(1)} %get-tuple-element.109.grad.refs_5_, bf16[2,1280,1024]{2,1,0:T(8,128)(2,1)S(1)} %get-tuple-element.135.masses, f32[2048,1280]{1,0:T(8,128)} %expr.8), custom_call_target="tpu_custom_call" | custom-call | tf_op jit(solution)/shard_map/back/pallas_call | solution.py:550
  139.4 1.4 collective-permute-start.33
  140.8 1.7 collective-permute-start.34
  142.5 1.9 grad.5
  144.4 8.0 %back.6 = (f32[8,1280]{1,0:T(8,128)S(1)}, f32[256,1280]{1,0:T(8,128)S(1)}, f32[256,1280]{1,0:T(8,128)S(1)}, f32[256,1280]{1,0:T(8,128)S(1)}) custom-call(s32[4]{0:T(128)S(1)} %pad_add_fusion.ids, bf16[2,8,256,1024]{3,2,1,0:T(8,128)(2,1)S(1)} %get-tuple-element.114.grad, bf16[2,1280,1024]{2,1,0:T(8,128)(2,1)S(1)} %get-tuple-element.135.masses, f32[2048,1280]{1,0:T(8,128)} %expr.8), custom_call_target="tpu_custom_call" | custom-call | tf_op jit(solution)/shard_map/back/pallas_call | solution.py:550
  153.3 8.0 %back.7 = (f32[8,1280]{1,0:T(8,128)S(1)}, f32[256,1280]{1,0:T(8,128)S(1)}, f32[256,1280]{1,0:T(8,128)S(1)}, f32[256,1280]{1,0:T(8,128)S(1)}) custom-call(s32[4]{0:T(128)S(1)} %pad_add_fusion.ids, bf16[2,8,256,1024]{3,2,1,0:T(8,128)(2,1)S(1)} %get-tuple-element.114.grad, bf16[2,1280,1024]{2,1,0:T(8,128)(2,1)S(1)} %get-tuple-element.135.masses, ...), custom_call_target="tpu_custom_call" | custom-call | tf_op jit(solution)/shard_map/back/pallas_call | solution.py:550
  163.2 2.6 %collective-permute-start.40 = (f32[256,1280]{1,0:T(8,128)S(1)}, f32[256,1280]{1,0:T(8,128)S(1)}, u32[]{:S(2)}, u32[]{:S(2)}) collective-permute-start(f32[256,1280]{1,0:T(8,128)S(1)} %get-tuple-element.146), channel_id=1, source_target_pairs={{0,6},{1,7},{2,0},{3,1},{4,2},{5,3},{6,4},{7,5},{8,14},{9,15},{10,... | collective-permute-start | bytes 3932168 | tf_op jit(solution)/shard_map/ppermute | solution.py:53
  165.8 1.3 collective-permute-start.32
  167.2 2.8 %collective-permute-done.32 = f32[32,1024]{1,0:T(8,128)S(1)} collective-permute-done((f32[32,1024]{1,0:T(8,128)S(1)}, f32[32,1024]{1,0:T(8,128)S(1)}, u32[]{:S(2)}, u32[]{:S(2)}) %collective-permute-start.32) | collective-permute-done | bytes 131104 | tf_op jit(solution)/shard_map/ppermute | solution.py:53
  170.1 3.0 %collective-permute-start.37 = (f32[32,1024]{1,0:T(8,128)S(1)}, f32[32,1024]{1,0:T(8,128)S(1)}, u32[]{:S(2)}, u32[]{:S(2)}) collective-permute-start(f32[32,1024]{1,0:T(8,128)S(1)} %add.88), channel_id=1, source_target_pairs={{0,96},{1,25},{2,98},{3,27},{4,100},{5,29},{6,102},{7,31},{8,104},... | collective-permute-start | bytes 393224 | tf_op jit(solution)/shard_map/ppermute | solution.py:53
  173.2 1.4 collective-permute-start.30
  176.8 21.3 %grad_map.1 = f32[1280,1024]{1,0:T(8,128)} custom-call(f32[2048,1280]{1,0:T(8,128)} %expr.8, bf16[2,2048,1024]{2,1,0:T(8,128)(2,1)S(1)} %bitcast.46, bf16[2,1280,1024]{2,1,0:T(8,128)(2,1)S(1)} %get-tuple-element.135.masses, f32[10,128]{1,0:T(8,128)S(1)} %bitcast.52, f32[8,1024]{1,0:T(8,128)S(1)} %select_select_fusion.spot), custom_call_target="tpu_custom_call" | custom-call | tf_op jit(solution)/shard_map/grad_map/pallas_call | solution.py:656
  (103 shorter events, 19.4 us)
Async XLA Ops:
  0.7 14.7 %copy-start = (s32[1280]{0:T(1024)S(1)}, s32[1280]{0:T(1024)}, u32[]{:S(2)}) copy-start(s32[1280]{0:T(1024)} %param.11) | copy-start | bytes 15364
  0.7 14.7 %copy-start.1 = (f32[1280]{0:T(1024)S(1)}, f32[1280]{0:T(1024)}, u32[]{:S(2)}) copy-start(f32[1280]{0:T(1024)} %param.8) | copy-start | bytes 15364
  10.6 17.5 %collective-permute-start = (f32[33,8,1024]{2,1,0:T(8,128)S(1)}, f32[33,8,1024]{2,1,0:T(8,128)S(1)}, u32[]{:S(2)}, u32[]{:S(2)}) collective-permute-start(f32[33,8,1024]{2,1,0:T(8,128)S(1)} %get-tuple-element.76), channel_id=1, source_target_pairs={{0,8},{1,33},{2,10},{3,35},{4,12},{5,37},{6,14},{7,39},{8,16},{9,4... | collective-permute-start | bytes 3244040 | tf_op jit(solution)/shard_map/ppermute | solution.py:53
  13.1 14.9 %collective-permute-start.1 = (f32[33,8,1024]{2,1,0:T(8,128)S(1)}, f32[33,8,1024]{2,1,0:T(8,128)S(1)}, u32[]{:S(2)}, u32[]{:S(2)}) collective-permute-start(f32[33,8,1024]{2,1,0:T(8,128)S(1)} %get-tuple-element.77), channel_id=1, source_target_pairs={{0,24},{1,97},{2,26},{3,99},{4,28},{5,101},{6,30},{7,103},{8,0},{9... | collective-permute-start | bytes 3244040 | tf_op jit(solution)/shard_map/ppermute | solution.py:53
  22.9 16.2 %collective-permute-start.2 = (f32[33,8,1024]{2,1,0:T(8,128)S(1)}, f32[33,8,1024]{2,1,0:T(8,128)S(1)}, u32[]{:S(2)}, u32[]{:S(2)}) collective-permute-start(f32[33,8,1024]{2,1,0:T(8,128)S(1)} %get-tuple-element.82), channel_id=1, source_target_pairs={{0,24},{1,97},{2,26},{3,99},{4,28},{5,101},{6,30},{7,103},{8,0},{9... | collective-permute-start | bytes 3244040 | tf_op jit(solution)/shard_map/ppermute | solution.py:53
  24.4 15.5 %collective-permute-start.3 = (f32[33,8,1024]{2,1,0:T(8,128)S(1)}, f32[33,8,1024]{2,1,0:T(8,128)S(1)}, u32[]{:S(2)}, u32[]{:S(2)}) collective-permute-start(f32[33,8,1024]{2,1,0:T(8,128)S(1)} %get-tuple-element.81), channel_id=1, source_target_pairs={{0,8},{1,33},{2,10},{3,35},{4,12},{5,37},{6,14},{7,39},{8,16},{9,4... | collective-permute-start | bytes 3244040 | tf_op jit(solution)/shard_map/ppermute | solution.py:53
  28.0 28.2 %slice-start = ((s8[8388608]{0:T(1024)(128)(4,1)}), s8[4194304]{0:T(1024)(128)(4,1)S(1)}, s32[]{:S(2)}) async-start(s8[8388608]{0:T(1024)(128)(4,1)} %bitcast.38), calls=%async_computation | async-start | bytes 8388608
  35.0 16.5 %collective-permute-start.4 = (f32[33,8,1024]{2,1,0:T(8,128)S(1)}, f32[33,8,1024]{2,1,0:T(8,128)S(1)}, u32[]{:S(2)}, u32[]{:S(2)}) collective-permute-start(f32[33,8,1024]{2,1,0:T(8,128)S(1)} %get-tuple-element.84), channel_id=1, source_target_pairs={{0,8},{1,33},{2,10},{3,35},{4,12},{5,37},{6,14},{7,39},{8,16},{9,4... | collective-permute-start | bytes 3244040 | tf_op jit(solution)/shard_map/ppermute | solution.py:53
  36.0 20.2 %slice-start.1 = ((s8[8388608]{0:T(1024)(128)(4,1)}), s8[4194304]{0:T(1024)(128)(4,1)S(1)}, s32[]{:S(2)}) async-start(s8[8388608]{0:T(1024)(128)(4,1)} %bitcast.38), calls=%async_computation.1 | async-start | bytes 8388608
  36.0 15.4 %collective-permute-start.5 = (f32[33,8,1024]{2,1,0:T(8,128)S(1)}, f32[33,8,1024]{2,1,0:T(8,128)S(1)}, u32[]{:S(2)}, u32[]{:S(2)}) collective-permute-start(f32[33,8,1024]{2,1,0:T(8,128)S(1)} %get-tuple-element.85), channel_id=1, source_target_pairs={{0,24},{1,97},{2,26},{3,99},{4,28},{5,101},{6,30},{7,103},{8,0},{9... | collective-permute-start | bytes 3244040 | tf_op jit(solution)/shard_map/ppermute | solution.py:53
  52.3 22.7 %collective-permute-start.10 = (f32[17,8,1024]{2,1,0:T(8,128)S(1)}, f32[17,8,1024]{2,1,0:T(8,128)S(1)}, u32[]{:S(2)}, u32[]{:S(2)}) collective-permute-start(f32[17,8,1024]{2,1,0:T(8,128)S(1)} %get-tuple-element.96), channel_id=1, source_target_pairs={{0,96},{1,25},{2,98},{3,27},{4,100},{5,29},{6,102},{7,31},{8,104},... | collective-permute-start | bytes 1671176 | tf_op jit(solution)/shard_map/ppermute | solution.py:53
  54.8 20.2 %collective-permute-start.8 = (f32[17,8,1024]{2,1,0:T(8,128)S(1)}, f32[17,8,1024]{2,1,0:T(8,128)S(1)}, u32[]{:S(2)}, u32[]{:S(2)}) collective-permute-start(f32[17,8,1024]{2,1,0:T(8,128)S(1)} %get-tuple-element.94), channel_id=1, source_target_pairs={{0,32},{1,9},{2,34},{3,11},{4,36},{5,13},{6,38},{7,15},{8,40},{9,1... | collective-permute-start | bytes 1671176 | tf_op jit(solution)/shard_map/ppermute | solution.py:53
  54.8 3.2 %copy-start.2 = (s32[1024]{0:T(1024)S(1)}, s32[1024]{0:T(1024)}, u32[]{:S(2)}) copy-start(s32[1024]{0:T(1024)} %param.12) | copy-start | bytes 12292
  54.8 3.2 %copy-start.3 = (s32[1024]{0:T(1024)S(1)}, s32[1024]{0:T(1024)}, u32[]{:S(2)}) copy-start(s32[1024]{0:T(1024)} %param.13) | copy-start | bytes 12292
  54.8 20.2 %collective-permute-start.9 = (f32[17,8,1024]{2,1,0:T(8,128)S(1)}, f32[17,8,1024]{2,1,0:T(8,128)S(1)}, u32[]{:S(2)}, u32[]{:S(2)}) collective-permute-start(f32[17,8,1024]{2,1,0:T(8,128)S(1)} %get-tuple-element.95), channel_id=1, source_target_pairs={{0,64},{1,17},{2,66},{3,19},{4,68},{5,21},{6,70},{7,23},{8,72},{9,... | collective-permute-start | bytes 1671176 | tf_op jit(solution)/shard_map/ppermute | solution.py:53
  56.9 5.7 %collective-permute-start.6 = (f32[32,1024]{1,0:T(8,128)S(1)}, f32[32,1024]{1,0:T(8,128)S(1)}, u32[]{:S(2)}, u32[]{:S(2)}) collective-permute-start(f32[32,1024]{1,0:T(8,128)S(1)} %get-tuple-element.92), channel_id=1, source_target_pairs={{0,8},{1,33},{2,10},{3,35},{4,12},{5,37},{6,14},{7,39},{8,0},{9,41... | collective-permute-start | bytes 393224 | tf_op jit(solution)/shard_map/ppermute | solution.py:53
  62.6 12.3 %collective-permute-start.7 = (f32[32,1024]{1,0:T(8,128)S(1)}, f32[32,1024]{1,0:T(8,128)S(1)}, u32[]{:S(2)}, u32[]{:S(2)}) collective-permute-start(f32[32,1024]{1,0:T(8,128)S(1)} %add.71), channel_id=1, source_target_pairs={{0,24},{1,97},{2,26},{3,99},{4,28},{5,101},{6,30},{7,103},{8,16},{... | collective-permute-start | bytes 393224 | tf_op jit(solution)/shard_map/ppermute | solution.py:53
  75.2 13.9 %collective-permute-start.12 = (f32[8,16,1024]{2,1,0:T(8,128)S(1)}, f32[8,16,1024]{2,1,0:T(8,128)S(1)}, u32[]{:S(2)}, u32[]{:S(2)}) collective-permute-start(f32[8,16,1024]{2,1,0:T(8,128)S(1)} %bitcast.47), channel_id=1, source_target_pairs={{0,64},{1,17},{2,66},{3,19},{4,68},{5,21},{6,70},{7,23},{8,72},{9,... | collective-permute-start | bytes 1572872 | tf_op jit(solution)/shard_map/ppermute | solution.py:53
  77.4 13.8 %collective-permute-start.13 = (f32[8,16,1024]{2,1,0:T(8,128)S(1)}, f32[8,16,1024]{2,1,0:T(8,128)S(1)}, u32[]{:S(2)}, u32[]{:S(2)}) collective-permute-start(f32[8,16,1024]{2,1,0:T(8,128)S(1)} %bitcast.48), channel_id=1, source_target_pairs={{0,32},{1,9},{2,34},{3,11},{4,36},{5,13},{6,38},{7,15},{8,40},{9,1... | collective-permute-start | bytes 1572872 | tf_op jit(solution)/shard_map/ppermute | solution.py:53
  77.7 13.5 %collective-permute-start.11 = (f32[8,16,1024]{2,1,0:T(8,128)S(1)}, f32[8,16,1024]{2,1,0:T(8,128)S(1)}, u32[]{:S(2)}, u32[]{:S(2)}) collective-permute-start(f32[8,16,1024]{2,1,0:T(8,128)S(1)} %bitcast.49), channel_id=1, source_target_pairs={{0,96},{1,25},{2,98},{3,27},{4,100},{5,29},{6,102},{7,31},{8,104},... | collective-permute-start | bytes 1572872 | tf_op jit(solution)/shard_map/ppermute | solution.py:53
  80.9 3.6 %collective-permute-start.14 = (f32[64,128]{1,0:T(8,128)S(1)}, f32[64,128]{1,0:T(8,128)S(1)}, u32[]{:S(2)}, u32[]{:S(2)}) collective-permute-start(f32[64,128]{1,0:T(8,128)S(1)} %get-tuple-element.97), channel_id=1, source_target_pairs={{0,8},{1,33},{2,10},{3,35},{4,12},{5,37},{6,14},{7,39},{8,0},{9,41... | collective-permute-start | bytes 98312 | tf_op jit(solution)/shard_map/ppermute | solution.py:53
  84.5 4.7 %collective-permute-start.15 = (f32[64,128]{1,0:T(8,128)S(1)}, f32[64,128]{1,0:T(8,128)S(1)}, u32[]{:S(2)}, u32[]{:S(2)}) collective-permute-start(f32[64,128]{1,0:T(8,128)S(1)} %add.76), channel_id=1, source_target_pairs={{0,24},{1,97},{2,26},{3,99},{4,28},{5,101},{6,30},{7,103},{8,16},{... | collective-permute-start | bytes 98312 | tf_op jit(solution)/shard_map/ppermute | solution.py:53
  91.3 15.6 %collective-permute-start.16 = (f32[2,8,16,1024]{3,2,1,0:T(8,128)S(1)}, f32[2,8,16,1024]{3,2,1,0:T(8,128)S(1)}, u32[]{:S(2)}, u32[]{:S(2)}) collective-permute-start(f32[2,8,16,1024]{3,2,1,0:T(8,128)S(1)} %pad_maximum_fusion.refs_0_), channel_id=1, source_target_pairs={{0,8},{1,33},{2,10},{3,35},{4,12},{5,37},{6,14},{7,39},{8,16},{9,4... | collective-permute-start | bytes 3145736 | tf_op jit(solution)/shard_map/ppermute | solution.py:53
  91.4 15.5 %collective-permute-start.17 = (f32[2,8,16,1024]{3,2,1,0:T(8,128)S(1)}, f32[2,8,16,1024]{3,2,1,0:T(8,128)S(1)}, u32[]{:S(2)}, u32[]{:S(2)}) collective-permute-start(f32[2,8,16,1024]{3,2,1,0:T(8,128)S(1)} %pad_maximum_fusion.1.refs_1_), channel_id=1, source_target_pairs={{0,24},{1,97},{2,26},{3,99},{4,28},{5,101},{6,30},{7,103},{8,0},{9... | collective-permute-start | bytes 3145736 | tf_op jit(solution)/shard_map/ppermute | solution.py:53
  94.1 3.4 %collective-permute-start.18 = (f32[64,128]{1,0:T(8,128)S(1)}, f32[64,128]{1,0:T(8,128)S(1)}, u32[]{:S(2)}, u32[]{:S(2)}) collective-permute-start(f32[64,128]{1,0:T(8,128)S(1)} %add.77), channel_id=1, source_target_pairs={{0,32},{1,9},{2,34},{3,11},{4,36},{5,13},{6,38},{7,15},{8,40},{9,1... | collective-permute-start | bytes 98312 | tf_op jit(solution)/shard_map/ppermute | solution.py:53
  97.5 4.7 %collective-permute-start.19 = (f32[64,128]{1,0:T(8,128)S(1)}, f32[64,128]{1,0:T(8,128)S(1)}, u32[]{:S(2)}, u32[]{:S(2)}) collective-permute-start(f32[64,128]{1,0:T(8,128)S(1)} %add.78), channel_id=1, source_target_pairs={{0,96},{1,25},{2,98},{3,27},{4,100},{5,29},{6,102},{7,31},{8,104},... | collective-permute-start | bytes 98312 | tf_op jit(solution)/shard_map/ppermute | solution.py:53
  99.2 19.0 %collective-permute-start.24 = (f32[2,8,16,1024]{3,2,1,0:T(8,128)S(1)}, f32[2,8,16,1024]{3,2,1,0:T(8,128)S(1)}, u32[]{:S(2)}, u32[]{:S(2)}) collective-permute-start(f32[2,8,16,1024]{3,2,1,0:T(8,128)S(1)} %pad_maximum_fusion.1.refs_1_), channel_id=1, source_target_pairs={{0,8},{1,33},{2,10},{3,35},{4,12},{5,37},{6,14},{7,39},{8,16},{9,4... | collective-permute-start | bytes 3145736 | tf_op jit(solution)/shard_map/ppermute | solution.py:53
  99.2 19.0 %collective-permute-start.25 = (f32[2,8,16,1024]{3,2,1,0:T(8,128)S(1)}, f32[2,8,16,1024]{3,2,1,0:T(8,128)S(1)}, u32[]{:S(2)}, u32[]{:S(2)}) collective-permute-start(f32[2,8,16,1024]{3,2,1,0:T(8,128)S(1)} %pad_maximum_fusion.refs_0_), channel_id=1, source_target_pairs={{0,24},{1,97},{2,26},{3,99},{4,28},{5,101},{6,30},{7,103},{8,0},{9... | collective-permute-start | bytes 3145736 | tf_op jit(solution)/shard_map/ppermute | solution.py:53
  106.9 22.5 %collective-permute-start.20 = (f32[2,8,16,1024]{3,2,1,0:T(8,128)S(1)}, f32[2,8,16,1024]{3,2,1,0:T(8,128)S(1)}, u32[]{:S(2)}, u32[]{:S(2)}) collective-permute-start(f32[2,8,16,1024]{3,2,1,0:T(8,128)S(1)} %collective-permute-done.16.refs_2_), channel_id=1, source_target_pairs={{0,8},{1,33},{2,10},{3,35},{4,12},{5,37},{6,14},{7,39},{8,16},{9,4... | collective-permute-start | bytes 3145736 | tf_op jit(solution)/shard_map/ppermute | solution.py:53
  106.9 22.5 %collective-permute-start.21 = (f32[2,8,16,1024]{3,2,1,0:T(8,128)S(1)}, f32[2,8,16,1024]{3,2,1,0:T(8,128)S(1)}, u32[]{:S(2)}, u32[]{:S(2)}) collective-permute-start(f32[2,8,16,1024]{3,2,1,0:T(8,128)S(1)} %collective-permute-done.17.refs_5_), channel_id=1, source_target_pairs={{0,24},{1,97},{2,26},{3,99},{4,28},{5,101},{6,30},{7,103},{8,0},{9... | collective-permute-start | bytes 3145736 | tf_op jit(solution)/shard_map/ppermute | solution.py:53
  109.6 3.5 %collective-permute-start.22 = (f32[56,128]{1,0:T(8,128)S(1)}, f32[56,128]{1,0:T(8,128)S(1)}, u32[]{:S(2)}, u32[]{:S(2)}) collective-permute-start(f32[56,128]{1,0:T(8,128)S(1)} %pad_maximum_fusion.2), channel_id=1, source_target_pairs={{0,1},{1,0},{2,3},{3,2},{4,5},{5,4},{6,7},{7,6},{8,9},{9,8},{10,11... | collective-permute-start | bytes 86024 | tf_op jit(solution)/shard_map/ppermute | solution.py:53
  113.1 3.0 %collective-permute-start.23 = (f32[56,128]{1,0:T(8,128)S(1)}, f32[56,128]{1,0:T(8,128)S(1)}, u32[]{:S(2)}, u32[]{:S(2)}) collective-permute-start(f32[56,128]{1,0:T(8,128)S(1)} %fusion.3), channel_id=1, source_target_pairs={{0,2},{1,3},{2,0},{3,1},{4,6},{5,7},{6,4},{7,5},{8,10},{9,11},{10,... | collective-permute-start | bytes 86024 | tf_op jit(solution)/shard_map/ppermute | solution.py:53
  118.1 4.3 %collective-permute-start.26 = (f32[56,128]{1,0:T(8,128)S(1)}, f32[56,128]{1,0:T(8,128)S(1)}, u32[]{:S(2)}, u32[]{:S(2)}) collective-permute-start(f32[56,128]{1,0:T(8,128)S(1)} %add.81), channel_id=1, source_target_pairs={{0,6},{1,7},{2,4},{3,5},{4,2},{5,3},{6,0},{7,1},{8,14},{9,15},{10,... | collective-permute-start | bytes 86024 | tf_op jit(solution)/shard_map/ppermute | solution.py:53
  133.4 5.7 %collective-permute-start.27 = (f32[256,1280]{1,0:T(8,128)S(1)}, f32[256,1280]{1,0:T(8,128)S(1)}, u32[]{:S(2)}, u32[]{:S(2)}) collective-permute-start(f32[256,1280]{1,0:T(8,128)S(1)} %get-tuple-element.110), channel_id=1, source_target_pairs={{0,1},{1,0},{2,3},{3,2},{4,5},{5,4},{6,7},{7,6},{8,9},{9,8},{10,11... | collective-permute-start | bytes 3932168 | tf_op jit(solution)/shard_map/ppermute | solution.py:53
  139.4 21.9 %collective-permute-start.33 = (f32[128,1280]{1,0:T(8,128)S(1)}, f32[128,1280]{1,0:T(8,128)S(1)}, u32[]{:S(2)}, u32[]{:S(2)}) collective-permute-start(f32[128,1280]{1,0:T(8,128)S(1)} %get-tuple-element.154), channel_id=1, source_target_pairs={{0,2},{1,3},{2,4},{3,5},{4,6},{5,7},{6,0},{7,1},{8,10},{9,11},{10,... | collective-permute-start | bytes 1966088 | tf_op jit(solution)/shard_map/ppermute | solution.py:53
  140.8 20.5 %collective-permute-start.34 = (f32[128,1280]{1,0:T(8,128)S(1)}, f32[128,1280]{1,0:T(8,128)S(1)}, u32[]{:S(2)}, u32[]{:S(2)}) collective-permute-start(f32[128,1280]{1,0:T(8,128)S(1)} %get-tuple-element.153), channel_id=1, source_target_pairs={{0,6},{1,7},{2,0},{3,1},{4,2},{5,3},{6,4},{7,5},{8,14},{9,15},{10,... | collective-permute-start | bytes 1966088 | tf_op jit(solution)/shard_map/ppermute | solution.py:53
  152.4 9.7 %collective-permute-start.35 = (f32[256,1280]{1,0:T(8,128)S(1)}, f32[256,1280]{1,0:T(8,128)S(1)}, u32[]{:S(2)}, u32[]{:S(2)}) collective-permute-start(f32[256,1280]{1,0:T(8,128)S(1)} %get-tuple-element.115), channel_id=1, source_target_pairs={{0,1},{1,0},{2,3},{3,2},{4,5},{5,4},{6,7},{7,6},{8,9},{9,8},{10,11... | collective-permute-start | bytes 3932168 | tf_op jit(solution)/shard_map/ppermute | solution.py:53
  152.8 9.3 %collective-permute-start.36 = (f32[256,1280]{1,0:T(8,128)S(1)}, f32[256,1280]{1,0:T(8,128)S(1)}, u32[]{:S(2)}, u32[]{:S(2)}) collective-permute-start(f32[256,1280]{1,0:T(8,128)S(1)} %get-tuple-element.130), channel_id=1, source_target_pairs={{0,1},{1,0},{2,3},{3,2},{4,5},{5,4},{6,7},{7,6},{8,9},{9,8},{10,11... | collective-permute-start | bytes 3932168 | tf_op jit(solution)/shard_map/ppermute | solution.py:53
  153.0 20.2 %collective-permute-start.38 = (f32[256,1280]{1,0:T(8,128)S(1)}, f32[256,1280]{1,0:T(8,128)S(1)}, u32[]{:S(2)}, u32[]{:S(2)}) collective-permute-start(f32[256,1280]{1,0:T(8,128)S(1)} %get-tuple-element.144), channel_id=1, source_target_pairs={{0,1},{1,0},{2,3},{3,2},{4,5},{5,4},{6,7},{7,6},{8,9},{9,8},{10,11... | collective-permute-start | bytes 3932168 | tf_op jit(solution)/shard_map/ppermute | solution.py:53
  163.1 36.3 %collective-permute-start.39 = (f32[256,1280]{1,0:T(8,128)S(1)}, f32[256,1280]{1,0:T(8,128)S(1)}, u32[]{:S(2)}, u32[]{:S(2)}) collective-permute-start(f32[256,1280]{1,0:T(8,128)S(1)} %get-tuple-element.131), channel_id=1, source_target_pairs={{0,2},{1,3},{2,4},{3,5},{4,6},{5,7},{6,0},{7,1},{8,10},{9,11},{10,... | collective-permute-start | bytes 3932168 | tf_op jit(solution)/shard_map/ppermute | solution.py:53
  163.2 36.2 %collective-permute-start.40 = (f32[256,1280]{1,0:T(8,128)S(1)}, f32[256,1280]{1,0:T(8,128)S(1)}, u32[]{:S(2)}, u32[]{:S(2)}) collective-permute-start(f32[256,1280]{1,0:T(8,128)S(1)} %get-tuple-element.146), channel_id=1, source_target_pairs={{0,6},{1,7},{2,0},{3,1},{4,2},{5,3},{6,4},{7,5},{8,14},{9,15},{10,... | collective-permute-start | bytes 3932168 | tf_op jit(solution)/shard_map/ppermute | solution.py:53
  165.8 4.2 %collective-permute-start.32 = (f32[32,1024]{1,0:T(8,128)S(1)}, f32[32,1024]{1,0:T(8,128)S(1)}, u32[]{:S(2)}, u32[]{:S(2)}) collective-permute-start(f32[32,1024]{1,0:T(8,128)S(1)} %add.72), channel_id=1, source_target_pairs={{0,32},{1,9},{2,34},{3,11},{4,36},{5,13},{6,38},{7,15},{8,40},{9,1... | collective-permute-start | bytes 393224 | tf_op jit(solution)/shard_map/ppermute | solution.py:53
  167.2 6.0 %collective-permute-start.28 = (f32[8,1280]{1,0:T(8,128)S(1)}, f32[8,1280]{1,0:T(8,128)S(1)}, u32[]{:S(2)}, u32[]{:S(2)}) collective-permute-start(f32[8,1280]{1,0:T(8,128)S(1)} %get-tuple-element.121), channel_id=1, source_target_pairs={{0,1},{1,0},{2,3},{3,2},{4,5},{5,4},{6,7},{7,6},{8,9},{9,8},{10,11... | collective-permute-start | bytes 122888 | tf_op jit(solution)/shard_map/ppermute | solution.py:53
  170.1 5.6 %collective-permute-start.37 = (f32[32,1024]{1,0:T(8,128)S(1)}, f32[32,1024]{1,0:T(8,128)S(1)}, u32[]{:S(2)}, u32[]{:S(2)}) collective-permute-start(f32[32,1024]{1,0:T(8,128)S(1)} %add.88), channel_id=1, source_target_pairs={{0,96},{1,25},{2,98},{3,27},{4,100},{5,29},{6,102},{7,31},{8,104},... | collective-permute-start | bytes 393224 | tf_op jit(solution)/shard_map/ppermute | solution.py:53
  173.1 25.0 %collective-permute-start.29 = (f32[8,1280]{1,0:T(8,128)S(1)}, f32[8,1280]{1,0:T(8,128)S(1)}, u32[]{:S(2)}, u32[]{:S(2)}) collective-permute-start(f32[8,1280]{1,0:T(8,128)S(1)} %add.84.last), channel_id=1, source_target_pairs={{0,2},{1,3},{2,4},{3,5},{4,6},{5,7},{6,0},{7,1},{8,10},{9,11},{10,... | collective-permute-start | bytes 122888 | tf_op jit(solution)/shard_map/ppermute | solution.py:53
  173.2 24.9 %collective-permute-start.30 = (f32[8,1280]{1,0:T(8,128)S(1)}, f32[8,1280]{1,0:T(8,128)S(1)}, u32[]{:S(2)}, u32[]{:S(2)}) collective-permute-start(f32[8,1280]{1,0:T(8,128)S(1)} %add.84.last), channel_id=1, source_target_pairs={{0,4},{1,5},{2,6},{3,7},{4,0},{5,1},{6,2},{7,3},{8,12},{9,13},{10,... | collective-permute-start | bytes 122888 | tf_op jit(solution)/shard_map/ppermute | solution.py:53
  175.7 22.4 %collective-permute-start.31 = (f32[8,1280]{1,0:T(8,128)S(1)}, f32[8,1280]{1,0:T(8,128)S(1)}, u32[]{:S(2)}, u32[]{:S(2)}) collective-permute-start(f32[8,1280]{1,0:T(8,128)S(1)} %add.84.last), channel_id=1, source_target_pairs={{0,6},{1,7},{2,0},{3,1},{4,2},{5,3},{6,4},{7,5},{8,14},{9,15},{10,... | collective-permute-start | bytes 122888 | tf_op jit(solution)/shard_map/ppermute | solution.py:53

commit v4 on v3

--- a/solution.py
+++ b/solution.py
@@ -810,20 +810,22 @@
     last, up_b, down_b, own_b = back_part(
         [(1, 0), (-1, 0), (0, 0)], grad, up_a, last=[sums_a, sums_b, sums_c, scalars]
     )
-    last = last + swap(last, 0, 0, 0, 1)
-    above, below = lift_call(up_b, down_b, far_up, far_down)
+    last_got = swap(last, 0, 0, 0, 1)
+    types = types + swap_across(after(types, up_a), 1)
+    above, below = lift_call(up_b, down_b, *after((far_up, far_down), types))
     above, below = join_call(above, below, up_got, down_got)
     near_up, near_down = up(above, 1), up(below, -1)
-    types = types + swap_across(after(types, up_b), 1)
-    types = types + swap_across(after(types, above), 3)
+    types_got = swap_across(after(types, above), 3)
     own = own_b + own_got
 
     column = jnp.sum(column_a + column_b + column_c, axis=0) * share + spot_coef[32] * mass
     map_rows = stacked([spot_coef[32], column])
     map_args = (expr, grad.reshape(2, genes, spots), masses, keep2, map_rows, all_cells * genes)
+    grad_map = map_call(*map_args)
+    types_got, last_got = after((types_got, last_got), grad_map)
+    types = types + types_got
+    last = after(last + last_got, own)
     got = [up(last, step) for step in (1, 2, 3)]
-    grad_map = map_call(*after(map_args[:-1], last, types), map_args[-1])
-    got = after(tuple(got), grad_map)
     grad_weighted = after(own, grad_map) + near_up + near_down
     grad_expr = grad_weighted * (keep * (genes * all_spots))[None, :]
 

time: 202 us -> 201 us (level)
  waiting for transfers between devices: 52.7 us -> 47.6 us
  starting transfers between devices: 54.3 us -> 58.8 us
    ppermute x41, waiting for transfers between devices: 52.7 us -> 47.6 us  [send(): return lax.ppermute(array, ('cells', 'spots'), route(target))]
    ppermute x41, starting transfers between devices: 54.3 us -> 58.8 us  [send(): return lax.ppermute(array, ('cells', 'spots'), route(target))]
where the time goes in v4:
time: 201 us; the launch traced here: 200 us
  Pallas kernels  88.3 us (44%)
  starting transfers between devices  58.8 us (29%)
  waiting for transfers between devices  47.6 us (24%)
  other arithmetic  3.85 us (2%)
    ppermute x41, starting transfers between devices, send(): return lax.ppermute(array, ('cells', 'spots'), route(target))  58.8 us
    ppermute x41, waiting for transfers between devices, send(): return lax.ppermute(array, ('cells', 'spots'), route(target))  47.6 us
    pallas_call x4, Pallas kernels, back_call(): pl.pallas_call(functools.partial(back_kernel, parts=parts, first=len(firs...  22.5 us
    pallas_call x3, Pallas kernels, pred_call(): pl.pallas_call(functools.partial(pred_kernel, cuts=cuts), grid_spec=pltpu...  21.9 us
    pallas_call x1, Pallas kernels, map_call(): pl.pallas_call(functools.partial(map_kernel, scale=scale), grid=(cells //...  21.3 us
    pallas_call x1, Pallas kernels, expo_call(): pl.pallas_call(expo_kernel, grid_spec=pltpu.PrefetchScalarGridSpec(num_sc...  9.85 us
    pallas_call x3, Pallas kernels, grad_call(): pl.pallas_call(functools.partial(grad_kernel, count=count, lane=lane, chi...  7.63 us
  transfers between devices with their start and end apart: 41, of which 19 were waited for; matrix products, arithmetic and copies ran while one was open for 1% of the time, Pallas kernels for 37%

profile of v4, /device:TPU:1, one launch (start us, length us, event | category | flops | bytes accessed | tf_op | source)
XLA Modules:
  0.0 200.2 jit_solution(3069655058554706836)
XLA Ops:
  0.7 9.9 %expo.1 = (bf16[2,1280,1024]{2,1,0:T(8,128)(2,1)S(1)}, f32[32,1024]{1,0:T(8,128)S(1)}, f32[8,1024]{1,0:T(8,128)S(1)}, f32[33,8,1024]{2,1,0:T(8,128)S(1)}, f32[33,8,1024]{2,1,0:T(8,128)S(1)}) custom-call(s32[4]{0:T(128)S(1)} %pad_add_fusion.ids, f32[1280,1024]{1,0:T(8,128)} %logits.1, s32[10,128]{1,0:T(8,128)} %bitcast.66, f32[10,128]{1,0:T(8,128)} %bitcast.67, ...), custom_call_target="tpu_custom_call" | custom-call | bytes 1310720 | tf_op jit(solution)/shard_map/expo/pallas_call | solution.py:176
  10.6 2.5 %collective-permute-start = (f32[33,8,1024]{2,1,0:T(8,128)S(1)}, f32[33,8,1024]{2,1,0:T(8,128)S(1)}, u32[]{:S(2)}, u32[]{:S(2)}) collective-permute-start(f32[33,8,1024]{2,1,0:T(8,128)S(1)} %get-tuple-element.73), channel_id=1, source_target_pairs={{0,8},{1,33},{2,10},{3,35},{4,12},{5,37},{6,14},{7,39},{8,16},{9,4... | collective-permute-start | bytes 3244040 | tf_op jit(solution)/shard_map/ppermute | solution.py:53
  13.1 2.3 %collective-permute-start.1 = (f32[33,8,1024]{2,1,0:T(8,128)S(1)}, f32[33,8,1024]{2,1,0:T(8,128)S(1)}, u32[]{:S(2)}, u32[]{:S(2)}) collective-permute-start(f32[33,8,1024]{2,1,0:T(8,128)S(1)} %get-tuple-element.74), channel_id=1, source_target_pairs={{0,24},{1,97},{2,26},{3,99},{4,28},{5,101},{6,30},{7,103},{8,0},{9... | collective-permute-start | bytes 3244040 | tf_op jit(solution)/shard_map/ppermute | solution.py:53
  15.5 7.5 %pred_.3 = (f32[33,8,1024]{2,1,0:T(8,128)S(1)}, f32[33,8,1024]{2,1,0:T(8,128)S(1)}) custom-call(s32[4]{0:T(128)S(1)} %pad_add_fusion.ids, f32[8,16,16,1280]{3,2,1,0:T(8,128)} %bitcast.57, f32[8,16,16,1280]{3,2,1,0:T(8,128)} %bitcast.58, f32[1,1280]{1,0:T(1,128)S(1)} %reshape.94.keep, bf16[2,1280,1024]{2,1,0:T(8,128)(2,1)S(1)} %get-tuple-element.76.masses, ...), custom_call_target="tpu_custom_call" | custom-call | flops 503316480 | bytes 1245184 | tf_op jit(solution)/shard_map/pred/pallas_call | solution.py:249
  22.9 1.5 collective-permute-start.2
  24.5 3.6 %collective-permute-done.refs_0_ = f32[33,8,1024]{2,1,0:T(8,128)S(1)} collective-permute-done((f32[33,8,1024]{2,1,0:T(8,128)S(1)}, f32[33,8,1024]{2,1,0:T(8,128)S(1)}, u32[]{:S(2)}, u32[]{:S(2)}) %collective-permute-start) | collective-permute-done | bytes 1081376 | tf_op jit(solution)/shard_map/ppermute | solution.py:53
  28.0 6.9 %pred_.4 = (f32[33,8,1024]{2,1,0:T(8,128)S(1)}, f32[33,8,1024]{2,1,0:T(8,128)S(1)}) custom-call(s32[4]{0:T(128)S(1)} %pad_add_fusion.ids, f32[8,16,16,1280]{3,2,1,0:T(8,128)} %bitcast.59, f32[8,16,16,1280]{3,2,1,0:T(8,128)} %bitcast.60, f32[1,1280]{1,0:T(1,128)S(1)} %reshape.94.keep, bf16[2,1280,1024]{2,1,0:T(8,128)(2,1)S(1)} %get-tuple-element.76.masses, ...), custom_call_target="tpu_custom_call" | custom-call | flops 503316480 | bytes 1245184 | tf_op jit(solution)/shard_map/pred/pallas_call | solution.py:249
  36.0 2.0 collective-permute-start.5
  39.9 7.6 %pred_.5 = (f32[33,8,1024]{2,1,0:T(8,128)S(1)}, f32[33,8,1024]{2,1,0:T(8,128)S(1)}) custom-call(s32[4]{0:T(128)S(1)} %pad_add_fusion.ids, f32[8,16,16,1280]{3,2,1,0:T(8,128)} %bitcast.61, f32[8,16,16,1280]{3,2,1,0:T(8,128)} %bitcast.62, f32[1,1280]{1,0:T(1,128)S(1)} %reshape.94.keep, bf16[2,1280,1024]{2,1,0:T(8,128)(2,1)S(1)} %get-tuple-element.76.masses, ...), custom_call_target="tpu_custom_call" | custom-call | flops 503316480 | bytes 1245184 | tf_op jit(solution)/shard_map/pred/pallas_call | solution.py:249
  47.5 4.0 %collective-permute-done.4.got0 = f32[33,8,1024]{2,1,0:T(8,128)S(1)} collective-permute-done((f32[33,8,1024]{2,1,0:T(8,128)S(1)}, f32[33,8,1024]{2,1,0:T(8,128)S(1)}, u32[]{:S(2)}, u32[]{:S(2)}) %collective-permute-start.4) | collective-permute-done | bytes 1081376 | tf_op jit(solution)/shard_map/ppermute | solution.py:53
  52.3 2.5 %collective-permute-start.10 = (f32[17,8,1024]{2,1,0:T(8,128)S(1)}, f32[17,8,1024]{2,1,0:T(8,128)S(1)}, u32[]{:S(2)}, u32[]{:S(2)}) collective-permute-start(f32[17,8,1024]{2,1,0:T(8,128)S(1)} %get-tuple-element.93), channel_id=1, source_target_pairs={{0,96},{1,25},{2,98},{3,27},{4,100},{5,29},{6,102},{7,31},{8,104},... | collective-permute-start | bytes 1671176 | tf_op jit(solution)/shard_map/ppermute | solution.py:53
  57.5 4.5 %collective-permute-done.6 = f32[32,1024]{1,0:T(8,128)S(1)} collective-permute-done((f32[32,1024]{1,0:T(8,128)S(1)}, f32[32,1024]{1,0:T(8,128)S(1)}, u32[]{:S(2)}, u32[]{:S(2)}) %collective-permute-start.6) | collective-permute-done | bytes 131104 | tf_op jit(solution)/shard_map/ppermute | solution.py:53
  62.0 2.0 collective-permute-start.7
  64.0 7.7 %collective-permute-done.7 = f32[32,1024]{1,0:T(8,128)S(1)} collective-permute-done((f32[32,1024]{1,0:T(8,128)S(1)}, f32[32,1024]{1,0:T(8,128)S(1)}, u32[]{:S(2)}, u32[]{:S(2)}) %collective-permute-start.7) | collective-permute-done | bytes 131104 | tf_op jit(solution)/shard_map/ppermute | solution.py:53
  72.0 2.4 %collective-permute-start.11 = (f32[8,16,1024]{2,1,0:T(8,128)S(1)}, f32[8,16,1024]{2,1,0:T(8,128)S(1)}, u32[]{:S(2)}, u32[]{:S(2)}) collective-permute-start(f32[8,16,1024]{2,1,0:T(8,128)S(1)} %bitcast.47), channel_id=1, source_target_pairs={{0,96},{1,25},{2,98},{3,27},{4,100},{5,29},{6,102},{7,31},{8,104},... | collective-permute-start | bytes 1572872 | tf_op jit(solution)/shard_map/ppermute | solution.py:53
  74.4 1.4 collective-permute-start.12
  77.7 2.4 %collective-permute-done.14 = f32[64,128]{1,0:T(8,128)S(1)} collective-permute-done((f32[64,128]{1,0:T(8,128)S(1)}, f32[64,128]{1,0:T(8,128)S(1)}, u32[]{:S(2)}, u32[]{:S(2)}) %collective-permute-start.14) | collective-permute-done | bytes 32800 | tf_op jit(solution)/shard_map/ppermute | solution.py:53
  80.1 3.3 %collective-permute-start.15 = (f32[64,128]{1,0:T(8,128)S(1)}, f32[64,128]{1,0:T(8,128)S(1)}, u32[]{:S(2)}, u32[]{:S(2)}) collective-permute-start(f32[64,128]{1,0:T(8,128)S(1)} %add.76), channel_id=1, source_target_pairs={{0,24},{1,97},{2,26},{3,99},{4,28},{5,101},{6,30},{7,103},{8,16},{... | collective-permute-start | bytes 98312 | tf_op jit(solution)/shard_map/ppermute | solution.py:53
  83.4 2.0 %collective-permute-done.15 = f32[64,128]{1,0:T(8,128)S(1)} collective-permute-done((f32[64,128]{1,0:T(8,128)S(1)}, f32[64,128]{1,0:T(8,128)S(1)}, u32[]{:S(2)}, u32[]{:S(2)}) %collective-permute-start.15) | collective-permute-done | bytes 32800 | tf_op jit(solution)/shard_map/ppermute | solution.py:53
  86.2 3.7 %collective-permute-done.13 = f32[8,16,1024]{2,1,0:T(8,128)S(1)} collective-permute-done((f32[8,16,1024]{2,1,0:T(8,128)S(1)}, f32[8,16,1024]{2,1,0:T(8,128)S(1)}, u32[]{:S(2)}, u32[]{:S(2)}) %collective-permute-start.13) | collective-permute-done | bytes 524320 | tf_op jit(solution)/shard_map/ppermute | solution.py:53
  90.1 3.4 %collective-permute-start.17 = (f32[2,8,16,1024]{3,2,1,0:T(8,128)S(1)}, f32[2,8,16,1024]{3,2,1,0:T(8,128)S(1)}, u32[]{:S(2)}, u32[]{:S(2)}) collective-permute-start(f32[2,8,16,1024]{3,2,1,0:T(8,128)S(1)} %pad_maximum_fusion.1.refs_1_), channel_id=1, source_target_pairs={{0,24},{1,97},{2,26},{3,99},{4,28},{5,101},{6,30},{7,103},{8,0},{9... | collective-permute-start | bytes 3145736 | tf_op jit(solution)/shard_map/ppermute | solution.py:53
  93.5 2.3 %collective-permute-start.18 = (f32[64,128]{1,0:T(8,128)S(1)}, f32[64,128]{1,0:T(8,128)S(1)}, u32[]{:S(2)}, u32[]{:S(2)}) collective-permute-start(f32[64,128]{1,0:T(8,128)S(1)} %add.77), channel_id=1, source_target_pairs={{0,32},{1,9},{2,34},{3,11},{4,36},{5,13},{6,38},{7,15},{8,40},{9,1... | collective-permute-start | bytes 98312 | tf_op jit(solution)/shard_map/ppermute | solution.py:53
  95.8 1.6 collective-permute-done.18
  97.5 2.7 %collective-permute-start.25 = (f32[2,8,16,1024]{3,2,1,0:T(8,128)S(1)}, f32[2,8,16,1024]{3,2,1,0:T(8,128)S(1)}, u32[]{:S(2)}, u32[]{:S(2)}) collective-permute-start(f32[2,8,16,1024]{3,2,1,0:T(8,128)S(1)} %pad_maximum_fusion.refs_0_), channel_id=1, source_target_pairs={{0,24},{1,97},{2,26},{3,99},{4,28},{5,101},{6,30},{7,103},{8,0},{9... | collective-permute-start | bytes 3145736 | tf_op jit(solution)/shard_map/ppermute | solution.py:53
  100.2 1.9 collective-permute-done.19
  102.1 4.1 %collective-permute-done.16.refs_2_ = f32[2,8,16,1024]{3,2,1,0:T(8,128)S(1)} collective-permute-done((f32[2,8,16,1024]{3,2,1,0:T(8,128)S(1)}, f32[2,8,16,1024]{3,2,1,0:T(8,128)S(1)}, u32[]{:S(2)}, u32[]{:S(2)}) %collective-permute-start.16) | collective-permute-done | bytes 1048608 | tf_op jit(solution)/shard_map/ppermute | solution.py:53
  107.1 1.9 collective-permute-start.21
  109.0 3.5 %collective-permute-start.22 = (f32[56,128]{1,0:T(8,128)S(1)}, f32[56,128]{1,0:T(8,128)S(1)}, u32[]{:S(2)}, u32[]{:S(2)}) collective-permute-start(f32[56,128]{1,0:T(8,128)S(1)} %pad_maximum_fusion.2), channel_id=1, source_target_pairs={{0,1},{1,0},{2,3},{3,2},{4,5},{5,4},{6,7},{7,6},{8,9},{9,8},{10,11... | collective-permute-start | bytes 86024 | tf_op jit(solution)/shard_map/ppermute | solution.py:53
  113.3 1.3 collective-permute-start.23
  114.6 1.7 collective-permute-done.23
  117.5 2.7 %collective-permute-start.26 = (f32[56,128]{1,0:T(8,128)S(1)}, f32[56,128]{1,0:T(8,128)S(1)}, u32[]{:S(2)}, u32[]{:S(2)}) collective-permute-start(f32[56,128]{1,0:T(8,128)S(1)} %add.81), channel_id=1, source_target_pairs={{0,6},{1,7},{2,4},{3,5},{4,2},{5,3},{6,0},{7,1},{8,14},{9,15},{10,... | collective-permute-start | bytes 86024 | tf_op jit(solution)/shard_map/ppermute | solution.py:53
  120.2 1.6 collective-permute-done.26
  122.6 4.7 %grad.3 = (bf16[2,8,256,1024]{3,2,1,0:T(8,128)(2,1)S(1)}, f32[8,1024]{1,0:T(8,128)S(1)}) custom-call(s32[4]{0:T(128)S(1)} %pad_add_fusion.ids, f32[2,8,16,1024]{3,2,1,0:T(8,128)S(1)} %pad_maximum_fusion.refs_0_, f32[2,8,16,1024]{3,2,1,0:T(8,128)S(1)} %pad_maximum_fusion.1.refs_1_, f32[2,8,16,1024]{3,2,1,0:T(8,128)S(1)} %collective-permute-done.16.refs_2_, ...), custom_call_target="tpu_custom_call" | custom-call | tf_op jit(solution)/shard_map/grad/pallas_call | solution.py:474
  127.4 1.4 collective-permute-done.20.refs_0_
  129.7 3.1 %back.4 = (f32[8,1280]{1,0:T(8,128)S(1)}, f32[256,1280]{1,0:T(8,128)S(1)}) custom-call(s32[4]{0:T(128)S(1)} %pad_add_fusion.ids, bf16[2,8,256,1024]{3,2,1,0:T(8,128)(2,1)S(1)} %get-tuple-element.106.grad.refs_5_, bf16[2,1280,1024]{2,1,0:T(8,128)(2,1)S(1)} %get-tuple-element.76.masses, f32[2048,1280]{1,0:T(8,128)} %expr.9, ...), custom_call_target="tpu_custom_call" | custom-call | tf_op jit(solution)/shard_map/back/pallas_call | solution.py:550
  132.8 3.1 %collective-permute-start.27 = (f32[256,1280]{1,0:T(8,128)S(1)}, f32[256,1280]{1,0:T(8,128)S(1)}, u32[]{:S(2)}, u32[]{:S(2)}) collective-permute-start(f32[256,1280]{1,0:T(8,128)S(1)} %get-tuple-element.107), channel_id=1, source_target_pairs={{0,1},{1,0},{2,3},{3,2},{4,5},{5,4},{6,7},{7,6},{8,9},{9,8},{10,11... | collective-permute-start | bytes 3932168 | tf_op jit(solution)/shard_map/ppermute | solution.py:53
  135.8 3.6 %back.5 = (f32[8,1280]{1,0:T(8,128)S(1)}, f32[256,1280]{1,0:T(8,128)S(1)}) custom-call(s32[4]{0:T(128)S(1)} %pad_add_fusion.ids, bf16[2,8,256,1024]{3,2,1,0:T(8,128)(2,1)S(1)} %get-tuple-element.106.grad.refs_5_, bf16[2,1280,1024]{2,1,0:T(8,128)(2,1)S(1)} %get-tuple-element.76.masses, f32[2048,1280]{1,0:T(8,128)} %expr.9), custom_call_target="tpu_custom_call" | custom-call | tf_op jit(solution)/shard_map/back/pallas_call | solution.py:550
  139.7 1.4 collective-permute-start.29
  141.1 1.7 collective-permute-start.30
  142.8 1.9 grad.5
  144.8 8.0 %back.6 = (f32[8,1280]{1,0:T(8,128)S(1)}, f32[256,1280]{1,0:T(8,128)S(1)}, f32[256,1280]{1,0:T(8,128)S(1)}, f32[256,1280]{1,0:T(8,128)S(1)}) custom-call(s32[4]{0:T(128)S(1)} %pad_add_fusion.ids, bf16[2,8,256,1024]{3,2,1,0:T(8,128)(2,1)S(1)} %get-tuple-element.111.grad, bf16[2,1280,1024]{2,1,0:T(8,128)(2,1)S(1)} %get-tuple-element.76.masses, f32[2048,1280]{1,0:T(8,128)} %expr.9), custom_call_target="tpu_custom_call" | custom-call | tf_op jit(solution)/shard_map/back/pallas_call | solution.py:550
  154.2 8.0 %back.7 = (f32[8,1280]{1,0:T(8,128)S(1)}, f32[256,1280]{1,0:T(8,128)S(1)}, f32[256,1280]{1,0:T(8,128)S(1)}, f32[256,1280]{1,0:T(8,128)S(1)}) custom-call(s32[4]{0:T(128)S(1)} %pad_add_fusion.ids, bf16[2,8,256,1024]{3,2,1,0:T(8,128)(2,1)S(1)} %get-tuple-element.111.grad, bf16[2,1280,1024]{2,1,0:T(8,128)(2,1)S(1)} %get-tuple-element.76.masses, ...), custom_call_target="tpu_custom_call" | custom-call | tf_op jit(solution)/shard_map/back/pallas_call | solution.py:550
  164.1 1.4 collective-permute-start.40
  166.8 1.9 collective-permute-start.33
  168.8 21.3 %grad_map.1 = f32[1280,1024]{1,0:T(8,128)} custom-call(f32[2048,1280]{1,0:T(8,128)} %expr.9, bf16[2,2048,1024]{2,1,0:T(8,128)(2,1)S(1)} %bitcast.46, bf16[2,1280,1024]{2,1,0:T(8,128)(2,1)S(1)} %get-tuple-element.76.masses, f32[10,128]{1,0:T(8,128)S(1)} %bitcast.52, f32[8,1024]{1,0:T(8,128)S(1)} %select_select_fusion.spot), custom_call_target="tpu_custom_call" | custom-call | tf_op jit(solution)/shard_map/grad_map/pallas_call | solution.py:656
  190.4 3.7 %collective-permute-start.37 = (f32[8,1280]{1,0:T(8,128)S(1)}, f32[8,1280]{1,0:T(8,128)S(1)}, u32[]{:S(2)}, u32[]{:S(2)}) collective-permute-start(f32[8,1280]{1,0:T(8,128)S(1)} %add.88.last), channel_id=1, source_target_pairs={{0,4},{1,5},{2,6},{3,7},{4,0},{5,1},{6,2},{7,3},{8,12},{9,13},{10,... | collective-permute-start | bytes 122888 | tf_op jit(solution)/shard_map/ppermute | solution.py:53
  194.8 2.8 %collective-permute-done.36.got1 = f32[8,1280]{1,0:T(8,128)S(1)} collective-permute-done((f32[8,1280]{1,0:T(8,128)S(1)}, f32[8,1280]{1,0:T(8,128)S(1)}, u32[]{:S(2)}, u32[]{:S(2)}) %collective-permute-start.36) | collective-permute-done | bytes 40992 | tf_op jit(solution)/shard_map/ppermute | solution.py:53
  198.9 1.3 add_multiply_fusion
  (103 shorter events, 21.8 us)
Async XLA Ops:
  0.7 14.7 %copy-start = (s32[1280]{0:T(1024)S(1)}, s32[1280]{0:T(1024)}, u32[]{:S(2)}) copy-start(s32[1280]{0:T(1024)} %param.11) | copy-start | bytes 15364
  0.7 14.7 %copy-start.1 = (f32[1280]{0:T(1024)S(1)}, f32[1280]{0:T(1024)}, u32[]{:S(2)}) copy-start(f32[1280]{0:T(1024)} %param.8) | copy-start | bytes 15364
  10.6 17.5 %collective-permute-start = (f32[33,8,1024]{2,1,0:T(8,128)S(1)}, f32[33,8,1024]{2,1,0:T(8,128)S(1)}, u32[]{:S(2)}, u32[]{:S(2)}) collective-permute-start(f32[33,8,1024]{2,1,0:T(8,128)S(1)} %get-tuple-element.73), channel_id=1, source_target_pairs={{0,8},{1,33},{2,10},{3,35},{4,12},{5,37},{6,14},{7,39},{8,16},{9,4... | collective-permute-start | bytes 3244040 | tf_op jit(solution)/shard_map/ppermute | solution.py:53
  13.1 14.9 %collective-permute-start.1 = (f32[33,8,1024]{2,1,0:T(8,128)S(1)}, f32[33,8,1024]{2,1,0:T(8,128)S(1)}, u32[]{:S(2)}, u32[]{:S(2)}) collective-permute-start(f32[33,8,1024]{2,1,0:T(8,128)S(1)} %get-tuple-element.74), channel_id=1, source_target_pairs={{0,24},{1,97},{2,26},{3,99},{4,28},{5,101},{6,30},{7,103},{8,0},{9... | collective-permute-start | bytes 3244040 | tf_op jit(solution)/shard_map/ppermute | solution.py:53
  22.9 16.2 %collective-permute-start.2 = (f32[33,8,1024]{2,1,0:T(8,128)S(1)}, f32[33,8,1024]{2,1,0:T(8,128)S(1)}, u32[]{:S(2)}, u32[]{:S(2)}) collective-permute-start(f32[33,8,1024]{2,1,0:T(8,128)S(1)} %get-tuple-element.79), channel_id=1, source_target_pairs={{0,24},{1,97},{2,26},{3,99},{4,28},{5,101},{6,30},{7,103},{8,0},{9... | collective-permute-start | bytes 3244040 | tf_op jit(solution)/shard_map/ppermute | solution.py:53
  24.4 15.5 %collective-permute-start.3 = (f32[33,8,1024]{2,1,0:T(8,128)S(1)}, f32[33,8,1024]{2,1,0:T(8,128)S(1)}, u32[]{:S(2)}, u32[]{:S(2)}) collective-permute-start(f32[33,8,1024]{2,1,0:T(8,128)S(1)} %get-tuple-element.78), channel_id=1, source_target_pairs={{0,8},{1,33},{2,10},{3,35},{4,12},{5,37},{6,14},{7,39},{8,16},{9,4... | collective-permute-start | bytes 3244040 | tf_op jit(solution)/shard_map/ppermute | solution.py:53
  28.0 27.6 %slice-start = ((s8[8388608]{0:T(1024)(128)(4,1)}), s8[4194304]{0:T(1024)(128)(4,1)S(1)}, s32[]{:S(2)}) async-start(s8[8388608]{0:T(1024)(128)(4,1)} %bitcast.38), calls=%async_computation | async-start | bytes 8388608
  35.0 16.5 %collective-permute-start.4 = (f32[33,8,1024]{2,1,0:T(8,128)S(1)}, f32[33,8,1024]{2,1,0:T(8,128)S(1)}, u32[]{:S(2)}, u32[]{:S(2)}) collective-permute-start(f32[33,8,1024]{2,1,0:T(8,128)S(1)} %get-tuple-element.81), channel_id=1, source_target_pairs={{0,8},{1,33},{2,10},{3,35},{4,12},{5,37},{6,14},{7,39},{8,16},{9,4... | collective-permute-start | bytes 3244040 | tf_op jit(solution)/shard_map/ppermute | solution.py:53
  36.0 19.6 %slice-start.1 = ((s8[8388608]{0:T(1024)(128)(4,1)}), s8[4194304]{0:T(1024)(128)(4,1)S(1)}, s32[]{:S(2)}) async-start(s8[8388608]{0:T(1024)(128)(4,1)} %bitcast.38), calls=%async_computation.1 | async-start | bytes 8388608
  36.0 15.5 %collective-permute-start.5 = (f32[33,8,1024]{2,1,0:T(8,128)S(1)}, f32[33,8,1024]{2,1,0:T(8,128)S(1)}, u32[]{:S(2)}, u32[]{:S(2)}) collective-permute-start(f32[33,8,1024]{2,1,0:T(8,128)S(1)} %get-tuple-element.82), channel_id=1, source_target_pairs={{0,24},{1,97},{2,26},{3,99},{4,28},{5,101},{6,30},{7,103},{8,0},{9... | collective-permute-start | bytes 3244040 | tf_op jit(solution)/shard_map/ppermute | solution.py:53
  52.3 19.5 %collective-permute-start.10 = (f32[17,8,1024]{2,1,0:T(8,128)S(1)}, f32[17,8,1024]{2,1,0:T(8,128)S(1)}, u32[]{:S(2)}, u32[]{:S(2)}) collective-permute-start(f32[17,8,1024]{2,1,0:T(8,128)S(1)} %get-tuple-element.93), channel_id=1, source_target_pairs={{0,96},{1,25},{2,98},{3,27},{4,100},{5,29},{6,102},{7,31},{8,104},... | collective-permute-start | bytes 1671176 | tf_op jit(solution)/shard_map/ppermute | solution.py:53
  54.8 16.9 %collective-permute-start.9 = (f32[17,8,1024]{2,1,0:T(8,128)S(1)}, f32[17,8,1024]{2,1,0:T(8,128)S(1)}, u32[]{:S(2)}, u32[]{:S(2)}) collective-permute-start(f32[17,8,1024]{2,1,0:T(8,128)S(1)} %get-tuple-element.92), channel_id=1, source_target_pairs={{0,64},{1,17},{2,66},{3,19},{4,68},{5,21},{6,70},{7,23},{8,72},{9,... | collective-permute-start | bytes 1671176 | tf_op jit(solution)/shard_map/ppermute | solution.py:53
  55.1 2.4 %copy-start.2 = (s32[1024]{0:T(1024)S(1)}, s32[1024]{0:T(1024)}, u32[]{:S(2)}) copy-start(s32[1024]{0:T(1024)} %param.13) | copy-start | bytes 12292
  55.1 2.4 %copy-start.3 = (s32[1024]{0:T(1024)S(1)}, s32[1024]{0:T(1024)}, u32[]{:S(2)}) copy-start(s32[1024]{0:T(1024)} %param.12) | copy-start | bytes 12292
  55.1 16.7 %collective-permute-start.8 = (f32[17,8,1024]{2,1,0:T(8,128)S(1)}, f32[17,8,1024]{2,1,0:T(8,128)S(1)}, u32[]{:S(2)}, u32[]{:S(2)}) collective-permute-start(f32[17,8,1024]{2,1,0:T(8,128)S(1)} %get-tuple-element.91), channel_id=1, source_target_pairs={{0,32},{1,9},{2,34},{3,11},{4,36},{5,13},{6,38},{7,15},{8,40},{9,1... | collective-permute-start | bytes 1671176 | tf_op jit(solution)/shard_map/ppermute | solution.py:53
  56.3 5.7 %collective-permute-start.6 = (f32[32,1024]{1,0:T(8,128)S(1)}, f32[32,1024]{1,0:T(8,128)S(1)}, u32[]{:S(2)}, u32[]{:S(2)}) collective-permute-start(f32[32,1024]{1,0:T(8,128)S(1)} %get-tuple-element.89), channel_id=1, source_target_pairs={{0,8},{1,33},{2,10},{3,35},{4,12},{5,37},{6,14},{7,39},{8,0},{9,41... | collective-permute-start | bytes 393224 | tf_op jit(solution)/shard_map/ppermute | solution.py:53
  62.0 9.7 %collective-permute-start.7 = (f32[32,1024]{1,0:T(8,128)S(1)}, f32[32,1024]{1,0:T(8,128)S(1)}, u32[]{:S(2)}, u32[]{:S(2)}) collective-permute-start(f32[32,1024]{1,0:T(8,128)S(1)} %add.71), channel_id=1, source_target_pairs={{0,24},{1,97},{2,26},{3,99},{4,28},{5,101},{6,30},{7,103},{8,16},{... | collective-permute-start | bytes 393224 | tf_op jit(solution)/shard_map/ppermute | solution.py:53
  72.0 14.1 %collective-permute-start.11 = (f32[8,16,1024]{2,1,0:T(8,128)S(1)}, f32[8,16,1024]{2,1,0:T(8,128)S(1)}, u32[]{:S(2)}, u32[]{:S(2)}) collective-permute-start(f32[8,16,1024]{2,1,0:T(8,128)S(1)} %bitcast.47), channel_id=1, source_target_pairs={{0,96},{1,25},{2,98},{3,27},{4,100},{5,29},{6,102},{7,31},{8,104},... | collective-permute-start | bytes 1572872 | tf_op jit(solution)/shard_map/ppermute | solution.py:53
  74.4 15.5 %collective-permute-start.13 = (f32[8,16,1024]{2,1,0:T(8,128)S(1)}, f32[8,16,1024]{2,1,0:T(8,128)S(1)}, u32[]{:S(2)}, u32[]{:S(2)}) collective-permute-start(f32[8,16,1024]{2,1,0:T(8,128)S(1)} %bitcast.48), channel_id=1, source_target_pairs={{0,32},{1,9},{2,34},{3,11},{4,36},{5,13},{6,38},{7,15},{8,40},{9,1... | collective-permute-start | bytes 1572872 | tf_op jit(solution)/shard_map/ppermute | solution.py:53
  74.4 15.5 %collective-permute-start.12 = (f32[8,16,1024]{2,1,0:T(8,128)S(1)}, f32[8,16,1024]{2,1,0:T(8,128)S(1)}, u32[]{:S(2)}, u32[]{:S(2)}) collective-permute-start(f32[8,16,1024]{2,1,0:T(8,128)S(1)} %bitcast.49), channel_id=1, source_target_pairs={{0,64},{1,17},{2,66},{3,19},{4,68},{5,21},{6,70},{7,23},{8,72},{9,... | collective-permute-start | bytes 1572872 | tf_op jit(solution)/shard_map/ppermute | solution.py:53
  76.7 3.4 %collective-permute-start.14 = (f32[64,128]{1,0:T(8,128)S(1)}, f32[64,128]{1,0:T(8,128)S(1)}, u32[]{:S(2)}, u32[]{:S(2)}) collective-permute-start(f32[64,128]{1,0:T(8,128)S(1)} %get-tuple-element.94), channel_id=1, source_target_pairs={{0,8},{1,33},{2,10},{3,35},{4,12},{5,37},{6,14},{7,39},{8,0},{9,41... | collective-permute-start | bytes 98312 | tf_op jit(solution)/shard_map/ppermute | solution.py:53
  80.1 5.3 %collective-permute-start.15 = (f32[64,128]{1,0:T(8,128)S(1)}, f32[64,128]{1,0:T(8,128)S(1)}, u32[]{:S(2)}, u32[]{:S(2)}) collective-permute-start(f32[64,128]{1,0:T(8,128)S(1)} %add.76), channel_id=1, source_target_pairs={{0,24},{1,97},{2,26},{3,99},{4,28},{5,101},{6,30},{7,103},{8,16},{... | collective-permute-start | bytes 98312 | tf_op jit(solution)/shard_map/ppermute | solution.py:53
  90.0 16.2 %collective-permute-start.16 = (f32[2,8,16,1024]{3,2,1,0:T(8,128)S(1)}, f32[2,8,16,1024]{3,2,1,0:T(8,128)S(1)}, u32[]{:S(2)}, u32[]{:S(2)}) collective-permute-start(f32[2,8,16,1024]{3,2,1,0:T(8,128)S(1)} %pad_maximum_fusion.refs_0_), channel_id=1, source_target_pairs={{0,8},{1,33},{2,10},{3,35},{4,12},{5,37},{6,14},{7,39},{8,16},{9,4... | collective-permute-start | bytes 3145736 | tf_op jit(solution)/shard_map/ppermute | solution.py:53
  90.1 16.2 %collective-permute-start.17 = (f32[2,8,16,1024]{3,2,1,0:T(8,128)S(1)}, f32[2,8,16,1024]{3,2,1,0:T(8,128)S(1)}, u32[]{:S(2)}, u32[]{:S(2)}) collective-permute-start(f32[2,8,16,1024]{3,2,1,0:T(8,128)S(1)} %pad_maximum_fusion.1.refs_1_), channel_id=1, source_target_pairs={{0,24},{1,97},{2,26},{3,99},{4,28},{5,101},{6,30},{7,103},{8,0},{9... | collective-permute-start | bytes 3145736 | tf_op jit(solution)/shard_map/ppermute | solution.py:53
  93.5 3.9 %collective-permute-start.18 = (f32[64,128]{1,0:T(8,128)S(1)}, f32[64,128]{1,0:T(8,128)S(1)}, u32[]{:S(2)}, u32[]{:S(2)}) collective-permute-start(f32[64,128]{1,0:T(8,128)S(1)} %add.77), channel_id=1, source_target_pairs={{0,32},{1,9},{2,34},{3,11},{4,36},{5,13},{6,38},{7,15},{8,40},{9,1... | collective-permute-start | bytes 98312 | tf_op jit(solution)/shard_map/ppermute | solution.py:53
  97.4 4.7 %collective-permute-start.19 = (f32[64,128]{1,0:T(8,128)S(1)}, f32[64,128]{1,0:T(8,128)S(1)}, u32[]{:S(2)}, u32[]{:S(2)}) collective-permute-start(f32[64,128]{1,0:T(8,128)S(1)} %add.78), channel_id=1, source_target_pairs={{0,96},{1,25},{2,98},{3,27},{4,100},{5,29},{6,102},{7,31},{8,104},... | collective-permute-start | bytes 98312 | tf_op jit(solution)/shard_map/ppermute | solution.py:53
  97.4 20.1 %collective-permute-start.24 = (f32[2,8,16,1024]{3,2,1,0:T(8,128)S(1)}, f32[2,8,16,1024]{3,2,1,0:T(8,128)S(1)}, u32[]{:S(2)}, u32[]{:S(2)}) collective-permute-start(f32[2,8,16,1024]{3,2,1,0:T(8,128)S(1)} %pad_maximum_fusion.1.refs_1_), channel_id=1, source_target_pairs={{0,8},{1,33},{2,10},{3,35},{4,12},{5,37},{6,14},{7,39},{8,16},{9,4... | collective-permute-start | bytes 3145736 | tf_op jit(solution)/shard_map/ppermute | solution.py:53
  97.5 20.0 %collective-permute-start.25 = (f32[2,8,16,1024]{3,2,1,0:T(8,128)S(1)}, f32[2,8,16,1024]{3,2,1,0:T(8,128)S(1)}, u32[]{:S(2)}, u32[]{:S(2)}) collective-permute-start(f32[2,8,16,1024]{3,2,1,0:T(8,128)S(1)} %pad_maximum_fusion.refs_0_), channel_id=1, source_target_pairs={{0,24},{1,97},{2,26},{3,99},{4,28},{5,101},{6,30},{7,103},{8,0},{9... | collective-permute-start | bytes 3145736 | tf_op jit(solution)/shard_map/ppermute | solution.py:53
  106.3 22.5 %collective-permute-start.20 = (f32[2,8,16,1024]{3,2,1,0:T(8,128)S(1)}, f32[2,8,16,1024]{3,2,1,0:T(8,128)S(1)}, u32[]{:S(2)}, u32[]{:S(2)}) collective-permute-start(f32[2,8,16,1024]{3,2,1,0:T(8,128)S(1)} %collective-permute-done.16.refs_2_), channel_id=1, source_target_pairs={{0,8},{1,33},{2,10},{3,35},{4,12},{5,37},{6,14},{7,39},{8,16},{9,4... | collective-permute-start | bytes 3145736 | tf_op jit(solution)/shard_map/ppermute | solution.py:53
  107.1 21.6 %collective-permute-start.21 = (f32[2,8,16,1024]{3,2,1,0:T(8,128)S(1)}, f32[2,8,16,1024]{3,2,1,0:T(8,128)S(1)}, u32[]{:S(2)}, u32[]{:S(2)}) collective-permute-start(f32[2,8,16,1024]{3,2,1,0:T(8,128)S(1)} %collective-permute-done.17.refs_5_), channel_id=1, source_target_pairs={{0,24},{1,97},{2,26},{3,99},{4,28},{5,101},{6,30},{7,103},{8,0},{9... | collective-permute-start | bytes 3145736 | tf_op jit(solution)/shard_map/ppermute | solution.py:53
  109.0 4.3 %collective-permute-start.22 = (f32[56,128]{1,0:T(8,128)S(1)}, f32[56,128]{1,0:T(8,128)S(1)}, u32[]{:S(2)}, u32[]{:S(2)}) collective-permute-start(f32[56,128]{1,0:T(8,128)S(1)} %pad_maximum_fusion.2), channel_id=1, source_target_pairs={{0,1},{1,0},{2,3},{3,2},{4,5},{5,4},{6,7},{7,6},{8,9},{9,8},{10,11... | collective-permute-start | bytes 86024 | tf_op jit(solution)/shard_map/ppermute | solution.py:53
  113.3 3.0 %collective-permute-start.23 = (f32[56,128]{1,0:T(8,128)S(1)}, f32[56,128]{1,0:T(8,128)S(1)}, u32[]{:S(2)}, u32[]{:S(2)}) collective-permute-start(f32[56,128]{1,0:T(8,128)S(1)} %fusion.3), channel_id=1, source_target_pairs={{0,2},{1,3},{2,0},{3,1},{4,6},{5,7},{6,4},{7,5},{8,10},{9,11},{10,... | collective-permute-start | bytes 86024 | tf_op jit(solution)/shard_map/ppermute | solution.py:53
  117.5 4.3 %collective-permute-start.26 = (f32[56,128]{1,0:T(8,128)S(1)}, f32[56,128]{1,0:T(8,128)S(1)}, u32[]{:S(2)}, u32[]{:S(2)}) collective-permute-start(f32[56,128]{1,0:T(8,128)S(1)} %add.81), channel_id=1, source_target_pairs={{0,6},{1,7},{2,4},{3,5},{4,2},{5,3},{6,0},{7,1},{8,14},{9,15},{10,... | collective-permute-start | bytes 86024 | tf_op jit(solution)/shard_map/ppermute | solution.py:53
  132.8 6.6 %collective-permute-start.27 = (f32[256,1280]{1,0:T(8,128)S(1)}, f32[256,1280]{1,0:T(8,128)S(1)}, u32[]{:S(2)}, u32[]{:S(2)}) collective-permute-start(f32[256,1280]{1,0:T(8,128)S(1)} %get-tuple-element.107), channel_id=1, source_target_pairs={{0,1},{1,0},{2,3},{3,2},{4,5},{5,4},{6,7},{7,6},{8,9},{9,8},{10,11... | collective-permute-start | bytes 3932168 | tf_op jit(solution)/shard_map/ppermute | solution.py:53
  139.7 22.6 %collective-permute-start.29 = (f32[128,1280]{1,0:T(8,128)S(1)}, f32[128,1280]{1,0:T(8,128)S(1)}, u32[]{:S(2)}, u32[]{:S(2)}) collective-permute-start(f32[128,1280]{1,0:T(8,128)S(1)} %get-tuple-element.146), channel_id=1, source_target_pairs={{0,2},{1,3},{2,4},{3,5},{4,6},{5,7},{6,0},{7,1},{8,10},{9,11},{10,... | collective-permute-start | bytes 1966088 | tf_op jit(solution)/shard_map/ppermute | solution.py:53
  141.1 21.2 %collective-permute-start.30 = (f32[128,1280]{1,0:T(8,128)S(1)}, f32[128,1280]{1,0:T(8,128)S(1)}, u32[]{:S(2)}, u32[]{:S(2)}) collective-permute-start(f32[128,1280]{1,0:T(8,128)S(1)} %get-tuple-element.145), channel_id=1, source_target_pairs={{0,6},{1,7},{2,0},{3,1},{4,2},{5,3},{6,4},{7,5},{8,14},{9,15},{10,... | collective-permute-start | bytes 1966088 | tf_op jit(solution)/shard_map/ppermute | solution.py:53
  152.8 10.4 %collective-permute-start.31 = (f32[256,1280]{1,0:T(8,128)S(1)}, f32[256,1280]{1,0:T(8,128)S(1)}, u32[]{:S(2)}, u32[]{:S(2)}) collective-permute-start(f32[256,1280]{1,0:T(8,128)S(1)} %get-tuple-element.112), channel_id=1, source_target_pairs={{0,1},{1,0},{2,3},{3,2},{4,5},{5,4},{6,7},{7,6},{8,9},{9,8},{10,11... | collective-permute-start | bytes 3932168 | tf_op jit(solution)/shard_map/ppermute | solution.py:53
  153.1 10.0 %collective-permute-start.32 = (f32[256,1280]{1,0:T(8,128)S(1)}, f32[256,1280]{1,0:T(8,128)S(1)}, u32[]{:S(2)}, u32[]{:S(2)}) collective-permute-start(f32[256,1280]{1,0:T(8,128)S(1)} %get-tuple-element.126), channel_id=1, source_target_pairs={{0,1},{1,0},{2,3},{3,2},{4,5},{5,4},{6,7},{7,6},{8,9},{9,8},{10,11... | collective-permute-start | bytes 3932168 | tf_op jit(solution)/shard_map/ppermute | solution.py:53
  153.3 8.9 %collective-permute-start.28 = (f32[32,1024]{1,0:T(8,128)S(1)}, f32[32,1024]{1,0:T(8,128)S(1)}, u32[]{:S(2)}, u32[]{:S(2)}) collective-permute-start(f32[32,1024]{1,0:T(8,128)S(1)} %add.72), channel_id=1, source_target_pairs={{0,32},{1,9},{2,34},{3,11},{4,36},{5,13},{6,38},{7,15},{8,40},{9,1... | collective-permute-start | bytes 393224 | tf_op jit(solution)/shard_map/ppermute | solution.py:53
  162.2 27.9 %collective-permute-start.35 = (f32[256,1280]{1,0:T(8,128)S(1)}, f32[256,1280]{1,0:T(8,128)S(1)}, u32[]{:S(2)}, u32[]{:S(2)}) collective-permute-start(f32[256,1280]{1,0:T(8,128)S(1)} %get-tuple-element.134), channel_id=1, source_target_pairs={{0,1},{1,0},{2,3},{3,2},{4,5},{5,4},{6,7},{7,6},{8,9},{9,8},{10,11... | collective-permute-start | bytes 3932168 | tf_op jit(solution)/shard_map/ppermute | solution.py:53
  164.1 34.8 %collective-permute-start.40 = (f32[256,1280]{1,0:T(8,128)S(1)}, f32[256,1280]{1,0:T(8,128)S(1)}, u32[]{:S(2)}, u32[]{:S(2)}) collective-permute-start(f32[256,1280]{1,0:T(8,128)S(1)} %get-tuple-element.140), channel_id=1, source_target_pairs={{0,6},{1,7},{2,0},{3,1},{4,2},{5,3},{6,4},{7,5},{8,14},{9,15},{10,... | collective-permute-start | bytes 3932168 | tf_op jit(solution)/shard_map/ppermute | solution.py:53
  165.5 33.4 %collective-permute-start.39 = (f32[256,1280]{1,0:T(8,128)S(1)}, f32[256,1280]{1,0:T(8,128)S(1)}, u32[]{:S(2)}, u32[]{:S(2)}) collective-permute-start(f32[256,1280]{1,0:T(8,128)S(1)} %get-tuple-element.127), channel_id=1, source_target_pairs={{0,2},{1,3},{2,4},{3,5},{4,6},{5,7},{6,0},{7,1},{8,10},{9,11},{10,... | collective-permute-start | bytes 3932168 | tf_op jit(solution)/shard_map/ppermute | solution.py:53
  165.7 24.7 %collective-permute-start.34 = (f32[8,1280]{1,0:T(8,128)S(1)}, f32[8,1280]{1,0:T(8,128)S(1)}, u32[]{:S(2)}, u32[]{:S(2)}) collective-permute-start(f32[8,1280]{1,0:T(8,128)S(1)} %get-tuple-element.118), channel_id=1, source_target_pairs={{0,1},{1,0},{2,3},{3,2},{4,5},{5,4},{6,7},{7,6},{8,9},{9,8},{10,11... | collective-permute-start | bytes 122888 | tf_op jit(solution)/shard_map/ppermute | solution.py:53
  166.8 23.5 %collective-permute-start.33 = (f32[32,1024]{1,0:T(8,128)S(1)}, f32[32,1024]{1,0:T(8,128)S(1)}, u32[]{:S(2)}, u32[]{:S(2)}) collective-permute-start(f32[32,1024]{1,0:T(8,128)S(1)} %add.84), channel_id=1, source_target_pairs={{0,96},{1,25},{2,98},{3,27},{4,100},{5,29},{6,102},{7,31},{8,104},... | collective-permute-start | bytes 393224 | tf_op jit(solution)/shard_map/ppermute | solution.py:53
  190.4 7.2 %collective-permute-start.36 = (f32[8,1280]{1,0:T(8,128)S(1)}, f32[8,1280]{1,0:T(8,128)S(1)}, u32[]{:S(2)}, u32[]{:S(2)}) collective-permute-start(f32[8,1280]{1,0:T(8,128)S(1)} %add.88.last), channel_id=1, source_target_pairs={{0,2},{1,3},{2,4},{3,5},{4,6},{5,7},{6,0},{7,1},{8,10},{9,11},{10,... | collective-permute-start | bytes 122888 | tf_op jit(solution)/shard_map/ppermute | solution.py:53
  190.4 7.1 %collective-permute-start.37 = (f32[8,1280]{1,0:T(8,128)S(1)}, f32[8,1280]{1,0:T(8,128)S(1)}, u32[]{:S(2)}, u32[]{:S(2)}) collective-permute-start(f32[8,1280]{1,0:T(8,128)S(1)} %add.88.last), channel_id=1, source_target_pairs={{0,4},{1,5},{2,6},{3,7},{4,0},{5,1},{6,2},{7,3},{8,12},{9,13},{10,... | collective-permute-start | bytes 122888 | tf_op jit(solution)/shard_map/ppermute | solution.py:53
  194.1 3.5 %collective-permute-start.38 = (f32[8,1280]{1,0:T(8,128)S(1)}, f32[8,1280]{1,0:T(8,128)S(1)}, u32[]{:S(2)}, u32[]{:S(2)}) collective-permute-start(f32[8,1280]{1,0:T(8,128)S(1)} %add.88.last), channel_id=1, source_target_pairs={{0,6},{1,7},{2,0},{3,1},{4,2},{5,3},{6,4},{7,5},{8,14},{9,15},{10,... | collective-permute-start | bytes 122888 | tf_op jit(solution)/shard_map/ppermute | solution.py:53

commit v5 on v4

--- a/solution.py
+++ b/solution.py
@@ -494,7 +494,7 @@
 
 
 def back_kernel(ids, grad, masses, expr, *refs, parts, first, last):
-    more, (sums, *outs), (held, ready) = refs[: first + 4 * last], refs[first + 4 * last : -2], refs[-2:]
+    more, (sums, *outs), (held, ready) = refs[: first + 5 * last], refs[first + 5 * last : -2], refs[-2:]
     step = pl.program_id(0)
     rows = grad.shape[2]
 
@@ -513,7 +513,7 @@
     @pl.when(step == 0)
     def _():
         if last:
-            sums[...] = more[0][...] + more[1][...] + more[2][...]
+            sums[...] = more[0][...] + more[1][...] + more[2][...] + more[3][...]
         else:
             sums[...] = jnp.zeros_like(sums)
 
@@ -541,14 +541,14 @@
             total = jnp.sum(sums[...], axis=0, keepdims=True)
             sums[...] = jnp.zeros_like(sums)
             sums[0:1, :] = total
-            sums[1:2, 0:128] = more[3][...]
+            sums[1:2, 0:128] = more[4][...]
 
 
 def back_call(ids, parts, grad, masses, expr, first=(), last=()):
     _, blocks, rows, spots = grad.shape
     cells = masses.shape[1]
     return pl.pallas_call(
-        functools.partial(back_kernel, parts=parts, first=len(first), last=len(last) // 4),
+        functools.partial(back_kernel, parts=parts, first=len(first), last=len(last) // 5),
         grid_spec=pltpu.PrefetchScalarGridSpec(
             num_scalar_prefetch=1,
             grid=(len(parts),),
@@ -807,15 +807,16 @@
     grad, column_c = last_grad((1, -1, 0), grad, far)
     sums_c, up_a, down_a, own_a = back_part([(1, 1), (-1, 1), (0, 1)], grad)
     up_got, down_got, own_got = (swap(one, 0, 0, 0, 1) for one in (up_a, down_a, own_a))
-    last, up_b, down_b, own_b = back_part(
-        [(1, 0), (-1, 0), (0, 0)], grad, up_a, last=[sums_a, sums_b, sums_c, scalars]
-    )
-    last_got = swap(last, 0, 0, 0, 1)
+    sums_d, up_b, down_b = back_part([(1, 0), (-1, 0)], grad, up_a)
     types = types + swap_across(after(types, up_a), 1)
     above, below = lift_call(up_b, down_b, *after((far_up, far_down), types))
     above, below = join_call(above, below, up_got, down_got)
     near_up, near_down = up(above, 1), up(below, -1)
     types_got = swap_across(after(types, above), 3)
+    last, own_b = back_part(
+        [(0, 0)], grad, above, below, last=[sums_a, sums_b, sums_c, sums_d, scalars]
+    )
+    last_got = swap(last, 0, 0, 0, 1)
     own = own_b + own_got
 
     column = jnp.sum(column_a + column_b + column_c, axis=0) * share + spot_coef[32] * mass

time: 201 us -> 200 us (level)
  starting transfers between devices: 58.8 us -> 54 us
  waiting for transfers between devices: 47.6 us -> 50.9 us
    ppermute x41, starting transfers between devices: 58.8 us -> 54 us  [send(): return lax.ppermute(array, ('cells', 'spots'), route(target))]
    ppermute x41, waiting for transfers between devices: 47.6 us -> 50.9 us  [send(): return lax.ppermute(array, ('cells', 'spots'), route(target))]
    pallas_call x4 -> x5, Pallas kernels: 22.5 us -> 23 us  [back_call(): pl.pallas_call(functools.partial(back_kernel, parts=parts, first=len(firs...]
  transfers between devices with their start and end apart: 41 -> 41, of which waited for: 19 -> 20; matrix products, arithmetic and copies ran while one was open for 1% -> 1% of each run, Pallas kernels for 37% -> 37%
where the time goes in v5:
time: 200 us; the launch traced here: 199 us
  Pallas kernels  88.8 us (44%)
  starting transfers between devices  54 us (27%)
  waiting for transfers between devices  50.9 us (25%)
  other arithmetic  3.77 us (2%)
    ppermute x41, starting transfers between devices, send(): return lax.ppermute(array, ('cells', 'spots'), route(target))  54 us
    ppermute x41, waiting for transfers between devices, send(): return lax.ppermute(array, ('cells', 'spots'), route(target))  50.9 us
    pallas_call x5, Pallas kernels, back_call(): pl.pallas_call(functools.partial(back_kernel, parts=parts, first=len(firs...  23 us
    pallas_call x3, Pallas kernels, pred_call(): pl.pallas_call(functools.partial(pred_kernel, cuts=cuts), grid_spec=pltpu...  21.9 us
    pallas_call x1, Pallas kernels, map_call(): pl.pallas_call(functools.partial(map_kernel, scale=scale), grid=(cells //...  21.3 us
    pallas_call x1, Pallas kernels, expo_call(): pl.pallas_call(expo_kernel, grid_spec=pltpu.PrefetchScalarGridSpec(num_sc...  9.85 us
    pallas_call x3, Pallas kernels, grad_call(): pl.pallas_call(functools.partial(grad_kernel, count=count, lane=lane, chi...  7.63 us
  transfers between devices with their start and end apart: 41, of which 20 were waited for; matrix products, arithmetic and copies ran while one was open for 1% of the time, Pallas kernels for 37%

profile of v5, /device:TPU:1, one launch (start us, length us, event | category | flops | bytes accessed | tf_op | source)
XLA Modules:
  0.0 199.3 jit_solution(15703813248236209853)
XLA Ops:
  0.7 9.9 %expo.1 = (bf16[2,1280,1024]{2,1,0:T(8,128)(2,1)S(1)}, f32[32,1024]{1,0:T(8,128)S(1)}, f32[8,1024]{1,0:T(8,128)S(1)}, f32[33,8,1024]{2,1,0:T(8,128)S(1)}, f32[33,8,1024]{2,1,0:T(8,128)S(1)}) custom-call(s32[4]{0:T(128)S(1)} %pad_add_fusion.ids, f32[1280,1024]{1,0:T(8,128)} %logits.1, s32[10,128]{1,0:T(8,128)} %bitcast.66, f32[10,128]{1,0:T(8,128)} %bitcast.67, ...), custom_call_target="tpu_custom_call" | custom-call | bytes 1310720 | tf_op jit(solution)/shard_map/expo/pallas_call | solution.py:176
  10.6 2.5 %collective-permute-start = (f32[33,8,1024]{2,1,0:T(8,128)S(1)}, f32[33,8,1024]{2,1,0:T(8,128)S(1)}, u32[]{:S(2)}, u32[]{:S(2)}) collective-permute-start(f32[33,8,1024]{2,1,0:T(8,128)S(1)} %get-tuple-element.75), channel_id=1, source_target_pairs={{0,8},{1,33},{2,10},{3,35},{4,12},{5,37},{6,14},{7,39},{8,16},{9,4... | collective-permute-start | bytes 3244040 | tf_op jit(solution)/shard_map/ppermute | solution.py:53
  13.1 2.3 %collective-permute-start.1 = (f32[33,8,1024]{2,1,0:T(8,128)S(1)}, f32[33,8,1024]{2,1,0:T(8,128)S(1)}, u32[]{:S(2)}, u32[]{:S(2)}) collective-permute-start(f32[33,8,1024]{2,1,0:T(8,128)S(1)} %get-tuple-element.76), channel_id=1, source_target_pairs={{0,24},{1,97},{2,26},{3,99},{4,28},{5,101},{6,30},{7,103},{8,0},{9... | collective-permute-start | bytes 3244040 | tf_op jit(solution)/shard_map/ppermute | solution.py:53
  15.4 7.5 %pred_.3 = (f32[33,8,1024]{2,1,0:T(8,128)S(1)}, f32[33,8,1024]{2,1,0:T(8,128)S(1)}) custom-call(s32[4]{0:T(128)S(1)} %pad_add_fusion.ids, f32[8,16,16,1280]{3,2,1,0:T(8,128)} %bitcast.57, f32[8,16,16,1280]{3,2,1,0:T(8,128)} %bitcast.58, f32[1,1280]{1,0:T(1,128)S(1)} %reshape.94.keep, bf16[2,1280,1024]{2,1,0:T(8,128)(2,1)S(1)} %get-tuple-element.78.masses, ...), custom_call_target="tpu_custom_call" | custom-call | flops 503316480 | bytes 1245184 | tf_op jit(solution)/shard_map/pred/pallas_call | solution.py:249
  22.9 1.4 collective-permute-start.2
  24.5 3.6 %collective-permute-done.refs_0_ = f32[33,8,1024]{2,1,0:T(8,128)S(1)} collective-permute-done((f32[33,8,1024]{2,1,0:T(8,128)S(1)}, f32[33,8,1024]{2,1,0:T(8,128)S(1)}, u32[]{:S(2)}, u32[]{:S(2)}) %collective-permute-start) | collective-permute-done | bytes 1081376 | tf_op jit(solution)/shard_map/ppermute | solution.py:53
  28.0 6.9 %pred_.4 = (f32[33,8,1024]{2,1,0:T(8,128)S(1)}, f32[33,8,1024]{2,1,0:T(8,128)S(1)}) custom-call(s32[4]{0:T(128)S(1)} %pad_add_fusion.ids, f32[8,16,16,1280]{3,2,1,0:T(8,128)} %bitcast.59, f32[8,16,16,1280]{3,2,1,0:T(8,128)} %bitcast.60, f32[1,1280]{1,0:T(1,128)S(1)} %reshape.94.keep, bf16[2,1280,1024]{2,1,0:T(8,128)(2,1)S(1)} %get-tuple-element.78.masses, ...), custom_call_target="tpu_custom_call" | custom-call | flops 503316480 | bytes 1245184 | tf_op jit(solution)/shard_map/pred/pallas_call | solution.py:249
  36.0 2.0 collective-permute-start.5
  39.9 7.6 %pred_.5 = (f32[33,8,1024]{2,1,0:T(8,128)S(1)}, f32[33,8,1024]{2,1,0:T(8,128)S(1)}) custom-call(s32[4]{0:T(128)S(1)} %pad_add_fusion.ids, f32[8,16,16,1280]{3,2,1,0:T(8,128)} %bitcast.61, f32[8,16,16,1280]{3,2,1,0:T(8,128)} %bitcast.62, f32[1,1280]{1,0:T(1,128)S(1)} %reshape.94.keep, bf16[2,1280,1024]{2,1,0:T(8,128)(2,1)S(1)} %get-tuple-element.78.masses, ...), custom_call_target="tpu_custom_call" | custom-call | flops 503316480 | bytes 1245184 | tf_op jit(solution)/shard_map/pred/pallas_call | solution.py:249
  47.5 4.0 %collective-permute-done.4.got0 = f32[33,8,1024]{2,1,0:T(8,128)S(1)} collective-permute-done((f32[33,8,1024]{2,1,0:T(8,128)S(1)}, f32[33,8,1024]{2,1,0:T(8,128)S(1)}, u32[]{:S(2)}, u32[]{:S(2)}) %collective-permute-start.4) | collective-permute-done | bytes 1081376 | tf_op jit(solution)/shard_map/ppermute | solution.py:53
  52.3 2.5 %collective-permute-start.10 = (f32[17,8,1024]{2,1,0:T(8,128)S(1)}, f32[17,8,1024]{2,1,0:T(8,128)S(1)}, u32[]{:S(2)}, u32[]{:S(2)}) collective-permute-start(f32[17,8,1024]{2,1,0:T(8,128)S(1)} %get-tuple-element.95), channel_id=1, source_target_pairs={{0,96},{1,25},{2,98},{3,27},{4,100},{5,29},{6,102},{7,31},{8,104},... | collective-permute-start | bytes 1671176 | tf_op jit(solution)/shard_map/ppermute | solution.py:53
  54.8 1.4 collective-permute-start.9
  58.1 4.5 %collective-permute-done.6 = f32[32,1024]{1,0:T(8,128)S(1)} collective-permute-done((f32[32,1024]{1,0:T(8,128)S(1)}, f32[32,1024]{1,0:T(8,128)S(1)}, u32[]{:S(2)}, u32[]{:S(2)}) %collective-permute-start.6) | collective-permute-done | bytes 131104 | tf_op jit(solution)/shard_map/ppermute | solution.py:53
  62.6 2.7 %collective-permute-start.7 = (f32[32,1024]{1,0:T(8,128)S(1)}, f32[32,1024]{1,0:T(8,128)S(1)}, u32[]{:S(2)}, u32[]{:S(2)}) collective-permute-start(f32[32,1024]{1,0:T(8,128)S(1)} %add.71), channel_id=1, source_target_pairs={{0,24},{1,97},{2,26},{3,99},{4,28},{5,101},{6,30},{7,103},{8,16},{... | collective-permute-start | bytes 393224 | tf_op jit(solution)/shard_map/ppermute | solution.py:53
  65.4 9.6 %collective-permute-done.7 = f32[32,1024]{1,0:T(8,128)S(1)} collective-permute-done((f32[32,1024]{1,0:T(8,128)S(1)}, f32[32,1024]{1,0:T(8,128)S(1)}, u32[]{:S(2)}, u32[]{:S(2)}) %collective-permute-start.7) | collective-permute-done | bytes 131104 | tf_op jit(solution)/shard_map/ppermute | solution.py:53
  75.2 2.1 %collective-permute-start.12 = (f32[8,16,1024]{2,1,0:T(8,128)S(1)}, f32[8,16,1024]{2,1,0:T(8,128)S(1)}, u32[]{:S(2)}, u32[]{:S(2)}) collective-permute-start(f32[8,16,1024]{2,1,0:T(8,128)S(1)} %bitcast.47), channel_id=1, source_target_pairs={{0,64},{1,17},{2,66},{3,19},{4,68},{5,21},{6,70},{7,23},{8,72},{9,... | collective-permute-start | bytes 1572872 | tf_op jit(solution)/shard_map/ppermute | solution.py:53
  77.7 2.4 %collective-permute-start.11 = (f32[8,16,1024]{2,1,0:T(8,128)S(1)}, f32[8,16,1024]{2,1,0:T(8,128)S(1)}, u32[]{:S(2)}, u32[]{:S(2)}) collective-permute-start(f32[8,16,1024]{2,1,0:T(8,128)S(1)} %bitcast.49), channel_id=1, source_target_pairs={{0,96},{1,25},{2,98},{3,27},{4,100},{5,29},{6,102},{7,31},{8,104},... | collective-permute-start | bytes 1572872 | tf_op jit(solution)/shard_map/ppermute | solution.py:53
  81.0 3.5 %collective-permute-done.14 = f32[64,128]{1,0:T(8,128)S(1)} collective-permute-done((f32[64,128]{1,0:T(8,128)S(1)}, f32[64,128]{1,0:T(8,128)S(1)}, u32[]{:S(2)}, u32[]{:S(2)}) %collective-permute-start.14) | collective-permute-done | bytes 32800 | tf_op jit(solution)/shard_map/ppermute | solution.py:53
  84.6 4.6 %collective-permute-done.15 = f32[64,128]{1,0:T(8,128)S(1)} collective-permute-done((f32[64,128]{1,0:T(8,128)S(1)}, f32[64,128]{1,0:T(8,128)S(1)}, u32[]{:S(2)}, u32[]{:S(2)}) %collective-permute-start.15) | collective-permute-done | bytes 32800 | tf_op jit(solution)/shard_map/ppermute | solution.py:53
  89.2 1.9 collective-permute-done.13
  91.4 2.7 %collective-permute-start.17 = (f32[2,8,16,1024]{3,2,1,0:T(8,128)S(1)}, f32[2,8,16,1024]{3,2,1,0:T(8,128)S(1)}, u32[]{:S(2)}, u32[]{:S(2)}) collective-permute-start(f32[2,8,16,1024]{3,2,1,0:T(8,128)S(1)} %pad_maximum_fusion.1.refs_1_), channel_id=1, source_target_pairs={{0,24},{1,97},{2,26},{3,99},{4,28},{5,101},{6,30},{7,103},{8,0},{9... | collective-permute-start | bytes 3145736 | tf_op jit(solution)/shard_map/ppermute | solution.py:53
  94.6 2.8 %collective-permute-done.18 = f32[64,128]{1,0:T(8,128)S(1)} collective-permute-done((f32[64,128]{1,0:T(8,128)S(1)}, f32[64,128]{1,0:T(8,128)S(1)}, u32[]{:S(2)}, u32[]{:S(2)}) %collective-permute-start.18) | collective-permute-done | bytes 32800 | tf_op jit(solution)/shard_map/ppermute | solution.py:53
  97.5 1.7 collective-permute-start.19
  99.1 2.7 %collective-permute-start.25 = (f32[2,8,16,1024]{3,2,1,0:T(8,128)S(1)}, f32[2,8,16,1024]{3,2,1,0:T(8,128)S(1)}, u32[]{:S(2)}, u32[]{:S(2)}) collective-permute-start(f32[2,8,16,1024]{3,2,1,0:T(8,128)S(1)} %pad_maximum_fusion.refs_0_), channel_id=1, source_target_pairs={{0,24},{1,97},{2,26},{3,99},{4,28},{5,101},{6,30},{7,103},{8,0},{9... | collective-permute-start | bytes 3145736 | tf_op jit(solution)/shard_map/ppermute | solution.py:53
  102.2 4.7 %collective-permute-done.16.refs_2_ = f32[2,8,16,1024]{3,2,1,0:T(8,128)S(1)} collective-permute-done((f32[2,8,16,1024]{3,2,1,0:T(8,128)S(1)}, f32[2,8,16,1024]{3,2,1,0:T(8,128)S(1)}, u32[]{:S(2)}, u32[]{:S(2)}) %collective-permute-start.16) | collective-permute-done | bytes 1048608 | tf_op jit(solution)/shard_map/ppermute | solution.py:53
  106.9 2.7 %collective-permute-start.21 = (f32[2,8,16,1024]{3,2,1,0:T(8,128)S(1)}, f32[2,8,16,1024]{3,2,1,0:T(8,128)S(1)}, u32[]{:S(2)}, u32[]{:S(2)}) collective-permute-start(f32[2,8,16,1024]{3,2,1,0:T(8,128)S(1)} %collective-permute-done.17.refs_5_), channel_id=1, source_target_pairs={{0,24},{1,97},{2,26},{3,99},{4,28},{5,101},{6,30},{7,103},{8,0},{9... | collective-permute-start | bytes 3145736 | tf_op jit(solution)/shard_map/ppermute | solution.py:53
  109.6 2.6 %collective-permute-start.22 = (f32[56,128]{1,0:T(8,128)S(1)}, f32[56,128]{1,0:T(8,128)S(1)}, u32[]{:S(2)}, u32[]{:S(2)}) collective-permute-start(f32[56,128]{1,0:T(8,128)S(1)} %pad_maximum_fusion.2), channel_id=1, source_target_pairs={{0,1},{1,0},{2,3},{3,2},{4,5},{5,4},{6,7},{7,6},{8,9},{9,8},{10,11... | collective-permute-start | bytes 86024 | tf_op jit(solution)/shard_map/ppermute | solution.py:53
  113.0 1.3 collective-permute-start.23
  114.4 1.7 collective-permute-done.23
  116.1 2.0 %collective-permute-done.24.refs_3_ = f32[2,8,16,1024]{3,2,1,0:T(8,128)S(1)} collective-permute-done((f32[2,8,16,1024]{3,2,1,0:T(8,128)S(1)}, f32[2,8,16,1024]{3,2,1,0:T(8,128)S(1)}, u32[]{:S(2)}, u32[]{:S(2)}) %collective-permute-start.24) | collective-permute-done | bytes 1048608 | tf_op jit(solution)/shard_map/ppermute | solution.py:53
  118.1 2.7 %collective-permute-start.26 = (f32[56,128]{1,0:T(8,128)S(1)}, f32[56,128]{1,0:T(8,128)S(1)}, u32[]{:S(2)}, u32[]{:S(2)}) collective-permute-start(f32[56,128]{1,0:T(8,128)S(1)} %add.81), channel_id=1, source_target_pairs={{0,6},{1,7},{2,4},{3,5},{4,2},{5,3},{6,0},{7,1},{8,14},{9,15},{10,... | collective-permute-start | bytes 86024 | tf_op jit(solution)/shard_map/ppermute | solution.py:53
  120.8 1.6 collective-permute-done.26
  123.2 4.7 %grad.3 = (bf16[2,8,256,1024]{3,2,1,0:T(8,128)(2,1)S(1)}, f32[8,1024]{1,0:T(8,128)S(1)}) custom-call(s32[4]{0:T(128)S(1)} %pad_add_fusion.ids, f32[2,8,16,1024]{3,2,1,0:T(8,128)S(1)} %pad_maximum_fusion.refs_0_, f32[2,8,16,1024]{3,2,1,0:T(8,128)S(1)} %pad_maximum_fusion.1.refs_1_, f32[2,8,16,1024]{3,2,1,0:T(8,128)S(1)} %collective-permute-done.16.refs_2_, ...), custom_call_target="tpu_custom_call" | custom-call | tf_op jit(solution)/shard_map/grad/pallas_call | solution.py:474
  128.0 1.4 collective-permute-done.20.refs_0_
  130.3 3.1 %back.5 = (f32[8,1280]{1,0:T(8,128)S(1)}, f32[256,1280]{1,0:T(8,128)S(1)}) custom-call(s32[4]{0:T(128)S(1)} %pad_add_fusion.ids, bf16[2,8,256,1024]{3,2,1,0:T(8,128)(2,1)S(1)} %get-tuple-element.108.grad.refs_5_, bf16[2,1280,1024]{2,1,0:T(8,128)(2,1)S(1)} %get-tuple-element.78.masses, f32[2048,1280]{1,0:T(8,128)} %expr.11, ...), custom_call_target="tpu_custom_call" | custom-call | tf_op jit(solution)/shard_map/back/pallas_call | solution.py:550
  133.4 2.1 %collective-permute-start.27 = (f32[256,1280]{1,0:T(8,128)S(1)}, f32[256,1280]{1,0:T(8,128)S(1)}, u32[]{:S(2)}, u32[]{:S(2)}) collective-permute-start(f32[256,1280]{1,0:T(8,128)S(1)} %get-tuple-element.109), channel_id=1, source_target_pairs={{0,1},{1,0},{2,3},{3,2},{4,5},{5,4},{6,7},{7,6},{8,9},{9,8},{10,11... | collective-permute-start | bytes 3932168 | tf_op jit(solution)/shard_map/ppermute | solution.py:53
  135.5 3.6 %back.6 = (f32[8,1280]{1,0:T(8,128)S(1)}, f32[256,1280]{1,0:T(8,128)S(1)}) custom-call(s32[4]{0:T(128)S(1)} %pad_add_fusion.ids, bf16[2,8,256,1024]{3,2,1,0:T(8,128)(2,1)S(1)} %get-tuple-element.108.grad.refs_5_, bf16[2,1280,1024]{2,1,0:T(8,128)(2,1)S(1)} %get-tuple-element.78.masses, f32[2048,1280]{1,0:T(8,128)} %expr.11), custom_call_target="tpu_custom_call" | custom-call | tf_op jit(solution)/shard_map/back/pallas_call | solution.py:550
  139.3 1.4 collective-permute-start.28
  140.7 1.7 collective-permute-start.29
  142.4 1.9 grad.5
  144.4 8.0 %back.7 = (f32[8,1280]{1,0:T(8,128)S(1)}, f32[256,1280]{1,0:T(8,128)S(1)}, f32[256,1280]{1,0:T(8,128)S(1)}, f32[256,1280]{1,0:T(8,128)S(1)}) custom-call(s32[4]{0:T(128)S(1)} %pad_add_fusion.ids, bf16[2,8,256,1024]{3,2,1,0:T(8,128)(2,1)S(1)} %get-tuple-element.113.grad, bf16[2,1280,1024]{2,1,0:T(8,128)(2,1)S(1)} %get-tuple-element.78.masses, f32[2048,1280]{1,0:T(8,128)} %expr.11), custom_call_target="tpu_custom_call" | custom-call | tf_op jit(solution)/shard_map/back/pallas_call | solution.py:550
  154.2 5.5 %back.8 = (f32[8,1280]{1,0:T(8,128)S(1)}, f32[256,1280]{1,0:T(8,128)S(1)}, f32[256,1280]{1,0:T(8,128)S(1)}) custom-call(s32[4]{0:T(128)S(1)} %pad_add_fusion.ids, bf16[2,8,256,1024]{3,2,1,0:T(8,128)(2,1)S(1)} %get-tuple-element.113.grad, bf16[2,1280,1024]{2,1,0:T(8,128)(2,1)S(1)} %get-tuple-element.78.masses, f32[2048,1280]{1,0:T(8,128)} %expr.11), custom_call_target="tpu_custom_call" | custom-call | tf_op jit(solution)/shard_map/back/pallas_call | solution.py:550
  161.7 2.7 %collective-permute-start.40 = (f32[256,1280]{1,0:T(8,128)S(1)}, f32[256,1280]{1,0:T(8,128)S(1)}, u32[]{:S(2)}, u32[]{:S(2)}) collective-permute-start(f32[256,1280]{1,0:T(8,128)S(1)} %get-tuple-element.125), channel_id=1, source_target_pairs={{0,6},{1,7},{2,0},{3,1},{4,2},{5,3},{6,4},{7,5},{8,14},{9,15},{10,... | collective-permute-start | bytes 3932168 | tf_op jit(solution)/shard_map/ppermute | solution.py:53
  164.4 2.1 %collective-permute-start.33 = (f32[32,1024]{1,0:T(8,128)S(1)}, f32[32,1024]{1,0:T(8,128)S(1)}, u32[]{:S(2)}, u32[]{:S(2)}) collective-permute-start(f32[32,1024]{1,0:T(8,128)S(1)} %add.84), channel_id=1, source_target_pairs={{0,96},{1,25},{2,98},{3,27},{4,100},{5,29},{6,102},{7,31},{8,104},... | collective-permute-start | bytes 393224 | tf_op jit(solution)/shard_map/ppermute | solution.py:53
  166.5 3.0 %back.9 = (f32[8,1280]{1,0:T(8,128)S(1)}, f32[256,1280]{1,0:T(8,128)S(1)}) custom-call(s32[4]{0:T(128)S(1)} %pad_add_fusion.ids, bf16[2,8,256,1024]{3,2,1,0:T(8,128)(2,1)S(1)} %get-tuple-element.113.grad, bf16[2,1280,1024]{2,1,0:T(8,128)(2,1)S(1)} %get-tuple-element.78.masses, f32[2048,1280]{1,0:T(8,128)} %expr.11, ...), custom_call_target="tpu_custom_call" | custom-call | tf_op jit(solution)/shard_map/back/pallas_call | solution.py:550
  169.6 21.3 %grad_map.1 = f32[1280,1024]{1,0:T(8,128)} custom-call(f32[2048,1280]{1,0:T(8,128)} %expr.11, bf16[2,2048,1024]{2,1,0:T(8,128)(2,1)S(1)} %bitcast.38, bf16[2,1280,1024]{2,1,0:T(8,128)(2,1)S(1)} %get-tuple-element.78.masses, f32[10,128]{1,0:T(8,128)S(1)} %bitcast.52, f32[8,1024]{1,0:T(8,128)S(1)} %select_select_fusion.spot), custom_call_target="tpu_custom_call" | custom-call | tf_op jit(solution)/shard_map/grad_map/pallas_call | solution.py:656
  191.2 1.4 collective-permute-start.37
  197.9 1.4 add_multiply_fusion
  (104 shorter events, 21.1 us)
Async XLA Ops:
  0.7 14.7 %copy-start = (s32[1280]{0:T(1024)S(1)}, s32[1280]{0:T(1024)}, u32[]{:S(2)}) copy-start(s32[1280]{0:T(1024)} %param.11) | copy-start | bytes 15364
  0.7 14.7 %copy-start.1 = (f32[1280]{0:T(1024)S(1)}, f32[1280]{0:T(1024)}, u32[]{:S(2)}) copy-start(f32[1280]{0:T(1024)} %param.8) | copy-start | bytes 15364
  10.6 17.5 %collective-permute-start = (f32[33,8,1024]{2,1,0:T(8,128)S(1)}, f32[33,8,1024]{2,1,0:T(8,128)S(1)}, u32[]{:S(2)}, u32[]{:S(2)}) collective-permute-start(f32[33,8,1024]{2,1,0:T(8,128)S(1)} %get-tuple-element.75), channel_id=1, source_target_pairs={{0,8},{1,33},{2,10},{3,35},{4,12},{5,37},{6,14},{7,39},{8,16},{9,4... | collective-permute-start | bytes 3244040 | tf_op jit(solution)/shard_map/ppermute | solution.py:53
  13.1 14.9 %collective-permute-start.1 = (f32[33,8,1024]{2,1,0:T(8,128)S(1)}, f32[33,8,1024]{2,1,0:T(8,128)S(1)}, u32[]{:S(2)}, u32[]{:S(2)}) collective-permute-start(f32[33,8,1024]{2,1,0:T(8,128)S(1)} %get-tuple-element.76), channel_id=1, source_target_pairs={{0,24},{1,97},{2,26},{3,99},{4,28},{5,101},{6,30},{7,103},{8,0},{9... | collective-permute-start | bytes 3244040 | tf_op jit(solution)/shard_map/ppermute | solution.py:53
  22.9 16.2 %collective-permute-start.2 = (f32[33,8,1024]{2,1,0:T(8,128)S(1)}, f32[33,8,1024]{2,1,0:T(8,128)S(1)}, u32[]{:S(2)}, u32[]{:S(2)}) collective-permute-start(f32[33,8,1024]{2,1,0:T(8,128)S(1)} %get-tuple-element.81), channel_id=1, source_target_pairs={{0,24},{1,97},{2,26},{3,99},{4,28},{5,101},{6,30},{7,103},{8,0},{9... | collective-permute-start | bytes 3244040 | tf_op jit(solution)/shard_map/ppermute | solution.py:53
  24.4 15.5 %collective-permute-start.3 = (f32[33,8,1024]{2,1,0:T(8,128)S(1)}, f32[33,8,1024]{2,1,0:T(8,128)S(1)}, u32[]{:S(2)}, u32[]{:S(2)}) collective-permute-start(f32[33,8,1024]{2,1,0:T(8,128)S(1)} %get-tuple-element.80), channel_id=1, source_target_pairs={{0,8},{1,33},{2,10},{3,35},{4,12},{5,37},{6,14},{7,39},{8,16},{9,4... | collective-permute-start | bytes 3244040 | tf_op jit(solution)/shard_map/ppermute | solution.py:53
  28.0 28.2 %slice-start = ((s8[8388608]{0:T(1024)(128)(4,1)}), s8[4194304]{0:T(1024)(128)(4,1)S(1)}, s32[]{:S(2)}) async-start(s8[8388608]{0:T(1024)(128)(4,1)} %bitcast.39), calls=%async_computation | async-start | bytes 8388608
  35.0 16.5 %collective-permute-start.4 = (f32[33,8,1024]{2,1,0:T(8,128)S(1)}, f32[33,8,1024]{2,1,0:T(8,128)S(1)}, u32[]{:S(2)}, u32[]{:S(2)}) collective-permute-start(f32[33,8,1024]{2,1,0:T(8,128)S(1)} %get-tuple-element.83), channel_id=1, source_target_pairs={{0,8},{1,33},{2,10},{3,35},{4,12},{5,37},{6,14},{7,39},{8,16},{9,4... | collective-permute-start | bytes 3244040 | tf_op jit(solution)/shard_map/ppermute | solution.py:53
  36.0 20.2 %slice-start.1 = ((s8[8388608]{0:T(1024)(128)(4,1)}), s8[4194304]{0:T(1024)(128)(4,1)S(1)}, s32[]{:S(2)}) async-start(s8[8388608]{0:T(1024)(128)(4,1)} %bitcast.39), calls=%async_computation.1 | async-start | bytes 8388608
  36.0 15.4 %collective-permute-start.5 = (f32[33,8,1024]{2,1,0:T(8,128)S(1)}, f32[33,8,1024]{2,1,0:T(8,128)S(1)}, u32[]{:S(2)}, u32[]{:S(2)}) collective-permute-start(f32[33,8,1024]{2,1,0:T(8,128)S(1)} %get-tuple-element.84), channel_id=1, source_target_pairs={{0,24},{1,97},{2,26},{3,99},{4,28},{5,101},{6,30},{7,103},{8,0},{9... | collective-permute-start | bytes 3244040 | tf_op jit(solution)/shard_map/ppermute | solution.py:53
  52.3 22.7 %collective-permute-start.10 = (f32[17,8,1024]{2,1,0:T(8,128)S(1)}, f32[17,8,1024]{2,1,0:T(8,128)S(1)}, u32[]{:S(2)}, u32[]{:S(2)}) collective-permute-start(f32[17,8,1024]{2,1,0:T(8,128)S(1)} %get-tuple-element.95), channel_id=1, source_target_pairs={{0,96},{1,25},{2,98},{3,27},{4,100},{5,29},{6,102},{7,31},{8,104},... | collective-permute-start | bytes 1671176 | tf_op jit(solution)/shard_map/ppermute | solution.py:53
  54.8 20.2 %collective-permute-start.8 = (f32[17,8,1024]{2,1,0:T(8,128)S(1)}, f32[17,8,1024]{2,1,0:T(8,128)S(1)}, u32[]{:S(2)}, u32[]{:S(2)}) collective-permute-start(f32[17,8,1024]{2,1,0:T(8,128)S(1)} %get-tuple-element.93), channel_id=1, source_target_pairs={{0,32},{1,9},{2,34},{3,11},{4,36},{5,13},{6,38},{7,15},{8,40},{9,1... | collective-permute-start | bytes 1671176 | tf_op jit(solution)/shard_map/ppermute | solution.py:53
  54.8 3.2 %copy-start.2 = (s32[1024]{0:T(1024)S(1)}, s32[1024]{0:T(1024)}, u32[]{:S(2)}) copy-start(s32[1024]{0:T(1024)} %param.12) | copy-start | bytes 12292
  54.8 3.2 %copy-start.3 = (s32[1024]{0:T(1024)S(1)}, s32[1024]{0:T(1024)}, u32[]{:S(2)}) copy-start(s32[1024]{0:T(1024)} %param.13) | copy-start | bytes 12292
  54.8 20.2 %collective-permute-start.9 = (f32[17,8,1024]{2,1,0:T(8,128)S(1)}, f32[17,8,1024]{2,1,0:T(8,128)S(1)}, u32[]{:S(2)}, u32[]{:S(2)}) collective-permute-start(f32[17,8,1024]{2,1,0:T(8,128)S(1)} %get-tuple-element.94), channel_id=1, source_target_pairs={{0,64},{1,17},{2,66},{3,19},{4,68},{5,21},{6,70},{7,23},{8,72},{9,... | collective-permute-start | bytes 1671176 | tf_op jit(solution)/shard_map/ppermute | solution.py:53
  56.9 5.7 %collective-permute-start.6 = (f32[32,1024]{1,0:T(8,128)S(1)}, f32[32,1024]{1,0:T(8,128)S(1)}, u32[]{:S(2)}, u32[]{:S(2)}) collective-permute-start(f32[32,1024]{1,0:T(8,128)S(1)} %get-tuple-element.91), channel_id=1, source_target_pairs={{0,8},{1,33},{2,10},{3,35},{4,12},{5,37},{6,14},{7,39},{8,0},{9,41... | collective-permute-start | bytes 393224 | tf_op jit(solution)/shard_map/ppermute | solution.py:53
  62.6 12.3 %collective-permute-start.7 = (f32[32,1024]{1,0:T(8,128)S(1)}, f32[32,1024]{1,0:T(8,128)S(1)}, u32[]{:S(2)}, u32[]{:S(2)}) collective-permute-start(f32[32,1024]{1,0:T(8,128)S(1)} %add.71), channel_id=1, source_target_pairs={{0,24},{1,97},{2,26},{3,99},{4,28},{5,101},{6,30},{7,103},{8,16},{... | collective-permute-start | bytes 393224 | tf_op jit(solution)/shard_map/ppermute | solution.py:53
  75.2 13.9 %collective-permute-start.12 = (f32[8,16,1024]{2,1,0:T(8,128)S(1)}, f32[8,16,1024]{2,1,0:T(8,128)S(1)}, u32[]{:S(2)}, u32[]{:S(2)}) collective-permute-start(f32[8,16,1024]{2,1,0:T(8,128)S(1)} %bitcast.47), channel_id=1, source_target_pairs={{0,64},{1,17},{2,66},{3,19},{4,68},{5,21},{6,70},{7,23},{8,72},{9,... | collective-permute-start | bytes 1572872 | tf_op jit(solution)/shard_map/ppermute | solution.py:53
  77.4 13.8 %collective-permute-start.13 = (f32[8,16,1024]{2,1,0:T(8,128)S(1)}, f32[8,16,1024]{2,1,0:T(8,128)S(1)}, u32[]{:S(2)}, u32[]{:S(2)}) collective-permute-start(f32[8,16,1024]{2,1,0:T(8,128)S(1)} %bitcast.48), channel_id=1, source_target_pairs={{0,32},{1,9},{2,34},{3,11},{4,36},{5,13},{6,38},{7,15},{8,40},{9,1... | collective-permute-start | bytes 1572872 | tf_op jit(solution)/shard_map/ppermute | solution.py:53
  77.7 13.5 %collective-permute-start.11 = (f32[8,16,1024]{2,1,0:T(8,128)S(1)}, f32[8,16,1024]{2,1,0:T(8,128)S(1)}, u32[]{:S(2)}, u32[]{:S(2)}) collective-permute-start(f32[8,16,1024]{2,1,0:T(8,128)S(1)} %bitcast.49), channel_id=1, source_target_pairs={{0,96},{1,25},{2,98},{3,27},{4,100},{5,29},{6,102},{7,31},{8,104},... | collective-permute-start | bytes 1572872 | tf_op jit(solution)/shard_map/ppermute | solution.py:53
  80.9 3.6 %collective-permute-start.14 = (f32[64,128]{1,0:T(8,128)S(1)}, f32[64,128]{1,0:T(8,128)S(1)}, u32[]{:S(2)}, u32[]{:S(2)}) collective-permute-start(f32[64,128]{1,0:T(8,128)S(1)} %get-tuple-element.96), channel_id=1, source_target_pairs={{0,8},{1,33},{2,10},{3,35},{4,12},{5,37},{6,14},{7,39},{8,0},{9,41... | collective-permute-start | bytes 98312 | tf_op jit(solution)/shard_map/ppermute | solution.py:53
  84.5 4.7 %collective-permute-start.15 = (f32[64,128]{1,0:T(8,128)S(1)}, f32[64,128]{1,0:T(8,128)S(1)}, u32[]{:S(2)}, u32[]{:S(2)}) collective-permute-start(f32[64,128]{1,0:T(8,128)S(1)} %add.76), channel_id=1, source_target_pairs={{0,24},{1,97},{2,26},{3,99},{4,28},{5,101},{6,30},{7,103},{8,16},{... | collective-permute-start | bytes 98312 | tf_op jit(solution)/shard_map/ppermute | solution.py:53
  91.3 15.6 %collective-permute-start.16 = (f32[2,8,16,1024]{3,2,1,0:T(8,128)S(1)}, f32[2,8,16,1024]{3,2,1,0:T(8,128)S(1)}, u32[]{:S(2)}, u32[]{:S(2)}) collective-permute-start(f32[2,8,16,1024]{3,2,1,0:T(8,128)S(1)} %pad_maximum_fusion.refs_0_), channel_id=1, source_target_pairs={{0,8},{1,33},{2,10},{3,35},{4,12},{5,37},{6,14},{7,39},{8,16},{9,4... | collective-permute-start | bytes 3145736 | tf_op jit(solution)/shard_map/ppermute | solution.py:53
  91.4 15.5 %collective-permute-start.17 = (f32[2,8,16,1024]{3,2,1,0:T(8,128)S(1)}, f32[2,8,16,1024]{3,2,1,0:T(8,128)S(1)}, u32[]{:S(2)}, u32[]{:S(2)}) collective-permute-start(f32[2,8,16,1024]{3,2,1,0:T(8,128)S(1)} %pad_maximum_fusion.1.refs_1_), channel_id=1, source_target_pairs={{0,24},{1,97},{2,26},{3,99},{4,28},{5,101},{6,30},{7,103},{8,0},{9... | collective-permute-start | bytes 3145736 | tf_op jit(solution)/shard_map/ppermute | solution.py:53
  94.0 3.4 %collective-permute-start.18 = (f32[64,128]{1,0:T(8,128)S(1)}, f32[64,128]{1,0:T(8,128)S(1)}, u32[]{:S(2)}, u32[]{:S(2)}) collective-permute-start(f32[64,128]{1,0:T(8,128)S(1)} %add.77), channel_id=1, source_target_pairs={{0,32},{1,9},{2,34},{3,11},{4,36},{5,13},{6,38},{7,15},{8,40},{9,1... | collective-permute-start | bytes 98312 | tf_op jit(solution)/shard_map/ppermute | solution.py:53
  97.5 4.7 %collective-permute-start.19 = (f32[64,128]{1,0:T(8,128)S(1)}, f32[64,128]{1,0:T(8,128)S(1)}, u32[]{:S(2)}, u32[]{:S(2)}) collective-permute-start(f32[64,128]{1,0:T(8,128)S(1)} %add.78), channel_id=1, source_target_pairs={{0,96},{1,25},{2,98},{3,27},{4,100},{5,29},{6,102},{7,31},{8,104},... | collective-permute-start | bytes 98312 | tf_op jit(solution)/shard_map/ppermute | solution.py:53
  99.1 19.0 %collective-permute-start.24 = (f32[2,8,16,1024]{3,2,1,0:T(8,128)S(1)}, f32[2,8,16,1024]{3,2,1,0:T(8,128)S(1)}, u32[]{:S(2)}, u32[]{:S(2)}) collective-permute-start(f32[2,8,16,1024]{3,2,1,0:T(8,128)S(1)} %pad_maximum_fusion.1.refs_1_), channel_id=1, source_target_pairs={{0,8},{1,33},{2,10},{3,35},{4,12},{5,37},{6,14},{7,39},{8,16},{9,4... | collective-permute-start | bytes 3145736 | tf_op jit(solution)/shard_map/ppermute | solution.py:53
  99.1 19.0 %collective-permute-start.25 = (f32[2,8,16,1024]{3,2,1,0:T(8,128)S(1)}, f32[2,8,16,1024]{3,2,1,0:T(8,128)S(1)}, u32[]{:S(2)}, u32[]{:S(2)}) collective-permute-start(f32[2,8,16,1024]{3,2,1,0:T(8,128)S(1)} %pad_maximum_fusion.refs_0_), channel_id=1, source_target_pairs={{0,24},{1,97},{2,26},{3,99},{4,28},{5,101},{6,30},{7,103},{8,0},{9... | collective-permute-start | bytes 3145736 | tf_op jit(solution)/shard_map/ppermute | solution.py:53
  106.9 22.5 %collective-permute-start.20 = (f32[2,8,16,1024]{3,2,1,0:T(8,128)S(1)}, f32[2,8,16,1024]{3,2,1,0:T(8,128)S(1)}, u32[]{:S(2)}, u32[]{:S(2)}) collective-permute-start(f32[2,8,16,1024]{3,2,1,0:T(8,128)S(1)} %collective-permute-done.16.refs_2_), channel_id=1, source_target_pairs={{0,8},{1,33},{2,10},{3,35},{4,12},{5,37},{6,14},{7,39},{8,16},{9,4... | collective-permute-start | bytes 3145736 | tf_op jit(solution)/shard_map/ppermute | solution.py:53
  106.9 22.5 %collective-permute-start.21 = (f32[2,8,16,1024]{3,2,1,0:T(8,128)S(1)}, f32[2,8,16,1024]{3,2,1,0:T(8,128)S(1)}, u32[]{:S(2)}, u32[]{:S(2)}) collective-permute-start(f32[2,8,16,1024]{3,2,1,0:T(8,128)S(1)} %collective-permute-done.17.refs_5_), channel_id=1, source_target_pairs={{0,24},{1,97},{2,26},{3,99},{4,28},{5,101},{6,30},{7,103},{8,0},{9... | collective-permute-start | bytes 3145736 | tf_op jit(solution)/shard_map/ppermute | solution.py:53
  109.6 3.5 %collective-permute-start.22 = (f32[56,128]{1,0:T(8,128)S(1)}, f32[56,128]{1,0:T(8,128)S(1)}, u32[]{:S(2)}, u32[]{:S(2)}) collective-permute-start(f32[56,128]{1,0:T(8,128)S(1)} %pad_maximum_fusion.2), channel_id=1, source_target_pairs={{0,1},{1,0},{2,3},{3,2},{4,5},{5,4},{6,7},{7,6},{8,9},{9,8},{10,11... | collective-permute-start | bytes 86024 | tf_op jit(solution)/shard_map/ppermute | solution.py:53
  113.0 3.0 %collective-permute-start.23 = (f32[56,128]{1,0:T(8,128)S(1)}, f32[56,128]{1,0:T(8,128)S(1)}, u32[]{:S(2)}, u32[]{:S(2)}) collective-permute-start(f32[56,128]{1,0:T(8,128)S(1)} %fusion.3), channel_id=1, source_target_pairs={{0,2},{1,3},{2,0},{3,1},{4,6},{5,7},{6,4},{7,5},{8,10},{9,11},{10,... | collective-permute-start | bytes 86024 | tf_op jit(solution)/shard_map/ppermute | solution.py:53
  118.1 4.3 %collective-permute-start.26 = (f32[56,128]{1,0:T(8,128)S(1)}, f32[56,128]{1,0:T(8,128)S(1)}, u32[]{:S(2)}, u32[]{:S(2)}) collective-permute-start(f32[56,128]{1,0:T(8,128)S(1)} %add.81), channel_id=1, source_target_pairs={{0,6},{1,7},{2,4},{3,5},{4,2},{5,3},{6,0},{7,1},{8,14},{9,15},{10,... | collective-permute-start | bytes 86024 | tf_op jit(solution)/shard_map/ppermute | solution.py:53
  133.4 5.7 %collective-permute-start.27 = (f32[256,1280]{1,0:T(8,128)S(1)}, f32[256,1280]{1,0:T(8,128)S(1)}, u32[]{:S(2)}, u32[]{:S(2)}) collective-permute-start(f32[256,1280]{1,0:T(8,128)S(1)} %get-tuple-element.109), channel_id=1, source_target_pairs={{0,1},{1,0},{2,3},{3,2},{4,5},{5,4},{6,7},{7,6},{8,9},{9,8},{10,11... | collective-permute-start | bytes 3932168 | tf_op jit(solution)/shard_map/ppermute | solution.py:53
  139.3 20.5 %collective-permute-start.28 = (f32[128,1280]{1,0:T(8,128)S(1)}, f32[128,1280]{1,0:T(8,128)S(1)}, u32[]{:S(2)}, u32[]{:S(2)}) collective-permute-start(f32[128,1280]{1,0:T(8,128)S(1)} %get-tuple-element.150), channel_id=1, source_target_pairs={{0,2},{1,3},{2,4},{3,5},{4,6},{5,7},{6,0},{7,1},{8,10},{9,11},{10,... | collective-permute-start | bytes 1966088 | tf_op jit(solution)/shard_map/ppermute | solution.py:53
  140.7 19.1 %collective-permute-start.29 = (f32[128,1280]{1,0:T(8,128)S(1)}, f32[128,1280]{1,0:T(8,128)S(1)}, u32[]{:S(2)}, u32[]{:S(2)}) collective-permute-start(f32[128,1280]{1,0:T(8,128)S(1)} %get-tuple-element.149), channel_id=1, source_target_pairs={{0,6},{1,7},{2,0},{3,1},{4,2},{5,3},{6,4},{7,5},{8,14},{9,15},{10,... | collective-permute-start | bytes 1966088 | tf_op jit(solution)/shard_map/ppermute | solution.py:53
  152.3 8.3 %collective-permute-start.31 = (f32[256,1280]{1,0:T(8,128)S(1)}, f32[256,1280]{1,0:T(8,128)S(1)}, u32[]{:S(2)}, u32[]{:S(2)}) collective-permute-start(f32[256,1280]{1,0:T(8,128)S(1)} %get-tuple-element.114), channel_id=1, source_target_pairs={{0,1},{1,0},{2,3},{3,2},{4,5},{5,4},{6,7},{7,6},{8,9},{9,8},{10,11... | collective-permute-start | bytes 3932168 | tf_op jit(solution)/shard_map/ppermute | solution.py:53
  152.7 7.9 %collective-permute-start.32 = (f32[256,1280]{1,0:T(8,128)S(1)}, f32[256,1280]{1,0:T(8,128)S(1)}, u32[]{:S(2)}, u32[]{:S(2)}) collective-permute-start(f32[256,1280]{1,0:T(8,128)S(1)} %get-tuple-element.123), channel_id=1, source_target_pairs={{0,1},{1,0},{2,3},{3,2},{4,5},{5,4},{6,7},{7,6},{8,9},{9,8},{10,11... | collective-permute-start | bytes 3932168 | tf_op jit(solution)/shard_map/ppermute | solution.py:53
  152.9 6.7 %collective-permute-start.30 = (f32[32,1024]{1,0:T(8,128)S(1)}, f32[32,1024]{1,0:T(8,128)S(1)}, u32[]{:S(2)}, u32[]{:S(2)}) collective-permute-start(f32[32,1024]{1,0:T(8,128)S(1)} %add.72), channel_id=1, source_target_pairs={{0,32},{1,9},{2,34},{3,11},{4,36},{5,13},{6,38},{7,15},{8,40},{9,1... | collective-permute-start | bytes 393224 | tf_op jit(solution)/shard_map/ppermute | solution.py:53
  159.7 31.3 %collective-permute-start.35 = (f32[256,1280]{1,0:T(8,128)S(1)}, f32[256,1280]{1,0:T(8,128)S(1)}, u32[]{:S(2)}, u32[]{:S(2)}) collective-permute-start(f32[256,1280]{1,0:T(8,128)S(1)} %get-tuple-element.139), channel_id=1, source_target_pairs={{0,1},{1,0},{2,3},{3,2},{4,5},{5,4},{6,7},{7,6},{8,9},{9,8},{10,11... | collective-permute-start | bytes 3932168 | tf_op jit(solution)/shard_map/ppermute | solution.py:53
  161.6 36.3 %collective-permute-start.39 = (f32[256,1280]{1,0:T(8,128)S(1)}, f32[256,1280]{1,0:T(8,128)S(1)}, u32[]{:S(2)}, u32[]{:S(2)}) collective-permute-start(f32[256,1280]{1,0:T(8,128)S(1)} %get-tuple-element.124), channel_id=1, source_target_pairs={{0,2},{1,3},{2,4},{3,5},{4,6},{5,7},{6,0},{7,1},{8,10},{9,11},{10,... | collective-permute-start | bytes 3932168 | tf_op jit(solution)/shard_map/ppermute | solution.py:53
  161.7 36.2 %collective-permute-start.40 = (f32[256,1280]{1,0:T(8,128)S(1)}, f32[256,1280]{1,0:T(8,128)S(1)}, u32[]{:S(2)}, u32[]{:S(2)}) collective-permute-start(f32[256,1280]{1,0:T(8,128)S(1)} %get-tuple-element.125), channel_id=1, source_target_pairs={{0,6},{1,7},{2,0},{3,1},{4,2},{5,3},{6,4},{7,5},{8,14},{9,15},{10,... | collective-permute-start | bytes 3932168 | tf_op jit(solution)/shard_map/ppermute | solution.py:53
  164.4 26.7 %collective-permute-start.33 = (f32[32,1024]{1,0:T(8,128)S(1)}, f32[32,1024]{1,0:T(8,128)S(1)}, u32[]{:S(2)}, u32[]{:S(2)}) collective-permute-start(f32[32,1024]{1,0:T(8,128)S(1)} %add.84), channel_id=1, source_target_pairs={{0,96},{1,25},{2,98},{3,27},{4,100},{5,29},{6,102},{7,31},{8,104},... | collective-permute-start | bytes 393224 | tf_op jit(solution)/shard_map/ppermute | solution.py:53
  169.4 21.7 %collective-permute-start.34 = (f32[8,1280]{1,0:T(8,128)S(1)}, f32[8,1280]{1,0:T(8,128)S(1)}, u32[]{:S(2)}, u32[]{:S(2)}) collective-permute-start(f32[8,1280]{1,0:T(8,128)S(1)} %get-tuple-element.132), channel_id=1, source_target_pairs={{0,1},{1,0},{2,3},{3,2},{4,5},{5,4},{6,7},{7,6},{8,9},{9,8},{10,11... | collective-permute-start | bytes 122888 | tf_op jit(solution)/shard_map/ppermute | solution.py:53
  191.2 4.1 %collective-permute-start.36 = (f32[8,1280]{1,0:T(8,128)S(1)}, f32[8,1280]{1,0:T(8,128)S(1)}, u32[]{:S(2)}, u32[]{:S(2)}) collective-permute-start(f32[8,1280]{1,0:T(8,128)S(1)} %add.88.last), channel_id=1, source_target_pairs={{0,2},{1,3},{2,4},{3,5},{4,6},{5,7},{6,0},{7,1},{8,10},{9,11},{10,... | collective-permute-start | bytes 122888 | tf_op jit(solution)/shard_map/ppermute | solution.py:53
  191.2 4.5 %collective-permute-start.37 = (f32[8,1280]{1,0:T(8,128)S(1)}, f32[8,1280]{1,0:T(8,128)S(1)}, u32[]{:S(2)}, u32[]{:S(2)}) collective-permute-start(f32[8,1280]{1,0:T(8,128)S(1)} %add.88.last), channel_id=1, source_target_pairs={{0,4},{1,5},{2,6},{3,7},{4,0},{5,1},{6,2},{7,3},{8,12},{9,13},{10,... | collective-permute-start | bytes 122888 | tf_op jit(solution)/shard_map/ppermute | solution.py:53
  192.7 3.9 %collective-permute-start.38 = (f32[8,1280]{1,0:T(8,128)S(1)}, f32[8,1280]{1,0:T(8,128)S(1)}, u32[]{:S(2)}, u32[]{:S(2)}) collective-permute-start(f32[8,1280]{1,0:T(8,128)S(1)} %add.88.last), channel_id=1, source_target_pairs={{0,6},{1,7},{2,0},{3,1},{4,2},{5,3},{6,4},{7,5},{8,14},{9,15},{10,... | collective-permute-start | bytes 122888 | tf_op jit(solution)/shard_map/ppermute | solution.py:53

commit v6 on v5

--- a/solution.py
+++ b/solution.py
@@ -692,7 +692,7 @@
     parts = (scalars[:, 0:1], total[1:2, 1:2], scalars[:, 2:3], count_term, reg_sum / nvalid)
     for index, one in enumerate(parts):
         out = jnp.where(lane == index, one, out)
-    terms[...] = out
+    terms[...] = out[0, :5]
 
 
 def finish_call(last, got, totals, scalars, kind, filt, all_cells):
@@ -700,10 +700,10 @@
         functools.partial(finish_kernel, all_cells=float(all_cells)),
         grid=(1,),
         in_specs=[fixed(one.shape) for one in (last, *got, totals, scalars, kind, filt)],
-        out_specs=[fixed((kind.shape[1] // 128, 128)), fixed((1, 128))],
+        out_specs=[fixed((kind.shape[1] // 128, 128)), fixed((5,))],
         out_shape=[
             jax.ShapeDtypeStruct((kind.shape[1] // 128, 128), F32),
-            jax.ShapeDtypeStruct((1, 128), F32),
+            jax.ShapeDtypeStruct((5,), F32),
         ],
         compiler_params=vmem(4),
         cost_estimate=NO_COST,
@@ -753,7 +753,6 @@
     pieces = [across(piece, step + 1) for step, piece in enumerate(pieces)]
     spatial_squares = jnp.sum(after(spatial, mine) ** 2, axis=0)
     types = types + swap_along(after(types, spatial_squares), 1)
-    types = types + swap_along(types, 3)
     spot_rows = stacked([spot_valid, slide_id.astype(F32), spatial_squares])
     mine = after(mine, spot_rows, types)
     piece = mine + pieces[0] + pieces[1] + pieces[2]
@@ -772,7 +771,8 @@
     )
     sums = sums + swap_along(sums, 1)
     sums = sums + swap_along(sums, 3)
-    mine = after((jnp.stack([piece, got[2]]), jnp.stack([got[1], got[0]])), sums)
+    types = types + swap_along(after(types, slides), 3)
+    mine = after((jnp.stack([piece, got[2]]), jnp.stack([got[1], got[0]])), sums, types)
     right0, left1 = along(mine[0], 1), along(mine[1], -1)
     right1, left0 = along(mine[1], 1), along(mine[0], -1)
     sums = sums + swap_across(after(sums, *mine), 1)
@@ -835,7 +835,7 @@
     grad_filter, loss_terms = finish_call(
         last, got, totals, scalars, cell_type.reshape(1, cells), filter_logits.reshape(1, cells), all_cells
     )
-    return (loss_terms[0, :5], type_fraction, grad_map, grad_filter.reshape(cells), grad_expr)
+    return (loss_terms, type_fraction, grad_map, grad_filter.reshape(cells), grad_expr)
 
 
 def solution(mesh):

time: 200 us -> 199 us (level)
  starting transfers between devices: 54 us -> 61 us
  waiting for transfers between devices: 50.9 us -> 44.6 us
    ppermute x41, starting transfers between devices: 54 us -> 61 us  [send(): return lax.ppermute(array, ('cells', 'spots'), route(target))]
    ppermute x41, waiting for transfers between devices: 50.9 us -> 44.6 us  [send(): return lax.ppermute(array, ('cells', 'spots'), route(target))]
  transfers between devices with their start and end apart: 41 -> 41, of which waited for: 20 -> 18; matrix products, arithmetic and copies ran while one was open for 1% -> 1% of each run, Pallas kernels for 37% -> 37%
where the time goes in v6:
time: 199 us
  Pallas kernels  88.5 us (44%)
  starting transfers between devices  61 us (31%)
  waiting for transfers between devices  44.6 us (22%)
  other arithmetic  3.77 us (2%)
    ppermute x41, starting transfers between devices, send(): return lax.ppermute(array, ('cells', 'spots'), route(target))  61 us
    ppermute x41, waiting for transfers between devices, send(): return lax.ppermute(array, ('cells', 'spots'), route(target))  44.6 us
    pallas_call x5, Pallas kernels, back_call(): pl.pallas_call(functools.partial(back_kernel, parts=parts, first=len(firs...  23 us
    pallas_call x3, Pallas kernels, pred_call(): pl.pallas_call(functools.partial(pred_kernel, cuts=cuts), grid_spec=pltpu...  21.7 us
    pallas_call x1, Pallas kernels, map_call(): pl.pallas_call(functools.partial(map_kernel, scale=scale), grid=(cells //...  21.3 us
    pallas_call x1, Pallas kernels, expo_call(): pl.pallas_call(expo_kernel, grid_spec=pltpu.PrefetchScalarGridSpec(num_sc...  9.85 us
    pallas_call x3, Pallas kernels, grad_call(): pl.pallas_call(functools.partial(grad_kernel, count=count, lane=lane, chi...  7.63 us
  transfers between devices with their start and end apart: 41, of which 18 were waited for; matrix products, arithmetic and copies ran while one was open for 1% of the time, Pallas kernels for 37%

profile of v6, /device:TPU:1, one launch (start us, length us, event | category | flops | bytes accessed | tf_op | source)
XLA Modules:
  0.0 199.2 jit_solution(17540441232608370164)
XLA Ops:
  0.7 9.9 %expo.1 = (bf16[2,1280,1024]{2,1,0:T(8,128)(2,1)S(1)}, f32[32,1024]{1,0:T(8,128)S(1)}, f32[8,1024]{1,0:T(8,128)S(1)}, f32[33,8,1024]{2,1,0:T(8,128)S(1)}, f32[33,8,1024]{2,1,0:T(8,128)S(1)}) custom-call(s32[4]{0:T(128)S(1)} %pad_add_fusion.ids, f32[1280,1024]{1,0:T(8,128)} %logits.1, s32[10,128]{1,0:T(8,128)} %bitcast.64, f32[10,128]{1,0:T(8,128)} %bitcast.65, ...), custom_call_target="tpu_custom_call" | custom-call | bytes 1310720 | tf_op jit(solution)/shard_map/expo/pallas_call | solution.py:176
  10.6 2.5 %collective-permute-start = (f32[33,8,1024]{2,1,0:T(8,128)S(1)}, f32[33,8,1024]{2,1,0:T(8,128)S(1)}, u32[]{:S(2)}, u32[]{:S(2)}) collective-permute-start(f32[33,8,1024]{2,1,0:T(8,128)S(1)} %get-tuple-element.76), channel_id=1, source_target_pairs={{0,8},{1,33},{2,10},{3,35},{4,12},{5,37},{6,14},{7,39},{8,16},{9,4... | collective-permute-start | bytes 3244040 | tf_op jit(solution)/shard_map/ppermute | solution.py:53
  13.1 2.3 %collective-permute-start.1 = (f32[33,8,1024]{2,1,0:T(8,128)S(1)}, f32[33,8,1024]{2,1,0:T(8,128)S(1)}, u32[]{:S(2)}, u32[]{:S(2)}) collective-permute-start(f32[33,8,1024]{2,1,0:T(8,128)S(1)} %get-tuple-element.77), channel_id=1, source_target_pairs={{0,24},{1,97},{2,26},{3,99},{4,28},{5,101},{6,30},{7,103},{8,0},{9... | collective-permute-start | bytes 3244040 | tf_op jit(solution)/shard_map/ppermute | solution.py:53
  15.4 7.5 %pred_.3 = (f32[33,8,1024]{2,1,0:T(8,128)S(1)}, f32[33,8,1024]{2,1,0:T(8,128)S(1)}) custom-call(s32[4]{0:T(128)S(1)} %pad_add_fusion.ids, f32[8,16,16,1280]{3,2,1,0:T(8,128)} %bitcast.55, f32[8,16,16,1280]{3,2,1,0:T(8,128)} %bitcast.56, f32[1,1280]{1,0:T(1,128)S(1)} %reshape.94.keep, bf16[2,1280,1024]{2,1,0:T(8,128)(2,1)S(1)} %get-tuple-element.79.masses, ...), custom_call_target="tpu_custom_call" | custom-call | flops 503316480 | bytes 1245184 | tf_op jit(solution)/shard_map/pred/pallas_call | solution.py:249
  22.9 1.4 collective-permute-start.2
  24.5 3.6 %collective-permute-done.refs_0_ = f32[33,8,1024]{2,1,0:T(8,128)S(1)} collective-permute-done((f32[33,8,1024]{2,1,0:T(8,128)S(1)}, f32[33,8,1024]{2,1,0:T(8,128)S(1)}, u32[]{:S(2)}, u32[]{:S(2)}) %collective-permute-start) | collective-permute-done | bytes 1081376 | tf_op jit(solution)/shard_map/ppermute | solution.py:53
  28.0 6.6 %pred_.4 = (f32[33,8,1024]{2,1,0:T(8,128)S(1)}, f32[33,8,1024]{2,1,0:T(8,128)S(1)}) custom-call(s32[4]{0:T(128)S(1)} %pad_add_fusion.ids, f32[8,16,16,1280]{3,2,1,0:T(8,128)} %bitcast.57, f32[8,16,16,1280]{3,2,1,0:T(8,128)} %bitcast.58, f32[1,1280]{1,0:T(1,128)S(1)} %reshape.94.keep, bf16[2,1280,1024]{2,1,0:T(8,128)(2,1)S(1)} %get-tuple-element.79.masses, ...), custom_call_target="tpu_custom_call" | custom-call | flops 503316480 | bytes 1245184 | tf_op jit(solution)/shard_map/pred/pallas_call | solution.py:249
  35.7 1.9 collective-permute-start.5
  37.8 1.4 collective-permute-done.2.refs_0_
  39.9 7.6 %pred_.5 = (f32[33,8,1024]{2,1,0:T(8,128)S(1)}, f32[33,8,1024]{2,1,0:T(8,128)S(1)}) custom-call(s32[4]{0:T(128)S(1)} %pad_add_fusion.ids, f32[8,16,16,1280]{3,2,1,0:T(8,128)} %bitcast.59, f32[8,16,16,1280]{3,2,1,0:T(8,128)} %bitcast.60, f32[1,1280]{1,0:T(1,128)S(1)} %reshape.94.keep, bf16[2,1280,1024]{2,1,0:T(8,128)(2,1)S(1)} %get-tuple-element.79.masses, ...), custom_call_target="tpu_custom_call" | custom-call | flops 503316480 | bytes 1245184 | tf_op jit(solution)/shard_map/pred/pallas_call | solution.py:249
  47.5 4.0 %collective-permute-done.4.got0 = f32[33,8,1024]{2,1,0:T(8,128)S(1)} collective-permute-done((f32[33,8,1024]{2,1,0:T(8,128)S(1)}, f32[33,8,1024]{2,1,0:T(8,128)S(1)}, u32[]{:S(2)}, u32[]{:S(2)}) %collective-permute-start.4) | collective-permute-done | bytes 1081376 | tf_op jit(solution)/shard_map/ppermute | solution.py:53
  53.3 2.7 %collective-permute-start.8 = (f32[17,8,1024]{2,1,0:T(8,128)S(1)}, f32[17,8,1024]{2,1,0:T(8,128)S(1)}, u32[]{:S(2)}, u32[]{:S(2)}) collective-permute-start(f32[17,8,1024]{2,1,0:T(8,128)S(1)} %get-tuple-element.95), channel_id=1, source_target_pairs={{0,64},{1,17},{2,66},{3,19},{4,68},{5,21},{6,70},{7,23},{8,72},{9,... | collective-permute-start | bytes 1671176 | tf_op jit(solution)/shard_map/ppermute | solution.py:53
  57.6 1.1 collective-permute-start.6
  58.7 4.4 %collective-permute-done.6 = f32[32,1024]{1,0:T(8,128)S(1)} collective-permute-done((f32[32,1024]{1,0:T(8,128)S(1)}, f32[32,1024]{1,0:T(8,128)S(1)}, u32[]{:S(2)}, u32[]{:S(2)}) %collective-permute-start.6) | collective-permute-done | bytes 131104 | tf_op jit(solution)/shard_map/ppermute | solution.py:53
  63.1 7.5 %collective-permute-done.8 = f32[17,8,1024]{2,1,0:T(8,128)S(1)} collective-permute-done((f32[17,8,1024]{2,1,0:T(8,128)S(1)}, f32[17,8,1024]{2,1,0:T(8,128)S(1)}, u32[]{:S(2)}, u32[]{:S(2)}) %collective-permute-start.8) | collective-permute-done | bytes 557088 | tf_op jit(solution)/shard_map/ppermute | solution.py:53
  70.8 2.2 %collective-permute-start.11 = (f32[8,16,1024]{2,1,0:T(8,128)S(1)}, f32[8,16,1024]{2,1,0:T(8,128)S(1)}, u32[]{:S(2)}, u32[]{:S(2)}) collective-permute-start(f32[8,16,1024]{2,1,0:T(8,128)S(1)} %bitcast.45), channel_id=1, source_target_pairs={{0,64},{1,17},{2,66},{3,19},{4,68},{5,21},{6,70},{7,23},{8,72},{9,... | collective-permute-start | bytes 1572872 | tf_op jit(solution)/shard_map/ppermute | solution.py:53
  73.0 2.7 %collective-permute-start.10 = (f32[8,16,1024]{2,1,0:T(8,128)S(1)}, f32[8,16,1024]{2,1,0:T(8,128)S(1)}, u32[]{:S(2)}, u32[]{:S(2)}) collective-permute-start(f32[8,16,1024]{2,1,0:T(8,128)S(1)} %bitcast.47), channel_id=1, source_target_pairs={{0,96},{1,25},{2,98},{3,27},{4,100},{5,29},{6,102},{7,31},{8,104},... | collective-permute-start | bytes 1572872 | tf_op jit(solution)/shard_map/ppermute | solution.py:53
  76.6 2.9 %collective-permute-start.15 = (f32[32,1024]{1,0:T(8,128)S(1)}, f32[32,1024]{1,0:T(8,128)S(1)}, u32[]{:S(2)}, u32[]{:S(2)}) collective-permute-start(f32[32,1024]{1,0:T(8,128)S(1)} %add.71), channel_id=1, source_target_pairs={{0,24},{1,97},{2,26},{3,99},{4,28},{5,101},{6,30},{7,103},{8,16},{... | collective-permute-start | bytes 393224 | tf_op jit(solution)/shard_map/ppermute | solution.py:53
  79.4 3.5 %collective-permute-done.13 = f32[64,128]{1,0:T(8,128)S(1)} collective-permute-done((f32[64,128]{1,0:T(8,128)S(1)}, f32[64,128]{1,0:T(8,128)S(1)}, u32[]{:S(2)}, u32[]{:S(2)}) %collective-permute-start.13) | collective-permute-done | bytes 32800 | tf_op jit(solution)/shard_map/ppermute | solution.py:53
  83.0 4.9 %collective-permute-done.14 = f32[64,128]{1,0:T(8,128)S(1)} collective-permute-done((f32[64,128]{1,0:T(8,128)S(1)}, f32[64,128]{1,0:T(8,128)S(1)}, u32[]{:S(2)}, u32[]{:S(2)}) %collective-permute-start.14) | collective-permute-done | bytes 32800 | tf_op jit(solution)/shard_map/ppermute | solution.py:53
  88.3 2.7 %collective-permute-start.17 = (f32[2,8,16,1024]{3,2,1,0:T(8,128)S(1)}, f32[2,8,16,1024]{3,2,1,0:T(8,128)S(1)}, u32[]{:S(2)}, u32[]{:S(2)}) collective-permute-start(f32[2,8,16,1024]{3,2,1,0:T(8,128)S(1)} %pad_maximum_fusion.1.refs_1_), channel_id=1, source_target_pairs={{0,24},{1,97},{2,26},{3,99},{4,28},{5,101},{6,30},{7,103},{8,0},{9... | collective-permute-start | bytes 3145736 | tf_op jit(solution)/shard_map/ppermute | solution.py:53
  91.1 2.6 %collective-permute-done.18 = f32[64,128]{1,0:T(8,128)S(1)} collective-permute-done((f32[64,128]{1,0:T(8,128)S(1)}, f32[64,128]{1,0:T(8,128)S(1)}, u32[]{:S(2)}, u32[]{:S(2)}) %collective-permute-start.18) | collective-permute-done | bytes 32800 | tf_op jit(solution)/shard_map/ppermute | solution.py:53
  93.7 1.5 collective-permute-start.19
  95.2 2.7 %collective-permute-start.25 = (f32[2,8,16,1024]{3,2,1,0:T(8,128)S(1)}, f32[2,8,16,1024]{3,2,1,0:T(8,128)S(1)}, u32[]{:S(2)}, u32[]{:S(2)}) collective-permute-start(f32[2,8,16,1024]{3,2,1,0:T(8,128)S(1)} %pad_maximum_fusion.refs_0_), channel_id=1, source_target_pairs={{0,24},{1,97},{2,26},{3,99},{4,28},{5,101},{6,30},{7,103},{8,0},{9... | collective-permute-start | bytes 3145736 | tf_op jit(solution)/shard_map/ppermute | solution.py:53
  98.3 5.1 %collective-permute-done.16.refs_2_ = f32[2,8,16,1024]{3,2,1,0:T(8,128)S(1)} collective-permute-done((f32[2,8,16,1024]{3,2,1,0:T(8,128)S(1)}, f32[2,8,16,1024]{3,2,1,0:T(8,128)S(1)}, u32[]{:S(2)}, u32[]{:S(2)}) %collective-permute-start.16) | collective-permute-done | bytes 1048608 | tf_op jit(solution)/shard_map/ppermute | solution.py:53
  103.4 1.2 collective-permute-start.20
  104.6 1.9 collective-permute-start.21
  106.4 5.6 %collective-permute-start.22 = (f32[56,128]{1,0:T(8,128)S(1)}, f32[56,128]{1,0:T(8,128)S(1)}, u32[]{:S(2)}, u32[]{:S(2)}) collective-permute-start(f32[56,128]{1,0:T(8,128)S(1)} %pad_maximum_fusion.2), channel_id=1, source_target_pairs={{0,1},{1,0},{2,3},{3,2},{4,5},{5,4},{6,7},{7,6},{8,9},{9,8},{10,11... | collective-permute-start | bytes 86024 | tf_op jit(solution)/shard_map/ppermute | solution.py:53
  112.9 1.3 collective-permute-start.23
  114.2 1.7 collective-permute-done.23
  116.0 2.8 %collective-permute-start.26 = (f32[56,128]{1,0:T(8,128)S(1)}, f32[56,128]{1,0:T(8,128)S(1)}, u32[]{:S(2)}, u32[]{:S(2)}) collective-permute-start(f32[56,128]{1,0:T(8,128)S(1)} %add.81), channel_id=1, source_target_pairs={{0,6},{1,7},{2,4},{3,5},{4,2},{5,3},{6,0},{7,1},{8,14},{9,15},{10,... | collective-permute-start | bytes 86024 | tf_op jit(solution)/shard_map/ppermute | solution.py:53
  118.8 1.6 collective-permute-done.26
  121.2 4.7 %grad.3 = (bf16[2,8,256,1024]{3,2,1,0:T(8,128)(2,1)S(1)}, f32[8,1024]{1,0:T(8,128)S(1)}) custom-call(s32[4]{0:T(128)S(1)} %pad_add_fusion.ids, f32[2,8,16,1024]{3,2,1,0:T(8,128)S(1)} %pad_maximum_fusion.refs_0_, f32[2,8,16,1024]{3,2,1,0:T(8,128)S(1)} %pad_maximum_fusion.1.refs_1_, f32[2,8,16,1024]{3,2,1,0:T(8,128)S(1)} %collective-permute-done.16.refs_2_, ...), custom_call_target="tpu_custom_call" | custom-call | tf_op jit(solution)/shard_map/grad/pallas_call | solution.py:474
  127.2 3.1 %back.5 = (f32[8,1280]{1,0:T(8,128)S(1)}, f32[256,1280]{1,0:T(8,128)S(1)}) custom-call(s32[4]{0:T(128)S(1)} %pad_add_fusion.ids, bf16[2,8,256,1024]{3,2,1,0:T(8,128)(2,1)S(1)} %get-tuple-element.110.grad.refs_5_, bf16[2,1280,1024]{2,1,0:T(8,128)(2,1)S(1)} %get-tuple-element.79.masses, f32[2048,1280]{1,0:T(8,128)} %expr.11, ...), custom_call_target="tpu_custom_call" | custom-call | tf_op jit(solution)/shard_map/back/pallas_call | solution.py:550
  130.3 5.2 %collective-permute-start.27 = (f32[256,1280]{1,0:T(8,128)S(1)}, f32[256,1280]{1,0:T(8,128)S(1)}, u32[]{:S(2)}, u32[]{:S(2)}) collective-permute-start(f32[256,1280]{1,0:T(8,128)S(1)} %get-tuple-element.111), channel_id=1, source_target_pairs={{0,1},{1,0},{2,3},{3,2},{4,5},{5,4},{6,7},{7,6},{8,9},{9,8},{10,11... | collective-permute-start | bytes 3932168 | tf_op jit(solution)/shard_map/ppermute | solution.py:53
  135.4 3.6 %back.6 = (f32[8,1280]{1,0:T(8,128)S(1)}, f32[256,1280]{1,0:T(8,128)S(1)}) custom-call(s32[4]{0:T(128)S(1)} %pad_add_fusion.ids, bf16[2,8,256,1024]{3,2,1,0:T(8,128)(2,1)S(1)} %get-tuple-element.110.grad.refs_5_, bf16[2,1280,1024]{2,1,0:T(8,128)(2,1)S(1)} %get-tuple-element.79.masses, f32[2048,1280]{1,0:T(8,128)} %expr.11), custom_call_target="tpu_custom_call" | custom-call | tf_op jit(solution)/shard_map/back/pallas_call | solution.py:550
  139.2 1.4 collective-permute-start.28
  140.6 1.7 collective-permute-start.29
  142.3 1.9 grad.5
  144.3 8.0 %back.7 = (f32[8,1280]{1,0:T(8,128)S(1)}, f32[256,1280]{1,0:T(8,128)S(1)}, f32[256,1280]{1,0:T(8,128)S(1)}, f32[256,1280]{1,0:T(8,128)S(1)}) custom-call(s32[4]{0:T(128)S(1)} %pad_add_fusion.ids, bf16[2,8,256,1024]{3,2,1,0:T(8,128)(2,1)S(1)} %get-tuple-element.115.grad, bf16[2,1280,1024]{2,1,0:T(8,128)(2,1)S(1)} %get-tuple-element.79.masses, f32[2048,1280]{1,0:T(8,128)} %expr.11), custom_call_target="tpu_custom_call" | custom-call | tf_op jit(solution)/shard_map/back/pallas_call | solution.py:550
  152.9 5.5 %back.8 = (f32[8,1280]{1,0:T(8,128)S(1)}, f32[256,1280]{1,0:T(8,128)S(1)}, f32[256,1280]{1,0:T(8,128)S(1)}) custom-call(s32[4]{0:T(128)S(1)} %pad_add_fusion.ids, bf16[2,8,256,1024]{3,2,1,0:T(8,128)(2,1)S(1)} %get-tuple-element.115.grad, bf16[2,1280,1024]{2,1,0:T(8,128)(2,1)S(1)} %get-tuple-element.79.masses, f32[2048,1280]{1,0:T(8,128)} %expr.11), custom_call_target="tpu_custom_call" | custom-call | tf_op jit(solution)/shard_map/back/pallas_call | solution.py:550
  160.6 2.7 %collective-permute-start.40 = (f32[256,1280]{1,0:T(8,128)S(1)}, f32[256,1280]{1,0:T(8,128)S(1)}, u32[]{:S(2)}, u32[]{:S(2)}) collective-permute-start(f32[256,1280]{1,0:T(8,128)S(1)} %get-tuple-element.127), channel_id=1, source_target_pairs={{0,6},{1,7},{2,0},{3,1},{4,2},{5,3},{6,4},{7,5},{8,14},{9,15},{10,... | collective-permute-start | bytes 3932168 | tf_op jit(solution)/shard_map/ppermute | solution.py:53
  163.4 2.6 %collective-permute-start.33 = (f32[32,1024]{1,0:T(8,128)S(1)}, f32[32,1024]{1,0:T(8,128)S(1)}, u32[]{:S(2)}, u32[]{:S(2)}) collective-permute-start(f32[32,1024]{1,0:T(8,128)S(1)} %add.84), channel_id=1, source_target_pairs={{0,96},{1,25},{2,98},{3,27},{4,100},{5,29},{6,102},{7,31},{8,104},... | collective-permute-start | bytes 393224 | tf_op jit(solution)/shard_map/ppermute | solution.py:53
  166.0 3.0 %back.9 = (f32[8,1280]{1,0:T(8,128)S(1)}, f32[256,1280]{1,0:T(8,128)S(1)}) custom-call(s32[4]{0:T(128)S(1)} %pad_add_fusion.ids, bf16[2,8,256,1024]{3,2,1,0:T(8,128)(2,1)S(1)} %get-tuple-element.115.grad, bf16[2,1280,1024]{2,1,0:T(8,128)(2,1)S(1)} %get-tuple-element.79.masses, f32[2048,1280]{1,0:T(8,128)} %expr.11, ...), custom_call_target="tpu_custom_call" | custom-call | tf_op jit(solution)/shard_map/back/pallas_call | solution.py:550
  169.9 21.3 %grad_map.1 = f32[1280,1024]{1,0:T(8,128)} custom-call(f32[2048,1280]{1,0:T(8,128)} %expr.11, bf16[2,2048,1024]{2,1,0:T(8,128)(2,1)S(1)} %bitcast.36, bf16[2,1280,1024]{2,1,0:T(8,128)(2,1)S(1)} %get-tuple-element.79.masses, f32[10,128]{1,0:T(8,128)S(1)} %bitcast.50, f32[8,1024]{1,0:T(8,128)S(1)} %select_select_fusion.spot), custom_call_target="tpu_custom_call" | custom-call | tf_op jit(solution)/shard_map/grad_map/pallas_call | solution.py:656
  191.5 1.4 collective-permute-start.37
  192.9 1.3 collective-permute-start.38
  197.8 1.4 add_multiply_fusion
  (103 shorter events, 18.4 us)
Async XLA Ops:
  0.7 14.7 %copy-start = (s32[1280]{0:T(1024)S(1)}, s32[1280]{0:T(1024)}, u32[]{:S(2)}) copy-start(s32[1280]{0:T(1024)} %param.11) | copy-start | bytes 15364
  0.7 14.7 %copy-start.1 = (f32[1280]{0:T(1024)S(1)}, f32[1280]{0:T(1024)}, u32[]{:S(2)}) copy-start(f32[1280]{0:T(1024)} %param.8) | copy-start | bytes 15364
  10.6 17.5 %collective-permute-start = (f32[33,8,1024]{2,1,0:T(8,128)S(1)}, f32[33,8,1024]{2,1,0:T(8,128)S(1)}, u32[]{:S(2)}, u32[]{:S(2)}) collective-permute-start(f32[33,8,1024]{2,1,0:T(8,128)S(1)} %get-tuple-element.76), channel_id=1, source_target_pairs={{0,8},{1,33},{2,10},{3,35},{4,12},{5,37},{6,14},{7,39},{8,16},{9,4... | collective-permute-start | bytes 3244040 | tf_op jit(solution)/shard_map/ppermute | solution.py:53
  13.1 14.9 %collective-permute-start.1 = (f32[33,8,1024]{2,1,0:T(8,128)S(1)}, f32[33,8,1024]{2,1,0:T(8,128)S(1)}, u32[]{:S(2)}, u32[]{:S(2)}) collective-permute-start(f32[33,8,1024]{2,1,0:T(8,128)S(1)} %get-tuple-element.77), channel_id=1, source_target_pairs={{0,24},{1,97},{2,26},{3,99},{4,28},{5,101},{6,30},{7,103},{8,0},{9... | collective-permute-start | bytes 3244040 | tf_op jit(solution)/shard_map/ppermute | solution.py:53
  22.9 16.2 %collective-permute-start.2 = (f32[33,8,1024]{2,1,0:T(8,128)S(1)}, f32[33,8,1024]{2,1,0:T(8,128)S(1)}, u32[]{:S(2)}, u32[]{:S(2)}) collective-permute-start(f32[33,8,1024]{2,1,0:T(8,128)S(1)} %get-tuple-element.82), channel_id=1, source_target_pairs={{0,24},{1,97},{2,26},{3,99},{4,28},{5,101},{6,30},{7,103},{8,0},{9... | collective-permute-start | bytes 3244040 | tf_op jit(solution)/shard_map/ppermute | solution.py:53
  24.4 13.3 %copy-start.2 = (s32[1024]{0:T(1024)S(1)}, s32[1024]{0:T(1024)}, u32[]{:S(2)}) copy-start(s32[1024]{0:T(1024)} %param.12) | copy-start | bytes 12292
  24.4 13.3 %copy-start.3 = (s32[1024]{0:T(1024)S(1)}, s32[1024]{0:T(1024)}, u32[]{:S(2)}) copy-start(s32[1024]{0:T(1024)} %param.13) | copy-start | bytes 12292
  24.4 15.5 %collective-permute-start.3 = (f32[33,8,1024]{2,1,0:T(8,128)S(1)}, f32[33,8,1024]{2,1,0:T(8,128)S(1)}, u32[]{:S(2)}, u32[]{:S(2)}) collective-permute-start(f32[33,8,1024]{2,1,0:T(8,128)S(1)} %get-tuple-element.81), channel_id=1, source_target_pairs={{0,8},{1,33},{2,10},{3,35},{4,12},{5,37},{6,14},{7,39},{8,16},{9,4... | collective-permute-start | bytes 3244040 | tf_op jit(solution)/shard_map/ppermute | solution.py:53
  34.7 16.8 %collective-permute-start.4 = (f32[33,8,1024]{2,1,0:T(8,128)S(1)}, f32[33,8,1024]{2,1,0:T(8,128)S(1)}, u32[]{:S(2)}, u32[]{:S(2)}) collective-permute-start(f32[33,8,1024]{2,1,0:T(8,128)S(1)} %get-tuple-element.84), channel_id=1, source_target_pairs={{0,8},{1,33},{2,10},{3,35},{4,12},{5,37},{6,14},{7,39},{8,16},{9,4... | collective-permute-start | bytes 3244040 | tf_op jit(solution)/shard_map/ppermute | solution.py:53
  35.7 15.7 %collective-permute-start.5 = (f32[33,8,1024]{2,1,0:T(8,128)S(1)}, f32[33,8,1024]{2,1,0:T(8,128)S(1)}, u32[]{:S(2)}, u32[]{:S(2)}) collective-permute-start(f32[33,8,1024]{2,1,0:T(8,128)S(1)} %get-tuple-element.85), channel_id=1, source_target_pairs={{0,24},{1,97},{2,26},{3,99},{4,28},{5,101},{6,30},{7,103},{8,0},{9... | collective-permute-start | bytes 3244040 | tf_op jit(solution)/shard_map/ppermute | solution.py:53
  37.7 19.2 %slice-start = ((s8[8388608]{0:T(1024)(128)(4,1)}), s8[4194304]{0:T(1024)(128)(4,1)S(1)}, s32[]{:S(2)}) async-start(s8[8388608]{0:T(1024)(128)(4,1)} %bitcast.37), calls=%async_computation | async-start | bytes 8388608
  37.7 19.1 %slice-start.1 = ((s8[8388608]{0:T(1024)(128)(4,1)}), s8[4194304]{0:T(1024)(128)(4,1)S(1)}, s32[]{:S(2)}) async-start(s8[8388608]{0:T(1024)(128)(4,1)} %bitcast.37), calls=%async_computation.1 | async-start | bytes 8388608
  52.3 10.8 %collective-permute-start.7 = (f32[17,8,1024]{2,1,0:T(8,128)S(1)}, f32[17,8,1024]{2,1,0:T(8,128)S(1)}, u32[]{:S(2)}, u32[]{:S(2)}) collective-permute-start(f32[17,8,1024]{2,1,0:T(8,128)S(1)} %get-tuple-element.94), channel_id=1, source_target_pairs={{0,32},{1,9},{2,34},{3,11},{4,36},{5,13},{6,38},{7,15},{8,40},{9,1... | collective-permute-start | bytes 1671176 | tf_op jit(solution)/shard_map/ppermute | solution.py:53
  53.3 17.3 %collective-permute-start.8 = (f32[17,8,1024]{2,1,0:T(8,128)S(1)}, f32[17,8,1024]{2,1,0:T(8,128)S(1)}, u32[]{:S(2)}, u32[]{:S(2)}) collective-permute-start(f32[17,8,1024]{2,1,0:T(8,128)S(1)} %get-tuple-element.95), channel_id=1, source_target_pairs={{0,64},{1,17},{2,66},{3,19},{4,68},{5,21},{6,70},{7,23},{8,72},{9,... | collective-permute-start | bytes 1671176 | tf_op jit(solution)/shard_map/ppermute | solution.py:53
  56.0 14.6 %collective-permute-start.9 = (f32[17,8,1024]{2,1,0:T(8,128)S(1)}, f32[17,8,1024]{2,1,0:T(8,128)S(1)}, u32[]{:S(2)}, u32[]{:S(2)}) collective-permute-start(f32[17,8,1024]{2,1,0:T(8,128)S(1)} %get-tuple-element.96), channel_id=1, source_target_pairs={{0,96},{1,25},{2,98},{3,27},{4,100},{5,29},{6,102},{7,31},{8,104},... | collective-permute-start | bytes 1671176 | tf_op jit(solution)/shard_map/ppermute | solution.py:53
  57.6 5.6 %collective-permute-start.6 = (f32[32,1024]{1,0:T(8,128)S(1)}, f32[32,1024]{1,0:T(8,128)S(1)}, u32[]{:S(2)}, u32[]{:S(2)}) collective-permute-start(f32[32,1024]{1,0:T(8,128)S(1)} %get-tuple-element.92), channel_id=1, source_target_pairs={{0,8},{1,33},{2,10},{3,35},{4,12},{5,37},{6,14},{7,39},{8,0},{9,41... | collective-permute-start | bytes 393224 | tf_op jit(solution)/shard_map/ppermute | solution.py:53
  70.8 17.1 %collective-permute-start.11 = (f32[8,16,1024]{2,1,0:T(8,128)S(1)}, f32[8,16,1024]{2,1,0:T(8,128)S(1)}, u32[]{:S(2)}, u32[]{:S(2)}) collective-permute-start(f32[8,16,1024]{2,1,0:T(8,128)S(1)} %bitcast.45), channel_id=1, source_target_pairs={{0,64},{1,17},{2,66},{3,19},{4,68},{5,21},{6,70},{7,23},{8,72},{9,... | collective-permute-start | bytes 1572872 | tf_op jit(solution)/shard_map/ppermute | solution.py:53
  73.0 15.0 %collective-permute-start.12 = (f32[8,16,1024]{2,1,0:T(8,128)S(1)}, f32[8,16,1024]{2,1,0:T(8,128)S(1)}, u32[]{:S(2)}, u32[]{:S(2)}) collective-permute-start(f32[8,16,1024]{2,1,0:T(8,128)S(1)} %bitcast.46), channel_id=1, source_target_pairs={{0,32},{1,9},{2,34},{3,11},{4,36},{5,13},{6,38},{7,15},{8,40},{9,1... | collective-permute-start | bytes 1572872 | tf_op jit(solution)/shard_map/ppermute | solution.py:53
  73.0 15.1 %collective-permute-start.10 = (f32[8,16,1024]{2,1,0:T(8,128)S(1)}, f32[8,16,1024]{2,1,0:T(8,128)S(1)}, u32[]{:S(2)}, u32[]{:S(2)}) collective-permute-start(f32[8,16,1024]{2,1,0:T(8,128)S(1)} %bitcast.47), channel_id=1, source_target_pairs={{0,96},{1,25},{2,98},{3,27},{4,100},{5,29},{6,102},{7,31},{8,104},... | collective-permute-start | bytes 1572872 | tf_op jit(solution)/shard_map/ppermute | solution.py:53
  76.6 11.4 %collective-permute-start.15 = (f32[32,1024]{1,0:T(8,128)S(1)}, f32[32,1024]{1,0:T(8,128)S(1)}, u32[]{:S(2)}, u32[]{:S(2)}) collective-permute-start(f32[32,1024]{1,0:T(8,128)S(1)} %add.71), channel_id=1, source_target_pairs={{0,24},{1,97},{2,26},{3,99},{4,28},{5,101},{6,30},{7,103},{8,16},{... | collective-permute-start | bytes 393224 | tf_op jit(solution)/shard_map/ppermute | solution.py:53
  79.4 3.5 %collective-permute-start.13 = (f32[64,128]{1,0:T(8,128)S(1)}, f32[64,128]{1,0:T(8,128)S(1)}, u32[]{:S(2)}, u32[]{:S(2)}) collective-permute-start(f32[64,128]{1,0:T(8,128)S(1)} %get-tuple-element.97), channel_id=1, source_target_pairs={{0,8},{1,33},{2,10},{3,35},{4,12},{5,37},{6,14},{7,39},{8,0},{9,41... | collective-permute-start | bytes 98312 | tf_op jit(solution)/shard_map/ppermute | solution.py:53
  82.9 5.0 %collective-permute-start.14 = (f32[64,128]{1,0:T(8,128)S(1)}, f32[64,128]{1,0:T(8,128)S(1)}, u32[]{:S(2)}, u32[]{:S(2)}) collective-permute-start(f32[64,128]{1,0:T(8,128)S(1)} %add.75), channel_id=1, source_target_pairs={{0,24},{1,97},{2,26},{3,99},{4,28},{5,101},{6,30},{7,103},{8,16},{... | collective-permute-start | bytes 98312 | tf_op jit(solution)/shard_map/ppermute | solution.py:53
  88.2 15.2 %collective-permute-start.16 = (f32[2,8,16,1024]{3,2,1,0:T(8,128)S(1)}, f32[2,8,16,1024]{3,2,1,0:T(8,128)S(1)}, u32[]{:S(2)}, u32[]{:S(2)}) collective-permute-start(f32[2,8,16,1024]{3,2,1,0:T(8,128)S(1)} %pad_maximum_fusion.refs_0_), channel_id=1, source_target_pairs={{0,8},{1,33},{2,10},{3,35},{4,12},{5,37},{6,14},{7,39},{8,16},{9,4... | collective-permute-start | bytes 3145736 | tf_op jit(solution)/shard_map/ppermute | solution.py:53
  88.3 15.1 %collective-permute-start.17 = (f32[2,8,16,1024]{3,2,1,0:T(8,128)S(1)}, f32[2,8,16,1024]{3,2,1,0:T(8,128)S(1)}, u32[]{:S(2)}, u32[]{:S(2)}) collective-permute-start(f32[2,8,16,1024]{3,2,1,0:T(8,128)S(1)} %pad_maximum_fusion.1.refs_1_), channel_id=1, source_target_pairs={{0,24},{1,97},{2,26},{3,99},{4,28},{5,101},{6,30},{7,103},{8,0},{9... | collective-permute-start | bytes 3145736 | tf_op jit(solution)/shard_map/ppermute | solution.py:53
  90.9 2.8 %collective-permute-start.18 = (f32[64,128]{1,0:T(8,128)S(1)}, f32[64,128]{1,0:T(8,128)S(1)}, u32[]{:S(2)}, u32[]{:S(2)}) collective-permute-start(f32[64,128]{1,0:T(8,128)S(1)} %add.76), channel_id=1, source_target_pairs={{0,32},{1,9},{2,34},{3,11},{4,36},{5,13},{6,38},{7,15},{8,40},{9,1... | collective-permute-start | bytes 98312 | tf_op jit(solution)/shard_map/ppermute | solution.py:53
  93.7 4.6 %collective-permute-start.19 = (f32[64,128]{1,0:T(8,128)S(1)}, f32[64,128]{1,0:T(8,128)S(1)}, u32[]{:S(2)}, u32[]{:S(2)}) collective-permute-start(f32[64,128]{1,0:T(8,128)S(1)} %add.78), channel_id=1, source_target_pairs={{0,96},{1,25},{2,98},{3,27},{4,100},{5,29},{6,102},{7,31},{8,104},... | collective-permute-start | bytes 98312 | tf_op jit(solution)/shard_map/ppermute | solution.py:53
  95.2 20.7 %collective-permute-start.24 = (f32[2,8,16,1024]{3,2,1,0:T(8,128)S(1)}, f32[2,8,16,1024]{3,2,1,0:T(8,128)S(1)}, u32[]{:S(2)}, u32[]{:S(2)}) collective-permute-start(f32[2,8,16,1024]{3,2,1,0:T(8,128)S(1)} %pad_maximum_fusion.1.refs_1_), channel_id=1, source_target_pairs={{0,8},{1,33},{2,10},{3,35},{4,12},{5,37},{6,14},{7,39},{8,16},{9,4... | collective-permute-start | bytes 3145736 | tf_op jit(solution)/shard_map/ppermute | solution.py:53
  95.2 20.7 %collective-permute-start.25 = (f32[2,8,16,1024]{3,2,1,0:T(8,128)S(1)}, f32[2,8,16,1024]{3,2,1,0:T(8,128)S(1)}, u32[]{:S(2)}, u32[]{:S(2)}) collective-permute-start(f32[2,8,16,1024]{3,2,1,0:T(8,128)S(1)} %pad_maximum_fusion.refs_0_), channel_id=1, source_target_pairs={{0,24},{1,97},{2,26},{3,99},{4,28},{5,101},{6,30},{7,103},{8,0},{9... | collective-permute-start | bytes 3145736 | tf_op jit(solution)/shard_map/ppermute | solution.py:53
  103.4 22.8 %collective-permute-start.20 = (f32[2,8,16,1024]{3,2,1,0:T(8,128)S(1)}, f32[2,8,16,1024]{3,2,1,0:T(8,128)S(1)}, u32[]{:S(2)}, u32[]{:S(2)}) collective-permute-start(f32[2,8,16,1024]{3,2,1,0:T(8,128)S(1)} %collective-permute-done.16.refs_2_), channel_id=1, source_target_pairs={{0,8},{1,33},{2,10},{3,35},{4,12},{5,37},{6,14},{7,39},{8,16},{9,4... | collective-permute-start | bytes 3145736 | tf_op jit(solution)/shard_map/ppermute | solution.py:53
  104.6 21.6 %collective-permute-start.21 = (f32[2,8,16,1024]{3,2,1,0:T(8,128)S(1)}, f32[2,8,16,1024]{3,2,1,0:T(8,128)S(1)}, u32[]{:S(2)}, u32[]{:S(2)}) collective-permute-start(f32[2,8,16,1024]{3,2,1,0:T(8,128)S(1)} %collective-permute-done.17.refs_5_), channel_id=1, source_target_pairs={{0,24},{1,97},{2,26},{3,99},{4,28},{5,101},{6,30},{7,103},{8,0},{9... | collective-permute-start | bytes 3145736 | tf_op jit(solution)/shard_map/ppermute | solution.py:53
  106.4 6.5 %collective-permute-start.22 = (f32[56,128]{1,0:T(8,128)S(1)}, f32[56,128]{1,0:T(8,128)S(1)}, u32[]{:S(2)}, u32[]{:S(2)}) collective-permute-start(f32[56,128]{1,0:T(8,128)S(1)} %pad_maximum_fusion.2), channel_id=1, source_target_pairs={{0,1},{1,0},{2,3},{3,2},{4,5},{5,4},{6,7},{7,6},{8,9},{9,8},{10,11... | collective-permute-start | bytes 86024 | tf_op jit(solution)/shard_map/ppermute | solution.py:53
  112.9 3.0 %collective-permute-start.23 = (f32[56,128]{1,0:T(8,128)S(1)}, f32[56,128]{1,0:T(8,128)S(1)}, u32[]{:S(2)}, u32[]{:S(2)}) collective-permute-start(f32[56,128]{1,0:T(8,128)S(1)} %fusion.3), channel_id=1, source_target_pairs={{0,2},{1,3},{2,0},{3,1},{4,6},{5,7},{6,4},{7,5},{8,10},{9,11},{10,... | collective-permute-start | bytes 86024 | tf_op jit(solution)/shard_map/ppermute | solution.py:53
  116.0 4.4 %collective-permute-start.26 = (f32[56,128]{1,0:T(8,128)S(1)}, f32[56,128]{1,0:T(8,128)S(1)}, u32[]{:S(2)}, u32[]{:S(2)}) collective-permute-start(f32[56,128]{1,0:T(8,128)S(1)} %add.81), channel_id=1, source_target_pairs={{0,6},{1,7},{2,4},{3,5},{4,2},{5,3},{6,0},{7,1},{8,14},{9,15},{10,... | collective-permute-start | bytes 86024 | tf_op jit(solution)/shard_map/ppermute | solution.py:53
  130.3 8.7 %collective-permute-start.27 = (f32[256,1280]{1,0:T(8,128)S(1)}, f32[256,1280]{1,0:T(8,128)S(1)}, u32[]{:S(2)}, u32[]{:S(2)}) collective-permute-start(f32[256,1280]{1,0:T(8,128)S(1)} %get-tuple-element.111), channel_id=1, source_target_pairs={{0,1},{1,0},{2,3},{3,2},{4,5},{5,4},{6,7},{7,6},{8,9},{9,8},{10,11... | collective-permute-start | bytes 3932168 | tf_op jit(solution)/shard_map/ppermute | solution.py:53
  139.2 19.5 %collective-permute-start.28 = (f32[128,1280]{1,0:T(8,128)S(1)}, f32[128,1280]{1,0:T(8,128)S(1)}, u32[]{:S(2)}, u32[]{:S(2)}) collective-permute-start(f32[128,1280]{1,0:T(8,128)S(1)} %get-tuple-element.152), channel_id=1, source_target_pairs={{0,2},{1,3},{2,4},{3,5},{4,6},{5,7},{6,0},{7,1},{8,10},{9,11},{10,... | collective-permute-start | bytes 1966088 | tf_op jit(solution)/shard_map/ppermute | solution.py:53
  140.6 18.2 %collective-permute-start.29 = (f32[128,1280]{1,0:T(8,128)S(1)}, f32[128,1280]{1,0:T(8,128)S(1)}, u32[]{:S(2)}, u32[]{:S(2)}) collective-permute-start(f32[128,1280]{1,0:T(8,128)S(1)} %get-tuple-element.151), channel_id=1, source_target_pairs={{0,6},{1,7},{2,0},{3,1},{4,2},{5,3},{6,4},{7,5},{8,14},{9,15},{10,... | collective-permute-start | bytes 1966088 | tf_op jit(solution)/shard_map/ppermute | solution.py:53
  152.3 7.3 %collective-permute-start.31 = (f32[256,1280]{1,0:T(8,128)S(1)}, f32[256,1280]{1,0:T(8,128)S(1)}, u32[]{:S(2)}, u32[]{:S(2)}) collective-permute-start(f32[256,1280]{1,0:T(8,128)S(1)} %get-tuple-element.116), channel_id=1, source_target_pairs={{0,1},{1,0},{2,3},{3,2},{4,5},{5,4},{6,7},{7,6},{8,9},{9,8},{10,11... | collective-permute-start | bytes 3932168 | tf_op jit(solution)/shard_map/ppermute | solution.py:53
  152.6 7.0 %collective-permute-start.32 = (f32[256,1280]{1,0:T(8,128)S(1)}, f32[256,1280]{1,0:T(8,128)S(1)}, u32[]{:S(2)}, u32[]{:S(2)}) collective-permute-start(f32[256,1280]{1,0:T(8,128)S(1)} %get-tuple-element.125), channel_id=1, source_target_pairs={{0,1},{1,0},{2,3},{3,2},{4,5},{5,4},{6,7},{7,6},{8,9},{9,8},{10,11... | collective-permute-start | bytes 3932168 | tf_op jit(solution)/shard_map/ppermute | solution.py:53
  152.8 5.5 %collective-permute-start.30 = (f32[32,1024]{1,0:T(8,128)S(1)}, f32[32,1024]{1,0:T(8,128)S(1)}, u32[]{:S(2)}, u32[]{:S(2)}) collective-permute-start(f32[32,1024]{1,0:T(8,128)S(1)} %add.77), channel_id=1, source_target_pairs={{0,32},{1,9},{2,34},{3,11},{4,36},{5,13},{6,38},{7,15},{8,40},{9,1... | collective-permute-start | bytes 393224 | tf_op jit(solution)/shard_map/ppermute | solution.py:53
  158.3 32.8 %collective-permute-start.35 = (f32[256,1280]{1,0:T(8,128)S(1)}, f32[256,1280]{1,0:T(8,128)S(1)}, u32[]{:S(2)}, u32[]{:S(2)}) collective-permute-start(f32[256,1280]{1,0:T(8,128)S(1)} %get-tuple-element.141), channel_id=1, source_target_pairs={{0,1},{1,0},{2,3},{3,2},{4,5},{5,4},{6,7},{7,6},{8,9},{9,8},{10,11... | collective-permute-start | bytes 3932168 | tf_op jit(solution)/shard_map/ppermute | solution.py:53
  160.5 37.2 %collective-permute-start.39 = (f32[256,1280]{1,0:T(8,128)S(1)}, f32[256,1280]{1,0:T(8,128)S(1)}, u32[]{:S(2)}, u32[]{:S(2)}) collective-permute-start(f32[256,1280]{1,0:T(8,128)S(1)} %get-tuple-element.126), channel_id=1, source_target_pairs={{0,2},{1,3},{2,4},{3,5},{4,6},{5,7},{6,0},{7,1},{8,10},{9,11},{10,... | collective-permute-start | bytes 3932168 | tf_op jit(solution)/shard_map/ppermute | solution.py:53
  160.6 37.2 %collective-permute-start.40 = (f32[256,1280]{1,0:T(8,128)S(1)}, f32[256,1280]{1,0:T(8,128)S(1)}, u32[]{:S(2)}, u32[]{:S(2)}) collective-permute-start(f32[256,1280]{1,0:T(8,128)S(1)} %get-tuple-element.127), channel_id=1, source_target_pairs={{0,6},{1,7},{2,0},{3,1},{4,2},{5,3},{6,4},{7,5},{8,14},{9,15},{10,... | collective-permute-start | bytes 3932168 | tf_op jit(solution)/shard_map/ppermute | solution.py:53
  163.4 28.0 %collective-permute-start.33 = (f32[32,1024]{1,0:T(8,128)S(1)}, f32[32,1024]{1,0:T(8,128)S(1)}, u32[]{:S(2)}, u32[]{:S(2)}) collective-permute-start(f32[32,1024]{1,0:T(8,128)S(1)} %add.84), channel_id=1, source_target_pairs={{0,96},{1,25},{2,98},{3,27},{4,100},{5,29},{6,102},{7,31},{8,104},... | collective-permute-start | bytes 393224 | tf_op jit(solution)/shard_map/ppermute | solution.py:53
  169.0 22.4 %collective-permute-start.34 = (f32[8,1280]{1,0:T(8,128)S(1)}, f32[8,1280]{1,0:T(8,128)S(1)}, u32[]{:S(2)}, u32[]{:S(2)}) collective-permute-start(f32[8,1280]{1,0:T(8,128)S(1)} %get-tuple-element.134), channel_id=1, source_target_pairs={{0,1},{1,0},{2,3},{3,2},{4,5},{5,4},{6,7},{7,6},{8,9},{9,8},{10,11... | collective-permute-start | bytes 122888 | tf_op jit(solution)/shard_map/ppermute | solution.py:53
  191.4 4.1 %collective-permute-start.36 = (f32[8,1280]{1,0:T(8,128)S(1)}, f32[8,1280]{1,0:T(8,128)S(1)}, u32[]{:S(2)}, u32[]{:S(2)}) collective-permute-start(f32[8,1280]{1,0:T(8,128)S(1)} %add.88.last), channel_id=1, source_target_pairs={{0,2},{1,3},{2,4},{3,5},{4,6},{5,7},{6,0},{7,1},{8,10},{9,11},{10,... | collective-permute-start | bytes 122888 | tf_op jit(solution)/shard_map/ppermute | solution.py:53
  191.5 4.5 %collective-permute-start.37 = (f32[8,1280]{1,0:T(8,128)S(1)}, f32[8,1280]{1,0:T(8,128)S(1)}, u32[]{:S(2)}, u32[]{:S(2)}) collective-permute-start(f32[8,1280]{1,0:T(8,128)S(1)} %add.88.last), channel_id=1, source_target_pairs={{0,4},{1,5},{2,6},{3,7},{4,0},{5,1},{6,2},{7,3},{8,12},{9,13},{10,... | collective-permute-start | bytes 122888 | tf_op jit(solution)/shard_map/ppermute | solution.py:53
  192.9 4.1 %collective-permute-start.38 = (f32[8,1280]{1,0:T(8,128)S(1)}, f32[8,1280]{1,0:T(8,128)S(1)}, u32[]{:S(2)}, u32[]{:S(2)}) collective-permute-start(f32[8,1280]{1,0:T(8,128)S(1)} %add.88.last), channel_id=1, source_target_pairs={{0,6},{1,7},{2,0},{3,1},{4,2},{5,3},{6,4},{7,5},{8,14},{9,15},{10,... | collective-permute-start | bytes 122888 | tf_op jit(solution)/shard_map/ppermute | solution.py:53

commit v7 on v6

--- a/solution.py
+++ b/solution.py
@@ -126,37 +126,40 @@
 def expo_kernel(ids, logits, kind, filt, *refs):
     expr, (masses, types, totals, out0, out1) = refs[:4], refs[4:]
     step = pl.program_id(0)
-    count = logits.shape[0] // 128
+    block = logits.shape[0]
+    count = block // 128
 
     @pl.when(step == 0)
     def _():
         for out in (types, totals, out0, out1):
             out[...] = jnp.zeros_like(out)
 
-    keeps = []
+    masses[0], masses[1] = split(jnp.exp(logits[...]))
+    labels = [kind[pl.ds(step * count + part, 1), :] for part in range(count)]
+    valids = [(label >= 0).astype(F32) for label in labels]
+    keeps = [
+        valid * jax.nn.sigmoid(filt[pl.ds(step * count + part, 1), :])
+        for part, valid in enumerate(valids)
+    ]
+    keep = jnp.concatenate(keeps, axis=1)
+    lane = lax.broadcasted_iota(jnp.int32, (1, block), 1) // 128
+    valid = jnp.concatenate(valids, axis=1)
+    row = lax.broadcasted_iota(jnp.int32, (16, block), 0)
+    extra = jnp.where(row == count, keep, jnp.where(row == lane, valid, 0.0))
+    weighted = jnp.concatenate([part[...].reshape(-1, block) for part in expr]) * keep
+    part = product(split(jnp.concatenate([weighted, extra])), masses, ((1,), (0,)))
+    half = weighted.shape[0] // 2
+    whole = [part[2 * half + k : 2 * half + k + 1] for k in range(count + 1)]
+    row = lax.broadcasted_iota(jnp.int32, types.shape, 0)
+    for label, one in zip(labels, whole):
+        types[...] += jnp.where(row == jnp.max(label, axis=1, keepdims=True), one, 0.0)
     lane = lax.broadcasted_iota(jnp.int32, (1, totals.shape[1]), 1)
     cell_sums = jnp.zeros(lane.shape, F32)
-    for part in range(count):
-        rows = slice(part * 128, part * 128 + 128)
-        label = kind[pl.ds(step * count + part, 1), :]
-        valid = (label >= 0).astype(F32)
-        keep = valid * jax.nn.sigmoid(filt[pl.ds(step * count + part, 1), :])
-        keeps.append(keep)
-        for k, one in enumerate((valid, keep, keep - keep * keep)):
-            cell_sums += jnp.where(lane == k, jnp.sum(one, axis=1, keepdims=True), 0.0)
-        expo = jnp.exp(logits[rows]) * as_column(valid)
-        masses[0, rows], masses[1, rows] = split(expo)
-        whole = jnp.sum(expo, axis=0, keepdims=True)
-        kept = jnp.sum(expo * as_column(keep), axis=0, keepdims=True)
-        row = lax.broadcasted_iota(jnp.int32, types.shape, 0)
-        types[...] += jnp.where(row == jnp.max(label, axis=1, keepdims=True), whole, 0.0)
-        row = lax.broadcasted_iota(jnp.int32, totals.shape, 0)
-        totals[...] += jnp.where(row == 0, whole, jnp.where(row == 1, kept, 0.0))
+    for k, one in enumerate((valid, keep, keep - keep * keep)):
+        cell_sums += jnp.where(lane == k, jnp.sum(one, axis=1, keepdims=True), 0.0)
+    totals[0:1, :] += sum(whole[1:count], whole[0])
+    totals[1:2, :] += whole[count]
     totals[2:3, :] += cell_sums
-    weighted = jnp.concatenate([part[...].reshape(-1, logits.shape[0]) for part in expr])
-    weighted = weighted * jnp.concatenate(keeps, axis=1)
-    part = product(split(weighted), masses, ((1,), (0,)))
-    half = part.shape[0] // 2
     for index, out in enumerate((out0, out1)):
         new = part[index * half : index * half + half].reshape(-1, 8, part.shape[1])
         out[: half // 8] += new
@@ -614,7 +617,7 @@
     )(above, below, got_above, got_below)
 
 
-def map_kernel(expr, grad, masses, keep, spot, out, held, ready, *, scale):
+def map_kernel(expr, grad, masses, keep, valid, spot, out, held, ready, *, scale):
     index = pl.program_id(0)
     quarter, block = held.shape[2:]
     count = held.shape[1]
@@ -645,11 +648,12 @@
     expo = masses[0, pl.ds(at, block), :].astype(F32) + masses[1, pl.ds(at, block), :].astype(F32)
     for part in range(block // 128):
         rows = slice(part * 128, part * 128 + 128)
-        weight = as_column(keep[pl.ds(index * (block // 128) + part, 1), :])
-        out[rows, :] = (scale * expo[rows]) * (weight * inner[rows] - spot[1:2, :])
-
-
-def map_call(expr, grad, masses, keep, spot, scale):
+        place = pl.ds(index * (block // 128) + part, 1)
+        weight, mask = as_column(keep[place, :]), as_column(valid[place, :])
+        out[rows, :] = (scale * expo[rows]) * (weight * inner[rows] - mask * spot[1:2, :])
+
+
+def map_call(expr, grad, masses, keep, valid, spot, scale):
     genes, cells = expr.shape
     spots = masses.shape[2]
     block, count = 256, 4
@@ -661,6 +665,7 @@
             RESIDENT,
             RESIDENT,
             fixed(keep.shape),
+            fixed(valid.shape),
             fixed((8, spots)),
         ],
         out_specs=pl.BlockSpec((block, spots), lambda i: (i, 0)),
@@ -672,7 +677,7 @@
         compiler_params=vmem(24),
         cost_estimate=NO_COST,
         name="grad_map",
-    )(streamed(expr), grad, masses, keep, spot)
+    )(streamed(expr), grad, masses, keep, valid, spot)
 
 
 def finish_kernel(last, got1, got2, got3, totals, scalars, kind, filt, grad_filter, terms, *, all_cells):
@@ -821,7 +826,8 @@
 
     column = jnp.sum(column_a + column_b + column_c, axis=0) * share + spot_coef[32] * mass
     map_rows = stacked([spot_coef[32], column])
-    map_args = (expr, grad.reshape(2, genes, spots), masses, keep2, map_rows, all_cells * genes)
+    valid2 = valid.reshape(blocks, 128)
+    map_args = (expr, grad.reshape(2, genes, spots), masses, keep2, valid2, map_rows, all_cells * genes)
     grad_map = map_call(*map_args)
     types_got, last_got = after((types_got, last_got), grad_map)
     types = types + types_got

time: 199 us -> 199 us (level)
  no operation moved by 1% of the time
where the time goes in v7:
time: 199 us; the launch traced here: 198 us
  Pallas kernels  87.6 us (44%)
  starting transfers between devices  60.5 us (30%)
  waiting for transfers between devices  45.1 us (23%)
  other arithmetic  3.77 us (2%)
    ppermute x41, starting transfers between devices, send(): return lax.ppermute(array, ('cells', 'spots'), route(target))  60.5 us
    ppermute x41, waiting for transfers between devices, send(): return lax.ppermute(array, ('cells', 'spots'), route(target))  45.1 us
    pallas_call x5, Pallas kernels, back_call(): pl.pallas_call(functools.partial(back_kernel, parts=parts, first=len(firs...  23 us
    pallas_call x3, Pallas kernels, pred_call(): pl.pallas_call(functools.partial(pred_kernel, cuts=cuts), grid_spec=pltpu...  21.7 us
    pallas_call x1, Pallas kernels, map_call(): pl.pallas_call(functools.partial(map_kernel, scale=scale), grid=(cells //...  21.5 us
    pallas_call x1, Pallas kernels, expo_call(): pl.pallas_call(expo_kernel, grid_spec=pltpu.PrefetchScalarGridSpec(num_sc...  8.8 us
    pallas_call x3, Pallas kernels, grad_call(): pl.pallas_call(functools.partial(grad_kernel, count=count, lane=lane, chi...  7.63 us
  transfers between devices with their start and end apart: 41, of which 18 were waited for; matrix products, arithmetic and copies ran while one was open for 1% of the time, Pallas kernels for 37%

profile of v7, /device:TPU:1, one launch (start us, length us, event | category | flops | bytes accessed | tf_op | source)
XLA Modules:
  0.0 198.3 jit_solution(17468654398560636988)
XLA Ops:
  0.7 8.8 %expo.1 = (bf16[2,1280,1024]{2,1,0:T(8,128)(2,1)S(1)}, f32[32,1024]{1,0:T(8,128)S(1)}, f32[8,1024]{1,0:T(8,128)S(1)}, f32[33,8,1024]{2,1,0:T(8,128)S(1)}, f32[33,8,1024]{2,1,0:T(8,128)S(1)}) custom-call(s32[4]{0:T(128)S(1)} %pad_add_fusion.ids, f32[1280,1024]{1,0:T(8,128)} %logits.1, s32[10,128]{1,0:T(8,128)} %bitcast.66, f32[10,128]{1,0:T(8,128)} %bitcast.67, ...), custom_call_target="tpu_custom_call" | custom-call | bytes 1310720 | tf_op jit(solution)/shard_map/expo/pallas_call | solution.py:179
  9.5 2.5 %collective-permute-start = (f32[33,8,1024]{2,1,0:T(8,128)S(1)}, f32[33,8,1024]{2,1,0:T(8,128)S(1)}, u32[]{:S(2)}, u32[]{:S(2)}) collective-permute-start(f32[33,8,1024]{2,1,0:T(8,128)S(1)} %get-tuple-element.76), channel_id=1, source_target_pairs={{0,8},{1,33},{2,10},{3,35},{4,12},{5,37},{6,14},{7,39},{8,16},{9,4... | collective-permute-start | bytes 3244040 | tf_op jit(solution)/shard_map/ppermute | solution.py:53
  12.1 2.3 %collective-permute-start.1 = (f32[33,8,1024]{2,1,0:T(8,128)S(1)}, f32[33,8,1024]{2,1,0:T(8,128)S(1)}, u32[]{:S(2)}, u32[]{:S(2)}) collective-permute-start(f32[33,8,1024]{2,1,0:T(8,128)S(1)} %get-tuple-element.77), channel_id=1, source_target_pairs={{0,24},{1,97},{2,26},{3,99},{4,28},{5,101},{6,30},{7,103},{8,0},{9... | collective-permute-start | bytes 3244040 | tf_op jit(solution)/shard_map/ppermute | solution.py:53
  14.4 7.5 %pred_.3 = (f32[33,8,1024]{2,1,0:T(8,128)S(1)}, f32[33,8,1024]{2,1,0:T(8,128)S(1)}) custom-call(s32[4]{0:T(128)S(1)} %pad_add_fusion.ids, f32[8,16,16,1280]{3,2,1,0:T(8,128)} %bitcast.57, f32[8,16,16,1280]{3,2,1,0:T(8,128)} %bitcast.58, f32[1,1280]{1,0:T(1,128)S(1)} %reshape.99.keep, bf16[2,1280,1024]{2,1,0:T(8,128)(2,1)S(1)} %get-tuple-element.79.masses, ...), custom_call_target="tpu_custom_call" | custom-call | flops 503316480 | bytes 1245184 | tf_op jit(solution)/shard_map/pred/pallas_call | solution.py:252
  21.9 1.5 collective-permute-start.2
  23.4 3.6 %collective-permute-done.refs_0_ = f32[33,8,1024]{2,1,0:T(8,128)S(1)} collective-permute-done((f32[33,8,1024]{2,1,0:T(8,128)S(1)}, f32[33,8,1024]{2,1,0:T(8,128)S(1)}, u32[]{:S(2)}, u32[]{:S(2)}) %collective-permute-start) | collective-permute-done | bytes 1081376 | tf_op jit(solution)/shard_map/ppermute | solution.py:53
  27.0 6.6 %pred_.4 = (f32[33,8,1024]{2,1,0:T(8,128)S(1)}, f32[33,8,1024]{2,1,0:T(8,128)S(1)}) custom-call(s32[4]{0:T(128)S(1)} %pad_add_fusion.ids, f32[8,16,16,1280]{3,2,1,0:T(8,128)} %bitcast.59, f32[8,16,16,1280]{3,2,1,0:T(8,128)} %bitcast.60, f32[1,1280]{1,0:T(1,128)S(1)} %reshape.99.keep, bf16[2,1280,1024]{2,1,0:T(8,128)(2,1)S(1)} %get-tuple-element.79.masses, ...), custom_call_target="tpu_custom_call" | custom-call | flops 503316480 | bytes 1245184 | tf_op jit(solution)/shard_map/pred/pallas_call | solution.py:252
  34.7 1.9 collective-permute-start.5
  36.7 1.4 collective-permute-done.2.refs_0_
  38.9 7.6 %pred_.5 = (f32[33,8,1024]{2,1,0:T(8,128)S(1)}, f32[33,8,1024]{2,1,0:T(8,128)S(1)}) custom-call(s32[4]{0:T(128)S(1)} %pad_add_fusion.ids, f32[8,16,16,1280]{3,2,1,0:T(8,128)} %bitcast.61, f32[8,16,16,1280]{3,2,1,0:T(8,128)} %bitcast.62, f32[1,1280]{1,0:T(1,128)S(1)} %reshape.99.keep, bf16[2,1280,1024]{2,1,0:T(8,128)(2,1)S(1)} %get-tuple-element.79.masses, ...), custom_call_target="tpu_custom_call" | custom-call | flops 503316480 | bytes 1245184 | tf_op jit(solution)/shard_map/pred/pallas_call | solution.py:252
  46.4 4.0 %collective-permute-done.4.got0 = f32[33,8,1024]{2,1,0:T(8,128)S(1)} collective-permute-done((f32[33,8,1024]{2,1,0:T(8,128)S(1)}, f32[33,8,1024]{2,1,0:T(8,128)S(1)}, u32[]{:S(2)}, u32[]{:S(2)}) %collective-permute-start.4) | collective-permute-done | bytes 1081376 | tf_op jit(solution)/shard_map/ppermute | solution.py:53
  52.2 2.8 %collective-permute-start.8 = (f32[17,8,1024]{2,1,0:T(8,128)S(1)}, f32[17,8,1024]{2,1,0:T(8,128)S(1)}, u32[]{:S(2)}, u32[]{:S(2)}) collective-permute-start(f32[17,8,1024]{2,1,0:T(8,128)S(1)} %get-tuple-element.95), channel_id=1, source_target_pairs={{0,64},{1,17},{2,66},{3,19},{4,68},{5,21},{6,70},{7,23},{8,72},{9,... | collective-permute-start | bytes 1671176 | tf_op jit(solution)/shard_map/ppermute | solution.py:53
  56.5 1.1 collective-permute-start.6
  57.7 4.4 %collective-permute-done.6 = f32[32,1024]{1,0:T(8,128)S(1)} collective-permute-done((f32[32,1024]{1,0:T(8,128)S(1)}, f32[32,1024]{1,0:T(8,128)S(1)}, u32[]{:S(2)}, u32[]{:S(2)}) %collective-permute-start.6) | collective-permute-done | bytes 131104 | tf_op jit(solution)/shard_map/ppermute | solution.py:53
  62.1 7.5 %collective-permute-done.8 = f32[17,8,1024]{2,1,0:T(8,128)S(1)} collective-permute-done((f32[17,8,1024]{2,1,0:T(8,128)S(1)}, f32[17,8,1024]{2,1,0:T(8,128)S(1)}, u32[]{:S(2)}, u32[]{:S(2)}) %collective-permute-start.8) | collective-permute-done | bytes 557088 | tf_op jit(solution)/shard_map/ppermute | solution.py:53
  69.8 2.2 %collective-permute-start.11 = (f32[8,16,1024]{2,1,0:T(8,128)S(1)}, f32[8,16,1024]{2,1,0:T(8,128)S(1)}, u32[]{:S(2)}, u32[]{:S(2)}) collective-permute-start(f32[8,16,1024]{2,1,0:T(8,128)S(1)} %bitcast.47), channel_id=1, source_target_pairs={{0,64},{1,17},{2,66},{3,19},{4,68},{5,21},{6,70},{7,23},{8,72},{9,... | collective-permute-start | bytes 1572872 | tf_op jit(solution)/shard_map/ppermute | solution.py:53
  72.0 2.7 %collective-permute-start.10 = (f32[8,16,1024]{2,1,0:T(8,128)S(1)}, f32[8,16,1024]{2,1,0:T(8,128)S(1)}, u32[]{:S(2)}, u32[]{:S(2)}) collective-permute-start(f32[8,16,1024]{2,1,0:T(8,128)S(1)} %bitcast.49), channel_id=1, source_target_pairs={{0,96},{1,25},{2,98},{3,27},{4,100},{5,29},{6,102},{7,31},{8,104},... | collective-permute-start | bytes 1572872 | tf_op jit(solution)/shard_map/ppermute | solution.py:53
  75.5 2.7 %collective-permute-start.15 = (f32[32,1024]{1,0:T(8,128)S(1)}, f32[32,1024]{1,0:T(8,128)S(1)}, u32[]{:S(2)}, u32[]{:S(2)}) collective-permute-start(f32[32,1024]{1,0:T(8,128)S(1)} %add.71), channel_id=1, source_target_pairs={{0,24},{1,97},{2,26},{3,99},{4,28},{5,101},{6,30},{7,103},{8,16},{... | collective-permute-start | bytes 393224 | tf_op jit(solution)/shard_map/ppermute | solution.py:53
  78.2 3.5 %collective-permute-done.13 = f32[64,128]{1,0:T(8,128)S(1)} collective-permute-done((f32[64,128]{1,0:T(8,128)S(1)}, f32[64,128]{1,0:T(8,128)S(1)}, u32[]{:S(2)}, u32[]{:S(2)}) %collective-permute-start.13) | collective-permute-done | bytes 32800 | tf_op jit(solution)/shard_map/ppermute | solution.py:53
  82.0 4.9 %collective-permute-done.14 = f32[64,128]{1,0:T(8,128)S(1)} collective-permute-done((f32[64,128]{1,0:T(8,128)S(1)}, f32[64,128]{1,0:T(8,128)S(1)}, u32[]{:S(2)}, u32[]{:S(2)}) %collective-permute-start.14) | collective-permute-done | bytes 32800 | tf_op jit(solution)/shard_map/ppermute | solution.py:53
  87.2 2.7 %collective-permute-start.17 = (f32[2,8,16,1024]{3,2,1,0:T(8,128)S(1)}, f32[2,8,16,1024]{3,2,1,0:T(8,128)S(1)}, u32[]{:S(2)}, u32[]{:S(2)}) collective-permute-start(f32[2,8,16,1024]{3,2,1,0:T(8,128)S(1)} %pad_maximum_fusion.1.refs_1_), channel_id=1, source_target_pairs={{0,24},{1,97},{2,26},{3,99},{4,28},{5,101},{6,30},{7,103},{8,0},{9... | collective-permute-start | bytes 3145736 | tf_op jit(solution)/shard_map/ppermute | solution.py:53
  89.9 2.7 %collective-permute-done.18 = f32[64,128]{1,0:T(8,128)S(1)} collective-permute-done((f32[64,128]{1,0:T(8,128)S(1)}, f32[64,128]{1,0:T(8,128)S(1)}, u32[]{:S(2)}, u32[]{:S(2)}) %collective-permute-start.18) | collective-permute-done | bytes 32800 | tf_op jit(solution)/shard_map/ppermute | solution.py:53
  92.6 1.2 collective-permute-start.19
  93.8 2.7 %collective-permute-start.25 = (f32[2,8,16,1024]{3,2,1,0:T(8,128)S(1)}, f32[2,8,16,1024]{3,2,1,0:T(8,128)S(1)}, u32[]{:S(2)}, u32[]{:S(2)}) collective-permute-start(f32[2,8,16,1024]{3,2,1,0:T(8,128)S(1)} %pad_maximum_fusion.refs_0_), channel_id=1, source_target_pairs={{0,24},{1,97},{2,26},{3,99},{4,28},{5,101},{6,30},{7,103},{8,0},{9... | collective-permute-start | bytes 3145736 | tf_op jit(solution)/shard_map/ppermute | solution.py:53
  97.2 5.1 %collective-permute-done.16.refs_2_ = f32[2,8,16,1024]{3,2,1,0:T(8,128)S(1)} collective-permute-done((f32[2,8,16,1024]{3,2,1,0:T(8,128)S(1)}, f32[2,8,16,1024]{3,2,1,0:T(8,128)S(1)}, u32[]{:S(2)}, u32[]{:S(2)}) %collective-permute-start.16) | collective-permute-done | bytes 1048608 | tf_op jit(solution)/shard_map/ppermute | solution.py:53
  102.4 1.2 collective-permute-start.20
  103.5 1.9 collective-permute-start.21
  105.4 5.6 %collective-permute-start.22 = (f32[56,128]{1,0:T(8,128)S(1)}, f32[56,128]{1,0:T(8,128)S(1)}, u32[]{:S(2)}, u32[]{:S(2)}) collective-permute-start(f32[56,128]{1,0:T(8,128)S(1)} %pad_maximum_fusion.2), channel_id=1, source_target_pairs={{0,1},{1,0},{2,3},{3,2},{4,5},{5,4},{6,7},{7,6},{8,9},{9,8},{10,11... | collective-permute-start | bytes 86024 | tf_op jit(solution)/shard_map/ppermute | solution.py:53
  111.9 1.3 collective-permute-start.23
  113.2 1.7 collective-permute-done.23
  114.9 2.8 %collective-permute-start.26 = (f32[56,128]{1,0:T(8,128)S(1)}, f32[56,128]{1,0:T(8,128)S(1)}, u32[]{:S(2)}, u32[]{:S(2)}) collective-permute-start(f32[56,128]{1,0:T(8,128)S(1)} %add.81), channel_id=1, source_target_pairs={{0,6},{1,7},{2,4},{3,5},{4,2},{5,3},{6,0},{7,1},{8,14},{9,15},{10,... | collective-permute-start | bytes 86024 | tf_op jit(solution)/shard_map/ppermute | solution.py:53
  117.7 1.6 collective-permute-done.26
  120.2 4.7 %grad.3 = (bf16[2,8,256,1024]{3,2,1,0:T(8,128)(2,1)S(1)}, f32[8,1024]{1,0:T(8,128)S(1)}) custom-call(s32[4]{0:T(128)S(1)} %pad_add_fusion.ids, f32[2,8,16,1024]{3,2,1,0:T(8,128)S(1)} %pad_maximum_fusion.refs_0_, f32[2,8,16,1024]{3,2,1,0:T(8,128)S(1)} %pad_maximum_fusion.1.refs_1_, f32[2,8,16,1024]{3,2,1,0:T(8,128)S(1)} %collective-permute-done.16.refs_2_, ...), custom_call_target="tpu_custom_call" | custom-call | tf_op jit(solution)/shard_map/grad/pallas_call | solution.py:477
  126.1 3.1 %back.5 = (f32[8,1280]{1,0:T(8,128)S(1)}, f32[256,1280]{1,0:T(8,128)S(1)}) custom-call(s32[4]{0:T(128)S(1)} %pad_add_fusion.ids, bf16[2,8,256,1024]{3,2,1,0:T(8,128)(2,1)S(1)} %get-tuple-element.110.grad.refs_5_, bf16[2,1280,1024]{2,1,0:T(8,128)(2,1)S(1)} %get-tuple-element.79.masses, f32[2048,1280]{1,0:T(8,128)} %expr.11, ...), custom_call_target="tpu_custom_call" | custom-call | tf_op jit(solution)/shard_map/back/pallas_call | solution.py:553
  129.2 5.2 %collective-permute-start.27 = (f32[256,1280]{1,0:T(8,128)S(1)}, f32[256,1280]{1,0:T(8,128)S(1)}, u32[]{:S(2)}, u32[]{:S(2)}) collective-permute-start(f32[256,1280]{1,0:T(8,128)S(1)} %get-tuple-element.111), channel_id=1, source_target_pairs={{0,1},{1,0},{2,3},{3,2},{4,5},{5,4},{6,7},{7,6},{8,9},{9,8},{10,11... | collective-permute-start | bytes 3932168 | tf_op jit(solution)/shard_map/ppermute | solution.py:53
  134.4 3.6 %back.6 = (f32[8,1280]{1,0:T(8,128)S(1)}, f32[256,1280]{1,0:T(8,128)S(1)}) custom-call(s32[4]{0:T(128)S(1)} %pad_add_fusion.ids, bf16[2,8,256,1024]{3,2,1,0:T(8,128)(2,1)S(1)} %get-tuple-element.110.grad.refs_5_, bf16[2,1280,1024]{2,1,0:T(8,128)(2,1)S(1)} %get-tuple-element.79.masses, f32[2048,1280]{1,0:T(8,128)} %expr.11), custom_call_target="tpu_custom_call" | custom-call | tf_op jit(solution)/shard_map/back/pallas_call | solution.py:553
  138.2 1.3 collective-permute-start.28
  139.6 1.8 collective-permute-start.29
  141.3 1.9 grad.5
  143.2 8.0 %back.7 = (f32[8,1280]{1,0:T(8,128)S(1)}, f32[256,1280]{1,0:T(8,128)S(1)}, f32[256,1280]{1,0:T(8,128)S(1)}, f32[256,1280]{1,0:T(8,128)S(1)}) custom-call(s32[4]{0:T(128)S(1)} %pad_add_fusion.ids, bf16[2,8,256,1024]{3,2,1,0:T(8,128)(2,1)S(1)} %get-tuple-element.115.grad, bf16[2,1280,1024]{2,1,0:T(8,128)(2,1)S(1)} %get-tuple-element.79.masses, f32[2048,1280]{1,0:T(8,128)} %expr.11), custom_call_target="tpu_custom_call" | custom-call | tf_op jit(solution)/shard_map/back/pallas_call | solution.py:553
  151.8 5.5 %back.8 = (f32[8,1280]{1,0:T(8,128)S(1)}, f32[256,1280]{1,0:T(8,128)S(1)}, f32[256,1280]{1,0:T(8,128)S(1)}) custom-call(s32[4]{0:T(128)S(1)} %pad_add_fusion.ids, bf16[2,8,256,1024]{3,2,1,0:T(8,128)(2,1)S(1)} %get-tuple-element.115.grad, bf16[2,1280,1024]{2,1,0:T(8,128)(2,1)S(1)} %get-tuple-element.79.masses, f32[2048,1280]{1,0:T(8,128)} %expr.11), custom_call_target="tpu_custom_call" | custom-call | tf_op jit(solution)/shard_map/back/pallas_call | solution.py:553
  159.6 2.7 %collective-permute-start.40 = (f32[256,1280]{1,0:T(8,128)S(1)}, f32[256,1280]{1,0:T(8,128)S(1)}, u32[]{:S(2)}, u32[]{:S(2)}) collective-permute-start(f32[256,1280]{1,0:T(8,128)S(1)} %get-tuple-element.127), channel_id=1, source_target_pairs={{0,6},{1,7},{2,0},{3,1},{4,2},{5,3},{6,4},{7,5},{8,14},{9,15},{10,... | collective-permute-start | bytes 3932168 | tf_op jit(solution)/shard_map/ppermute | solution.py:53
  162.3 2.7 %collective-permute-start.33 = (f32[32,1024]{1,0:T(8,128)S(1)}, f32[32,1024]{1,0:T(8,128)S(1)}, u32[]{:S(2)}, u32[]{:S(2)}) collective-permute-start(f32[32,1024]{1,0:T(8,128)S(1)} %add.84), channel_id=1, source_target_pairs={{0,96},{1,25},{2,98},{3,27},{4,100},{5,29},{6,102},{7,31},{8,104},... | collective-permute-start | bytes 393224 | tf_op jit(solution)/shard_map/ppermute | solution.py:53
  165.0 3.0 %back.9 = (f32[8,1280]{1,0:T(8,128)S(1)}, f32[256,1280]{1,0:T(8,128)S(1)}) custom-call(s32[4]{0:T(128)S(1)} %pad_add_fusion.ids, bf16[2,8,256,1024]{3,2,1,0:T(8,128)(2,1)S(1)} %get-tuple-element.115.grad, bf16[2,1280,1024]{2,1,0:T(8,128)(2,1)S(1)} %get-tuple-element.79.masses, f32[2048,1280]{1,0:T(8,128)} %expr.11, ...), custom_call_target="tpu_custom_call" | custom-call | tf_op jit(solution)/shard_map/back/pallas_call | solution.py:553
  168.8 21.5 %grad_map.1 = f32[1280,1024]{1,0:T(8,128)} custom-call(f32[2048,1280]{1,0:T(8,128)} %expr.11, bf16[2,2048,1024]{2,1,0:T(8,128)(2,1)S(1)} %bitcast.38, bf16[2,1280,1024]{2,1,0:T(8,128)(2,1)S(1)} %get-tuple-element.79.masses, f32[10,128]{1,0:T(8,128)S(1)} %bitcast.52, f32[10,128]{1,0:T(8,128)S(1)} %convert_bitcast_fusion.valid, ...), custom_call_target="tpu_custom_call" | custom-call | tf_op jit(solution)/shard_map/grad_map/pallas_call | solution.py:660
  190.7 1.4 collective-permute-start.37
  192.1 1.3 collective-permute-start.38
  196.9 1.4 add_multiply_fusion
  (104 shorter events, 18.7 us)
Async XLA Ops:
  0.7 13.6 %copy-start = (s32[1280]{0:T(1024)S(1)}, s32[1280]{0:T(1024)}, u32[]{:S(2)}) copy-start(s32[1280]{0:T(1024)} %param.11) | copy-start | bytes 15364
  0.7 13.6 %copy-start.1 = (f32[1280]{0:T(1024)S(1)}, f32[1280]{0:T(1024)}, u32[]{:S(2)}) copy-start(f32[1280]{0:T(1024)} %param.8) | copy-start | bytes 15364
  9.5 17.5 %collective-permute-start = (f32[33,8,1024]{2,1,0:T(8,128)S(1)}, f32[33,8,1024]{2,1,0:T(8,128)S(1)}, u32[]{:S(2)}, u32[]{:S(2)}) collective-permute-start(f32[33,8,1024]{2,1,0:T(8,128)S(1)} %get-tuple-element.76), channel_id=1, source_target_pairs={{0,8},{1,33},{2,10},{3,35},{4,12},{5,37},{6,14},{7,39},{8,16},{9,4... | collective-permute-start | bytes 3244040 | tf_op jit(solution)/shard_map/ppermute | solution.py:53
  12.1 14.9 %collective-permute-start.1 = (f32[33,8,1024]{2,1,0:T(8,128)S(1)}, f32[33,8,1024]{2,1,0:T(8,128)S(1)}, u32[]{:S(2)}, u32[]{:S(2)}) collective-permute-start(f32[33,8,1024]{2,1,0:T(8,128)S(1)} %get-tuple-element.77), channel_id=1, source_target_pairs={{0,24},{1,97},{2,26},{3,99},{4,28},{5,101},{6,30},{7,103},{8,0},{9... | collective-permute-start | bytes 3244040 | tf_op jit(solution)/shard_map/ppermute | solution.py:53
  21.9 16.3 %collective-permute-start.2 = (f32[33,8,1024]{2,1,0:T(8,128)S(1)}, f32[33,8,1024]{2,1,0:T(8,128)S(1)}, u32[]{:S(2)}, u32[]{:S(2)}) collective-permute-start(f32[33,8,1024]{2,1,0:T(8,128)S(1)} %get-tuple-element.82), channel_id=1, source_target_pairs={{0,24},{1,97},{2,26},{3,99},{4,28},{5,101},{6,30},{7,103},{8,0},{9... | collective-permute-start | bytes 3244040 | tf_op jit(solution)/shard_map/ppermute | solution.py:53
  23.3 13.3 %copy-start.2 = (s32[1024]{0:T(1024)S(1)}, s32[1024]{0:T(1024)}, u32[]{:S(2)}) copy-start(s32[1024]{0:T(1024)} %param.12) | copy-start | bytes 12292
  23.3 13.3 %copy-start.3 = (s32[1024]{0:T(1024)S(1)}, s32[1024]{0:T(1024)}, u32[]{:S(2)}) copy-start(s32[1024]{0:T(1024)} %param.13) | copy-start | bytes 12292
  23.4 15.5 %collective-permute-start.3 = (f32[33,8,1024]{2,1,0:T(8,128)S(1)}, f32[33,8,1024]{2,1,0:T(8,128)S(1)}, u32[]{:S(2)}, u32[]{:S(2)}) collective-permute-start(f32[33,8,1024]{2,1,0:T(8,128)S(1)} %get-tuple-element.81), channel_id=1, source_target_pairs={{0,8},{1,33},{2,10},{3,35},{4,12},{5,37},{6,14},{7,39},{8,16},{9,4... | collective-permute-start | bytes 3244040 | tf_op jit(solution)/shard_map/ppermute | solution.py:53
  33.6 16.8 %collective-permute-start.4 = (f32[33,8,1024]{2,1,0:T(8,128)S(1)}, f32[33,8,1024]{2,1,0:T(8,128)S(1)}, u32[]{:S(2)}, u32[]{:S(2)}) collective-permute-start(f32[33,8,1024]{2,1,0:T(8,128)S(1)} %get-tuple-element.84), channel_id=1, source_target_pairs={{0,8},{1,33},{2,10},{3,35},{4,12},{5,37},{6,14},{7,39},{8,16},{9,4... | collective-permute-start | bytes 3244040 | tf_op jit(solution)/shard_map/ppermute | solution.py:53
  34.7 15.7 %collective-permute-start.5 = (f32[33,8,1024]{2,1,0:T(8,128)S(1)}, f32[33,8,1024]{2,1,0:T(8,128)S(1)}, u32[]{:S(2)}, u32[]{:S(2)}) collective-permute-start(f32[33,8,1024]{2,1,0:T(8,128)S(1)} %get-tuple-element.85), channel_id=1, source_target_pairs={{0,24},{1,97},{2,26},{3,99},{4,28},{5,101},{6,30},{7,103},{8,0},{9... | collective-permute-start | bytes 3244040 | tf_op jit(solution)/shard_map/ppermute | solution.py:53
  36.7 19.2 %slice-start = ((s8[8388608]{0:T(1024)(128)(4,1)}), s8[4194304]{0:T(1024)(128)(4,1)S(1)}, s32[]{:S(2)}) async-start(s8[8388608]{0:T(1024)(128)(4,1)} %bitcast.39), calls=%async_computation | async-start | bytes 8388608
  36.7 19.2 %slice-start.1 = ((s8[8388608]{0:T(1024)(128)(4,1)}), s8[4194304]{0:T(1024)(128)(4,1)S(1)}, s32[]{:S(2)}) async-start(s8[8388608]{0:T(1024)(128)(4,1)} %bitcast.39), calls=%async_computation.1 | async-start | bytes 8388608
  51.2 10.9 %collective-permute-start.7 = (f32[17,8,1024]{2,1,0:T(8,128)S(1)}, f32[17,8,1024]{2,1,0:T(8,128)S(1)}, u32[]{:S(2)}, u32[]{:S(2)}) collective-permute-start(f32[17,8,1024]{2,1,0:T(8,128)S(1)} %get-tuple-element.94), channel_id=1, source_target_pairs={{0,32},{1,9},{2,34},{3,11},{4,36},{5,13},{6,38},{7,15},{8,40},{9,1... | collective-permute-start | bytes 1671176 | tf_op jit(solution)/shard_map/ppermute | solution.py:53
  52.2 17.3 %collective-permute-start.8 = (f32[17,8,1024]{2,1,0:T(8,128)S(1)}, f32[17,8,1024]{2,1,0:T(8,128)S(1)}, u32[]{:S(2)}, u32[]{:S(2)}) collective-permute-start(f32[17,8,1024]{2,1,0:T(8,128)S(1)} %get-tuple-element.95), channel_id=1, source_target_pairs={{0,64},{1,17},{2,66},{3,19},{4,68},{5,21},{6,70},{7,23},{8,72},{9,... | collective-permute-start | bytes 1671176 | tf_op jit(solution)/shard_map/ppermute | solution.py:53
  55.0 14.6 %collective-permute-start.9 = (f32[17,8,1024]{2,1,0:T(8,128)S(1)}, f32[17,8,1024]{2,1,0:T(8,128)S(1)}, u32[]{:S(2)}, u32[]{:S(2)}) collective-permute-start(f32[17,8,1024]{2,1,0:T(8,128)S(1)} %get-tuple-element.96), channel_id=1, source_target_pairs={{0,96},{1,25},{2,98},{3,27},{4,100},{5,29},{6,102},{7,31},{8,104},... | collective-permute-start | bytes 1671176 | tf_op jit(solution)/shard_map/ppermute | solution.py:53
  56.5 5.5 %collective-permute-start.6 = (f32[32,1024]{1,0:T(8,128)S(1)}, f32[32,1024]{1,0:T(8,128)S(1)}, u32[]{:S(2)}, u32[]{:S(2)}) collective-permute-start(f32[32,1024]{1,0:T(8,128)S(1)} %get-tuple-element.92), channel_id=1, source_target_pairs={{0,8},{1,33},{2,10},{3,35},{4,12},{5,37},{6,14},{7,39},{8,0},{9,41... | collective-permute-start | bytes 393224 | tf_op jit(solution)/shard_map/ppermute | solution.py:53
  69.8 17.1 %collective-permute-start.11 = (f32[8,16,1024]{2,1,0:T(8,128)S(1)}, f32[8,16,1024]{2,1,0:T(8,128)S(1)}, u32[]{:S(2)}, u32[]{:S(2)}) collective-permute-start(f32[8,16,1024]{2,1,0:T(8,128)S(1)} %bitcast.47), channel_id=1, source_target_pairs={{0,64},{1,17},{2,66},{3,19},{4,68},{5,21},{6,70},{7,23},{8,72},{9,... | collective-permute-start | bytes 1572872 | tf_op jit(solution)/shard_map/ppermute | solution.py:53
  72.0 15.0 %collective-permute-start.12 = (f32[8,16,1024]{2,1,0:T(8,128)S(1)}, f32[8,16,1024]{2,1,0:T(8,128)S(1)}, u32[]{:S(2)}, u32[]{:S(2)}) collective-permute-start(f32[8,16,1024]{2,1,0:T(8,128)S(1)} %bitcast.48), channel_id=1, source_target_pairs={{0,32},{1,9},{2,34},{3,11},{4,36},{5,13},{6,38},{7,15},{8,40},{9,1... | collective-permute-start | bytes 1572872 | tf_op jit(solution)/shard_map/ppermute | solution.py:53
  72.0 15.0 %collective-permute-start.10 = (f32[8,16,1024]{2,1,0:T(8,128)S(1)}, f32[8,16,1024]{2,1,0:T(8,128)S(1)}, u32[]{:S(2)}, u32[]{:S(2)}) collective-permute-start(f32[8,16,1024]{2,1,0:T(8,128)S(1)} %bitcast.49), channel_id=1, source_target_pairs={{0,96},{1,25},{2,98},{3,27},{4,100},{5,29},{6,102},{7,31},{8,104},... | collective-permute-start | bytes 1572872 | tf_op jit(solution)/shard_map/ppermute | solution.py:53
  75.5 11.4 %collective-permute-start.15 = (f32[32,1024]{1,0:T(8,128)S(1)}, f32[32,1024]{1,0:T(8,128)S(1)}, u32[]{:S(2)}, u32[]{:S(2)}) collective-permute-start(f32[32,1024]{1,0:T(8,128)S(1)} %add.71), channel_id=1, source_target_pairs={{0,24},{1,97},{2,26},{3,99},{4,28},{5,101},{6,30},{7,103},{8,16},{... | collective-permute-start | bytes 393224 | tf_op jit(solution)/shard_map/ppermute | solution.py:53
  78.2 3.5 %collective-permute-start.13 = (f32[64,128]{1,0:T(8,128)S(1)}, f32[64,128]{1,0:T(8,128)S(1)}, u32[]{:S(2)}, u32[]{:S(2)}) collective-permute-start(f32[64,128]{1,0:T(8,128)S(1)} %get-tuple-element.97), channel_id=1, source_target_pairs={{0,8},{1,33},{2,10},{3,35},{4,12},{5,37},{6,14},{7,39},{8,0},{9,41... | collective-permute-start | bytes 98312 | tf_op jit(solution)/shard_map/ppermute | solution.py:53
  81.7 5.2 %collective-permute-start.14 = (f32[64,128]{1,0:T(8,128)S(1)}, f32[64,128]{1,0:T(8,128)S(1)}, u32[]{:S(2)}, u32[]{:S(2)}) collective-permute-start(f32[64,128]{1,0:T(8,128)S(1)} %add.75), channel_id=1, source_target_pairs={{0,24},{1,97},{2,26},{3,99},{4,28},{5,101},{6,30},{7,103},{8,16},{... | collective-permute-start | bytes 98312 | tf_op jit(solution)/shard_map/ppermute | solution.py:53
  87.1 15.2 %collective-permute-start.16 = (f32[2,8,16,1024]{3,2,1,0:T(8,128)S(1)}, f32[2,8,16,1024]{3,2,1,0:T(8,128)S(1)}, u32[]{:S(2)}, u32[]{:S(2)}) collective-permute-start(f32[2,8,16,1024]{3,2,1,0:T(8,128)S(1)} %pad_maximum_fusion.refs_0_), channel_id=1, source_target_pairs={{0,8},{1,33},{2,10},{3,35},{4,12},{5,37},{6,14},{7,39},{8,16},{9,4... | collective-permute-start | bytes 3145736 | tf_op jit(solution)/shard_map/ppermute | solution.py:53
  87.2 15.1 %collective-permute-start.17 = (f32[2,8,16,1024]{3,2,1,0:T(8,128)S(1)}, f32[2,8,16,1024]{3,2,1,0:T(8,128)S(1)}, u32[]{:S(2)}, u32[]{:S(2)}) collective-permute-start(f32[2,8,16,1024]{3,2,1,0:T(8,128)S(1)} %pad_maximum_fusion.1.refs_1_), channel_id=1, source_target_pairs={{0,24},{1,97},{2,26},{3,99},{4,28},{5,101},{6,30},{7,103},{8,0},{9... | collective-permute-start | bytes 3145736 | tf_op jit(solution)/shard_map/ppermute | solution.py:53
  89.9 2.8 %collective-permute-start.18 = (f32[64,128]{1,0:T(8,128)S(1)}, f32[64,128]{1,0:T(8,128)S(1)}, u32[]{:S(2)}, u32[]{:S(2)}) collective-permute-start(f32[64,128]{1,0:T(8,128)S(1)} %add.76), channel_id=1, source_target_pairs={{0,32},{1,9},{2,34},{3,11},{4,36},{5,13},{6,38},{7,15},{8,40},{9,1... | collective-permute-start | bytes 98312 | tf_op jit(solution)/shard_map/ppermute | solution.py:53
  92.6 4.6 %collective-permute-start.19 = (f32[64,128]{1,0:T(8,128)S(1)}, f32[64,128]{1,0:T(8,128)S(1)}, u32[]{:S(2)}, u32[]{:S(2)}) collective-permute-start(f32[64,128]{1,0:T(8,128)S(1)} %add.78), channel_id=1, source_target_pairs={{0,96},{1,25},{2,98},{3,27},{4,100},{5,29},{6,102},{7,31},{8,104},... | collective-permute-start | bytes 98312 | tf_op jit(solution)/shard_map/ppermute | solution.py:53
  93.8 21.1 %collective-permute-start.24 = (f32[2,8,16,1024]{3,2,1,0:T(8,128)S(1)}, f32[2,8,16,1024]{3,2,1,0:T(8,128)S(1)}, u32[]{:S(2)}, u32[]{:S(2)}) collective-permute-start(f32[2,8,16,1024]{3,2,1,0:T(8,128)S(1)} %pad_maximum_fusion.1.refs_1_), channel_id=1, source_target_pairs={{0,8},{1,33},{2,10},{3,35},{4,12},{5,37},{6,14},{7,39},{8,16},{9,4... | collective-permute-start | bytes 3145736 | tf_op jit(solution)/shard_map/ppermute | solution.py:53
  93.8 21.1 %collective-permute-start.25 = (f32[2,8,16,1024]{3,2,1,0:T(8,128)S(1)}, f32[2,8,16,1024]{3,2,1,0:T(8,128)S(1)}, u32[]{:S(2)}, u32[]{:S(2)}) collective-permute-start(f32[2,8,16,1024]{3,2,1,0:T(8,128)S(1)} %pad_maximum_fusion.refs_0_), channel_id=1, source_target_pairs={{0,24},{1,97},{2,26},{3,99},{4,28},{5,101},{6,30},{7,103},{8,0},{9... | collective-permute-start | bytes 3145736 | tf_op jit(solution)/shard_map/ppermute | solution.py:53
  102.4 22.8 %collective-permute-start.20 = (f32[2,8,16,1024]{3,2,1,0:T(8,128)S(1)}, f32[2,8,16,1024]{3,2,1,0:T(8,128)S(1)}, u32[]{:S(2)}, u32[]{:S(2)}) collective-permute-start(f32[2,8,16,1024]{3,2,1,0:T(8,128)S(1)} %collective-permute-done.16.refs_2_), channel_id=1, source_target_pairs={{0,8},{1,33},{2,10},{3,35},{4,12},{5,37},{6,14},{7,39},{8,16},{9,4... | collective-permute-start | bytes 3145736 | tf_op jit(solution)/shard_map/ppermute | solution.py:53
  103.5 21.6 %collective-permute-start.21 = (f32[2,8,16,1024]{3,2,1,0:T(8,128)S(1)}, f32[2,8,16,1024]{3,2,1,0:T(8,128)S(1)}, u32[]{:S(2)}, u32[]{:S(2)}) collective-permute-start(f32[2,8,16,1024]{3,2,1,0:T(8,128)S(1)} %collective-permute-done.17.refs_5_), channel_id=1, source_target_pairs={{0,24},{1,97},{2,26},{3,99},{4,28},{5,101},{6,30},{7,103},{8,0},{9... | collective-permute-start | bytes 3145736 | tf_op jit(solution)/shard_map/ppermute | solution.py:53
  105.4 6.5 %collective-permute-start.22 = (f32[56,128]{1,0:T(8,128)S(1)}, f32[56,128]{1,0:T(8,128)S(1)}, u32[]{:S(2)}, u32[]{:S(2)}) collective-permute-start(f32[56,128]{1,0:T(8,128)S(1)} %pad_maximum_fusion.2), channel_id=1, source_target_pairs={{0,1},{1,0},{2,3},{3,2},{4,5},{5,4},{6,7},{7,6},{8,9},{9,8},{10,11... | collective-permute-start | bytes 86024 | tf_op jit(solution)/shard_map/ppermute | solution.py:53
  111.9 3.0 %collective-permute-start.23 = (f32[56,128]{1,0:T(8,128)S(1)}, f32[56,128]{1,0:T(8,128)S(1)}, u32[]{:S(2)}, u32[]{:S(2)}) collective-permute-start(f32[56,128]{1,0:T(8,128)S(1)} %fusion.3), channel_id=1, source_target_pairs={{0,2},{1,3},{2,0},{3,1},{4,6},{5,7},{6,4},{7,5},{8,10},{9,11},{10,... | collective-permute-start | bytes 86024 | tf_op jit(solution)/shard_map/ppermute | solution.py:53
  114.9 4.4 %collective-permute-start.26 = (f32[56,128]{1,0:T(8,128)S(1)}, f32[56,128]{1,0:T(8,128)S(1)}, u32[]{:S(2)}, u32[]{:S(2)}) collective-permute-start(f32[56,128]{1,0:T(8,128)S(1)} %add.81), channel_id=1, source_target_pairs={{0,6},{1,7},{2,4},{3,5},{4,2},{5,3},{6,0},{7,1},{8,14},{9,15},{10,... | collective-permute-start | bytes 86024 | tf_op jit(solution)/shard_map/ppermute | solution.py:53
  129.2 8.7 %collective-permute-start.27 = (f32[256,1280]{1,0:T(8,128)S(1)}, f32[256,1280]{1,0:T(8,128)S(1)}, u32[]{:S(2)}, u32[]{:S(2)}) collective-permute-start(f32[256,1280]{1,0:T(8,128)S(1)} %get-tuple-element.111), channel_id=1, source_target_pairs={{0,1},{1,0},{2,3},{3,2},{4,5},{5,4},{6,7},{7,6},{8,9},{9,8},{10,11... | collective-permute-start | bytes 3932168 | tf_op jit(solution)/shard_map/ppermute | solution.py:53
  138.2 19.5 %collective-permute-start.28 = (f32[128,1280]{1,0:T(8,128)S(1)}, f32[128,1280]{1,0:T(8,128)S(1)}, u32[]{:S(2)}, u32[]{:S(2)}) collective-permute-start(f32[128,1280]{1,0:T(8,128)S(1)} %get-tuple-element.153), channel_id=1, source_target_pairs={{0,2},{1,3},{2,4},{3,5},{4,6},{5,7},{6,0},{7,1},{8,10},{9,11},{10,... | collective-permute-start | bytes 1966088 | tf_op jit(solution)/shard_map/ppermute | solution.py:53
  139.6 18.2 %collective-permute-start.29 = (f32[128,1280]{1,0:T(8,128)S(1)}, f32[128,1280]{1,0:T(8,128)S(1)}, u32[]{:S(2)}, u32[]{:S(2)}) collective-permute-start(f32[128,1280]{1,0:T(8,128)S(1)} %get-tuple-element.152), channel_id=1, source_target_pairs={{0,6},{1,7},{2,0},{3,1},{4,2},{5,3},{6,4},{7,5},{8,14},{9,15},{10,... | collective-permute-start | bytes 1966088 | tf_op jit(solution)/shard_map/ppermute | solution.py:53
  151.2 7.3 %collective-permute-start.31 = (f32[256,1280]{1,0:T(8,128)S(1)}, f32[256,1280]{1,0:T(8,128)S(1)}, u32[]{:S(2)}, u32[]{:S(2)}) collective-permute-start(f32[256,1280]{1,0:T(8,128)S(1)} %get-tuple-element.116), channel_id=1, source_target_pairs={{0,1},{1,0},{2,3},{3,2},{4,5},{5,4},{6,7},{7,6},{8,9},{9,8},{10,11... | collective-permute-start | bytes 3932168 | tf_op jit(solution)/shard_map/ppermute | solution.py:53
  151.6 7.0 %collective-permute-start.32 = (f32[256,1280]{1,0:T(8,128)S(1)}, f32[256,1280]{1,0:T(8,128)S(1)}, u32[]{:S(2)}, u32[]{:S(2)}) collective-permute-start(f32[256,1280]{1,0:T(8,128)S(1)} %get-tuple-element.125), channel_id=1, source_target_pairs={{0,1},{1,0},{2,3},{3,2},{4,5},{5,4},{6,7},{7,6},{8,9},{9,8},{10,11... | collective-permute-start | bytes 3932168 | tf_op jit(solution)/shard_map/ppermute | solution.py:53
  151.8 5.5 %collective-permute-start.30 = (f32[32,1024]{1,0:T(8,128)S(1)}, f32[32,1024]{1,0:T(8,128)S(1)}, u32[]{:S(2)}, u32[]{:S(2)}) collective-permute-start(f32[32,1024]{1,0:T(8,128)S(1)} %add.77), channel_id=1, source_target_pairs={{0,32},{1,9},{2,34},{3,11},{4,36},{5,13},{6,38},{7,15},{8,40},{9,1... | collective-permute-start | bytes 393224 | tf_op jit(solution)/shard_map/ppermute | solution.py:53
  157.3 33.0 %collective-permute-start.35 = (f32[256,1280]{1,0:T(8,128)S(1)}, f32[256,1280]{1,0:T(8,128)S(1)}, u32[]{:S(2)}, u32[]{:S(2)}) collective-permute-start(f32[256,1280]{1,0:T(8,128)S(1)} %get-tuple-element.141), channel_id=1, source_target_pairs={{0,1},{1,0},{2,3},{3,2},{4,5},{5,4},{6,7},{7,6},{8,9},{9,8},{10,11... | collective-permute-start | bytes 3932168 | tf_op jit(solution)/shard_map/ppermute | solution.py:53
  159.5 37.4 %collective-permute-start.39 = (f32[256,1280]{1,0:T(8,128)S(1)}, f32[256,1280]{1,0:T(8,128)S(1)}, u32[]{:S(2)}, u32[]{:S(2)}) collective-permute-start(f32[256,1280]{1,0:T(8,128)S(1)} %get-tuple-element.126), channel_id=1, source_target_pairs={{0,2},{1,3},{2,4},{3,5},{4,6},{5,7},{6,0},{7,1},{8,10},{9,11},{10,... | collective-permute-start | bytes 3932168 | tf_op jit(solution)/shard_map/ppermute | solution.py:53
  159.6 37.3 %collective-permute-start.40 = (f32[256,1280]{1,0:T(8,128)S(1)}, f32[256,1280]{1,0:T(8,128)S(1)}, u32[]{:S(2)}, u32[]{:S(2)}) collective-permute-start(f32[256,1280]{1,0:T(8,128)S(1)} %get-tuple-element.127), channel_id=1, source_target_pairs={{0,6},{1,7},{2,0},{3,1},{4,2},{5,3},{6,4},{7,5},{8,14},{9,15},{10,... | collective-permute-start | bytes 3932168 | tf_op jit(solution)/shard_map/ppermute | solution.py:53
  162.3 28.2 %collective-permute-start.33 = (f32[32,1024]{1,0:T(8,128)S(1)}, f32[32,1024]{1,0:T(8,128)S(1)}, u32[]{:S(2)}, u32[]{:S(2)}) collective-permute-start(f32[32,1024]{1,0:T(8,128)S(1)} %add.84), channel_id=1, source_target_pairs={{0,96},{1,25},{2,98},{3,27},{4,100},{5,29},{6,102},{7,31},{8,104},... | collective-permute-start | bytes 393224 | tf_op jit(solution)/shard_map/ppermute | solution.py:53
  168.0 22.6 %collective-permute-start.34 = (f32[8,1280]{1,0:T(8,128)S(1)}, f32[8,1280]{1,0:T(8,128)S(1)}, u32[]{:S(2)}, u32[]{:S(2)}) collective-permute-start(f32[8,1280]{1,0:T(8,128)S(1)} %get-tuple-element.134), channel_id=1, source_target_pairs={{0,1},{1,0},{2,3},{3,2},{4,5},{5,4},{6,7},{7,6},{8,9},{9,8},{10,11... | collective-permute-start | bytes 122888 | tf_op jit(solution)/shard_map/ppermute | solution.py:53
  190.6 4.1 %collective-permute-start.36 = (f32[8,1280]{1,0:T(8,128)S(1)}, f32[8,1280]{1,0:T(8,128)S(1)}, u32[]{:S(2)}, u32[]{:S(2)}) collective-permute-start(f32[8,1280]{1,0:T(8,128)S(1)} %add.88.last), channel_id=1, source_target_pairs={{0,2},{1,3},{2,4},{3,5},{4,6},{5,7},{6,0},{7,1},{8,10},{9,11},{10,... | collective-permute-start | bytes 122888 | tf_op jit(solution)/shard_map/ppermute | solution.py:53
  190.7 4.5 %collective-permute-start.37 = (f32[8,1280]{1,0:T(8,128)S(1)}, f32[8,1280]{1,0:T(8,128)S(1)}, u32[]{:S(2)}, u32[]{:S(2)}) collective-permute-start(f32[8,1280]{1,0:T(8,128)S(1)} %add.88.last), channel_id=1, source_target_pairs={{0,4},{1,5},{2,6},{3,7},{4,0},{5,1},{6,2},{7,3},{8,12},{9,13},{10,... | collective-permute-start | bytes 122888 | tf_op jit(solution)/shard_map/ppermute | solution.py:53
  192.1 4.1 %collective-permute-start.38 = (f32[8,1280]{1,0:T(8,128)S(1)}, f32[8,1280]{1,0:T(8,128)S(1)}, u32[]{:S(2)}, u32[]{:S(2)}) collective-permute-start(f32[8,1280]{1,0:T(8,128)S(1)} %add.88.last), channel_id=1, source_target_pairs={{0,6},{1,7},{2,0},{3,1},{4,2},{5,3},{6,4},{7,5},{8,14},{9,15},{10,... | collective-permute-start | bytes 122888 | tf_op jit(solution)/shard_map/ppermute | solution.py:53

commit v8 on v7

--- a/solution.py
+++ b/solution.py
@@ -835,6 +835,7 @@
     got = [up(last, step) for step in (1, 2, 3)]
     grad_weighted = after(own, grad_map) + near_up + near_down
     grad_expr = grad_weighted * (keep * (genes * all_spots))[None, :]
+    got = after(tuple(got), grad_expr)
 
     type_fraction = types * share
 

time: 199 us -> 198 us (level)
  starting transfers between devices: 60.5 us -> 52.9 us
  waiting for transfers between devices: 45.1 us -> 51.6 us
    ppermute x41, starting transfers between devices: 60.5 us -> 52.9 us  [send(): return lax.ppermute(array, ('cells', 'spots'), route(target))]
    ppermute x41, waiting for transfers between devices: 45.1 us -> 51.6 us  [send(): return lax.ppermute(array, ('cells', 'spots'), route(target))]
  transfers between devices with their start and end apart: 41 -> 41, of which waited for: 18 -> 18; matrix products, arithmetic and copies ran while one was open for 1% -> 2% of each run, Pallas kernels for 37% -> 37%
where the time goes in v8:
time: 198 us; the launch traced here: 197 us
  Pallas kernels  87.7 us (44%)
  starting transfers between devices  52.9 us (27%)
  waiting for transfers between devices  51.6 us (26%)
  other arithmetic  3.69 us (2%)
    ppermute x41, starting transfers between devices, send(): return lax.ppermute(array, ('cells', 'spots'), route(target))  52.9 us
    ppermute x41, waiting for transfers between devices, send(): return lax.ppermute(array, ('cells', 'spots'), route(target))  51.6 us
    pallas_call x5, Pallas kernels, back_call(): pl.pallas_call(functools.partial(back_kernel, parts=parts, first=len(firs...  23 us
    pallas_call x3, Pallas kernels, pred_call(): pl.pallas_call(functools.partial(pred_kernel, cuts=cuts), grid_spec=pltpu...  21.7 us
    pallas_call x1, Pallas kernels, map_call(): pl.pallas_call(functools.partial(map_kernel, scale=scale), grid=(cells //...  21.5 us
    pallas_call x1, Pallas kernels, expo_call(): pl.pallas_call(expo_kernel, grid_spec=pltpu.PrefetchScalarGridSpec(num_sc...  8.81 us
    pallas_call x3, Pallas kernels, grad_call(): pl.pallas_call(functools.partial(grad_kernel, count=count, lane=lane, chi...  7.63 us
  transfers between devices with their start and end apart: 41, of which 18 were waited for; matrix products, arithmetic and copies ran while one was open for 2% of the time, Pallas kernels for 37%

profile of v8, /device:TPU:1, one launch (start us, length us, event | category | flops | bytes accessed | tf_op | source)
XLA Modules:
  0.0 197.1 jit_solution(13563193361416276812)
XLA Ops:
  0.7 8.8 %expo.1 = (bf16[2,1280,1024]{2,1,0:T(8,128)(2,1)S(1)}, f32[32,1024]{1,0:T(8,128)S(1)}, f32[8,1024]{1,0:T(8,128)S(1)}, f32[33,8,1024]{2,1,0:T(8,128)S(1)}, f32[33,8,1024]{2,1,0:T(8,128)S(1)}) custom-call(s32[4]{0:T(128)S(1)} %pad_add_fusion.ids, f32[1280,1024]{1,0:T(8,128)} %logits.1, s32[10,128]{1,0:T(8,128)} %bitcast.66, f32[10,128]{1,0:T(8,128)} %bitcast.67, ...), custom_call_target="tpu_custom_call" | custom-call | bytes 1310720 | tf_op jit(solution)/shard_map/expo/pallas_call | solution.py:179
  9.5 2.5 %collective-permute-start = (f32[33,8,1024]{2,1,0:T(8,128)S(1)}, f32[33,8,1024]{2,1,0:T(8,128)S(1)}, u32[]{:S(2)}, u32[]{:S(2)}) collective-permute-start(f32[33,8,1024]{2,1,0:T(8,128)S(1)} %get-tuple-element.79), channel_id=1, source_target_pairs={{0,8},{1,33},{2,10},{3,35},{4,12},{5,37},{6,14},{7,39},{8,16},{9,4... | collective-permute-start | bytes 3244040 | tf_op jit(solution)/shard_map/ppermute | solution.py:53
  12.1 2.3 %collective-permute-start.1 = (f32[33,8,1024]{2,1,0:T(8,128)S(1)}, f32[33,8,1024]{2,1,0:T(8,128)S(1)}, u32[]{:S(2)}, u32[]{:S(2)}) collective-permute-start(f32[33,8,1024]{2,1,0:T(8,128)S(1)} %get-tuple-element.80), channel_id=1, source_target_pairs={{0,24},{1,97},{2,26},{3,99},{4,28},{5,101},{6,30},{7,103},{8,0},{9... | collective-permute-start | bytes 3244040 | tf_op jit(solution)/shard_map/ppermute | solution.py:53
  14.4 7.5 %pred_.3 = (f32[33,8,1024]{2,1,0:T(8,128)S(1)}, f32[33,8,1024]{2,1,0:T(8,128)S(1)}) custom-call(s32[4]{0:T(128)S(1)} %pad_add_fusion.ids, f32[8,16,16,1280]{3,2,1,0:T(8,128)} %bitcast.57, f32[8,16,16,1280]{3,2,1,0:T(8,128)} %bitcast.58, f32[1,1280]{1,0:T(1,128)S(1)} %reshape.99.keep, bf16[2,1280,1024]{2,1,0:T(8,128)(2,1)S(1)} %get-tuple-element.82.masses, ...), custom_call_target="tpu_custom_call" | custom-call | flops 503316480 | bytes 1245184 | tf_op jit(solution)/shard_map/pred/pallas_call | solution.py:252
  21.9 1.5 collective-permute-start.2
  23.4 3.6 %collective-permute-done.refs_0_ = f32[33,8,1024]{2,1,0:T(8,128)S(1)} collective-permute-done((f32[33,8,1024]{2,1,0:T(8,128)S(1)}, f32[33,8,1024]{2,1,0:T(8,128)S(1)}, u32[]{:S(2)}, u32[]{:S(2)}) %collective-permute-start) | collective-permute-done | bytes 1081376 | tf_op jit(solution)/shard_map/ppermute | solution.py:53
  27.0 6.6 %pred_.4 = (f32[33,8,1024]{2,1,0:T(8,128)S(1)}, f32[33,8,1024]{2,1,0:T(8,128)S(1)}) custom-call(s32[4]{0:T(128)S(1)} %pad_add_fusion.ids, f32[8,16,16,1280]{3,2,1,0:T(8,128)} %bitcast.59, f32[8,16,16,1280]{3,2,1,0:T(8,128)} %bitcast.60, f32[1,1280]{1,0:T(1,128)S(1)} %reshape.99.keep, bf16[2,1280,1024]{2,1,0:T(8,128)(2,1)S(1)} %get-tuple-element.82.masses, ...), custom_call_target="tpu_custom_call" | custom-call | flops 503316480 | bytes 1245184 | tf_op jit(solution)/shard_map/pred/pallas_call | solution.py:252
  34.7 2.0 collective-permute-start.5
  36.7 1.4 collective-permute-done.2.refs_0_
  38.9 7.6 %pred_.5 = (f32[33,8,1024]{2,1,0:T(8,128)S(1)}, f32[33,8,1024]{2,1,0:T(8,128)S(1)}) custom-call(s32[4]{0:T(128)S(1)} %pad_add_fusion.ids, f32[8,16,16,1280]{3,2,1,0:T(8,128)} %bitcast.61, f32[8,16,16,1280]{3,2,1,0:T(8,128)} %bitcast.62, f32[1,1280]{1,0:T(1,128)S(1)} %reshape.99.keep, bf16[2,1280,1024]{2,1,0:T(8,128)(2,1)S(1)} %get-tuple-element.82.masses, ...), custom_call_target="tpu_custom_call" | custom-call | flops 503316480 | bytes 1245184 | tf_op jit(solution)/shard_map/pred/pallas_call | solution.py:252
  46.4 4.0 %collective-permute-done.4.got0 = f32[33,8,1024]{2,1,0:T(8,128)S(1)} collective-permute-done((f32[33,8,1024]{2,1,0:T(8,128)S(1)}, f32[33,8,1024]{2,1,0:T(8,128)S(1)}, u32[]{:S(2)}, u32[]{:S(2)}) %collective-permute-start.4) | collective-permute-done | bytes 1081376 | tf_op jit(solution)/shard_map/ppermute | solution.py:53
  51.2 2.5 %collective-permute-start.9 = (f32[17,8,1024]{2,1,0:T(8,128)S(1)}, f32[17,8,1024]{2,1,0:T(8,128)S(1)}, u32[]{:S(2)}, u32[]{:S(2)}) collective-permute-start(f32[17,8,1024]{2,1,0:T(8,128)S(1)} %get-tuple-element.99), channel_id=1, source_target_pairs={{0,96},{1,25},{2,98},{3,27},{4,100},{5,29},{6,102},{7,31},{8,104},... | collective-permute-start | bytes 1671176 | tf_op jit(solution)/shard_map/ppermute | solution.py:53
  56.5 4.5 %collective-permute-done.6 = f32[32,1024]{1,0:T(8,128)S(1)} collective-permute-done((f32[32,1024]{1,0:T(8,128)S(1)}, f32[32,1024]{1,0:T(8,128)S(1)}, u32[]{:S(2)}, u32[]{:S(2)}) %collective-permute-start.6) | collective-permute-done | bytes 131104 | tf_op jit(solution)/shard_map/ppermute | solution.py:53
  61.0 2.0 %collective-permute-done.9 = f32[17,8,1024]{2,1,0:T(8,128)S(1)} collective-permute-done((f32[17,8,1024]{2,1,0:T(8,128)S(1)}, f32[17,8,1024]{2,1,0:T(8,128)S(1)}, u32[]{:S(2)}, u32[]{:S(2)}) %collective-permute-start.9) | collective-permute-done | bytes 557088 | tf_op jit(solution)/shard_map/ppermute | solution.py:53
  63.0 1.4 collective-permute-done.8
  64.4 5.5 %collective-permute-done.7 = f32[17,8,1024]{2,1,0:T(8,128)S(1)} collective-permute-done((f32[17,8,1024]{2,1,0:T(8,128)S(1)}, f32[17,8,1024]{2,1,0:T(8,128)S(1)}, u32[]{:S(2)}, u32[]{:S(2)}) %collective-permute-start.7) | collective-permute-done | bytes 557088 | tf_op jit(solution)/shard_map/ppermute | solution.py:53
  70.1 1.9 collective-permute-start.10
  74.1 2.7 %collective-permute-start.15 = (f32[32,1024]{1,0:T(8,128)S(1)}, f32[32,1024]{1,0:T(8,128)S(1)}, u32[]{:S(2)}, u32[]{:S(2)}) collective-permute-start(f32[32,1024]{1,0:T(8,128)S(1)} %add.71), channel_id=1, source_target_pairs={{0,24},{1,97},{2,26},{3,99},{4,28},{5,101},{6,30},{7,103},{8,16},{... | collective-permute-start | bytes 393224 | tf_op jit(solution)/shard_map/ppermute | solution.py:53
  76.8 3.5 %collective-permute-done.13 = f32[64,128]{1,0:T(8,128)S(1)} collective-permute-done((f32[64,128]{1,0:T(8,128)S(1)}, f32[64,128]{1,0:T(8,128)S(1)}, u32[]{:S(2)}, u32[]{:S(2)}) %collective-permute-start.13) | collective-permute-done | bytes 32800 | tf_op jit(solution)/shard_map/ppermute | solution.py:53
  80.6 9.8 %collective-permute-done.14 = f32[64,128]{1,0:T(8,128)S(1)} collective-permute-done((f32[64,128]{1,0:T(8,128)S(1)}, f32[64,128]{1,0:T(8,128)S(1)}, u32[]{:S(2)}, u32[]{:S(2)}) %collective-permute-start.14) | collective-permute-done | bytes 32800 | tf_op jit(solution)/shard_map/ppermute | solution.py:53
  90.7 2.7 %collective-permute-start.17 = (f32[2,8,16,1024]{3,2,1,0:T(8,128)S(1)}, f32[2,8,16,1024]{3,2,1,0:T(8,128)S(1)}, u32[]{:S(2)}, u32[]{:S(2)}) collective-permute-start(f32[2,8,16,1024]{3,2,1,0:T(8,128)S(1)} %pad_maximum_fusion.1.refs_1_), channel_id=1, source_target_pairs={{0,24},{1,97},{2,26},{3,99},{4,28},{5,101},{6,30},{7,103},{8,0},{9... | collective-permute-start | bytes 3145736 | tf_op jit(solution)/shard_map/ppermute | solution.py:53
  94.4 2.0 %collective-permute-done.18 = f32[64,128]{1,0:T(8,128)S(1)} collective-permute-done((f32[64,128]{1,0:T(8,128)S(1)}, f32[64,128]{1,0:T(8,128)S(1)}, u32[]{:S(2)}, u32[]{:S(2)}) %collective-permute-start.18) | collective-permute-done | bytes 32800 | tf_op jit(solution)/shard_map/ppermute | solution.py:53
  96.4 2.0 %collective-permute-start.19 = (f32[64,128]{1,0:T(8,128)S(1)}, f32[64,128]{1,0:T(8,128)S(1)}, u32[]{:S(2)}, u32[]{:S(2)}) collective-permute-start(f32[64,128]{1,0:T(8,128)S(1)} %add.78), channel_id=1, source_target_pairs={{0,96},{1,25},{2,98},{3,27},{4,100},{5,29},{6,102},{7,31},{8,104},... | collective-permute-start | bytes 98312 | tf_op jit(solution)/shard_map/ppermute | solution.py:53
  98.4 2.7 %collective-permute-start.25 = (f32[2,8,16,1024]{3,2,1,0:T(8,128)S(1)}, f32[2,8,16,1024]{3,2,1,0:T(8,128)S(1)}, u32[]{:S(2)}, u32[]{:S(2)}) collective-permute-start(f32[2,8,16,1024]{3,2,1,0:T(8,128)S(1)} %pad_maximum_fusion.refs_0_), channel_id=1, source_target_pairs={{0,24},{1,97},{2,26},{3,99},{4,28},{5,101},{6,30},{7,103},{8,0},{9... | collective-permute-start | bytes 3145736 | tf_op jit(solution)/shard_map/ppermute | solution.py:53
  101.1 5.1 %collective-permute-done.16.refs_2_ = f32[2,8,16,1024]{3,2,1,0:T(8,128)S(1)} collective-permute-done((f32[2,8,16,1024]{3,2,1,0:T(8,128)S(1)}, f32[2,8,16,1024]{3,2,1,0:T(8,128)S(1)}, u32[]{:S(2)}, u32[]{:S(2)}) %collective-permute-start.16) | collective-permute-done | bytes 1048608 | tf_op jit(solution)/shard_map/ppermute | solution.py:53
  106.2 2.7 %collective-permute-start.21 = (f32[2,8,16,1024]{3,2,1,0:T(8,128)S(1)}, f32[2,8,16,1024]{3,2,1,0:T(8,128)S(1)}, u32[]{:S(2)}, u32[]{:S(2)}) collective-permute-start(f32[2,8,16,1024]{3,2,1,0:T(8,128)S(1)} %collective-permute-done.17.refs_5_), channel_id=1, source_target_pairs={{0,24},{1,97},{2,26},{3,99},{4,28},{5,101},{6,30},{7,103},{8,0},{9... | collective-permute-start | bytes 3145736 | tf_op jit(solution)/shard_map/ppermute | solution.py:53
  108.9 3.1 %collective-permute-start.22 = (f32[56,128]{1,0:T(8,128)S(1)}, f32[56,128]{1,0:T(8,128)S(1)}, u32[]{:S(2)}, u32[]{:S(2)}) collective-permute-start(f32[56,128]{1,0:T(8,128)S(1)} %pad_maximum_fusion.2), channel_id=1, source_target_pairs={{0,1},{1,0},{2,3},{3,2},{4,5},{5,4},{6,7},{7,6},{8,9},{9,8},{10,11... | collective-permute-start | bytes 86024 | tf_op jit(solution)/shard_map/ppermute | solution.py:53
  112.8 1.3 collective-permute-start.23
  114.1 1.7 collective-permute-done.23
  115.9 1.6 collective-permute-done.24.refs_3_
  117.4 2.7 %collective-permute-start.26 = (f32[56,128]{1,0:T(8,128)S(1)}, f32[56,128]{1,0:T(8,128)S(1)}, u32[]{:S(2)}, u32[]{:S(2)}) collective-permute-start(f32[56,128]{1,0:T(8,128)S(1)} %add.81), channel_id=1, source_target_pairs={{0,6},{1,7},{2,4},{3,5},{4,2},{5,3},{6,0},{7,1},{8,14},{9,15},{10,... | collective-permute-start | bytes 86024 | tf_op jit(solution)/shard_map/ppermute | solution.py:53
  120.2 1.6 collective-permute-done.26
  122.6 4.7 %grad.3 = (bf16[2,8,256,1024]{3,2,1,0:T(8,128)(2,1)S(1)}, f32[8,1024]{1,0:T(8,128)S(1)}) custom-call(s32[4]{0:T(128)S(1)} %pad_add_fusion.ids, f32[2,8,16,1024]{3,2,1,0:T(8,128)S(1)} %pad_maximum_fusion.refs_0_, f32[2,8,16,1024]{3,2,1,0:T(8,128)S(1)} %pad_maximum_fusion.1.refs_1_, f32[2,8,16,1024]{3,2,1,0:T(8,128)S(1)} %collective-permute-done.16.refs_2_, ...), custom_call_target="tpu_custom_call" | custom-call | tf_op jit(solution)/shard_map/grad/pallas_call | solution.py:477
  127.3 1.3 collective-permute-done.20.refs_0_
  129.6 3.1 %back.5 = (f32[8,1280]{1,0:T(8,128)S(1)}, f32[256,1280]{1,0:T(8,128)S(1)}) custom-call(s32[4]{0:T(128)S(1)} %pad_add_fusion.ids, bf16[2,8,256,1024]{3,2,1,0:T(8,128)(2,1)S(1)} %get-tuple-element.113.grad.refs_5_, bf16[2,1280,1024]{2,1,0:T(8,128)(2,1)S(1)} %get-tuple-element.82.masses, f32[2048,1280]{1,0:T(8,128)} %expr.11, ...), custom_call_target="tpu_custom_call" | custom-call | tf_op jit(solution)/shard_map/back/pallas_call | solution.py:553
  132.7 2.6 %collective-permute-start.27 = (f32[256,1280]{1,0:T(8,128)S(1)}, f32[256,1280]{1,0:T(8,128)S(1)}, u32[]{:S(2)}, u32[]{:S(2)}) collective-permute-start(f32[256,1280]{1,0:T(8,128)S(1)} %get-tuple-element.114), channel_id=1, source_target_pairs={{0,1},{1,0},{2,3},{3,2},{4,5},{5,4},{6,7},{7,6},{8,9},{9,8},{10,11... | collective-permute-start | bytes 3932168 | tf_op jit(solution)/shard_map/ppermute | solution.py:53
  135.3 3.6 %back.6 = (f32[8,1280]{1,0:T(8,128)S(1)}, f32[256,1280]{1,0:T(8,128)S(1)}) custom-call(s32[4]{0:T(128)S(1)} %pad_add_fusion.ids, bf16[2,8,256,1024]{3,2,1,0:T(8,128)(2,1)S(1)} %get-tuple-element.113.grad.refs_5_, bf16[2,1280,1024]{2,1,0:T(8,128)(2,1)S(1)} %get-tuple-element.82.masses, f32[2048,1280]{1,0:T(8,128)} %expr.11), custom_call_target="tpu_custom_call" | custom-call | tf_op jit(solution)/shard_map/back/pallas_call | solution.py:553
  139.2 1.4 collective-permute-start.28
  140.5 1.8 collective-permute-start.29
  142.3 1.9 grad.5
  144.2 8.0 %back.7 = (f32[8,1280]{1,0:T(8,128)S(1)}, f32[256,1280]{1,0:T(8,128)S(1)}, f32[256,1280]{1,0:T(8,128)S(1)}, f32[256,1280]{1,0:T(8,128)S(1)}) custom-call(s32[4]{0:T(128)S(1)} %pad_add_fusion.ids, bf16[2,8,256,1024]{3,2,1,0:T(8,128)(2,1)S(1)} %get-tuple-element.118.grad, bf16[2,1280,1024]{2,1,0:T(8,128)(2,1)S(1)} %get-tuple-element.82.masses, f32[2048,1280]{1,0:T(8,128)} %expr.11), custom_call_target="tpu_custom_call" | custom-call | tf_op jit(solution)/shard_map/back/pallas_call | solution.py:553
  152.9 5.5 %back.8 = (f32[8,1280]{1,0:T(8,128)S(1)}, f32[256,1280]{1,0:T(8,128)S(1)}, f32[256,1280]{1,0:T(8,128)S(1)}) custom-call(s32[4]{0:T(128)S(1)} %pad_add_fusion.ids, bf16[2,8,256,1024]{3,2,1,0:T(8,128)(2,1)S(1)} %get-tuple-element.118.grad, bf16[2,1280,1024]{2,1,0:T(8,128)(2,1)S(1)} %get-tuple-element.82.masses, f32[2048,1280]{1,0:T(8,128)} %expr.11), custom_call_target="tpu_custom_call" | custom-call | tf_op jit(solution)/shard_map/back/pallas_call | solution.py:553
  160.4 1.6 collective-permute-start.40
  162.1 2.4 %collective-permute-start.33 = (f32[32,1024]{1,0:T(8,128)S(1)}, f32[32,1024]{1,0:T(8,128)S(1)}, u32[]{:S(2)}, u32[]{:S(2)}) collective-permute-start(f32[32,1024]{1,0:T(8,128)S(1)} %add.84), channel_id=1, source_target_pairs={{0,96},{1,25},{2,98},{3,27},{4,100},{5,29},{6,102},{7,31},{8,104},... | collective-permute-start | bytes 393224 | tf_op jit(solution)/shard_map/ppermute | solution.py:53
  164.5 3.0 %back.9 = (f32[8,1280]{1,0:T(8,128)S(1)}, f32[256,1280]{1,0:T(8,128)S(1)}) custom-call(s32[4]{0:T(128)S(1)} %pad_add_fusion.ids, bf16[2,8,256,1024]{3,2,1,0:T(8,128)(2,1)S(1)} %get-tuple-element.118.grad, bf16[2,1280,1024]{2,1,0:T(8,128)(2,1)S(1)} %get-tuple-element.82.masses, f32[2048,1280]{1,0:T(8,128)} %expr.11, ...), custom_call_target="tpu_custom_call" | custom-call | tf_op jit(solution)/shard_map/back/pallas_call | solution.py:553
  167.6 21.5 %grad_map.1 = f32[1280,1024]{1,0:T(8,128)} custom-call(f32[2048,1280]{1,0:T(8,128)} %expr.11, bf16[2,2048,1024]{2,1,0:T(8,128)(2,1)S(1)} %bitcast.38, bf16[2,1280,1024]{2,1,0:T(8,128)(2,1)S(1)} %get-tuple-element.82.masses, f32[10,128]{1,0:T(8,128)S(1)} %bitcast.52, f32[10,128]{1,0:T(8,128)S(1)} %convert_bitcast_fusion.valid, ...), custom_call_target="tpu_custom_call" | custom-call | tf_op jit(solution)/shard_map/grad_map/pallas_call | solution.py:660
  189.5 3.8 %collective-permute-start.37 = (f32[8,1280]{1,0:T(8,128)S(1)}, f32[8,1280]{1,0:T(8,128)S(1)}, u32[]{:S(2)}, u32[]{:S(2)}) collective-permute-start(f32[8,1280]{1,0:T(8,128)S(1)} %add.88.last), channel_id=1, source_target_pairs={{0,4},{1,5},{2,6},{3,7},{4,0},{5,1},{6,2},{7,3},{8,12},{9,13},{10,... | collective-permute-start | bytes 122888 | tf_op jit(solution)/shard_map/ppermute | solution.py:53
  194.0 1.3 add_multiply_fusion
  (104 shorter events, 18.3 us)
Async XLA Ops:
  0.7 13.7 %copy-start = (s32[1280]{0:T(1024)S(1)}, s32[1280]{0:T(1024)}, u32[]{:S(2)}) copy-start(s32[1280]{0:T(1024)} %param.11) | copy-start | bytes 15364
  0.7 13.7 %copy-start.1 = (f32[1280]{0:T(1024)S(1)}, f32[1280]{0:T(1024)}, u32[]{:S(2)}) copy-start(f32[1280]{0:T(1024)} %param.8) | copy-start | bytes 15364
  9.5 17.4 %collective-permute-start = (f32[33,8,1024]{2,1,0:T(8,128)S(1)}, f32[33,8,1024]{2,1,0:T(8,128)S(1)}, u32[]{:S(2)}, u32[]{:S(2)}) collective-permute-start(f32[33,8,1024]{2,1,0:T(8,128)S(1)} %get-tuple-element.79), channel_id=1, source_target_pairs={{0,8},{1,33},{2,10},{3,35},{4,12},{5,37},{6,14},{7,39},{8,16},{9,4... | collective-permute-start | bytes 3244040 | tf_op jit(solution)/shard_map/ppermute | solution.py:53
  12.1 14.9 %collective-permute-start.1 = (f32[33,8,1024]{2,1,0:T(8,128)S(1)}, f32[33,8,1024]{2,1,0:T(8,128)S(1)}, u32[]{:S(2)}, u32[]{:S(2)}) collective-permute-start(f32[33,8,1024]{2,1,0:T(8,128)S(1)} %get-tuple-element.80), channel_id=1, source_target_pairs={{0,24},{1,97},{2,26},{3,99},{4,28},{5,101},{6,30},{7,103},{8,0},{9... | collective-permute-start | bytes 3244040 | tf_op jit(solution)/shard_map/ppermute | solution.py:53
  21.9 16.2 %collective-permute-start.2 = (f32[33,8,1024]{2,1,0:T(8,128)S(1)}, f32[33,8,1024]{2,1,0:T(8,128)S(1)}, u32[]{:S(2)}, u32[]{:S(2)}) collective-permute-start(f32[33,8,1024]{2,1,0:T(8,128)S(1)} %get-tuple-element.85), channel_id=1, source_target_pairs={{0,24},{1,97},{2,26},{3,99},{4,28},{5,101},{6,30},{7,103},{8,0},{9... | collective-permute-start | bytes 3244040 | tf_op jit(solution)/shard_map/ppermute | solution.py:53
  23.3 13.3 %copy-start.2 = (s32[1024]{0:T(1024)S(1)}, s32[1024]{0:T(1024)}, u32[]{:S(2)}) copy-start(s32[1024]{0:T(1024)} %param.13) | copy-start | bytes 12292
  23.3 13.3 %copy-start.3 = (s32[1024]{0:T(1024)S(1)}, s32[1024]{0:T(1024)}, u32[]{:S(2)}) copy-start(s32[1024]{0:T(1024)} %param.12) | copy-start | bytes 12292
  23.4 15.5 %collective-permute-start.3 = (f32[33,8,1024]{2,1,0:T(8,128)S(1)}, f32[33,8,1024]{2,1,0:T(8,128)S(1)}, u32[]{:S(2)}, u32[]{:S(2)}) collective-permute-start(f32[33,8,1024]{2,1,0:T(8,128)S(1)} %get-tuple-element.84), channel_id=1, source_target_pairs={{0,8},{1,33},{2,10},{3,35},{4,12},{5,37},{6,14},{7,39},{8,16},{9,4... | collective-permute-start | bytes 3244040 | tf_op jit(solution)/shard_map/ppermute | solution.py:53
  33.6 16.8 %collective-permute-start.4 = (f32[33,8,1024]{2,1,0:T(8,128)S(1)}, f32[33,8,1024]{2,1,0:T(8,128)S(1)}, u32[]{:S(2)}, u32[]{:S(2)}) collective-permute-start(f32[33,8,1024]{2,1,0:T(8,128)S(1)} %get-tuple-element.87), channel_id=1, source_target_pairs={{0,8},{1,33},{2,10},{3,35},{4,12},{5,37},{6,14},{7,39},{8,16},{9,4... | collective-permute-start | bytes 3244040 | tf_op jit(solution)/shard_map/ppermute | solution.py:53
  34.7 15.7 %collective-permute-start.5 = (f32[33,8,1024]{2,1,0:T(8,128)S(1)}, f32[33,8,1024]{2,1,0:T(8,128)S(1)}, u32[]{:S(2)}, u32[]{:S(2)}) collective-permute-start(f32[33,8,1024]{2,1,0:T(8,128)S(1)} %get-tuple-element.88), channel_id=1, source_target_pairs={{0,24},{1,97},{2,26},{3,99},{4,28},{5,101},{6,30},{7,103},{8,0},{9... | collective-permute-start | bytes 3244040 | tf_op jit(solution)/shard_map/ppermute | solution.py:53
  36.7 17.9 %slice-start = ((s8[8388608]{0:T(1024)(128)(4,1)}), s8[4194304]{0:T(1024)(128)(4,1)S(1)}, s32[]{:S(2)}) async-start(s8[8388608]{0:T(1024)(128)(4,1)} %bitcast.39), calls=%async_computation | async-start | bytes 8388608
  36.7 17.9 %slice-start.1 = ((s8[8388608]{0:T(1024)(128)(4,1)}), s8[4194304]{0:T(1024)(128)(4,1)S(1)}, s32[]{:S(2)}) async-start(s8[8388608]{0:T(1024)(128)(4,1)} %bitcast.39), calls=%async_computation.1 | async-start | bytes 8388608
  51.2 11.8 %collective-permute-start.9 = (f32[17,8,1024]{2,1,0:T(8,128)S(1)}, f32[17,8,1024]{2,1,0:T(8,128)S(1)}, u32[]{:S(2)}, u32[]{:S(2)}) collective-permute-start(f32[17,8,1024]{2,1,0:T(8,128)S(1)} %get-tuple-element.99), channel_id=1, source_target_pairs={{0,96},{1,25},{2,98},{3,27},{4,100},{5,29},{6,102},{7,31},{8,104},... | collective-permute-start | bytes 1671176 | tf_op jit(solution)/shard_map/ppermute | solution.py:53
  53.8 10.6 %collective-permute-start.8 = (f32[17,8,1024]{2,1,0:T(8,128)S(1)}, f32[17,8,1024]{2,1,0:T(8,128)S(1)}, u32[]{:S(2)}, u32[]{:S(2)}) collective-permute-start(f32[17,8,1024]{2,1,0:T(8,128)S(1)} %get-tuple-element.98), channel_id=1, source_target_pairs={{0,64},{1,17},{2,66},{3,19},{4,68},{5,21},{6,70},{7,23},{8,72},{9,... | collective-permute-start | bytes 1671176 | tf_op jit(solution)/shard_map/ppermute | solution.py:53
  54.0 15.9 %collective-permute-start.7 = (f32[17,8,1024]{2,1,0:T(8,128)S(1)}, f32[17,8,1024]{2,1,0:T(8,128)S(1)}, u32[]{:S(2)}, u32[]{:S(2)}) collective-permute-start(f32[17,8,1024]{2,1,0:T(8,128)S(1)} %get-tuple-element.97), channel_id=1, source_target_pairs={{0,32},{1,9},{2,34},{3,11},{4,36},{5,13},{6,38},{7,15},{8,40},{9,1... | collective-permute-start | bytes 1671176 | tf_op jit(solution)/shard_map/ppermute | solution.py:53
  55.3 5.7 %collective-permute-start.6 = (f32[32,1024]{1,0:T(8,128)S(1)}, f32[32,1024]{1,0:T(8,128)S(1)}, u32[]{:S(2)}, u32[]{:S(2)}) collective-permute-start(f32[32,1024]{1,0:T(8,128)S(1)} %get-tuple-element.95), channel_id=1, source_target_pairs={{0,8},{1,33},{2,10},{3,35},{4,12},{5,37},{6,14},{7,39},{8,0},{9,41... | collective-permute-start | bytes 393224 | tf_op jit(solution)/shard_map/ppermute | solution.py:53
  70.1 20.3 %collective-permute-start.10 = (f32[8,16,1024]{2,1,0:T(8,128)S(1)}, f32[8,16,1024]{2,1,0:T(8,128)S(1)}, u32[]{:S(2)}, u32[]{:S(2)}) collective-permute-start(f32[8,16,1024]{2,1,0:T(8,128)S(1)} %bitcast.47), channel_id=1, source_target_pairs={{0,96},{1,25},{2,98},{3,27},{4,100},{5,29},{6,102},{7,31},{8,104},... | collective-permute-start | bytes 1572872 | tf_op jit(solution)/shard_map/ppermute | solution.py:53
  72.0 18.5 %collective-permute-start.12 = (f32[8,16,1024]{2,1,0:T(8,128)S(1)}, f32[8,16,1024]{2,1,0:T(8,128)S(1)}, u32[]{:S(2)}, u32[]{:S(2)}) collective-permute-start(f32[8,16,1024]{2,1,0:T(8,128)S(1)} %bitcast.48), channel_id=1, source_target_pairs={{0,32},{1,9},{2,34},{3,11},{4,36},{5,13},{6,38},{7,15},{8,40},{9,1... | collective-permute-start | bytes 1572872 | tf_op jit(solution)/shard_map/ppermute | solution.py:53
  72.0 18.5 %collective-permute-start.11 = (f32[8,16,1024]{2,1,0:T(8,128)S(1)}, f32[8,16,1024]{2,1,0:T(8,128)S(1)}, u32[]{:S(2)}, u32[]{:S(2)}) collective-permute-start(f32[8,16,1024]{2,1,0:T(8,128)S(1)} %bitcast.49), channel_id=1, source_target_pairs={{0,64},{1,17},{2,66},{3,19},{4,68},{5,21},{6,70},{7,23},{8,72},{9,... | collective-permute-start | bytes 1572872 | tf_op jit(solution)/shard_map/ppermute | solution.py:53
  74.1 16.3 %collective-permute-start.15 = (f32[32,1024]{1,0:T(8,128)S(1)}, f32[32,1024]{1,0:T(8,128)S(1)}, u32[]{:S(2)}, u32[]{:S(2)}) collective-permute-start(f32[32,1024]{1,0:T(8,128)S(1)} %add.71), channel_id=1, source_target_pairs={{0,24},{1,97},{2,26},{3,99},{4,28},{5,101},{6,30},{7,103},{8,16},{... | collective-permute-start | bytes 393224 | tf_op jit(solution)/shard_map/ppermute | solution.py:53
  76.8 3.5 %collective-permute-start.13 = (f32[64,128]{1,0:T(8,128)S(1)}, f32[64,128]{1,0:T(8,128)S(1)}, u32[]{:S(2)}, u32[]{:S(2)}) collective-permute-start(f32[64,128]{1,0:T(8,128)S(1)} %get-tuple-element.100), channel_id=1, source_target_pairs={{0,8},{1,33},{2,10},{3,35},{4,12},{5,37},{6,14},{7,39},{8,0},{9,41... | collective-permute-start | bytes 98312 | tf_op jit(solution)/shard_map/ppermute | solution.py:53
  80.3 10.1 %collective-permute-start.14 = (f32[64,128]{1,0:T(8,128)S(1)}, f32[64,128]{1,0:T(8,128)S(1)}, u32[]{:S(2)}, u32[]{:S(2)}) collective-permute-start(f32[64,128]{1,0:T(8,128)S(1)} %add.75), channel_id=1, source_target_pairs={{0,24},{1,97},{2,26},{3,99},{4,28},{5,101},{6,30},{7,103},{8,16},{... | collective-permute-start | bytes 98312 | tf_op jit(solution)/shard_map/ppermute | solution.py:53
  90.6 15.6 %collective-permute-start.16 = (f32[2,8,16,1024]{3,2,1,0:T(8,128)S(1)}, f32[2,8,16,1024]{3,2,1,0:T(8,128)S(1)}, u32[]{:S(2)}, u32[]{:S(2)}) collective-permute-start(f32[2,8,16,1024]{3,2,1,0:T(8,128)S(1)} %pad_maximum_fusion.refs_0_), channel_id=1, source_target_pairs={{0,8},{1,33},{2,10},{3,35},{4,12},{5,37},{6,14},{7,39},{8,16},{9,4... | collective-permute-start | bytes 3145736 | tf_op jit(solution)/shard_map/ppermute | solution.py:53
  90.7 15.5 %collective-permute-start.17 = (f32[2,8,16,1024]{3,2,1,0:T(8,128)S(1)}, f32[2,8,16,1024]{3,2,1,0:T(8,128)S(1)}, u32[]{:S(2)}, u32[]{:S(2)}) collective-permute-start(f32[2,8,16,1024]{3,2,1,0:T(8,128)S(1)} %pad_maximum_fusion.1.refs_1_), channel_id=1, source_target_pairs={{0,24},{1,97},{2,26},{3,99},{4,28},{5,101},{6,30},{7,103},{8,0},{9... | collective-permute-start | bytes 3145736 | tf_op jit(solution)/shard_map/ppermute | solution.py:53
  93.4 3.1 %collective-permute-start.18 = (f32[64,128]{1,0:T(8,128)S(1)}, f32[64,128]{1,0:T(8,128)S(1)}, u32[]{:S(2)}, u32[]{:S(2)}) collective-permute-start(f32[64,128]{1,0:T(8,128)S(1)} %add.76), channel_id=1, source_target_pairs={{0,32},{1,9},{2,34},{3,11},{4,36},{5,13},{6,38},{7,15},{8,40},{9,1... | collective-permute-start | bytes 98312 | tf_op jit(solution)/shard_map/ppermute | solution.py:53
  96.4 4.7 %collective-permute-start.19 = (f32[64,128]{1,0:T(8,128)S(1)}, f32[64,128]{1,0:T(8,128)S(1)}, u32[]{:S(2)}, u32[]{:S(2)}) collective-permute-start(f32[64,128]{1,0:T(8,128)S(1)} %add.78), channel_id=1, source_target_pairs={{0,96},{1,25},{2,98},{3,27},{4,100},{5,29},{6,102},{7,31},{8,104},... | collective-permute-start | bytes 98312 | tf_op jit(solution)/shard_map/ppermute | solution.py:53
  98.4 19.0 %collective-permute-start.24 = (f32[2,8,16,1024]{3,2,1,0:T(8,128)S(1)}, f32[2,8,16,1024]{3,2,1,0:T(8,128)S(1)}, u32[]{:S(2)}, u32[]{:S(2)}) collective-permute-start(f32[2,8,16,1024]{3,2,1,0:T(8,128)S(1)} %pad_maximum_fusion.1.refs_1_), channel_id=1, source_target_pairs={{0,8},{1,33},{2,10},{3,35},{4,12},{5,37},{6,14},{7,39},{8,16},{9,4... | collective-permute-start | bytes 3145736 | tf_op jit(solution)/shard_map/ppermute | solution.py:53
  98.4 19.0 %collective-permute-start.25 = (f32[2,8,16,1024]{3,2,1,0:T(8,128)S(1)}, f32[2,8,16,1024]{3,2,1,0:T(8,128)S(1)}, u32[]{:S(2)}, u32[]{:S(2)}) collective-permute-start(f32[2,8,16,1024]{3,2,1,0:T(8,128)S(1)} %pad_maximum_fusion.refs_0_), channel_id=1, source_target_pairs={{0,24},{1,97},{2,26},{3,99},{4,28},{5,101},{6,30},{7,103},{8,0},{9... | collective-permute-start | bytes 3145736 | tf_op jit(solution)/shard_map/ppermute | solution.py:53
  106.2 22.5 %collective-permute-start.20 = (f32[2,8,16,1024]{3,2,1,0:T(8,128)S(1)}, f32[2,8,16,1024]{3,2,1,0:T(8,128)S(1)}, u32[]{:S(2)}, u32[]{:S(2)}) collective-permute-start(f32[2,8,16,1024]{3,2,1,0:T(8,128)S(1)} %collective-permute-done.16.refs_2_), channel_id=1, source_target_pairs={{0,8},{1,33},{2,10},{3,35},{4,12},{5,37},{6,14},{7,39},{8,16},{9,4... | collective-permute-start | bytes 3145736 | tf_op jit(solution)/shard_map/ppermute | solution.py:53
  106.2 22.5 %collective-permute-start.21 = (f32[2,8,16,1024]{3,2,1,0:T(8,128)S(1)}, f32[2,8,16,1024]{3,2,1,0:T(8,128)S(1)}, u32[]{:S(2)}, u32[]{:S(2)}) collective-permute-start(f32[2,8,16,1024]{3,2,1,0:T(8,128)S(1)} %collective-permute-done.17.refs_5_), channel_id=1, source_target_pairs={{0,24},{1,97},{2,26},{3,99},{4,28},{5,101},{6,30},{7,103},{8,0},{9... | collective-permute-start | bytes 3145736 | tf_op jit(solution)/shard_map/ppermute | solution.py:53
  108.9 3.9 %collective-permute-start.22 = (f32[56,128]{1,0:T(8,128)S(1)}, f32[56,128]{1,0:T(8,128)S(1)}, u32[]{:S(2)}, u32[]{:S(2)}) collective-permute-start(f32[56,128]{1,0:T(8,128)S(1)} %pad_maximum_fusion.2), channel_id=1, source_target_pairs={{0,1},{1,0},{2,3},{3,2},{4,5},{5,4},{6,7},{7,6},{8,9},{9,8},{10,11... | collective-permute-start | bytes 86024 | tf_op jit(solution)/shard_map/ppermute | solution.py:53
  112.8 3.0 %collective-permute-start.23 = (f32[56,128]{1,0:T(8,128)S(1)}, f32[56,128]{1,0:T(8,128)S(1)}, u32[]{:S(2)}, u32[]{:S(2)}) collective-permute-start(f32[56,128]{1,0:T(8,128)S(1)} %fusion.3), channel_id=1, source_target_pairs={{0,2},{1,3},{2,0},{3,1},{4,6},{5,7},{6,4},{7,5},{8,10},{9,11},{10,... | collective-permute-start | bytes 86024 | tf_op jit(solution)/shard_map/ppermute | solution.py:53
  117.4 4.3 %collective-permute-start.26 = (f32[56,128]{1,0:T(8,128)S(1)}, f32[56,128]{1,0:T(8,128)S(1)}, u32[]{:S(2)}, u32[]{:S(2)}) collective-permute-start(f32[56,128]{1,0:T(8,128)S(1)} %add.81), channel_id=1, source_target_pairs={{0,6},{1,7},{2,4},{3,5},{4,2},{5,3},{6,0},{7,1},{8,14},{9,15},{10,... | collective-permute-start | bytes 86024 | tf_op jit(solution)/shard_map/ppermute | solution.py:53
  132.7 6.2 %collective-permute-start.27 = (f32[256,1280]{1,0:T(8,128)S(1)}, f32[256,1280]{1,0:T(8,128)S(1)}, u32[]{:S(2)}, u32[]{:S(2)}) collective-permute-start(f32[256,1280]{1,0:T(8,128)S(1)} %get-tuple-element.114), channel_id=1, source_target_pairs={{0,1},{1,0},{2,3},{3,2},{4,5},{5,4},{6,7},{7,6},{8,9},{9,8},{10,11... | collective-permute-start | bytes 3932168 | tf_op jit(solution)/shard_map/ppermute | solution.py:53
  139.2 19.5 %collective-permute-start.28 = (f32[128,1280]{1,0:T(8,128)S(1)}, f32[128,1280]{1,0:T(8,128)S(1)}, u32[]{:S(2)}, u32[]{:S(2)}) collective-permute-start(f32[128,1280]{1,0:T(8,128)S(1)} %get-tuple-element.159), channel_id=1, source_target_pairs={{0,2},{1,3},{2,4},{3,5},{4,6},{5,7},{6,0},{7,1},{8,10},{9,11},{10,... | collective-permute-start | bytes 1966088 | tf_op jit(solution)/shard_map/ppermute | solution.py:53
  140.5 18.2 %collective-permute-start.29 = (f32[128,1280]{1,0:T(8,128)S(1)}, f32[128,1280]{1,0:T(8,128)S(1)}, u32[]{:S(2)}, u32[]{:S(2)}) collective-permute-start(f32[128,1280]{1,0:T(8,128)S(1)} %get-tuple-element.158), channel_id=1, source_target_pairs={{0,6},{1,7},{2,0},{3,1},{4,2},{5,3},{6,4},{7,5},{8,14},{9,15},{10,... | collective-permute-start | bytes 1966088 | tf_op jit(solution)/shard_map/ppermute | solution.py:53
  152.2 7.3 %collective-permute-start.31 = (f32[256,1280]{1,0:T(8,128)S(1)}, f32[256,1280]{1,0:T(8,128)S(1)}, u32[]{:S(2)}, u32[]{:S(2)}) collective-permute-start(f32[256,1280]{1,0:T(8,128)S(1)} %get-tuple-element.119), channel_id=1, source_target_pairs={{0,1},{1,0},{2,3},{3,2},{4,5},{5,4},{6,7},{7,6},{8,9},{9,8},{10,11... | collective-permute-start | bytes 3932168 | tf_op jit(solution)/shard_map/ppermute | solution.py:53
  152.6 6.9 %collective-permute-start.32 = (f32[256,1280]{1,0:T(8,128)S(1)}, f32[256,1280]{1,0:T(8,128)S(1)}, u32[]{:S(2)}, u32[]{:S(2)}) collective-permute-start(f32[256,1280]{1,0:T(8,128)S(1)} %get-tuple-element.128), channel_id=1, source_target_pairs={{0,1},{1,0},{2,3},{3,2},{4,5},{5,4},{6,7},{7,6},{8,9},{9,8},{10,11... | collective-permute-start | bytes 3932168 | tf_op jit(solution)/shard_map/ppermute | solution.py:53
  152.8 5.6 %collective-permute-start.30 = (f32[32,1024]{1,0:T(8,128)S(1)}, f32[32,1024]{1,0:T(8,128)S(1)}, u32[]{:S(2)}, u32[]{:S(2)}) collective-permute-start(f32[32,1024]{1,0:T(8,128)S(1)} %add.77), channel_id=1, source_target_pairs={{0,32},{1,9},{2,34},{3,11},{4,36},{5,13},{6,38},{7,15},{8,40},{9,1... | collective-permute-start | bytes 393224 | tf_op jit(solution)/shard_map/ppermute | solution.py:53
  158.4 30.8 %collective-permute-start.35 = (f32[256,1280]{1,0:T(8,128)S(1)}, f32[256,1280]{1,0:T(8,128)S(1)}, u32[]{:S(2)}, u32[]{:S(2)}) collective-permute-start(f32[256,1280]{1,0:T(8,128)S(1)} %get-tuple-element.144), channel_id=1, source_target_pairs={{0,1},{1,0},{2,3},{3,2},{4,5},{5,4},{6,7},{7,6},{8,9},{9,8},{10,11... | collective-permute-start | bytes 3932168 | tf_op jit(solution)/shard_map/ppermute | solution.py:53
  160.4 33.5 %collective-permute-start.40 = (f32[256,1280]{1,0:T(8,128)S(1)}, f32[256,1280]{1,0:T(8,128)S(1)}, u32[]{:S(2)}, u32[]{:S(2)}) collective-permute-start(f32[256,1280]{1,0:T(8,128)S(1)} %get-tuple-element.130), channel_id=1, source_target_pairs={{0,6},{1,7},{2,0},{3,1},{4,2},{5,3},{6,4},{7,5},{8,14},{9,15},{10,... | collective-permute-start | bytes 3932168 | tf_op jit(solution)/shard_map/ppermute | solution.py:53
  162.0 32.0 %collective-permute-start.39 = (f32[256,1280]{1,0:T(8,128)S(1)}, f32[256,1280]{1,0:T(8,128)S(1)}, u32[]{:S(2)}, u32[]{:S(2)}) collective-permute-start(f32[256,1280]{1,0:T(8,128)S(1)} %get-tuple-element.129), channel_id=1, source_target_pairs={{0,2},{1,3},{2,4},{3,5},{4,6},{5,7},{6,0},{7,1},{8,10},{9,11},{10,... | collective-permute-start | bytes 3932168 | tf_op jit(solution)/shard_map/ppermute | solution.py:53
  162.1 27.3 %collective-permute-start.33 = (f32[32,1024]{1,0:T(8,128)S(1)}, f32[32,1024]{1,0:T(8,128)S(1)}, u32[]{:S(2)}, u32[]{:S(2)}) collective-permute-start(f32[32,1024]{1,0:T(8,128)S(1)} %add.84), channel_id=1, source_target_pairs={{0,96},{1,25},{2,98},{3,27},{4,100},{5,29},{6,102},{7,31},{8,104},... | collective-permute-start | bytes 393224 | tf_op jit(solution)/shard_map/ppermute | solution.py:53
  167.4 21.9 %collective-permute-start.34 = (f32[8,1280]{1,0:T(8,128)S(1)}, f32[8,1280]{1,0:T(8,128)S(1)}, u32[]{:S(2)}, u32[]{:S(2)}) collective-permute-start(f32[8,1280]{1,0:T(8,128)S(1)} %get-tuple-element.137), channel_id=1, source_target_pairs={{0,1},{1,0},{2,3},{3,2},{4,5},{5,4},{6,7},{7,6},{8,9},{9,8},{10,11... | collective-permute-start | bytes 122888 | tf_op jit(solution)/shard_map/ppermute | solution.py:53
  189.4 5.9 %collective-permute-start.36 = (f32[8,1280]{1,0:T(8,128)S(1)}, f32[8,1280]{1,0:T(8,128)S(1)}, u32[]{:S(2)}, u32[]{:S(2)}) collective-permute-start(f32[8,1280]{1,0:T(8,128)S(1)} %add.88.last), channel_id=1, source_target_pairs={{0,2},{1,3},{2,4},{3,5},{4,6},{5,7},{6,0},{7,1},{8,10},{9,11},{10,... | collective-permute-start | bytes 122888 | tf_op jit(solution)/shard_map/ppermute | solution.py:53
  189.5 5.8 %collective-permute-start.37 = (f32[8,1280]{1,0:T(8,128)S(1)}, f32[8,1280]{1,0:T(8,128)S(1)}, u32[]{:S(2)}, u32[]{:S(2)}) collective-permute-start(f32[8,1280]{1,0:T(8,128)S(1)} %add.88.last), channel_id=1, source_target_pairs={{0,4},{1,5},{2,6},{3,7},{4,0},{5,1},{6,2},{7,3},{8,12},{9,13},{10,... | collective-permute-start | bytes 122888 | tf_op jit(solution)/shard_map/ppermute | solution.py:53
  193.3 3.1 %collective-permute-start.38 = (f32[8,1280]{1,0:T(8,128)S(1)}, f32[8,1280]{1,0:T(8,128)S(1)}, u32[]{:S(2)}, u32[]{:S(2)}) collective-permute-start(f32[8,1280]{1,0:T(8,128)S(1)} %add.88.last), channel_id=1, source_target_pairs={{0,6},{1,7},{2,0},{3,1},{4,2},{5,3},{6,4},{7,5},{8,14},{9,15},{10,... | collective-permute-start | bytes 122888 | tf_op jit(solution)/shard_map/ppermute | solution.py:53

commit v9 on v7

--- a/solution.py
+++ b/solution.py
@@ -617,15 +617,16 @@
     )(above, below, got_above, got_below)
 
 
-def map_kernel(expr, grad, masses, keep, valid, spot, out, held, ready, *, scale):
+def map_kernel(expr, grad, masses, keep, valid, spot, *rest, scale, start):
+    out, held, ready, inner = rest[-4:]
     index = pl.program_id(0)
     quarter, block = held.shape[2:]
     count = held.shape[1]
 
     def fetch(at, k):
-        columns = pl.ds(pl.multiple_of(at * block, block), block)
+        columns = pl.ds(pl.multiple_of((at + start) * block, block), block)
         return pltpu.make_async_copy(
-            expr.at[pl.ds(k * quarter, quarter), columns], held.at[at & 1, k], ready.at[at & 1, k]
+            expr.at[pl.ds(pl.multiple_of(k * quarter, quarter), quarter), columns], held.at[at & 1, k], ready.at[at & 1, k]
         )
 
     @pl.when(index == 0)
@@ -638,28 +639,32 @@
         for k in range(count):
             fetch(index + 1, k).start()
 
-    inner = spot[0:1, :]
-    for k in range(count):
+    inner[...] = jnp.broadcast_to(spot[0:1, :], inner.shape)
+
+    def add(k, _):
         fetch(index, k).wait()
-        rows = slice(k * quarter, k * quarter + quarter)
+        rows = pl.ds(pl.multiple_of(k * quarter, quarter), quarter)
         pair = grad[0, rows, :], grad[1, rows, :]
-        inner = inner + product(split(held[index & 1, k]), pair, ((0,), (0,)))
-    at = pl.multiple_of(index * block, block)
+        inner[...] += product(split(held[index & 1, k]), pair, ((0,), (0,)))
+        return 0
+
+    lax.fori_loop(0, count, add, 0)
+    at = pl.multiple_of((index + start) * block, block)
     expo = masses[0, pl.ds(at, block), :].astype(F32) + masses[1, pl.ds(at, block), :].astype(F32)
     for part in range(block // 128):
         rows = slice(part * 128, part * 128 + 128)
-        place = pl.ds(index * (block // 128) + part, 1)
+        place = pl.ds((index + start) * (block // 128) + part, 1)
         weight, mask = as_column(keep[place, :]), as_column(valid[place, :])
-        out[rows, :] = (scale * expo[rows]) * (weight * inner[rows] - mask * spot[1:2, :])
-
-
-def map_call(expr, grad, masses, keep, valid, spot, scale):
+        out[rows, :] = (scale * expo[rows]) * (weight * inner[rows, :] - mask * spot[1:2, :])
+
+
+def map_call(start, stop, expr, grad, masses, keep, valid, spot, scale, done=()):
     genes, cells = expr.shape
     spots = masses.shape[2]
     block, count = 256, 4
     return pl.pallas_call(
-        functools.partial(map_kernel, scale=scale),
-        grid=(cells // block,),
+        functools.partial(map_kernel, scale=scale, start=start),
+        grid=(stop - start,),
         in_specs=[
             pl.BlockSpec(memory_space=pl.ANY),
             RESIDENT,
@@ -667,17 +672,20 @@
             fixed(keep.shape),
             fixed(valid.shape),
             fixed((8, spots)),
-        ],
-        out_specs=pl.BlockSpec((block, spots), lambda i: (i, 0)),
+        ]
+        + [pl.BlockSpec(memory_space=pl.ANY)] * len(done),
+        out_specs=pl.BlockSpec((block, spots), lambda i: (i + start, 0)),
         out_shape=jax.ShapeDtypeStruct((cells, spots), F32),
         scratch_shapes=[
             pltpu.VMEM((2, count, genes // count, block), F32),
             pltpu.SemaphoreType.DMA((2, count)),
+            pltpu.VMEM((block, spots), F32),
         ],
+        input_output_aliases={6: 0} if done else {},
         compiler_params=vmem(24),
         cost_estimate=NO_COST,
         name="grad_map",
-    )(streamed(expr), grad, masses, keep, valid, spot)
+    )(streamed(expr), grad, masses, keep, valid, spot, *done)
 
 
 def finish_kernel(last, got1, got2, got3, totals, scalars, kind, filt, grad_filter, terms, *, all_cells):
@@ -828,13 +836,17 @@
     map_rows = stacked([spot_coef[32], column])
     valid2 = valid.reshape(blocks, 128)
     map_args = (expr, grad.reshape(2, genes, spots), masses, keep2, valid2, map_rows, all_cells * genes)
-    grad_map = map_call(*map_args)
+    steps = cells // 256
+    grad_map = map_call(0, steps - 2, *map_args)
     types_got, last_got = after((types_got, last_got), grad_map)
     types = types + types_got
     last = after(last + last_got, own)
     got = [up(last, step) for step in (1, 2, 3)]
+    grad_map = map_call(steps - 2, steps, *map_args, done=(after(grad_map, last),))
+    got = after(tuple(got), grad_map)
     grad_weighted = after(own, grad_map) + near_up + near_down
     grad_expr = grad_weighted * (keep * (genes * all_spots))[None, :]
+    got = after(got, grad_expr)
 
     type_fraction = types * share
 

time: 199 us -> 204 us (1.025)
  Pallas kernels: 87.6 us -> 93.4 us
    pallas_call x1 -> x2, Pallas kernels: 21.5 us -> 27.2 us  [map_call(): pl.pallas_call(functools.partial(map_kernel, scale=scale, start=start), g...]
  transfers between devices with their start and end apart: 41 -> 41, of which waited for: 18 -> 16; matrix products, arithmetic and copies ran while one was open for 1% -> 1% of each run, Pallas kernels for 37% -> 39%
where the time goes in v9:
time: 204 us; the launch traced here: 203 us
  Pallas kernels  93.4 us (46%)
  starting transfers between devices  58.9 us (29%)
  waiting for transfers between devices  46 us (23%)
  other arithmetic  3.77 us (2%)
    ppermute x41, starting transfers between devices, send(): return lax.ppermute(array, ('cells', 'spots'), route(target))  58.9 us
    ppermute x41, waiting for transfers between devices, send(): return lax.ppermute(array, ('cells', 'spots'), route(target))  46 us
    pallas_call x2, Pallas kernels, map_call(): pl.pallas_call(functools.partial(map_kernel, scale=scale, start=start), g...  27.2 us
    pallas_call x5, Pallas kernels, back_call(): pl.pallas_call(functools.partial(back_kernel, parts=parts, first=len(firs...  23.1 us
    pallas_call x3, Pallas kernels, pred_call(): pl.pallas_call(functools.partial(pred_kernel, cuts=cuts), grid_spec=pltpu...  21.7 us
    pallas_call x1, Pallas kernels, expo_call(): pl.pallas_call(expo_kernel, grid_spec=pltpu.PrefetchScalarGridSpec(num_sc...  8.81 us
    pallas_call x3, Pallas kernels, grad_call(): pl.pallas_call(functools.partial(grad_kernel, count=count, lane=lane, chi...  7.63 us
  transfers between devices with their start and end apart: 41, of which 16 were waited for; matrix products, arithmetic and copies ran while one was open for 1% of the time, Pallas kernels for 39%

profile of v9, /device:TPU:1, one launch (start us, length us, event | category | flops | bytes accessed | tf_op | source)
XLA Modules:
  0.0 203.4 jit_solution(1164236651559286134)
XLA Ops:
  0.7 8.8 %expo.1 = (bf16[2,1280,1024]{2,1,0:T(8,128)(2,1)S(1)}, f32[32,1024]{1,0:T(8,128)S(1)}, f32[8,1024]{1,0:T(8,128)S(1)}, f32[33,8,1024]{2,1,0:T(8,128)S(1)}, f32[33,8,1024]{2,1,0:T(8,128)S(1)}) custom-call(s32[4]{0:T(128)S(1)} %pad_add_fusion.ids, f32[1280,1024]{1,0:T(8,128)} %logits.1, s32[10,128]{1,0:T(8,128)} %bitcast.69, f32[10,128]{1,0:T(8,128)} %bitcast.68, ...), custom_call_target="tpu_custom_call" | custom-call | bytes 1310720 | tf_op jit(solution)/shard_map/expo/pallas_call | solution.py:179
  9.5 2.5 %collective-permute-start = (f32[33,8,1024]{2,1,0:T(8,128)S(1)}, f32[33,8,1024]{2,1,0:T(8,128)S(1)}, u32[]{:S(2)}, u32[]{:S(2)}) collective-permute-start(f32[33,8,1024]{2,1,0:T(8,128)S(1)} %get-tuple-element.83), channel_id=1, source_target_pairs={{0,8},{1,33},{2,10},{3,35},{4,12},{5,37},{6,14},{7,39},{8,16},{9,4... | collective-permute-start | bytes 3244040 | tf_op jit(solution)/shard_map/ppermute | solution.py:53
  12.1 2.3 %collective-permute-start.1 = (f32[33,8,1024]{2,1,0:T(8,128)S(1)}, f32[33,8,1024]{2,1,0:T(8,128)S(1)}, u32[]{:S(2)}, u32[]{:S(2)}) collective-permute-start(f32[33,8,1024]{2,1,0:T(8,128)S(1)} %get-tuple-element.84), channel_id=1, source_target_pairs={{0,24},{1,97},{2,26},{3,99},{4,28},{5,101},{6,30},{7,103},{8,0},{9... | collective-permute-start | bytes 3244040 | tf_op jit(solution)/shard_map/ppermute | solution.py:53
  14.4 7.5 %pred_.3 = (f32[33,8,1024]{2,1,0:T(8,128)S(1)}, f32[33,8,1024]{2,1,0:T(8,128)S(1)}) custom-call(s32[4]{0:T(128)S(1)} %pad_add_fusion.ids, f32[8,16,16,1280]{3,2,1,0:T(8,128)} %bitcast.59, f32[8,16,16,1280]{3,2,1,0:T(8,128)} %bitcast.60, f32[1,1280]{1,0:T(1,128)S(1)} %reshape.99.keep, bf16[2,1280,1024]{2,1,0:T(8,128)(2,1)S(1)} %get-tuple-element.86.masses, ...), custom_call_target="tpu_custom_call" | custom-call | flops 503316480 | bytes 1245184 | tf_op jit(solution)/shard_map/pred/pallas_call | solution.py:252
  22.0 2.6 %collective-permute-start.2 = (f32[33,8,1024]{2,1,0:T(8,128)S(1)}, f32[33,8,1024]{2,1,0:T(8,128)S(1)}, u32[]{:S(2)}, u32[]{:S(2)}) collective-permute-start(f32[33,8,1024]{2,1,0:T(8,128)S(1)} %get-tuple-element.89), channel_id=1, source_target_pairs={{0,24},{1,97},{2,26},{3,99},{4,28},{5,101},{6,30},{7,103},{8,0},{9... | collective-permute-start | bytes 3244040 | tf_op jit(solution)/shard_map/ppermute | solution.py:53
  24.6 2.5 %collective-permute-done.refs_0_ = f32[33,8,1024]{2,1,0:T(8,128)S(1)} collective-permute-done((f32[33,8,1024]{2,1,0:T(8,128)S(1)}, f32[33,8,1024]{2,1,0:T(8,128)S(1)}, u32[]{:S(2)}, u32[]{:S(2)}) %collective-permute-start) | collective-permute-done | bytes 1081376 | tf_op jit(solution)/shard_map/ppermute | solution.py:53
  27.1 6.6 %pred_.4 = (f32[33,8,1024]{2,1,0:T(8,128)S(1)}, f32[33,8,1024]{2,1,0:T(8,128)S(1)}) custom-call(s32[4]{0:T(128)S(1)} %pad_add_fusion.ids, f32[8,16,16,1280]{3,2,1,0:T(8,128)} %bitcast.61, f32[8,16,16,1280]{3,2,1,0:T(8,128)} %bitcast.62, f32[1,1280]{1,0:T(1,128)S(1)} %reshape.99.keep, bf16[2,1280,1024]{2,1,0:T(8,128)(2,1)S(1)} %get-tuple-element.86.masses, ...), custom_call_target="tpu_custom_call" | custom-call | flops 503316480 | bytes 1245184 | tf_op jit(solution)/shard_map/pred/pallas_call | solution.py:252
  34.7 2.0 collective-permute-start.5
  36.7 1.9 collective-permute-done.3.refs_1_
  38.6 7.6 %pred_.5 = (f32[33,8,1024]{2,1,0:T(8,128)S(1)}, f32[33,8,1024]{2,1,0:T(8,128)S(1)}) custom-call(s32[4]{0:T(128)S(1)} %pad_add_fusion.ids, f32[8,16,16,1280]{3,2,1,0:T(8,128)} %bitcast.63, f32[8,16,16,1280]{3,2,1,0:T(8,128)} %bitcast.64, f32[1,1280]{1,0:T(1,128)S(1)} %reshape.99.keep, bf16[2,1280,1024]{2,1,0:T(8,128)(2,1)S(1)} %get-tuple-element.86.masses, ...), custom_call_target="tpu_custom_call" | custom-call | flops 503316480 | bytes 1245184 | tf_op jit(solution)/shard_map/pred/pallas_call | solution.py:252
  46.2 4.1 %collective-permute-done.4.got0 = f32[33,8,1024]{2,1,0:T(8,128)S(1)} collective-permute-done((f32[33,8,1024]{2,1,0:T(8,128)S(1)}, f32[33,8,1024]{2,1,0:T(8,128)S(1)}, u32[]{:S(2)}, u32[]{:S(2)}) %collective-permute-start.4) | collective-permute-done | bytes 1081376 | tf_op jit(solution)/shard_map/ppermute | solution.py:53
  52.1 2.7 %collective-permute-start.8 = (f32[17,8,1024]{2,1,0:T(8,128)S(1)}, f32[17,8,1024]{2,1,0:T(8,128)S(1)}, u32[]{:S(2)}, u32[]{:S(2)}) collective-permute-start(f32[17,8,1024]{2,1,0:T(8,128)S(1)} %get-tuple-element.102), channel_id=1, source_target_pairs={{0,64},{1,17},{2,66},{3,19},{4,68},{5,21},{6,70},{7,23},{8,72},{9,... | collective-permute-start | bytes 1671176 | tf_op jit(solution)/shard_map/ppermute | solution.py:53
  57.7 4.3 %collective-permute-done.6 = f32[32,1024]{1,0:T(8,128)S(1)} collective-permute-done((f32[32,1024]{1,0:T(8,128)S(1)}, f32[32,1024]{1,0:T(8,128)S(1)}, u32[]{:S(2)}, u32[]{:S(2)}) %collective-permute-start.6) | collective-permute-done | bytes 131104 | tf_op jit(solution)/shard_map/ppermute | solution.py:53
  62.0 7.4 %collective-permute-done.8 = f32[17,8,1024]{2,1,0:T(8,128)S(1)} collective-permute-done((f32[17,8,1024]{2,1,0:T(8,128)S(1)}, f32[17,8,1024]{2,1,0:T(8,128)S(1)}, u32[]{:S(2)}, u32[]{:S(2)}) %collective-permute-start.8) | collective-permute-done | bytes 557088 | tf_op jit(solution)/shard_map/ppermute | solution.py:53
  69.7 2.2 %collective-permute-start.11 = (f32[8,16,1024]{2,1,0:T(8,128)S(1)}, f32[8,16,1024]{2,1,0:T(8,128)S(1)}, u32[]{:S(2)}, u32[]{:S(2)}) collective-permute-start(f32[8,16,1024]{2,1,0:T(8,128)S(1)} %bitcast.49), channel_id=1, source_target_pairs={{0,64},{1,17},{2,66},{3,19},{4,68},{5,21},{6,70},{7,23},{8,72},{9,... | collective-permute-start | bytes 1572872 | tf_op jit(solution)/shard_map/ppermute | solution.py:53
  71.9 2.0 collective-permute-start.10
  74.8 2.8 %collective-permute-start.15 = (f32[32,1024]{1,0:T(8,128)S(1)}, f32[32,1024]{1,0:T(8,128)S(1)}, u32[]{:S(2)}, u32[]{:S(2)}) collective-permute-start(f32[32,1024]{1,0:T(8,128)S(1)} %add.71), channel_id=1, source_target_pairs={{0,24},{1,97},{2,26},{3,99},{4,28},{5,101},{6,30},{7,103},{8,16},{... | collective-permute-start | bytes 393224 | tf_op jit(solution)/shard_map/ppermute | solution.py:53
  77.6 3.5 %collective-permute-done.13 = f32[64,128]{1,0:T(8,128)S(1)} collective-permute-done((f32[64,128]{1,0:T(8,128)S(1)}, f32[64,128]{1,0:T(8,128)S(1)}, u32[]{:S(2)}, u32[]{:S(2)}) %collective-permute-start.13) | collective-permute-done | bytes 32800 | tf_op jit(solution)/shard_map/ppermute | solution.py:53
  81.3 7.6 %collective-permute-done.14 = f32[64,128]{1,0:T(8,128)S(1)} collective-permute-done((f32[64,128]{1,0:T(8,128)S(1)}, f32[64,128]{1,0:T(8,128)S(1)}, u32[]{:S(2)}, u32[]{:S(2)}) %collective-permute-start.14) | collective-permute-done | bytes 32800 | tf_op jit(solution)/shard_map/ppermute | solution.py:53
  89.3 2.7 %collective-permute-start.17 = (f32[2,8,16,1024]{3,2,1,0:T(8,128)S(1)}, f32[2,8,16,1024]{3,2,1,0:T(8,128)S(1)}, u32[]{:S(2)}, u32[]{:S(2)}) collective-permute-start(f32[2,8,16,1024]{3,2,1,0:T(8,128)S(1)} %pad_maximum_fusion.1.refs_1_), channel_id=1, source_target_pairs={{0,24},{1,97},{2,26},{3,99},{4,28},{5,101},{6,30},{7,103},{8,0},{9... | collective-permute-start | bytes 3145736 | tf_op jit(solution)/shard_map/ppermute | solution.py:53
  92.0 1.3 collective-permute-start.18
  93.3 1.5 collective-permute-done.18
  94.7 2.7 %collective-permute-start.19 = (f32[64,128]{1,0:T(8,128)S(1)}, f32[64,128]{1,0:T(8,128)S(1)}, u32[]{:S(2)}, u32[]{:S(2)}) collective-permute-start(f32[64,128]{1,0:T(8,128)S(1)} %add.78), channel_id=1, source_target_pairs={{0,96},{1,25},{2,98},{3,27},{4,100},{5,29},{6,102},{7,31},{8,104},... | collective-permute-start | bytes 98312 | tf_op jit(solution)/shard_map/ppermute | solution.py:53
  97.5 1.5 collective-permute-start.24
  99.5 5.3 %collective-permute-done.16.refs_2_ = f32[2,8,16,1024]{3,2,1,0:T(8,128)S(1)} collective-permute-done((f32[2,8,16,1024]{3,2,1,0:T(8,128)S(1)}, f32[2,8,16,1024]{3,2,1,0:T(8,128)S(1)}, u32[]{:S(2)}, u32[]{:S(2)}) %collective-permute-start.16) | collective-permute-done | bytes 1048608 | tf_op jit(solution)/shard_map/ppermute | solution.py:53
  104.8 2.7 %collective-permute-start.21 = (f32[2,8,16,1024]{3,2,1,0:T(8,128)S(1)}, f32[2,8,16,1024]{3,2,1,0:T(8,128)S(1)}, u32[]{:S(2)}, u32[]{:S(2)}) collective-permute-start(f32[2,8,16,1024]{3,2,1,0:T(8,128)S(1)} %collective-permute-done.17.refs_5_), channel_id=1, source_target_pairs={{0,24},{1,97},{2,26},{3,99},{4,28},{5,101},{6,30},{7,103},{8,0},{9... | collective-permute-start | bytes 3145736 | tf_op jit(solution)/shard_map/ppermute | solution.py:53
  107.5 2.8 %collective-permute-start.22 = (f32[56,128]{1,0:T(8,128)S(1)}, f32[56,128]{1,0:T(8,128)S(1)}, u32[]{:S(2)}, u32[]{:S(2)}) collective-permute-start(f32[56,128]{1,0:T(8,128)S(1)} %pad_maximum_fusion.2), channel_id=1, source_target_pairs={{0,1},{1,0},{2,3},{3,2},{4,5},{5,4},{6,7},{7,6},{8,9},{9,8},{10,11... | collective-permute-start | bytes 86024 | tf_op jit(solution)/shard_map/ppermute | solution.py:53
  111.1 1.3 collective-permute-start.23
  112.4 1.7 collective-permute-done.23
  116.0 2.7 %collective-permute-start.26 = (f32[56,128]{1,0:T(8,128)S(1)}, f32[56,128]{1,0:T(8,128)S(1)}, u32[]{:S(2)}, u32[]{:S(2)}) collective-permute-start(f32[56,128]{1,0:T(8,128)S(1)} %add.81), channel_id=1, source_target_pairs={{0,6},{1,7},{2,4},{3,5},{4,2},{5,3},{6,0},{7,1},{8,14},{9,15},{10,... | collective-permute-start | bytes 86024 | tf_op jit(solution)/shard_map/ppermute | solution.py:53
  118.8 1.6 collective-permute-done.26
  121.2 4.7 %grad.3 = (bf16[2,8,256,1024]{3,2,1,0:T(8,128)(2,1)S(1)}, f32[8,1024]{1,0:T(8,128)S(1)}) custom-call(s32[4]{0:T(128)S(1)} %pad_add_fusion.ids, f32[2,8,16,1024]{3,2,1,0:T(8,128)S(1)} %pad_maximum_fusion.refs_0_, f32[2,8,16,1024]{3,2,1,0:T(8,128)S(1)} %pad_maximum_fusion.1.refs_1_, f32[2,8,16,1024]{3,2,1,0:T(8,128)S(1)} %collective-permute-done.16.refs_2_, ...), custom_call_target="tpu_custom_call" | custom-call | tf_op jit(solution)/shard_map/grad/pallas_call | solution.py:477
  125.9 1.3 collective-permute-done.20.refs_0_
  128.2 3.1 %back.5 = (f32[8,1280]{1,0:T(8,128)S(1)}, f32[256,1280]{1,0:T(8,128)S(1)}) custom-call(s32[4]{0:T(128)S(1)} %pad_add_fusion.ids, bf16[2,8,256,1024]{3,2,1,0:T(8,128)(2,1)S(1)} %get-tuple-element.117.grad.refs_5_, bf16[2,1280,1024]{2,1,0:T(8,128)(2,1)S(1)} %get-tuple-element.86.masses, f32[2048,1280]{1,0:T(8,128)} %expr.13, ...), custom_call_target="tpu_custom_call" | custom-call | tf_op jit(solution)/shard_map/back/pallas_call | solution.py:553
  131.3 2.3 %collective-permute-start.27 = (f32[256,1280]{1,0:T(8,128)S(1)}, f32[256,1280]{1,0:T(8,128)S(1)}, u32[]{:S(2)}, u32[]{:S(2)}) collective-permute-start(f32[256,1280]{1,0:T(8,128)S(1)} %get-tuple-element.118), channel_id=1, source_target_pairs={{0,1},{1,0},{2,3},{3,2},{4,5},{5,4},{6,7},{7,6},{8,9},{9,8},{10,11... | collective-permute-start | bytes 3932168 | tf_op jit(solution)/shard_map/ppermute | solution.py:53
  133.6 3.6 %back.6 = (f32[8,1280]{1,0:T(8,128)S(1)}, f32[256,1280]{1,0:T(8,128)S(1)}) custom-call(s32[4]{0:T(128)S(1)} %pad_add_fusion.ids, bf16[2,8,256,1024]{3,2,1,0:T(8,128)(2,1)S(1)} %get-tuple-element.117.grad.refs_5_, bf16[2,1280,1024]{2,1,0:T(8,128)(2,1)S(1)} %get-tuple-element.86.masses, f32[2048,1280]{1,0:T(8,128)} %expr.13), custom_call_target="tpu_custom_call" | custom-call | tf_op jit(solution)/shard_map/back/pallas_call | solution.py:553
  137.4 2.8 %collective-permute-start.29 = (f32[128,1280]{1,0:T(8,128)S(1)}, f32[128,1280]{1,0:T(8,128)S(1)}, u32[]{:S(2)}, u32[]{:S(2)}) collective-permute-start(f32[128,1280]{1,0:T(8,128)S(1)} %get-tuple-element.166), channel_id=1, source_target_pairs={{0,6},{1,7},{2,0},{3,1},{4,2},{5,3},{6,4},{7,5},{8,14},{9,15},{10,... | collective-permute-start | bytes 1966088 | tf_op jit(solution)/shard_map/ppermute | solution.py:53
  140.3 1.9 grad.5
  142.2 8.0 %back.7 = (f32[8,1280]{1,0:T(8,128)S(1)}, f32[256,1280]{1,0:T(8,128)S(1)}, f32[256,1280]{1,0:T(8,128)S(1)}, f32[256,1280]{1,0:T(8,128)S(1)}) custom-call(s32[4]{0:T(128)S(1)} %pad_add_fusion.ids, bf16[2,8,256,1024]{3,2,1,0:T(8,128)(2,1)S(1)} %get-tuple-element.122.grad, bf16[2,1280,1024]{2,1,0:T(8,128)(2,1)S(1)} %get-tuple-element.86.masses, f32[2048,1280]{1,0:T(8,128)} %expr.13), custom_call_target="tpu_custom_call" | custom-call | tf_op jit(solution)/shard_map/back/pallas_call | solution.py:553
  150.8 1.3 collective-permute-start.30
  152.1 5.5 %back.8 = (f32[8,1280]{1,0:T(8,128)S(1)}, f32[256,1280]{1,0:T(8,128)S(1)}, f32[256,1280]{1,0:T(8,128)S(1)}) custom-call(s32[4]{0:T(128)S(1)} %pad_add_fusion.ids, bf16[2,8,256,1024]{3,2,1,0:T(8,128)(2,1)S(1)} %get-tuple-element.122.grad, bf16[2,1280,1024]{2,1,0:T(8,128)(2,1)S(1)} %get-tuple-element.86.masses, f32[2048,1280]{1,0:T(8,128)} %expr.13), custom_call_target="tpu_custom_call" | custom-call | tf_op jit(solution)/shard_map/back/pallas_call | solution.py:553
  160.3 3.0 %collective-permute-start.40 = (f32[256,1280]{1,0:T(8,128)S(1)}, f32[256,1280]{1,0:T(8,128)S(1)}, u32[]{:S(2)}, u32[]{:S(2)}) collective-permute-start(f32[256,1280]{1,0:T(8,128)S(1)} %get-tuple-element.134), channel_id=1, source_target_pairs={{0,6},{1,7},{2,0},{3,1},{4,2},{5,3},{6,4},{7,5},{8,14},{9,15},{10,... | collective-permute-start | bytes 3932168 | tf_op jit(solution)/shard_map/ppermute | solution.py:53
  163.4 3.0 %collective-permute-start.33 = (f32[32,1024]{1,0:T(8,128)S(1)}, f32[32,1024]{1,0:T(8,128)S(1)}, u32[]{:S(2)}, u32[]{:S(2)}) collective-permute-start(f32[32,1024]{1,0:T(8,128)S(1)} %add.84), channel_id=1, source_target_pairs={{0,96},{1,25},{2,98},{3,27},{4,100},{5,29},{6,102},{7,31},{8,104},... | collective-permute-start | bytes 393224 | tf_op jit(solution)/shard_map/ppermute | solution.py:53
  166.4 3.0 %back.9 = (f32[8,1280]{1,0:T(8,128)S(1)}, f32[256,1280]{1,0:T(8,128)S(1)}) custom-call(s32[4]{0:T(128)S(1)} %pad_add_fusion.ids, bf16[2,8,256,1024]{3,2,1,0:T(8,128)(2,1)S(1)} %get-tuple-element.122.grad, bf16[2,1280,1024]{2,1,0:T(8,128)(2,1)S(1)} %get-tuple-element.86.masses, f32[2048,1280]{1,0:T(8,128)} %expr.13, ...), custom_call_target="tpu_custom_call" | custom-call | tf_op jit(solution)/shard_map/back/pallas_call | solution.py:553
  169.6 16.0 %grad_map.2.rest_0_ = f32[1280,1024]{1,0:T(8,128)} custom-call(f32[2048,1280]{1,0:T(8,128)} %expr.13, bf16[2,2048,1024]{2,1,0:T(8,128)(2,1)S(1)} %bitcast.38, bf16[2,1280,1024]{2,1,0:T(8,128)(2,1)S(1)} %get-tuple-element.86.masses, f32[10,128]{1,0:T(8,128)S(1)} %bitcast.53, f32[10,128]{1,0:T(8,128)S(1)} %convert_bitcast_fusion.valid, ...), custom_call_target="tpu_custom_call" | custom-call | tf_op jit(solution)/shard_map/grad_map/pallas_call | solution.py:665
  185.8 2.7 %collective-permute-start.38 = (f32[8,1280]{1,0:T(8,128)S(1)}, f32[8,1280]{1,0:T(8,128)S(1)}, u32[]{:S(2)}, u32[]{:S(2)}) collective-permute-start(f32[8,1280]{1,0:T(8,128)S(1)} %add.88.last), channel_id=1, source_target_pairs={{0,6},{1,7},{2,0},{3,1},{4,2},{5,3},{6,4},{7,5},{8,14},{9,15},{10,... | collective-permute-start | bytes 122888 | tf_op jit(solution)/shard_map/ppermute | solution.py:53
  189.9 11.3 %grad_map.3 = f32[1280,1024]{1,0:T(8,128)} custom-call(f32[2048,1280]{1,0:T(8,128)} %expr.13, bf16[2,2048,1024]{2,1,0:T(8,128)(2,1)S(1)} %bitcast.39, bf16[2,1280,1024]{2,1,0:T(8,128)(2,1)S(1)} %get-tuple-element.86.masses, f32[10,128]{1,0:T(8,128)S(1)} %bitcast.54, f32[10,128]{1,0:T(8,128)S(1)} %convert_bitcast_fusion.valid, ...), custom_call_target="tpu_custom_call", output_to_operand_aliasing={{}: (6, {})} | custom-call | tf_op jit(solution)/shard_map/grad_map/pallas_call | solution.py:665
  201.2 1.4 add_multiply_fusion
  (105 shorter events, 18.7 us)
Async XLA Ops:
  0.7 13.7 %copy-start = (f32[1280]{0:T(1024)S(1)}, f32[1280]{0:T(1024)}, u32[]{:S(2)}) copy-start(f32[1280]{0:T(1024)} %param.8) | copy-start | bytes 15364
  0.7 13.7 %copy-start.1 = (s32[1280]{0:T(1024)S(1)}, s32[1280]{0:T(1024)}, u32[]{:S(2)}) copy-start(s32[1280]{0:T(1024)} %param.11) | copy-start | bytes 15364
  9.5 17.6 %collective-permute-start = (f32[33,8,1024]{2,1,0:T(8,128)S(1)}, f32[33,8,1024]{2,1,0:T(8,128)S(1)}, u32[]{:S(2)}, u32[]{:S(2)}) collective-permute-start(f32[33,8,1024]{2,1,0:T(8,128)S(1)} %get-tuple-element.83), channel_id=1, source_target_pairs={{0,8},{1,33},{2,10},{3,35},{4,12},{5,37},{6,14},{7,39},{8,16},{9,4... | collective-permute-start | bytes 3244040 | tf_op jit(solution)/shard_map/ppermute | solution.py:53
  12.1 15.1 %collective-permute-start.1 = (f32[33,8,1024]{2,1,0:T(8,128)S(1)}, f32[33,8,1024]{2,1,0:T(8,128)S(1)}, u32[]{:S(2)}, u32[]{:S(2)}) collective-permute-start(f32[33,8,1024]{2,1,0:T(8,128)S(1)} %get-tuple-element.84), channel_id=1, source_target_pairs={{0,24},{1,97},{2,26},{3,99},{4,28},{5,101},{6,30},{7,103},{8,0},{9... | collective-permute-start | bytes 3244040 | tf_op jit(solution)/shard_map/ppermute | solution.py:53
  21.9 16.7 %collective-permute-start.3 = (f32[33,8,1024]{2,1,0:T(8,128)S(1)}, f32[33,8,1024]{2,1,0:T(8,128)S(1)}, u32[]{:S(2)}, u32[]{:S(2)}) collective-permute-start(f32[33,8,1024]{2,1,0:T(8,128)S(1)} %get-tuple-element.88), channel_id=1, source_target_pairs={{0,8},{1,33},{2,10},{3,35},{4,12},{5,37},{6,14},{7,39},{8,16},{9,4... | collective-permute-start | bytes 3244040 | tf_op jit(solution)/shard_map/ppermute | solution.py:53
  22.0 14.7 %copy-start.2 = (s32[1024]{0:T(1024)S(1)}, s32[1024]{0:T(1024)}, u32[]{:S(2)}) copy-start(s32[1024]{0:T(1024)} %param.12) | copy-start | bytes 12292
  22.0 14.7 %copy-start.3 = (s32[1024]{0:T(1024)S(1)}, s32[1024]{0:T(1024)}, u32[]{:S(2)}) copy-start(s32[1024]{0:T(1024)} %param.13) | copy-start | bytes 12292
  22.0 16.6 %collective-permute-start.2 = (f32[33,8,1024]{2,1,0:T(8,128)S(1)}, f32[33,8,1024]{2,1,0:T(8,128)S(1)}, u32[]{:S(2)}, u32[]{:S(2)}) collective-permute-start(f32[33,8,1024]{2,1,0:T(8,128)S(1)} %get-tuple-element.89), channel_id=1, source_target_pairs={{0,24},{1,97},{2,26},{3,99},{4,28},{5,101},{6,30},{7,103},{8,0},{9... | collective-permute-start | bytes 3244040 | tf_op jit(solution)/shard_map/ppermute | solution.py:53
  33.8 16.5 %collective-permute-start.4 = (f32[33,8,1024]{2,1,0:T(8,128)S(1)}, f32[33,8,1024]{2,1,0:T(8,128)S(1)}, u32[]{:S(2)}, u32[]{:S(2)}) collective-permute-start(f32[33,8,1024]{2,1,0:T(8,128)S(1)} %get-tuple-element.91), channel_id=1, source_target_pairs={{0,8},{1,33},{2,10},{3,35},{4,12},{5,37},{6,14},{7,39},{8,16},{9,4... | collective-permute-start | bytes 3244040 | tf_op jit(solution)/shard_map/ppermute | solution.py:53
  34.7 15.6 %collective-permute-start.5 = (f32[33,8,1024]{2,1,0:T(8,128)S(1)}, f32[33,8,1024]{2,1,0:T(8,128)S(1)}, u32[]{:S(2)}, u32[]{:S(2)}) collective-permute-start(f32[33,8,1024]{2,1,0:T(8,128)S(1)} %get-tuple-element.92), channel_id=1, source_target_pairs={{0,24},{1,97},{2,26},{3,99},{4,28},{5,101},{6,30},{7,103},{8,0},{9... | collective-permute-start | bytes 3244040 | tf_op jit(solution)/shard_map/ppermute | solution.py:53
  36.7 19.0 %slice-start = ((s8[8388608]{0:T(1024)(128)(4,1)}), s8[4194304]{0:T(1024)(128)(4,1)S(1)}, s32[]{:S(2)}) async-start(s8[8388608]{0:T(1024)(128)(4,1)} %bitcast.40), calls=%async_computation | async-start | bytes 8388608
  36.7 19.0 %slice-start.1 = ((s8[8388608]{0:T(1024)(128)(4,1)}), s8[4194304]{0:T(1024)(128)(4,1)S(1)}, s32[]{:S(2)}) async-start(s8[8388608]{0:T(1024)(128)(4,1)} %bitcast.40), calls=%async_computation.1 | async-start | bytes 8388608
  51.1 10.9 %collective-permute-start.7 = (f32[17,8,1024]{2,1,0:T(8,128)S(1)}, f32[17,8,1024]{2,1,0:T(8,128)S(1)}, u32[]{:S(2)}, u32[]{:S(2)}) collective-permute-start(f32[17,8,1024]{2,1,0:T(8,128)S(1)} %get-tuple-element.101), channel_id=1, source_target_pairs={{0,32},{1,9},{2,34},{3,11},{4,36},{5,13},{6,38},{7,15},{8,40},{9,1... | collective-permute-start | bytes 1671176 | tf_op jit(solution)/shard_map/ppermute | solution.py:53
  52.1 17.3 %collective-permute-start.8 = (f32[17,8,1024]{2,1,0:T(8,128)S(1)}, f32[17,8,1024]{2,1,0:T(8,128)S(1)}, u32[]{:S(2)}, u32[]{:S(2)}) collective-permute-start(f32[17,8,1024]{2,1,0:T(8,128)S(1)} %get-tuple-element.102), channel_id=1, source_target_pairs={{0,64},{1,17},{2,66},{3,19},{4,68},{5,21},{6,70},{7,23},{8,72},{9,... | collective-permute-start | bytes 1671176 | tf_op jit(solution)/shard_map/ppermute | solution.py:53
  54.8 14.6 %collective-permute-start.9 = (f32[17,8,1024]{2,1,0:T(8,128)S(1)}, f32[17,8,1024]{2,1,0:T(8,128)S(1)}, u32[]{:S(2)}, u32[]{:S(2)}) collective-permute-start(f32[17,8,1024]{2,1,0:T(8,128)S(1)} %get-tuple-element.103), channel_id=1, source_target_pairs={{0,96},{1,25},{2,98},{3,27},{4,100},{5,29},{6,102},{7,31},{8,104},... | collective-permute-start | bytes 1671176 | tf_op jit(solution)/shard_map/ppermute | solution.py:53
  56.4 5.6 %collective-permute-start.6 = (f32[32,1024]{1,0:T(8,128)S(1)}, f32[32,1024]{1,0:T(8,128)S(1)}, u32[]{:S(2)}, u32[]{:S(2)}) collective-permute-start(f32[32,1024]{1,0:T(8,128)S(1)} %get-tuple-element.99), channel_id=1, source_target_pairs={{0,8},{1,33},{2,10},{3,35},{4,12},{5,37},{6,14},{7,39},{8,0},{9,41... | collective-permute-start | bytes 393224 | tf_op jit(solution)/shard_map/ppermute | solution.py:53
  69.7 19.3 %collective-permute-start.12 = (f32[8,16,1024]{2,1,0:T(8,128)S(1)}, f32[8,16,1024]{2,1,0:T(8,128)S(1)}, u32[]{:S(2)}, u32[]{:S(2)}) collective-permute-start(f32[8,16,1024]{2,1,0:T(8,128)S(1)} %bitcast.48), channel_id=1, source_target_pairs={{0,32},{1,9},{2,34},{3,11},{4,36},{5,13},{6,38},{7,15},{8,40},{9,1... | collective-permute-start | bytes 1572872 | tf_op jit(solution)/shard_map/ppermute | solution.py:53
  69.7 19.3 %collective-permute-start.11 = (f32[8,16,1024]{2,1,0:T(8,128)S(1)}, f32[8,16,1024]{2,1,0:T(8,128)S(1)}, u32[]{:S(2)}, u32[]{:S(2)}) collective-permute-start(f32[8,16,1024]{2,1,0:T(8,128)S(1)} %bitcast.49), channel_id=1, source_target_pairs={{0,64},{1,17},{2,66},{3,19},{4,68},{5,21},{6,70},{7,23},{8,72},{9,... | collective-permute-start | bytes 1572872 | tf_op jit(solution)/shard_map/ppermute | solution.py:53
  71.9 17.2 %collective-permute-start.10 = (f32[8,16,1024]{2,1,0:T(8,128)S(1)}, f32[8,16,1024]{2,1,0:T(8,128)S(1)}, u32[]{:S(2)}, u32[]{:S(2)}) collective-permute-start(f32[8,16,1024]{2,1,0:T(8,128)S(1)} %bitcast.50), channel_id=1, source_target_pairs={{0,96},{1,25},{2,98},{3,27},{4,100},{5,29},{6,102},{7,31},{8,104},... | collective-permute-start | bytes 1572872 | tf_op jit(solution)/shard_map/ppermute | solution.py:53
  74.8 14.2 %collective-permute-start.15 = (f32[32,1024]{1,0:T(8,128)S(1)}, f32[32,1024]{1,0:T(8,128)S(1)}, u32[]{:S(2)}, u32[]{:S(2)}) collective-permute-start(f32[32,1024]{1,0:T(8,128)S(1)} %add.71), channel_id=1, source_target_pairs={{0,24},{1,97},{2,26},{3,99},{4,28},{5,101},{6,30},{7,103},{8,16},{... | collective-permute-start | bytes 393224 | tf_op jit(solution)/shard_map/ppermute | solution.py:53
  77.6 3.5 %collective-permute-start.13 = (f32[64,128]{1,0:T(8,128)S(1)}, f32[64,128]{1,0:T(8,128)S(1)}, u32[]{:S(2)}, u32[]{:S(2)}) collective-permute-start(f32[64,128]{1,0:T(8,128)S(1)} %get-tuple-element.104), channel_id=1, source_target_pairs={{0,8},{1,33},{2,10},{3,35},{4,12},{5,37},{6,14},{7,39},{8,0},{9,41... | collective-permute-start | bytes 98312 | tf_op jit(solution)/shard_map/ppermute | solution.py:53
  81.1 7.9 %collective-permute-start.14 = (f32[64,128]{1,0:T(8,128)S(1)}, f32[64,128]{1,0:T(8,128)S(1)}, u32[]{:S(2)}, u32[]{:S(2)}) collective-permute-start(f32[64,128]{1,0:T(8,128)S(1)} %add.75), channel_id=1, source_target_pairs={{0,24},{1,97},{2,26},{3,99},{4,28},{5,101},{6,30},{7,103},{8,16},{... | collective-permute-start | bytes 98312 | tf_op jit(solution)/shard_map/ppermute | solution.py:53
  89.2 15.6 %collective-permute-start.16 = (f32[2,8,16,1024]{3,2,1,0:T(8,128)S(1)}, f32[2,8,16,1024]{3,2,1,0:T(8,128)S(1)}, u32[]{:S(2)}, u32[]{:S(2)}) collective-permute-start(f32[2,8,16,1024]{3,2,1,0:T(8,128)S(1)} %pad_maximum_fusion.refs_0_), channel_id=1, source_target_pairs={{0,8},{1,33},{2,10},{3,35},{4,12},{5,37},{6,14},{7,39},{8,16},{9,4... | collective-permute-start | bytes 3145736 | tf_op jit(solution)/shard_map/ppermute | solution.py:53
  89.3 15.5 %collective-permute-start.17 = (f32[2,8,16,1024]{3,2,1,0:T(8,128)S(1)}, f32[2,8,16,1024]{3,2,1,0:T(8,128)S(1)}, u32[]{:S(2)}, u32[]{:S(2)}) collective-permute-start(f32[2,8,16,1024]{3,2,1,0:T(8,128)S(1)} %pad_maximum_fusion.1.refs_1_), channel_id=1, source_target_pairs={{0,24},{1,97},{2,26},{3,99},{4,28},{5,101},{6,30},{7,103},{8,0},{9... | collective-permute-start | bytes 3145736 | tf_op jit(solution)/shard_map/ppermute | solution.py:53
  92.0 2.8 %collective-permute-start.18 = (f32[64,128]{1,0:T(8,128)S(1)}, f32[64,128]{1,0:T(8,128)S(1)}, u32[]{:S(2)}, u32[]{:S(2)}) collective-permute-start(f32[64,128]{1,0:T(8,128)S(1)} %add.76), channel_id=1, source_target_pairs={{0,32},{1,9},{2,34},{3,11},{4,36},{5,13},{6,38},{7,15},{8,40},{9,1... | collective-permute-start | bytes 98312 | tf_op jit(solution)/shard_map/ppermute | solution.py:53
  94.7 4.7 %collective-permute-start.19 = (f32[64,128]{1,0:T(8,128)S(1)}, f32[64,128]{1,0:T(8,128)S(1)}, u32[]{:S(2)}, u32[]{:S(2)}) collective-permute-start(f32[64,128]{1,0:T(8,128)S(1)} %add.78), channel_id=1, source_target_pairs={{0,96},{1,25},{2,98},{3,27},{4,100},{5,29},{6,102},{7,31},{8,104},... | collective-permute-start | bytes 98312 | tf_op jit(solution)/shard_map/ppermute | solution.py:53
  97.5 17.8 %collective-permute-start.25 = (f32[2,8,16,1024]{3,2,1,0:T(8,128)S(1)}, f32[2,8,16,1024]{3,2,1,0:T(8,128)S(1)}, u32[]{:S(2)}, u32[]{:S(2)}) collective-permute-start(f32[2,8,16,1024]{3,2,1,0:T(8,128)S(1)} %pad_maximum_fusion.refs_0_), channel_id=1, source_target_pairs={{0,24},{1,97},{2,26},{3,99},{4,28},{5,101},{6,30},{7,103},{8,0},{9... | collective-permute-start | bytes 3145736 | tf_op jit(solution)/shard_map/ppermute | solution.py:53
  97.5 18.6 %collective-permute-start.24 = (f32[2,8,16,1024]{3,2,1,0:T(8,128)S(1)}, f32[2,8,16,1024]{3,2,1,0:T(8,128)S(1)}, u32[]{:S(2)}, u32[]{:S(2)}) collective-permute-start(f32[2,8,16,1024]{3,2,1,0:T(8,128)S(1)} %pad_maximum_fusion.1.refs_1_), channel_id=1, source_target_pairs={{0,8},{1,33},{2,10},{3,35},{4,12},{5,37},{6,14},{7,39},{8,16},{9,4... | collective-permute-start | bytes 3145736 | tf_op jit(solution)/shard_map/ppermute | solution.py:53
  104.8 22.5 %collective-permute-start.20 = (f32[2,8,16,1024]{3,2,1,0:T(8,128)S(1)}, f32[2,8,16,1024]{3,2,1,0:T(8,128)S(1)}, u32[]{:S(2)}, u32[]{:S(2)}) collective-permute-start(f32[2,8,16,1024]{3,2,1,0:T(8,128)S(1)} %collective-permute-done.16.refs_2_), channel_id=1, source_target_pairs={{0,8},{1,33},{2,10},{3,35},{4,12},{5,37},{6,14},{7,39},{8,16},{9,4... | collective-permute-start | bytes 3145736 | tf_op jit(solution)/shard_map/ppermute | solution.py:53
  104.8 22.5 %collective-permute-start.21 = (f32[2,8,16,1024]{3,2,1,0:T(8,128)S(1)}, f32[2,8,16,1024]{3,2,1,0:T(8,128)S(1)}, u32[]{:S(2)}, u32[]{:S(2)}) collective-permute-start(f32[2,8,16,1024]{3,2,1,0:T(8,128)S(1)} %collective-permute-done.17.refs_5_), channel_id=1, source_target_pairs={{0,24},{1,97},{2,26},{3,99},{4,28},{5,101},{6,30},{7,103},{8,0},{9... | collective-permute-start | bytes 3145736 | tf_op jit(solution)/shard_map/ppermute | solution.py:53
  107.5 3.7 %collective-permute-start.22 = (f32[56,128]{1,0:T(8,128)S(1)}, f32[56,128]{1,0:T(8,128)S(1)}, u32[]{:S(2)}, u32[]{:S(2)}) collective-permute-start(f32[56,128]{1,0:T(8,128)S(1)} %pad_maximum_fusion.2), channel_id=1, source_target_pairs={{0,1},{1,0},{2,3},{3,2},{4,5},{5,4},{6,7},{7,6},{8,9},{9,8},{10,11... | collective-permute-start | bytes 86024 | tf_op jit(solution)/shard_map/ppermute | solution.py:53
  111.1 3.0 %collective-permute-start.23 = (f32[56,128]{1,0:T(8,128)S(1)}, f32[56,128]{1,0:T(8,128)S(1)}, u32[]{:S(2)}, u32[]{:S(2)}) collective-permute-start(f32[56,128]{1,0:T(8,128)S(1)} %fusion.3), channel_id=1, source_target_pairs={{0,2},{1,3},{2,0},{3,1},{4,6},{5,7},{6,4},{7,5},{8,10},{9,11},{10,... | collective-permute-start | bytes 86024 | tf_op jit(solution)/shard_map/ppermute | solution.py:53
  116.0 4.3 %collective-permute-start.26 = (f32[56,128]{1,0:T(8,128)S(1)}, f32[56,128]{1,0:T(8,128)S(1)}, u32[]{:S(2)}, u32[]{:S(2)}) collective-permute-start(f32[56,128]{1,0:T(8,128)S(1)} %add.81), channel_id=1, source_target_pairs={{0,6},{1,7},{2,4},{3,5},{4,2},{5,3},{6,0},{7,1},{8,14},{9,15},{10,... | collective-permute-start | bytes 86024 | tf_op jit(solution)/shard_map/ppermute | solution.py:53
  131.3 5.9 %collective-permute-start.27 = (f32[256,1280]{1,0:T(8,128)S(1)}, f32[256,1280]{1,0:T(8,128)S(1)}, u32[]{:S(2)}, u32[]{:S(2)}) collective-permute-start(f32[256,1280]{1,0:T(8,128)S(1)} %get-tuple-element.118), channel_id=1, source_target_pairs={{0,1},{1,0},{2,3},{3,2},{4,5},{5,4},{6,7},{7,6},{8,9},{9,8},{10,11... | collective-permute-start | bytes 3932168 | tf_op jit(solution)/shard_map/ppermute | solution.py:53
  137.4 21.1 %collective-permute-start.29 = (f32[128,1280]{1,0:T(8,128)S(1)}, f32[128,1280]{1,0:T(8,128)S(1)}, u32[]{:S(2)}, u32[]{:S(2)}) collective-permute-start(f32[128,1280]{1,0:T(8,128)S(1)} %get-tuple-element.166), channel_id=1, source_target_pairs={{0,6},{1,7},{2,0},{3,1},{4,2},{5,3},{6,4},{7,5},{8,14},{9,15},{10,... | collective-permute-start | bytes 1966088 | tf_op jit(solution)/shard_map/ppermute | solution.py:53
  140.3 18.3 %collective-permute-start.28 = (f32[128,1280]{1,0:T(8,128)S(1)}, f32[128,1280]{1,0:T(8,128)S(1)}, u32[]{:S(2)}, u32[]{:S(2)}) collective-permute-start(f32[128,1280]{1,0:T(8,128)S(1)} %get-tuple-element.167), channel_id=1, source_target_pairs={{0,2},{1,3},{2,4},{3,5},{4,6},{5,7},{6,0},{7,1},{8,10},{9,11},{10,... | collective-permute-start | bytes 1966088 | tf_op jit(solution)/shard_map/ppermute | solution.py:53
  150.2 9.2 %collective-permute-start.32 = (f32[256,1280]{1,0:T(8,128)S(1)}, f32[256,1280]{1,0:T(8,128)S(1)}, u32[]{:S(2)}, u32[]{:S(2)}) collective-permute-start(f32[256,1280]{1,0:T(8,128)S(1)} %get-tuple-element.132), channel_id=1, source_target_pairs={{0,1},{1,0},{2,3},{3,2},{4,5},{5,4},{6,7},{7,6},{8,9},{9,8},{10,11... | collective-permute-start | bytes 3932168 | tf_op jit(solution)/shard_map/ppermute | solution.py:53
  150.6 8.8 %collective-permute-start.31 = (f32[256,1280]{1,0:T(8,128)S(1)}, f32[256,1280]{1,0:T(8,128)S(1)}, u32[]{:S(2)}, u32[]{:S(2)}) collective-permute-start(f32[256,1280]{1,0:T(8,128)S(1)} %get-tuple-element.123), channel_id=1, source_target_pairs={{0,1},{1,0},{2,3},{3,2},{4,5},{5,4},{6,7},{7,6},{8,9},{9,8},{10,11... | collective-permute-start | bytes 3932168 | tf_op jit(solution)/shard_map/ppermute | solution.py:53
  150.8 6.8 %collective-permute-start.30 = (f32[32,1024]{1,0:T(8,128)S(1)}, f32[32,1024]{1,0:T(8,128)S(1)}, u32[]{:S(2)}, u32[]{:S(2)}) collective-permute-start(f32[32,1024]{1,0:T(8,128)S(1)} %add.77), channel_id=1, source_target_pairs={{0,32},{1,9},{2,34},{3,11},{4,36},{5,13},{6,38},{7,15},{8,40},{9,1... | collective-permute-start | bytes 393224 | tf_op jit(solution)/shard_map/ppermute | solution.py:53
  157.6 27.9 %collective-permute-start.35 = (f32[256,1280]{1,0:T(8,128)S(1)}, f32[256,1280]{1,0:T(8,128)S(1)}, u32[]{:S(2)}, u32[]{:S(2)}) collective-permute-start(f32[256,1280]{1,0:T(8,128)S(1)} %get-tuple-element.148), channel_id=1, source_target_pairs={{0,1},{1,0},{2,3},{3,2},{4,5},{5,4},{6,7},{7,6},{8,9},{9,8},{10,11... | collective-permute-start | bytes 3932168 | tf_op jit(solution)/shard_map/ppermute | solution.py:53
  160.3 40.9 %collective-permute-start.40 = (f32[256,1280]{1,0:T(8,128)S(1)}, f32[256,1280]{1,0:T(8,128)S(1)}, u32[]{:S(2)}, u32[]{:S(2)}) collective-permute-start(f32[256,1280]{1,0:T(8,128)S(1)} %get-tuple-element.134), channel_id=1, source_target_pairs={{0,6},{1,7},{2,0},{3,1},{4,2},{5,3},{6,4},{7,5},{8,14},{9,15},{10,... | collective-permute-start | bytes 3932168 | tf_op jit(solution)/shard_map/ppermute | solution.py:53
  163.3 37.9 %collective-permute-start.39 = (f32[256,1280]{1,0:T(8,128)S(1)}, f32[256,1280]{1,0:T(8,128)S(1)}, u32[]{:S(2)}, u32[]{:S(2)}) collective-permute-start(f32[256,1280]{1,0:T(8,128)S(1)} %get-tuple-element.133), channel_id=1, source_target_pairs={{0,2},{1,3},{2,4},{3,5},{4,6},{5,7},{6,0},{7,1},{8,10},{9,11},{10,... | collective-permute-start | bytes 3932168 | tf_op jit(solution)/shard_map/ppermute | solution.py:53
  163.4 22.3 %collective-permute-start.33 = (f32[32,1024]{1,0:T(8,128)S(1)}, f32[32,1024]{1,0:T(8,128)S(1)}, u32[]{:S(2)}, u32[]{:S(2)}) collective-permute-start(f32[32,1024]{1,0:T(8,128)S(1)} %add.84), channel_id=1, source_target_pairs={{0,96},{1,25},{2,98},{3,27},{4,100},{5,29},{6,102},{7,31},{8,104},... | collective-permute-start | bytes 393224 | tf_op jit(solution)/shard_map/ppermute | solution.py:53
  169.4 16.3 %collective-permute-start.34 = (f32[8,1280]{1,0:T(8,128)S(1)}, f32[8,1280]{1,0:T(8,128)S(1)}, u32[]{:S(2)}, u32[]{:S(2)}) collective-permute-start(f32[8,1280]{1,0:T(8,128)S(1)} %get-tuple-element.141), channel_id=1, source_target_pairs={{0,1},{1,0},{2,3},{3,2},{4,5},{5,4},{6,7},{7,6},{8,9},{9,8},{10,11... | collective-permute-start | bytes 122888 | tf_op jit(solution)/shard_map/ppermute | solution.py:53
  185.8 15.4 %collective-permute-start.38 = (f32[8,1280]{1,0:T(8,128)S(1)}, f32[8,1280]{1,0:T(8,128)S(1)}, u32[]{:S(2)}, u32[]{:S(2)}) collective-permute-start(f32[8,1280]{1,0:T(8,128)S(1)} %add.88.last), channel_id=1, source_target_pairs={{0,6},{1,7},{2,0},{3,1},{4,2},{5,3},{6,4},{7,5},{8,14},{9,15},{10,... | collective-permute-start | bytes 122888 | tf_op jit(solution)/shard_map/ppermute | solution.py:53
  188.5 12.7 %collective-permute-start.37 = (f32[8,1280]{1,0:T(8,128)S(1)}, f32[8,1280]{1,0:T(8,128)S(1)}, u32[]{:S(2)}, u32[]{:S(2)}) collective-permute-start(f32[8,1280]{1,0:T(8,128)S(1)} %add.88.last), channel_id=1, source_target_pairs={{0,4},{1,5},{2,6},{3,7},{4,0},{5,1},{6,2},{7,3},{8,12},{9,13},{10,... | collective-permute-start | bytes 122888 | tf_op jit(solution)/shard_map/ppermute | solution.py:53
  188.5 12.7 %collective-permute-start.36 = (f32[8,1280]{1,0:T(8,128)S(1)}, f32[8,1280]{1,0:T(8,128)S(1)}, u32[]{:S(2)}, u32[]{:S(2)}) collective-permute-start(f32[8,1280]{1,0:T(8,128)S(1)} %add.88.last), channel_id=1, source_target_pairs={{0,2},{1,3},{2,4},{3,5},{4,6},{5,7},{6,0},{7,1},{8,10},{9,11},{10,... | collective-permute-start | bytes 122888 | tf_op jit(solution)/shard_map/ppermute | solution.py:53

commit v10 on v8

--- a/solution.py
+++ b/solution.py
@@ -825,14 +825,14 @@
     own = own_b + own_got
 
     column = jnp.sum(column_a + column_b + column_c, axis=0) * share + spot_coef[32] * mass
-    map_rows = stacked([spot_coef[32], column])
+    types = types + types_got
+    last = after(last + last_got, (own, types))
+    got = [up(last, step) for step in (1, 2, 3)]
+    map_rows = after(stacked([spot_coef[32], column]), last)
     valid2 = valid.reshape(blocks, 128)
     map_args = (expr, grad.reshape(2, genes, spots), masses, keep2, valid2, map_rows, all_cells * genes)
     grad_map = map_call(*map_args)
-    types_got, last_got = after((types_got, last_got), grad_map)
-    types = types + types_got
-    last = after(last + last_got, own)
-    got = [up(last, step) for step in (1, 2, 3)]
+    got = after(tuple(got), grad_map)
     grad_weighted = after(own, grad_map) + near_up + near_down
     grad_expr = grad_weighted * (keep * (genes * all_spots))[None, :]
     got = after(tuple(got), grad_expr)

time: 198 us -> 197 us (level)
  waiting for transfers between devices: 51.6 us -> 43.7 us
  starting transfers between devices: 52.9 us -> 60.4 us
    ppermute x41, waiting for transfers between devices: 51.6 us -> 43.7 us  [send(): return lax.ppermute(array, ('cells', 'spots'), route(target))]
    ppermute x41, starting transfers between devices: 52.9 us -> 60.4 us  [send(): return lax.ppermute(array, ('cells', 'spots'), route(target))]
  transfers between devices with their start and end apart: 41 -> 41, of which waited for: 18 -> 16; matrix products, arithmetic and copies ran while one was open for 2% -> 1% of each run, Pallas kernels for 37% -> 37%
where the time goes in v10:
time: 197 us
  Pallas kernels  87.6 us (44%)
  starting transfers between devices  60.4 us (31%)
  waiting for transfers between devices  43.7 us (22%)
  other arithmetic  3.7 us (2%)
    ppermute x41, starting transfers between devices, send(): return lax.ppermute(array, ('cells', 'spots'), route(target))  60.4 us
    ppermute x41, waiting for transfers between devices, send(): return lax.ppermute(array, ('cells', 'spots'), route(target))  43.7 us
    pallas_call x5, Pallas kernels, back_call(): pl.pallas_call(functools.partial(back_kernel, parts=parts, first=len(firs...  23 us
    pallas_call x3, Pallas kernels, pred_call(): pl.pallas_call(functools.partial(pred_kernel, cuts=cuts), grid_spec=pltpu...  21.7 us
    pallas_call x1, Pallas kernels, map_call(): pl.pallas_call(functools.partial(map_kernel, scale=scale), grid=(cells //...  21.5 us
    pallas_call x1, Pallas kernels, expo_call(): pl.pallas_call(expo_kernel, grid_spec=pltpu.PrefetchScalarGridSpec(num_sc...  8.8 us
    pallas_call x3, Pallas kernels, grad_call(): pl.pallas_call(functools.partial(grad_kernel, count=count, lane=lane, chi...  7.63 us
  transfers between devices with their start and end apart: 41, of which 16 were waited for; matrix products, arithmetic and copies ran while one was open for 1% of the time, Pallas kernels for 37%

profile of v10, /device:TPU:1, one launch (start us, length us, event | category | flops | bytes accessed | tf_op | source)
XLA Modules:
  0.0 196.7 jit_solution(4097968789986977539)
XLA Ops:
  0.7 8.8 %expo.1 = (bf16[2,1280,1024]{2,1,0:T(8,128)(2,1)S(1)}, f32[32,1024]{1,0:T(8,128)S(1)}, f32[8,1024]{1,0:T(8,128)S(1)}, f32[33,8,1024]{2,1,0:T(8,128)S(1)}, f32[33,8,1024]{2,1,0:T(8,128)S(1)}) custom-call(s32[4]{0:T(128)S(1)} %pad_add_fusion.ids, f32[1280,1024]{1,0:T(8,128)} %logits.1, s32[10,128]{1,0:T(8,128)} %bitcast.66, f32[10,128]{1,0:T(8,128)} %bitcast.67, ...), custom_call_target="tpu_custom_call" | custom-call | bytes 1310720 | tf_op jit(solution)/shard_map/expo/pallas_call | solution.py:179
  9.5 2.5 %collective-permute-start = (f32[33,8,1024]{2,1,0:T(8,128)S(1)}, f32[33,8,1024]{2,1,0:T(8,128)S(1)}, u32[]{:S(2)}, u32[]{:S(2)}) collective-permute-start(f32[33,8,1024]{2,1,0:T(8,128)S(1)} %get-tuple-element.81), channel_id=1, source_target_pairs={{0,8},{1,33},{2,10},{3,35},{4,12},{5,37},{6,14},{7,39},{8,16},{9,4... | collective-permute-start | bytes 3244040 | tf_op jit(solution)/shard_map/ppermute | solution.py:53
  12.1 2.3 %collective-permute-start.1 = (f32[33,8,1024]{2,1,0:T(8,128)S(1)}, f32[33,8,1024]{2,1,0:T(8,128)S(1)}, u32[]{:S(2)}, u32[]{:S(2)}) collective-permute-start(f32[33,8,1024]{2,1,0:T(8,128)S(1)} %get-tuple-element.82), channel_id=1, source_target_pairs={{0,24},{1,97},{2,26},{3,99},{4,28},{5,101},{6,30},{7,103},{8,0},{9... | collective-permute-start | bytes 3244040 | tf_op jit(solution)/shard_map/ppermute | solution.py:53
  14.4 7.5 %pred_.3 = (f32[33,8,1024]{2,1,0:T(8,128)S(1)}, f32[33,8,1024]{2,1,0:T(8,128)S(1)}) custom-call(s32[4]{0:T(128)S(1)} %pad_add_fusion.ids, f32[8,16,16,1280]{3,2,1,0:T(8,128)} %bitcast.57, f32[8,16,16,1280]{3,2,1,0:T(8,128)} %bitcast.58, f32[1,1280]{1,0:T(1,128)S(1)} %reshape.99.keep, bf16[2,1280,1024]{2,1,0:T(8,128)(2,1)S(1)} %get-tuple-element.84.masses, ...), custom_call_target="tpu_custom_call" | custom-call | flops 503316480 | bytes 1245184 | tf_op jit(solution)/shard_map/pred/pallas_call | solution.py:252
  21.9 1.5 collective-permute-start.2
  23.4 3.6 %collective-permute-done.refs_0_ = f32[33,8,1024]{2,1,0:T(8,128)S(1)} collective-permute-done((f32[33,8,1024]{2,1,0:T(8,128)S(1)}, f32[33,8,1024]{2,1,0:T(8,128)S(1)}, u32[]{:S(2)}, u32[]{:S(2)}) %collective-permute-start) | collective-permute-done | bytes 1081376 | tf_op jit(solution)/shard_map/ppermute | solution.py:53
  27.0 6.6 %pred_.4 = (f32[33,8,1024]{2,1,0:T(8,128)S(1)}, f32[33,8,1024]{2,1,0:T(8,128)S(1)}) custom-call(s32[4]{0:T(128)S(1)} %pad_add_fusion.ids, f32[8,16,16,1280]{3,2,1,0:T(8,128)} %bitcast.59, f32[8,16,16,1280]{3,2,1,0:T(8,128)} %bitcast.60, f32[1,1280]{1,0:T(1,128)S(1)} %reshape.99.keep, bf16[2,1280,1024]{2,1,0:T(8,128)(2,1)S(1)} %get-tuple-element.84.masses, ...), custom_call_target="tpu_custom_call" | custom-call | flops 503316480 | bytes 1245184 | tf_op jit(solution)/shard_map/pred/pallas_call | solution.py:252
  34.7 1.9 collective-permute-start.5
  36.7 1.4 collective-permute-done.2.refs_0_
  38.9 7.6 %pred_.5 = (f32[33,8,1024]{2,1,0:T(8,128)S(1)}, f32[33,8,1024]{2,1,0:T(8,128)S(1)}) custom-call(s32[4]{0:T(128)S(1)} %pad_add_fusion.ids, f32[8,16,16,1280]{3,2,1,0:T(8,128)} %bitcast.61, f32[8,16,16,1280]{3,2,1,0:T(8,128)} %bitcast.62, f32[1,1280]{1,0:T(1,128)S(1)} %reshape.99.keep, bf16[2,1280,1024]{2,1,0:T(8,128)(2,1)S(1)} %get-tuple-element.84.masses, ...), custom_call_target="tpu_custom_call" | custom-call | flops 503316480 | bytes 1245184 | tf_op jit(solution)/shard_map/pred/pallas_call | solution.py:252
  46.4 4.0 %collective-permute-done.4.got0 = f32[33,8,1024]{2,1,0:T(8,128)S(1)} collective-permute-done((f32[33,8,1024]{2,1,0:T(8,128)S(1)}, f32[33,8,1024]{2,1,0:T(8,128)S(1)}, u32[]{:S(2)}, u32[]{:S(2)}) %collective-permute-start.4) | collective-permute-done | bytes 1081376 | tf_op jit(solution)/shard_map/ppermute | solution.py:53
  52.2 2.8 %collective-permute-start.8 = (f32[17,8,1024]{2,1,0:T(8,128)S(1)}, f32[17,8,1024]{2,1,0:T(8,128)S(1)}, u32[]{:S(2)}, u32[]{:S(2)}) collective-permute-start(f32[17,8,1024]{2,1,0:T(8,128)S(1)} %get-tuple-element.100), channel_id=1, source_target_pairs={{0,64},{1,17},{2,66},{3,19},{4,68},{5,21},{6,70},{7,23},{8,72},{9,... | collective-permute-start | bytes 1671176 | tf_op jit(solution)/shard_map/ppermute | solution.py:53
  56.5 1.1 collective-permute-start.6
  57.7 4.4 %collective-permute-done.6 = f32[32,1024]{1,0:T(8,128)S(1)} collective-permute-done((f32[32,1024]{1,0:T(8,128)S(1)}, f32[32,1024]{1,0:T(8,128)S(1)}, u32[]{:S(2)}, u32[]{:S(2)}) %collective-permute-start.6) | collective-permute-done | bytes 131104 | tf_op jit(solution)/shard_map/ppermute | solution.py:53
  62.1 7.5 %collective-permute-done.8 = f32[17,8,1024]{2,1,0:T(8,128)S(1)} collective-permute-done((f32[17,8,1024]{2,1,0:T(8,128)S(1)}, f32[17,8,1024]{2,1,0:T(8,128)S(1)}, u32[]{:S(2)}, u32[]{:S(2)}) %collective-permute-start.8) | collective-permute-done | bytes 557088 | tf_op jit(solution)/shard_map/ppermute | solution.py:53
  69.8 2.2 %collective-permute-start.11 = (f32[8,16,1024]{2,1,0:T(8,128)S(1)}, f32[8,16,1024]{2,1,0:T(8,128)S(1)}, u32[]{:S(2)}, u32[]{:S(2)}) collective-permute-start(f32[8,16,1024]{2,1,0:T(8,128)S(1)} %bitcast.47), channel_id=1, source_target_pairs={{0,64},{1,17},{2,66},{3,19},{4,68},{5,21},{6,70},{7,23},{8,72},{9,... | collective-permute-start | bytes 1572872 | tf_op jit(solution)/shard_map/ppermute | solution.py:53
  72.0 2.7 %collective-permute-start.10 = (f32[8,16,1024]{2,1,0:T(8,128)S(1)}, f32[8,16,1024]{2,1,0:T(8,128)S(1)}, u32[]{:S(2)}, u32[]{:S(2)}) collective-permute-start(f32[8,16,1024]{2,1,0:T(8,128)S(1)} %bitcast.49), channel_id=1, source_target_pairs={{0,96},{1,25},{2,98},{3,27},{4,100},{5,29},{6,102},{7,31},{8,104},... | collective-permute-start | bytes 1572872 | tf_op jit(solution)/shard_map/ppermute | solution.py:53
  75.5 2.7 %collective-permute-start.15 = (f32[32,1024]{1,0:T(8,128)S(1)}, f32[32,1024]{1,0:T(8,128)S(1)}, u32[]{:S(2)}, u32[]{:S(2)}) collective-permute-start(f32[32,1024]{1,0:T(8,128)S(1)} %add.71), channel_id=1, source_target_pairs={{0,24},{1,97},{2,26},{3,99},{4,28},{5,101},{6,30},{7,103},{8,16},{... | collective-permute-start | bytes 393224 | tf_op jit(solution)/shard_map/ppermute | solution.py:53
  78.2 3.5 %collective-permute-done.13 = f32[64,128]{1,0:T(8,128)S(1)} collective-permute-done((f32[64,128]{1,0:T(8,128)S(1)}, f32[64,128]{1,0:T(8,128)S(1)}, u32[]{:S(2)}, u32[]{:S(2)}) %collective-permute-start.13) | collective-permute-done | bytes 32800 | tf_op jit(solution)/shard_map/ppermute | solution.py:53
  82.0 4.9 %collective-permute-done.14 = f32[64,128]{1,0:T(8,128)S(1)} collective-permute-done((f32[64,128]{1,0:T(8,128)S(1)}, f32[64,128]{1,0:T(8,128)S(1)}, u32[]{:S(2)}, u32[]{:S(2)}) %collective-permute-start.14) | collective-permute-done | bytes 32800 | tf_op jit(solution)/shard_map/ppermute | solution.py:53
  87.2 2.7 %collective-permute-start.17 = (f32[2,8,16,1024]{3,2,1,0:T(8,128)S(1)}, f32[2,8,16,1024]{3,2,1,0:T(8,128)S(1)}, u32[]{:S(2)}, u32[]{:S(2)}) collective-permute-start(f32[2,8,16,1024]{3,2,1,0:T(8,128)S(1)} %pad_maximum_fusion.1.refs_1_), channel_id=1, source_target_pairs={{0,24},{1,97},{2,26},{3,99},{4,28},{5,101},{6,30},{7,103},{8,0},{9... | collective-permute-start | bytes 3145736 | tf_op jit(solution)/shard_map/ppermute | solution.py:53
  89.9 2.7 %collective-permute-done.18 = f32[64,128]{1,0:T(8,128)S(1)} collective-permute-done((f32[64,128]{1,0:T(8,128)S(1)}, f32[64,128]{1,0:T(8,128)S(1)}, u32[]{:S(2)}, u32[]{:S(2)}) %collective-permute-start.18) | collective-permute-done | bytes 32800 | tf_op jit(solution)/shard_map/ppermute | solution.py:53
  92.6 1.2 collective-permute-start.19
  93.8 2.7 %collective-permute-start.25 = (f32[2,8,16,1024]{3,2,1,0:T(8,128)S(1)}, f32[2,8,16,1024]{3,2,1,0:T(8,128)S(1)}, u32[]{:S(2)}, u32[]{:S(2)}) collective-permute-start(f32[2,8,16,1024]{3,2,1,0:T(8,128)S(1)} %pad_maximum_fusion.refs_0_), channel_id=1, source_target_pairs={{0,24},{1,97},{2,26},{3,99},{4,28},{5,101},{6,30},{7,103},{8,0},{9... | collective-permute-start | bytes 3145736 | tf_op jit(solution)/shard_map/ppermute | solution.py:53
  97.2 5.1 %collective-permute-done.16.refs_2_ = f32[2,8,16,1024]{3,2,1,0:T(8,128)S(1)} collective-permute-done((f32[2,8,16,1024]{3,2,1,0:T(8,128)S(1)}, f32[2,8,16,1024]{3,2,1,0:T(8,128)S(1)}, u32[]{:S(2)}, u32[]{:S(2)}) %collective-permute-start.16) | collective-permute-done | bytes 1048608 | tf_op jit(solution)/shard_map/ppermute | solution.py:53
  102.4 1.2 collective-permute-start.20
  103.5 1.9 collective-permute-start.21
  105.4 5.6 %collective-permute-start.22 = (f32[56,128]{1,0:T(8,128)S(1)}, f32[56,128]{1,0:T(8,128)S(1)}, u32[]{:S(2)}, u32[]{:S(2)}) collective-permute-start(f32[56,128]{1,0:T(8,128)S(1)} %pad_maximum_fusion.2), channel_id=1, source_target_pairs={{0,1},{1,0},{2,3},{3,2},{4,5},{5,4},{6,7},{7,6},{8,9},{9,8},{10,11... | collective-permute-start | bytes 86024 | tf_op jit(solution)/shard_map/ppermute | solution.py:53
  111.9 1.3 collective-permute-start.23
  113.2 1.7 collective-permute-done.23
  114.9 2.8 %collective-permute-start.26 = (f32[56,128]{1,0:T(8,128)S(1)}, f32[56,128]{1,0:T(8,128)S(1)}, u32[]{:S(2)}, u32[]{:S(2)}) collective-permute-start(f32[56,128]{1,0:T(8,128)S(1)} %add.81), channel_id=1, source_target_pairs={{0,6},{1,7},{2,4},{3,5},{4,2},{5,3},{6,0},{7,1},{8,14},{9,15},{10,... | collective-permute-start | bytes 86024 | tf_op jit(solution)/shard_map/ppermute | solution.py:53
  117.7 1.6 collective-permute-done.26
  120.2 4.7 %grad.3 = (bf16[2,8,256,1024]{3,2,1,0:T(8,128)(2,1)S(1)}, f32[8,1024]{1,0:T(8,128)S(1)}) custom-call(s32[4]{0:T(128)S(1)} %pad_add_fusion.ids, f32[2,8,16,1024]{3,2,1,0:T(8,128)S(1)} %pad_maximum_fusion.refs_0_, f32[2,8,16,1024]{3,2,1,0:T(8,128)S(1)} %pad_maximum_fusion.1.refs_1_, f32[2,8,16,1024]{3,2,1,0:T(8,128)S(1)} %collective-permute-done.16.refs_2_, ...), custom_call_target="tpu_custom_call" | custom-call | tf_op jit(solution)/shard_map/grad/pallas_call | solution.py:477
  126.1 3.1 %back.5 = (f32[8,1280]{1,0:T(8,128)S(1)}, f32[256,1280]{1,0:T(8,128)S(1)}) custom-call(s32[4]{0:T(128)S(1)} %pad_add_fusion.ids, bf16[2,8,256,1024]{3,2,1,0:T(8,128)(2,1)S(1)} %get-tuple-element.115.grad.refs_5_, bf16[2,1280,1024]{2,1,0:T(8,128)(2,1)S(1)} %get-tuple-element.84.masses, f32[2048,1280]{1,0:T(8,128)} %expr.11, ...), custom_call_target="tpu_custom_call" | custom-call | tf_op jit(solution)/shard_map/back/pallas_call | solution.py:553
  129.2 5.2 %collective-permute-start.27 = (f32[256,1280]{1,0:T(8,128)S(1)}, f32[256,1280]{1,0:T(8,128)S(1)}, u32[]{:S(2)}, u32[]{:S(2)}) collective-permute-start(f32[256,1280]{1,0:T(8,128)S(1)} %get-tuple-element.116), channel_id=1, source_target_pairs={{0,1},{1,0},{2,3},{3,2},{4,5},{5,4},{6,7},{7,6},{8,9},{9,8},{10,11... | collective-permute-start | bytes 3932168 | tf_op jit(solution)/shard_map/ppermute | solution.py:53
  134.4 3.6 %back.6 = (f32[8,1280]{1,0:T(8,128)S(1)}, f32[256,1280]{1,0:T(8,128)S(1)}) custom-call(s32[4]{0:T(128)S(1)} %pad_add_fusion.ids, bf16[2,8,256,1024]{3,2,1,0:T(8,128)(2,1)S(1)} %get-tuple-element.115.grad.refs_5_, bf16[2,1280,1024]{2,1,0:T(8,128)(2,1)S(1)} %get-tuple-element.84.masses, f32[2048,1280]{1,0:T(8,128)} %expr.11), custom_call_target="tpu_custom_call" | custom-call | tf_op jit(solution)/shard_map/back/pallas_call | solution.py:553
  138.2 1.3 collective-permute-start.28
  139.6 1.8 collective-permute-start.29
  141.3 1.9 grad.5
  143.2 8.0 %back.7 = (f32[8,1280]{1,0:T(8,128)S(1)}, f32[256,1280]{1,0:T(8,128)S(1)}, f32[256,1280]{1,0:T(8,128)S(1)}, f32[256,1280]{1,0:T(8,128)S(1)}) custom-call(s32[4]{0:T(128)S(1)} %pad_add_fusion.ids, bf16[2,8,256,1024]{3,2,1,0:T(8,128)(2,1)S(1)} %get-tuple-element.120.grad, bf16[2,1280,1024]{2,1,0:T(8,128)(2,1)S(1)} %get-tuple-element.84.masses, f32[2048,1280]{1,0:T(8,128)} %expr.11), custom_call_target="tpu_custom_call" | custom-call | tf_op jit(solution)/shard_map/back/pallas_call | solution.py:553
  151.8 5.5 %back.8 = (f32[8,1280]{1,0:T(8,128)S(1)}, f32[256,1280]{1,0:T(8,128)S(1)}, f32[256,1280]{1,0:T(8,128)S(1)}) custom-call(s32[4]{0:T(128)S(1)} %pad_add_fusion.ids, bf16[2,8,256,1024]{3,2,1,0:T(8,128)(2,1)S(1)} %get-tuple-element.120.grad, bf16[2,1280,1024]{2,1,0:T(8,128)(2,1)S(1)} %get-tuple-element.84.masses, f32[2048,1280]{1,0:T(8,128)} %expr.11), custom_call_target="tpu_custom_call" | custom-call | tf_op jit(solution)/shard_map/back/pallas_call | solution.py:553
  159.6 2.7 %collective-permute-start.40 = (f32[256,1280]{1,0:T(8,128)S(1)}, f32[256,1280]{1,0:T(8,128)S(1)}, u32[]{:S(2)}, u32[]{:S(2)}) collective-permute-start(f32[256,1280]{1,0:T(8,128)S(1)} %get-tuple-element.132), channel_id=1, source_target_pairs={{0,6},{1,7},{2,0},{3,1},{4,2},{5,3},{6,4},{7,5},{8,14},{9,15},{10,... | collective-permute-start | bytes 3932168 | tf_op jit(solution)/shard_map/ppermute | solution.py:53
  162.3 2.7 %collective-permute-start.35 = (f32[32,1024]{1,0:T(8,128)S(1)}, f32[32,1024]{1,0:T(8,128)S(1)}, u32[]{:S(2)}, u32[]{:S(2)}) collective-permute-start(f32[32,1024]{1,0:T(8,128)S(1)} %add.84), channel_id=1, source_target_pairs={{0,96},{1,25},{2,98},{3,27},{4,100},{5,29},{6,102},{7,31},{8,104},... | collective-permute-start | bytes 393224 | tf_op jit(solution)/shard_map/ppermute | solution.py:53
  165.0 3.0 %back.9 = (f32[8,1280]{1,0:T(8,128)S(1)}, f32[256,1280]{1,0:T(8,128)S(1)}) custom-call(s32[4]{0:T(128)S(1)} %pad_add_fusion.ids, bf16[2,8,256,1024]{3,2,1,0:T(8,128)(2,1)S(1)} %get-tuple-element.120.grad, bf16[2,1280,1024]{2,1,0:T(8,128)(2,1)S(1)} %get-tuple-element.84.masses, f32[2048,1280]{1,0:T(8,128)} %expr.11, ...), custom_call_target="tpu_custom_call" | custom-call | tf_op jit(solution)/shard_map/back/pallas_call | solution.py:553
  170.3 1.4 collective-permute-start.37
  171.7 1.2 collective-permute-start.38
  173.1 21.5 %grad_map.1 = f32[1280,1024]{1,0:T(8,128)} custom-call(f32[2048,1280]{1,0:T(8,128)} %expr.11, bf16[2,2048,1024]{2,1,0:T(8,128)(2,1)S(1)} %bitcast.38, bf16[2,1280,1024]{2,1,0:T(8,128)(2,1)S(1)} %get-tuple-element.84.masses, f32[10,128]{1,0:T(8,128)S(1)} %bitcast.52, f32[10,128]{1,0:T(8,128)S(1)} %convert_bitcast_fusion.valid, ...), custom_call_target="tpu_custom_call" | custom-call | tf_op jit(solution)/shard_map/grad_map/pallas_call | solution.py:660
  194.6 1.3 add_multiply_fusion
  (104 shorter events, 17.1 us)
Async XLA Ops:
  0.7 13.6 %copy-start = (s32[1280]{0:T(1024)S(1)}, s32[1280]{0:T(1024)}, u32[]{:S(2)}) copy-start(s32[1280]{0:T(1024)} %param.11) | copy-start | bytes 15364
  0.7 13.6 %copy-start.1 = (f32[1280]{0:T(1024)S(1)}, f32[1280]{0:T(1024)}, u32[]{:S(2)}) copy-start(f32[1280]{0:T(1024)} %param.8) | copy-start | bytes 15364
  9.5 17.5 %collective-permute-start = (f32[33,8,1024]{2,1,0:T(8,128)S(1)}, f32[33,8,1024]{2,1,0:T(8,128)S(1)}, u32[]{:S(2)}, u32[]{:S(2)}) collective-permute-start(f32[33,8,1024]{2,1,0:T(8,128)S(1)} %get-tuple-element.81), channel_id=1, source_target_pairs={{0,8},{1,33},{2,10},{3,35},{4,12},{5,37},{6,14},{7,39},{8,16},{9,4... | collective-permute-start | bytes 3244040 | tf_op jit(solution)/shard_map/ppermute | solution.py:53
  12.1 14.9 %collective-permute-start.1 = (f32[33,8,1024]{2,1,0:T(8,128)S(1)}, f32[33,8,1024]{2,1,0:T(8,128)S(1)}, u32[]{:S(2)}, u32[]{:S(2)}) collective-permute-start(f32[33,8,1024]{2,1,0:T(8,128)S(1)} %get-tuple-element.82), channel_id=1, source_target_pairs={{0,24},{1,97},{2,26},{3,99},{4,28},{5,101},{6,30},{7,103},{8,0},{9... | collective-permute-start | bytes 3244040 | tf_op jit(solution)/shard_map/ppermute | solution.py:53
  21.9 16.3 %collective-permute-start.2 = (f32[33,8,1024]{2,1,0:T(8,128)S(1)}, f32[33,8,1024]{2,1,0:T(8,128)S(1)}, u32[]{:S(2)}, u32[]{:S(2)}) collective-permute-start(f32[33,8,1024]{2,1,0:T(8,128)S(1)} %get-tuple-element.87), channel_id=1, source_target_pairs={{0,24},{1,97},{2,26},{3,99},{4,28},{5,101},{6,30},{7,103},{8,0},{9... | collective-permute-start | bytes 3244040 | tf_op jit(solution)/shard_map/ppermute | solution.py:53
  23.3 13.3 %copy-start.2 = (s32[1024]{0:T(1024)S(1)}, s32[1024]{0:T(1024)}, u32[]{:S(2)}) copy-start(s32[1024]{0:T(1024)} %param.12) | copy-start | bytes 12292
  23.3 13.3 %copy-start.3 = (s32[1024]{0:T(1024)S(1)}, s32[1024]{0:T(1024)}, u32[]{:S(2)}) copy-start(s32[1024]{0:T(1024)} %param.13) | copy-start | bytes 12292
  23.4 15.5 %collective-permute-start.3 = (f32[33,8,1024]{2,1,0:T(8,128)S(1)}, f32[33,8,1024]{2,1,0:T(8,128)S(1)}, u32[]{:S(2)}, u32[]{:S(2)}) collective-permute-start(f32[33,8,1024]{2,1,0:T(8,128)S(1)} %get-tuple-element.86), channel_id=1, source_target_pairs={{0,8},{1,33},{2,10},{3,35},{4,12},{5,37},{6,14},{7,39},{8,16},{9,4... | collective-permute-start | bytes 3244040 | tf_op jit(solution)/shard_map/ppermute | solution.py:53
  33.6 16.8 %collective-permute-start.4 = (f32[33,8,1024]{2,1,0:T(8,128)S(1)}, f32[33,8,1024]{2,1,0:T(8,128)S(1)}, u32[]{:S(2)}, u32[]{:S(2)}) collective-permute-start(f32[33,8,1024]{2,1,0:T(8,128)S(1)} %get-tuple-element.89), channel_id=1, source_target_pairs={{0,8},{1,33},{2,10},{3,35},{4,12},{5,37},{6,14},{7,39},{8,16},{9,4... | collective-permute-start | bytes 3244040 | tf_op jit(solution)/shard_map/ppermute | solution.py:53
  34.7 15.7 %collective-permute-start.5 = (f32[33,8,1024]{2,1,0:T(8,128)S(1)}, f32[33,8,1024]{2,1,0:T(8,128)S(1)}, u32[]{:S(2)}, u32[]{:S(2)}) collective-permute-start(f32[33,8,1024]{2,1,0:T(8,128)S(1)} %get-tuple-element.90), channel_id=1, source_target_pairs={{0,24},{1,97},{2,26},{3,99},{4,28},{5,101},{6,30},{7,103},{8,0},{9... | collective-permute-start | bytes 3244040 | tf_op jit(solution)/shard_map/ppermute | solution.py:53
  36.7 19.2 %slice-start = ((s8[8388608]{0:T(1024)(128)(4,1)}), s8[4194304]{0:T(1024)(128)(4,1)S(1)}, s32[]{:S(2)}) async-start(s8[8388608]{0:T(1024)(128)(4,1)} %bitcast.39), calls=%async_computation | async-start | bytes 8388608
  36.7 19.2 %slice-start.1 = ((s8[8388608]{0:T(1024)(128)(4,1)}), s8[4194304]{0:T(1024)(128)(4,1)S(1)}, s32[]{:S(2)}) async-start(s8[8388608]{0:T(1024)(128)(4,1)} %bitcast.39), calls=%async_computation.1 | async-start | bytes 8388608
  51.2 10.9 %collective-permute-start.7 = (f32[17,8,1024]{2,1,0:T(8,128)S(1)}, f32[17,8,1024]{2,1,0:T(8,128)S(1)}, u32[]{:S(2)}, u32[]{:S(2)}) collective-permute-start(f32[17,8,1024]{2,1,0:T(8,128)S(1)} %get-tuple-element.99), channel_id=1, source_target_pairs={{0,32},{1,9},{2,34},{3,11},{4,36},{5,13},{6,38},{7,15},{8,40},{9,1... | collective-permute-start | bytes 1671176 | tf_op jit(solution)/shard_map/ppermute | solution.py:53
  52.2 17.3 %collective-permute-start.8 = (f32[17,8,1024]{2,1,0:T(8,128)S(1)}, f32[17,8,1024]{2,1,0:T(8,128)S(1)}, u32[]{:S(2)}, u32[]{:S(2)}) collective-permute-start(f32[17,8,1024]{2,1,0:T(8,128)S(1)} %get-tuple-element.100), channel_id=1, source_target_pairs={{0,64},{1,17},{2,66},{3,19},{4,68},{5,21},{6,70},{7,23},{8,72},{9,... | collective-permute-start | bytes 1671176 | tf_op jit(solution)/shard_map/ppermute | solution.py:53
  55.0 14.6 %collective-permute-start.9 = (f32[17,8,1024]{2,1,0:T(8,128)S(1)}, f32[17,8,1024]{2,1,0:T(8,128)S(1)}, u32[]{:S(2)}, u32[]{:S(2)}) collective-permute-start(f32[17,8,1024]{2,1,0:T(8,128)S(1)} %get-tuple-element.101), channel_id=1, source_target_pairs={{0,96},{1,25},{2,98},{3,27},{4,100},{5,29},{6,102},{7,31},{8,104},... | collective-permute-start | bytes 1671176 | tf_op jit(solution)/shard_map/ppermute | solution.py:53
  56.5 5.5 %collective-permute-start.6 = (f32[32,1024]{1,0:T(8,128)S(1)}, f32[32,1024]{1,0:T(8,128)S(1)}, u32[]{:S(2)}, u32[]{:S(2)}) collective-permute-start(f32[32,1024]{1,0:T(8,128)S(1)} %get-tuple-element.97), channel_id=1, source_target_pairs={{0,8},{1,33},{2,10},{3,35},{4,12},{5,37},{6,14},{7,39},{8,0},{9,41... | collective-permute-start | bytes 393224 | tf_op jit(solution)/shard_map/ppermute | solution.py:53
  69.8 17.1 %collective-permute-start.11 = (f32[8,16,1024]{2,1,0:T(8,128)S(1)}, f32[8,16,1024]{2,1,0:T(8,128)S(1)}, u32[]{:S(2)}, u32[]{:S(2)}) collective-permute-start(f32[8,16,1024]{2,1,0:T(8,128)S(1)} %bitcast.47), channel_id=1, source_target_pairs={{0,64},{1,17},{2,66},{3,19},{4,68},{5,21},{6,70},{7,23},{8,72},{9,... | collective-permute-start | bytes 1572872 | tf_op jit(solution)/shard_map/ppermute | solution.py:53
  72.0 15.0 %collective-permute-start.12 = (f32[8,16,1024]{2,1,0:T(8,128)S(1)}, f32[8,16,1024]{2,1,0:T(8,128)S(1)}, u32[]{:S(2)}, u32[]{:S(2)}) collective-permute-start(f32[8,16,1024]{2,1,0:T(8,128)S(1)} %bitcast.48), channel_id=1, source_target_pairs={{0,32},{1,9},{2,34},{3,11},{4,36},{5,13},{6,38},{7,15},{8,40},{9,1... | collective-permute-start | bytes 1572872 | tf_op jit(solution)/shard_map/ppermute | solution.py:53
  72.0 15.0 %collective-permute-start.10 = (f32[8,16,1024]{2,1,0:T(8,128)S(1)}, f32[8,16,1024]{2,1,0:T(8,128)S(1)}, u32[]{:S(2)}, u32[]{:S(2)}) collective-permute-start(f32[8,16,1024]{2,1,0:T(8,128)S(1)} %bitcast.49), channel_id=1, source_target_pairs={{0,96},{1,25},{2,98},{3,27},{4,100},{5,29},{6,102},{7,31},{8,104},... | collective-permute-start | bytes 1572872 | tf_op jit(solution)/shard_map/ppermute | solution.py:53
  75.5 11.4 %collective-permute-start.15 = (f32[32,1024]{1,0:T(8,128)S(1)}, f32[32,1024]{1,0:T(8,128)S(1)}, u32[]{:S(2)}, u32[]{:S(2)}) collective-permute-start(f32[32,1024]{1,0:T(8,128)S(1)} %add.71), channel_id=1, source_target_pairs={{0,24},{1,97},{2,26},{3,99},{4,28},{5,101},{6,30},{7,103},{8,16},{... | collective-permute-start | bytes 393224 | tf_op jit(solution)/shard_map/ppermute | solution.py:53
  78.2 3.5 %collective-permute-start.13 = (f32[64,128]{1,0:T(8,128)S(1)}, f32[64,128]{1,0:T(8,128)S(1)}, u32[]{:S(2)}, u32[]{:S(2)}) collective-permute-start(f32[64,128]{1,0:T(8,128)S(1)} %get-tuple-element.102), channel_id=1, source_target_pairs={{0,8},{1,33},{2,10},{3,35},{4,12},{5,37},{6,14},{7,39},{8,0},{9,41... | collective-permute-start | bytes 98312 | tf_op jit(solution)/shard_map/ppermute | solution.py:53
  81.7 5.2 %collective-permute-start.14 = (f32[64,128]{1,0:T(8,128)S(1)}, f32[64,128]{1,0:T(8,128)S(1)}, u32[]{:S(2)}, u32[]{:S(2)}) collective-permute-start(f32[64,128]{1,0:T(8,128)S(1)} %add.75), channel_id=1, source_target_pairs={{0,24},{1,97},{2,26},{3,99},{4,28},{5,101},{6,30},{7,103},{8,16},{... | collective-permute-start | bytes 98312 | tf_op jit(solution)/shard_map/ppermute | solution.py:53
  87.1 15.2 %collective-permute-start.16 = (f32[2,8,16,1024]{3,2,1,0:T(8,128)S(1)}, f32[2,8,16,1024]{3,2,1,0:T(8,128)S(1)}, u32[]{:S(2)}, u32[]{:S(2)}) collective-permute-start(f32[2,8,16,1024]{3,2,1,0:T(8,128)S(1)} %pad_maximum_fusion.refs_0_), channel_id=1, source_target_pairs={{0,8},{1,33},{2,10},{3,35},{4,12},{5,37},{6,14},{7,39},{8,16},{9,4... | collective-permute-start | bytes 3145736 | tf_op jit(solution)/shard_map/ppermute | solution.py:53
  87.2 15.1 %collective-permute-start.17 = (f32[2,8,16,1024]{3,2,1,0:T(8,128)S(1)}, f32[2,8,16,1024]{3,2,1,0:T(8,128)S(1)}, u32[]{:S(2)}, u32[]{:S(2)}) collective-permute-start(f32[2,8,16,1024]{3,2,1,0:T(8,128)S(1)} %pad_maximum_fusion.1.refs_1_), channel_id=1, source_target_pairs={{0,24},{1,97},{2,26},{3,99},{4,28},{5,101},{6,30},{7,103},{8,0},{9... | collective-permute-start | bytes 3145736 | tf_op jit(solution)/shard_map/ppermute | solution.py:53
  89.9 2.8 %collective-permute-start.18 = (f32[64,128]{1,0:T(8,128)S(1)}, f32[64,128]{1,0:T(8,128)S(1)}, u32[]{:S(2)}, u32[]{:S(2)}) collective-permute-start(f32[64,128]{1,0:T(8,128)S(1)} %add.76), channel_id=1, source_target_pairs={{0,32},{1,9},{2,34},{3,11},{4,36},{5,13},{6,38},{7,15},{8,40},{9,1... | collective-permute-start | bytes 98312 | tf_op jit(solution)/shard_map/ppermute | solution.py:53
  92.6 4.6 %collective-permute-start.19 = (f32[64,128]{1,0:T(8,128)S(1)}, f32[64,128]{1,0:T(8,128)S(1)}, u32[]{:S(2)}, u32[]{:S(2)}) collective-permute-start(f32[64,128]{1,0:T(8,128)S(1)} %add.78), channel_id=1, source_target_pairs={{0,96},{1,25},{2,98},{3,27},{4,100},{5,29},{6,102},{7,31},{8,104},... | collective-permute-start | bytes 98312 | tf_op jit(solution)/shard_map/ppermute | solution.py:53
  93.8 21.1 %collective-permute-start.24 = (f32[2,8,16,1024]{3,2,1,0:T(8,128)S(1)}, f32[2,8,16,1024]{3,2,1,0:T(8,128)S(1)}, u32[]{:S(2)}, u32[]{:S(2)}) collective-permute-start(f32[2,8,16,1024]{3,2,1,0:T(8,128)S(1)} %pad_maximum_fusion.1.refs_1_), channel_id=1, source_target_pairs={{0,8},{1,33},{2,10},{3,35},{4,12},{5,37},{6,14},{7,39},{8,16},{9,4... | collective-permute-start | bytes 3145736 | tf_op jit(solution)/shard_map/ppermute | solution.py:53
  93.8 21.1 %collective-permute-start.25 = (f32[2,8,16,1024]{3,2,1,0:T(8,128)S(1)}, f32[2,8,16,1024]{3,2,1,0:T(8,128)S(1)}, u32[]{:S(2)}, u32[]{:S(2)}) collective-permute-start(f32[2,8,16,1024]{3,2,1,0:T(8,128)S(1)} %pad_maximum_fusion.refs_0_), channel_id=1, source_target_pairs={{0,24},{1,97},{2,26},{3,99},{4,28},{5,101},{6,30},{7,103},{8,0},{9... | collective-permute-start | bytes 3145736 | tf_op jit(solution)/shard_map/ppermute | solution.py:53
  102.4 22.8 %collective-permute-start.20 = (f32[2,8,16,1024]{3,2,1,0:T(8,128)S(1)}, f32[2,8,16,1024]{3,2,1,0:T(8,128)S(1)}, u32[]{:S(2)}, u32[]{:S(2)}) collective-permute-start(f32[2,8,16,1024]{3,2,1,0:T(8,128)S(1)} %collective-permute-done.16.refs_2_), channel_id=1, source_target_pairs={{0,8},{1,33},{2,10},{3,35},{4,12},{5,37},{6,14},{7,39},{8,16},{9,4... | collective-permute-start | bytes 3145736 | tf_op jit(solution)/shard_map/ppermute | solution.py:53
  103.5 21.6 %collective-permute-start.21 = (f32[2,8,16,1024]{3,2,1,0:T(8,128)S(1)}, f32[2,8,16,1024]{3,2,1,0:T(8,128)S(1)}, u32[]{:S(2)}, u32[]{:S(2)}) collective-permute-start(f32[2,8,16,1024]{3,2,1,0:T(8,128)S(1)} %collective-permute-done.17.refs_5_), channel_id=1, source_target_pairs={{0,24},{1,97},{2,26},{3,99},{4,28},{5,101},{6,30},{7,103},{8,0},{9... | collective-permute-start | bytes 3145736 | tf_op jit(solution)/shard_map/ppermute | solution.py:53
  105.4 6.5 %collective-permute-start.22 = (f32[56,128]{1,0:T(8,128)S(1)}, f32[56,128]{1,0:T(8,128)S(1)}, u32[]{:S(2)}, u32[]{:S(2)}) collective-permute-start(f32[56,128]{1,0:T(8,128)S(1)} %pad_maximum_fusion.2), channel_id=1, source_target_pairs={{0,1},{1,0},{2,3},{3,2},{4,5},{5,4},{6,7},{7,6},{8,9},{9,8},{10,11... | collective-permute-start | bytes 86024 | tf_op jit(solution)/shard_map/ppermute | solution.py:53
  111.9 3.0 %collective-permute-start.23 = (f32[56,128]{1,0:T(8,128)S(1)}, f32[56,128]{1,0:T(8,128)S(1)}, u32[]{:S(2)}, u32[]{:S(2)}) collective-permute-start(f32[56,128]{1,0:T(8,128)S(1)} %fusion.3), channel_id=1, source_target_pairs={{0,2},{1,3},{2,0},{3,1},{4,6},{5,7},{6,4},{7,5},{8,10},{9,11},{10,... | collective-permute-start | bytes 86024 | tf_op jit(solution)/shard_map/ppermute | solution.py:53
  114.9 4.4 %collective-permute-start.26 = (f32[56,128]{1,0:T(8,128)S(1)}, f32[56,128]{1,0:T(8,128)S(1)}, u32[]{:S(2)}, u32[]{:S(2)}) collective-permute-start(f32[56,128]{1,0:T(8,128)S(1)} %add.81), channel_id=1, source_target_pairs={{0,6},{1,7},{2,4},{3,5},{4,2},{5,3},{6,0},{7,1},{8,14},{9,15},{10,... | collective-permute-start | bytes 86024 | tf_op jit(solution)/shard_map/ppermute | solution.py:53
  129.2 8.7 %collective-permute-start.27 = (f32[256,1280]{1,0:T(8,128)S(1)}, f32[256,1280]{1,0:T(8,128)S(1)}, u32[]{:S(2)}, u32[]{:S(2)}) collective-permute-start(f32[256,1280]{1,0:T(8,128)S(1)} %get-tuple-element.116), channel_id=1, source_target_pairs={{0,1},{1,0},{2,3},{3,2},{4,5},{5,4},{6,7},{7,6},{8,9},{9,8},{10,11... | collective-permute-start | bytes 3932168 | tf_op jit(solution)/shard_map/ppermute | solution.py:53
  138.2 19.5 %collective-permute-start.28 = (f32[128,1280]{1,0:T(8,128)S(1)}, f32[128,1280]{1,0:T(8,128)S(1)}, u32[]{:S(2)}, u32[]{:S(2)}) collective-permute-start(f32[128,1280]{1,0:T(8,128)S(1)} %get-tuple-element.165), channel_id=1, source_target_pairs={{0,2},{1,3},{2,4},{3,5},{4,6},{5,7},{6,0},{7,1},{8,10},{9,11},{10,... | collective-permute-start | bytes 1966088 | tf_op jit(solution)/shard_map/ppermute | solution.py:53
  139.6 18.2 %collective-permute-start.29 = (f32[128,1280]{1,0:T(8,128)S(1)}, f32[128,1280]{1,0:T(8,128)S(1)}, u32[]{:S(2)}, u32[]{:S(2)}) collective-permute-start(f32[128,1280]{1,0:T(8,128)S(1)} %get-tuple-element.164), channel_id=1, source_target_pairs={{0,6},{1,7},{2,0},{3,1},{4,2},{5,3},{6,4},{7,5},{8,14},{9,15},{10,... | collective-permute-start | bytes 1966088 | tf_op jit(solution)/shard_map/ppermute | solution.py:53
  151.2 7.3 %collective-permute-start.31 = (f32[256,1280]{1,0:T(8,128)S(1)}, f32[256,1280]{1,0:T(8,128)S(1)}, u32[]{:S(2)}, u32[]{:S(2)}) collective-permute-start(f32[256,1280]{1,0:T(8,128)S(1)} %get-tuple-element.121), channel_id=1, source_target_pairs={{0,1},{1,0},{2,3},{3,2},{4,5},{5,4},{6,7},{7,6},{8,9},{9,8},{10,11... | collective-permute-start | bytes 3932168 | tf_op jit(solution)/shard_map/ppermute | solution.py:53
  151.6 7.0 %collective-permute-start.32 = (f32[256,1280]{1,0:T(8,128)S(1)}, f32[256,1280]{1,0:T(8,128)S(1)}, u32[]{:S(2)}, u32[]{:S(2)}) collective-permute-start(f32[256,1280]{1,0:T(8,128)S(1)} %get-tuple-element.130), channel_id=1, source_target_pairs={{0,1},{1,0},{2,3},{3,2},{4,5},{5,4},{6,7},{7,6},{8,9},{9,8},{10,11... | collective-permute-start | bytes 3932168 | tf_op jit(solution)/shard_map/ppermute | solution.py:53
  151.8 5.5 %collective-permute-start.30 = (f32[32,1024]{1,0:T(8,128)S(1)}, f32[32,1024]{1,0:T(8,128)S(1)}, u32[]{:S(2)}, u32[]{:S(2)}) collective-permute-start(f32[32,1024]{1,0:T(8,128)S(1)} %add.77), channel_id=1, source_target_pairs={{0,32},{1,9},{2,34},{3,11},{4,36},{5,13},{6,38},{7,15},{8,40},{9,1... | collective-permute-start | bytes 393224 | tf_op jit(solution)/shard_map/ppermute | solution.py:53
  157.3 11.4 %collective-permute-start.34 = (f32[256,1280]{1,0:T(8,128)S(1)}, f32[256,1280]{1,0:T(8,128)S(1)}, u32[]{:S(2)}, u32[]{:S(2)}) collective-permute-start(f32[256,1280]{1,0:T(8,128)S(1)} %get-tuple-element.141), channel_id=1, source_target_pairs={{0,1},{1,0},{2,3},{3,2},{4,5},{5,4},{6,7},{7,6},{8,9},{9,8},{10,11... | collective-permute-start | bytes 3932168 | tf_op jit(solution)/shard_map/ppermute | solution.py:53
  159.5 35.1 %collective-permute-start.39 = (f32[256,1280]{1,0:T(8,128)S(1)}, f32[256,1280]{1,0:T(8,128)S(1)}, u32[]{:S(2)}, u32[]{:S(2)}) collective-permute-start(f32[256,1280]{1,0:T(8,128)S(1)} %get-tuple-element.131), channel_id=1, source_target_pairs={{0,2},{1,3},{2,4},{3,5},{4,6},{5,7},{6,0},{7,1},{8,10},{9,11},{10,... | collective-permute-start | bytes 3932168 | tf_op jit(solution)/shard_map/ppermute | solution.py:53
  159.6 35.0 %collective-permute-start.40 = (f32[256,1280]{1,0:T(8,128)S(1)}, f32[256,1280]{1,0:T(8,128)S(1)}, u32[]{:S(2)}, u32[]{:S(2)}) collective-permute-start(f32[256,1280]{1,0:T(8,128)S(1)} %get-tuple-element.132), channel_id=1, source_target_pairs={{0,6},{1,7},{2,0},{3,1},{4,2},{5,3},{6,4},{7,5},{8,14},{9,15},{10,... | collective-permute-start | bytes 3932168 | tf_op jit(solution)/shard_map/ppermute | solution.py:53
  162.3 7.3 %collective-permute-start.35 = (f32[32,1024]{1,0:T(8,128)S(1)}, f32[32,1024]{1,0:T(8,128)S(1)}, u32[]{:S(2)}, u32[]{:S(2)}) collective-permute-start(f32[32,1024]{1,0:T(8,128)S(1)} %add.84), channel_id=1, source_target_pairs={{0,96},{1,25},{2,98},{3,27},{4,100},{5,29},{6,102},{7,31},{8,104},... | collective-permute-start | bytes 393224 | tf_op jit(solution)/shard_map/ppermute | solution.py:53
  167.9 1.7 collective-permute-start.33
  170.3 24.3 %collective-permute-start.36 = (f32[8,1280]{1,0:T(8,128)S(1)}, f32[8,1280]{1,0:T(8,128)S(1)}, u32[]{:S(2)}, u32[]{:S(2)}) collective-permute-start(f32[8,1280]{1,0:T(8,128)S(1)} %add.85.last), channel_id=1, source_target_pairs={{0,2},{1,3},{2,4},{3,5},{4,6},{5,7},{6,0},{7,1},{8,10},{9,11},{10,... | collective-permute-start | bytes 122888 | tf_op jit(solution)/shard_map/ppermute | solution.py:53
  170.3 24.3 %collective-permute-start.37 = (f32[8,1280]{1,0:T(8,128)S(1)}, f32[8,1280]{1,0:T(8,128)S(1)}, u32[]{:S(2)}, u32[]{:S(2)}) collective-permute-start(f32[8,1280]{1,0:T(8,128)S(1)} %add.85.last), channel_id=1, source_target_pairs={{0,4},{1,5},{2,6},{3,7},{4,0},{5,1},{6,2},{7,3},{8,12},{9,13},{10,... | collective-permute-start | bytes 122888 | tf_op jit(solution)/shard_map/ppermute | solution.py:53
  171.7 22.8 %collective-permute-start.38 = (f32[8,1280]{1,0:T(8,128)S(1)}, f32[8,1280]{1,0:T(8,128)S(1)}, u32[]{:S(2)}, u32[]{:S(2)}) collective-permute-start(f32[8,1280]{1,0:T(8,128)S(1)} %add.85.last), channel_id=1, source_target_pairs={{0,6},{1,7},{2,0},{3,1},{4,2},{5,3},{6,4},{7,5},{8,14},{9,15},{10,... | collective-permute-start | bytes 122888 | tf_op jit(solution)/shard_map/ppermute | solution.py:53
